TPU v7x, 32 devices: a whole 2x2x4 slice. The times are simulated.
32 devices in a mesh: rep: 4 (over y, x), fsdp: 8 (over z, core).
Axes of the slice: x: 2, y: 2, z: 4, core: 2. Of those that a mesh axis runs over, the one named last changes fastest.
Arguments:
- tokens_in: bfloat16 [8192, 768], P(('rep', 'fsdp')), may hold values from -6 to 6
- masked_flags: int32 [8192], P(('rep', 'fsdp')), may hold values 0 or 1
- mask_embedding: bfloat16 [768], replicated, may hold values from -6 to 6
- out_cotangent: bfloat16 [8192, 768], P(('rep', 'fsdp')), may hold values from -6 to 6
- w_qkv: float32 [2, 768, 2304], P(None, 'fsdp'), may hold values from -0.21875 to 0.21875
- m_qkv: float32 [2, 768, 2304], P(None, 'fsdp'), may hold values from -0.00011507027 to 0.00011507027
- v_qkv: float32 [2, 768, 2304], P(None, 'fsdp'), may hold values from 5.2964664e-11 to 2.1185866e-10
- w_out: float32 [2, 768, 768], P(None, 'fsdp'), may hold values from -0.4375 to 0.4375
- m_out: float32 [2, 768, 768], P(None, 'fsdp'), may hold values from -0.00011507027 to 0.00011507027
- v_out: float32 [2, 768, 768], P(None, 'fsdp'), may hold values from 5.2964664e-11 to 2.1185866e-10
- w_gu: float32 [2, 768, 6144], P(None, 'fsdp'), may hold values from -0.21875 to 0.21875
- m_gu: float32 [2, 768, 6144], P(None, 'fsdp'), may hold values from -0.00011507027 to 0.00011507027
- v_gu: float32 [2, 768, 6144], P(None, 'fsdp'), may hold values from 5.2964664e-11 to 2.1185866e-10
- w_down: float32 [2, 3072, 768], P(None, 'fsdp'), may hold values from -0.109375 to 0.109375
- m_down: float32 [2, 3072, 768], P(None, 'fsdp'), may hold values from -0.00011507027 to 0.00011507027
- v_down: float32 [2, 3072, 768], P(None, 'fsdp'), may hold values from 5.2964664e-11 to 2.1185866e-10
- norm_params: float32 [2, 4, 768], P(None, None, 'fsdp'), may hold values from -1 to 2
- m_norms: float32 [2, 4, 768], P(None, None, 'fsdp'), may hold values from -0.00046028107 to 0.00046028107
- v_norms: float32 [2, 4, 768], P(None, None, 'fsdp'), may hold values from 8.474346e-10 to 3.3897385e-09
Outputs:
- activations: bfloat16 [8192, 768], P(('rep', 'fsdp'))
- input_grad: float32 [8192, 768], P(('rep', 'fsdp'))
- grad_norm: float32 [], replicated
- new_w_qkv: float32 [2, 768, 2304], P(None, 'fsdp')
- new_m_qkv: float32 [2, 768, 2304], P(None, 'fsdp')
- new_v_qkv: float32 [2, 768, 2304], P(None, 'fsdp')
- new_w_out: float32 [2, 768, 768], P(None, 'fsdp')
- new_m_out: float32 [2, 768, 768], P(None, 'fsdp')
- new_v_out: float32 [2, 768, 768], P(None, 'fsdp')
- new_w_gu: float32 [2, 768, 6144], P(None, 'fsdp')
- new_m_gu: float32 [2, 768, 6144], P(None, 'fsdp')
- new_v_gu: float32 [2, 768, 6144], P(None, 'fsdp')
- new_w_down: float32 [2, 3072, 768], P(None, 'fsdp')
- new_m_down: float32 [2, 3072, 768], P(None, 'fsdp')
- new_v_down: float32 [2, 3072, 768], P(None, 'fsdp')
- new_norms: float32 [2, 4, 768], P(None, None, 'fsdp')
- new_m_norms: float32 [2, 4, 768], P(None, None, 'fsdp')
- new_v_norms: float32 [2, 4, 768], P(None, None, 'fsdp')
All inputs are finite; a program needn't handle non-finite values. No bound on the sum of `masked_flags` on one device may be relied on, other than what follows from the above.
Results may differ from a plain program's by a relative error of at most 0.025.
Values may be sent and summed in bfloat16 or wider, within the bound.
No kernel may reach another device: no remote copies, remote signals or barrier semaphores. Data moves between devices by JAX's collectives and lax.ppermute only.
A program may use at most 256 MiB of HBM per device.

v0:
```python
import jax
import jax.numpy as jnp
from jax import lax
from jax.sharding import PartitionSpec as P

D = 768
HEADS = 12
HEAD_DIM = 64
FF = 3072
SEQ_LEN = 128
STEP = 10


beta_first = 0.9
beta_second = 0.999
adam_eps = 1e-08
clip_norm = 1.0
rate_matrix = 0.03
rate_norm = 0.5
decay_matrix = 0.01
norm_eps = 1e-05


def alibi_bias(length, head_count):
    slopes = 2.0 ** (-8.0 * (jnp.arange(head_count).astype(jnp.float32) + 1.0) / head_count)
    places = jnp.arange(length).astype(jnp.float32)
    distance = jnp.abs(places[:, None] - places[None, :])
    return -slopes[:, None, None] * distance[None, :, :]


def layer_norm(values_in, norm_gain, norm_shift):
    center = values_in - jnp.mean(values_in, axis=-1, keepdims=True)
    spread = jnp.mean(center * center, axis=-1, keepdims=True)
    return center * lax.rsqrt(spread + norm_eps) * norm_gain + norm_shift


def gelu_gate(gate_part, up_part):
    return jax.nn.gelu(gate_part, approximate=False) * up_part


def outer_sum(left_rows, right_rows):
    return lax.dot_general(
        left_rows, right_rows, (((0,), (0,)), ((), ())), preferred_element_type=jnp.float32
    )


def back_product(gradient, weight):
    return lax.dot_general(
        gradient, weight, (((1,), (1,)), ((), ())), preferred_element_type=jnp.float32
    )


def split_heads(qkv_low):
    sections = qkv_low.reshape(-1, SEQ_LEN, 3, HEADS, HEAD_DIM)
    return (sections[:, :, 0], sections[:, :, 1], sections[:, :, 2])


def score_block(query_rows, key_rows):
    raw_scores = jnp.einsum(
        "sqhd,skhd->shqk", query_rows, key_rows, preferred_element_type=jnp.float32
    )
    return raw_scores * HEAD_DIM ** (-0.5) + alibi_bias(SEQ_LEN, HEADS)[None]


def forward_layer(hidden, weights):
    weight_qkv, weight_out, weight_gu, weight_down, norm_low = weights
    norm_set = norm_low.astype(jnp.float32)
    inputs_low = hidden.astype(jnp.bfloat16)
    qkv_low = jnp.dot(inputs_low, weight_qkv, preferred_element_type=jnp.float32).astype(
        jnp.bfloat16
    )
    query_rows, key_rows, value_rows = split_heads(qkv_low)
    scores = score_block(query_rows, key_rows)
    summit = jnp.max(scores, axis=-1, keepdims=True)
    log_total = summit + jnp.log(jnp.sum(jnp.exp(scores - summit), axis=-1, keepdims=True))
    attention = jnp.exp(scores - log_total)
    mixture = jnp.einsum(
        "shqk,skhd->sqhd",
        attention.astype(jnp.bfloat16),
        value_rows,
        preferred_element_type=jnp.float32,
    )
    mixture_low = mixture.reshape(hidden.shape[0], D).astype(jnp.bfloat16)
    residual_one = hidden + jnp.dot(mixture_low, weight_out, preferred_element_type=jnp.float32)
    normed_one = layer_norm(residual_one, norm_set[0], norm_set[1])
    normed_low = normed_one.astype(jnp.bfloat16)
    gate_up = jnp.dot(normed_low, weight_gu, preferred_element_type=jnp.float32)
    product_low = gelu_gate(gate_up[:, :FF], gate_up[:, FF:]).astype(jnp.bfloat16)
    residual_two = normed_one + jnp.dot(
        product_low, weight_down, preferred_element_type=jnp.float32
    )
    result = layer_norm(residual_two, norm_set[2], norm_set[3])
    kept_state = (
        inputs_low,
        qkv_low,
        log_total,
        mixture_low,
        residual_one,
        normed_low,
        gate_up,
        product_low,
        residual_two,
    )
    return (result, kept_state)


def backward_layer(grad_result, weights, kept_state):
    weight_qkv, weight_out, weight_gu, weight_down, norm_low = weights
    norm_set = norm_low.astype(jnp.float32)
    (
        inputs_low,
        qkv_low,
        log_total,
        mixture_low,
        residual_one,
        normed_low,
        gate_up,
        product_low,
        residual_two,
    ) = kept_state
    _, pull_two = jax.vjp(layer_norm, residual_two, norm_set[2], norm_set[3])
    grad_two, gain_two, shift_two = pull_two(grad_result)
    branch_low = grad_two.astype(jnp.bfloat16)
    grad_down = outer_sum(product_low, branch_low)
    product_grad = back_product(branch_low, weight_down).astype(jnp.bfloat16).astype(jnp.float32)
    _, pull_gate = jax.vjp(gelu_gate, gate_up[:, :FF], gate_up[:, FF:])
    grad_gate, grad_up = pull_gate(product_grad)
    gate_up_low = jnp.concatenate([grad_gate, grad_up], axis=1).astype(jnp.bfloat16)
    grad_gu = outer_sum(normed_low, gate_up_low)
    grad_normed = grad_two + back_product(gate_up_low, weight_gu)
    _, pull_one = jax.vjp(layer_norm, residual_one, norm_set[0], norm_set[1])
    grad_one, gain_one, shift_one = pull_one(grad_normed)
    attend_low = grad_one.astype(jnp.bfloat16)
    grad_out_weight = outer_sum(mixture_low, attend_low)
    mixture_grad = (
        back_product(attend_low, weight_out)
        .astype(jnp.bfloat16)
        .reshape(-1, SEQ_LEN, HEADS, HEAD_DIM)
    )
    query_rows, key_rows, value_rows = split_heads(qkv_low)
    attention = jnp.exp(score_block(query_rows, key_rows) - log_total)
    attention_grad = jnp.einsum(
        "sqhd,skhd->shqk", mixture_grad, value_rows, preferred_element_type=jnp.float32
    )
    value_grad = jnp.einsum(
        "shqk,sqhd->skhd",
        attention.astype(jnp.bfloat16),
        mixture_grad,
        preferred_element_type=jnp.float32,
    )
    score_grad = attention * (
        attention_grad - jnp.sum(attention * attention_grad, axis=-1, keepdims=True)
    )
    score_low = score_grad.astype(jnp.bfloat16)
    query_grad = jnp.einsum(
        "shqk,skhd->sqhd", score_low, key_rows, preferred_element_type=jnp.float32
    ) * HEAD_DIM ** (-0.5)
    key_grad = jnp.einsum(
        "shqk,sqhd->skhd", score_low, query_rows, preferred_element_type=jnp.float32
    ) * HEAD_DIM ** (-0.5)
    qkv_grad = (
        jnp.stack([query_grad, key_grad, value_grad], axis=2)
        .reshape(inputs_low.shape[0], 3 * D)
        .astype(jnp.bfloat16)
    )
    grad_qkv = outer_sum(inputs_low, qkv_grad)
    grad_input = grad_one + back_product(qkv_grad, weight_qkv)
    grad_norms = jnp.stack([gain_one, shift_one, gain_two, shift_two])
    return (grad_input, (grad_qkv, grad_out_weight, grad_gu, grad_down, grad_norms))


def adam_step(weight, first_moment, second_moment, gradient, factor, step_rate, decay_rate):
    gradient = gradient * factor
    first_moment = beta_first * first_moment + (1.0 - beta_first) * gradient
    second_moment = beta_second * second_moment + (1.0 - beta_second) * gradient * gradient
    first_hat = first_moment / (1.0 - beta_first**STEP)
    second_hat = second_moment / (1.0 - beta_second**STEP)
    weight = weight - step_rate * (
        first_hat / (jnp.sqrt(second_hat) + adam_eps) + decay_rate * weight
    )
    return (weight, first_moment, second_moment)


def rep_share(values_in, share_dim, share_index, share_count):
    width = values_in.shape[share_dim] // share_count
    return lax.dynamic_slice_in_dim(values_in, share_index * width, width, share_dim)


def body(
    tokens_in,
    masked_flags,
    mask_embedding,
    out_cotangent,
    w_qkv,
    m_qkv,
    v_qkv,
    w_out,
    m_out,
    v_out,
    w_gu,
    m_gu,
    v_gu,
    w_down,
    m_down,
    v_down,
    norm_params,
    m_norms,
    v_norms,
):
    layer_count = w_qkv.shape[0]
    masked = masked_flags[:, None] == 1
    hidden = jnp.where(
        masked, mask_embedding.astype(jnp.float32)[None, :], tokens_in.astype(jnp.float32)
    )
    kept_list = []
    for layer_index in range(layer_count):
        weights = (
            lax.all_gather(w_qkv[layer_index].astype(jnp.bfloat16), "fsdp", axis=0, tiled=True),
            lax.all_gather(w_out[layer_index].astype(jnp.bfloat16), "fsdp", axis=0, tiled=True),
            lax.all_gather(w_gu[layer_index].astype(jnp.bfloat16), "fsdp", axis=0, tiled=True),
            lax.all_gather(w_down[layer_index].astype(jnp.bfloat16), "fsdp", axis=0, tiled=True),
            lax.all_gather(
                norm_params[layer_index].astype(jnp.bfloat16), "fsdp", axis=1, tiled=True
            ),
        )
        hidden, kept_state = forward_layer(hidden, weights)
        kept_list.append(kept_state)
    activations = hidden.astype(jnp.bfloat16)
    grad_hidden = out_cotangent.astype(jnp.float32) * masked_flags[:, None].astype(jnp.float32)
    shard_list = [None] * layer_count
    for layer_index in reversed(range(layer_count)):
        weights = (
            lax.all_gather(w_qkv[layer_index].astype(jnp.bfloat16), "fsdp", axis=0, tiled=True),
            lax.all_gather(w_out[layer_index].astype(jnp.bfloat16), "fsdp", axis=0, tiled=True),
            lax.all_gather(w_gu[layer_index].astype(jnp.bfloat16), "fsdp", axis=0, tiled=True),
            lax.all_gather(w_down[layer_index].astype(jnp.bfloat16), "fsdp", axis=0, tiled=True),
            lax.all_gather(
                norm_params[layer_index].astype(jnp.bfloat16), "fsdp", axis=1, tiled=True
            ),
        )
        grad_hidden, local_grads = backward_layer(grad_hidden, weights, kept_list[layer_index])
        shard_list[layer_index] = (
            lax.psum_scatter(local_grads[0], "fsdp", scatter_dimension=0, tiled=True),
            lax.psum_scatter(local_grads[1], "fsdp", scatter_dimension=0, tiled=True),
            lax.psum_scatter(local_grads[2], "fsdp", scatter_dimension=0, tiled=True),
            lax.psum_scatter(local_grads[3], "fsdp", scatter_dimension=0, tiled=True),
            lax.psum_scatter(local_grads[4], "fsdp", scatter_dimension=1, tiled=True),
        )
    shards = tuple(
        (
            jnp.stack([shard_list[layer_index][kind_index] for layer_index in range(layer_count)])
            for kind_index in range(5)
        )
    )
    reduced = (
        lax.psum_scatter(shards[0], "rep", scatter_dimension=2, tiled=True),
        lax.psum_scatter(shards[1], "rep", scatter_dimension=2, tiled=True),
        lax.psum_scatter(shards[2], "rep", scatter_dimension=2, tiled=True),
        lax.psum_scatter(shards[3], "rep", scatter_dimension=2, tiled=True),
        lax.psum_scatter(shards[4], "rep", scatter_dimension=1, tiled=True),
    )
    squares = jnp.float32(0.0)
    for piece_grad in reduced:
        squares = squares + jnp.sum(piece_grad * piece_grad)
    total_squares = lax.psum(squares, ("rep", "fsdp"))
    grad_norm = jnp.sqrt(total_squares)
    factor = clip_norm / jnp.maximum(grad_norm, clip_norm)
    rep_index = lax.axis_index("rep")
    rep_count = lax.axis_size("rep")

    def owned(values_in, share_dim):
        return rep_share(values_in, share_dim, rep_index, rep_count)

    new_qkv = adam_step(
        owned(w_qkv, 2),
        owned(m_qkv, 2),
        owned(v_qkv, 2),
        reduced[0],
        factor,
        rate_matrix,
        decay_matrix,
    )
    new_out = adam_step(
        owned(w_out, 2),
        owned(m_out, 2),
        owned(v_out, 2),
        reduced[1],
        factor,
        rate_matrix,
        decay_matrix,
    )
    new_gu = adam_step(
        owned(w_gu, 2),
        owned(m_gu, 2),
        owned(v_gu, 2),
        reduced[2],
        factor,
        rate_matrix,
        decay_matrix,
    )
    new_down = adam_step(
        owned(w_down, 2),
        owned(m_down, 2),
        owned(v_down, 2),
        reduced[3],
        factor,
        rate_matrix,
        decay_matrix,
    )
    new_norm = adam_step(
        owned(norm_params, 1),
        owned(m_norms, 1),
        owned(v_norms, 1),
        reduced[4],
        factor,
        rate_norm,
        0.0,
    )
    updated = (
        lax.all_gather(new_qkv[0], "rep", axis=2, tiled=True),
        lax.all_gather(new_qkv[1], "rep", axis=2, tiled=True),
        lax.all_gather(new_qkv[2], "rep", axis=2, tiled=True),
        lax.all_gather(new_out[0], "rep", axis=2, tiled=True),
        lax.all_gather(new_out[1], "rep", axis=2, tiled=True),
        lax.all_gather(new_out[2], "rep", axis=2, tiled=True),
        lax.all_gather(new_gu[0], "rep", axis=2, tiled=True),
        lax.all_gather(new_gu[1], "rep", axis=2, tiled=True),
        lax.all_gather(new_gu[2], "rep", axis=2, tiled=True),
        lax.all_gather(new_down[0], "rep", axis=2, tiled=True),
        lax.all_gather(new_down[1], "rep", axis=2, tiled=True),
        lax.all_gather(new_down[2], "rep", axis=2, tiled=True),
        lax.all_gather(new_norm[0], "rep", axis=1, tiled=True),
        lax.all_gather(new_norm[1], "rep", axis=1, tiled=True),
        lax.all_gather(new_norm[2], "rep", axis=1, tiled=True),
    )
    input_grad = jnp.where(masked, 0.0, grad_hidden)
    return (
        activations,
        input_grad,
        grad_norm,
        updated[0],
        updated[1],
        updated[2],
        updated[3],
        updated[4],
        updated[5],
        updated[6],
        updated[7],
        updated[8],
        updated[9],
        updated[10],
        updated[11],
        updated[12],
        updated[13],
        updated[14],
    )


def solution(mesh):
    return jax.shard_map(
        body,
        mesh=mesh,
        in_specs=(
            P(("rep", "fsdp"), None),
            P(("rep", "fsdp")),
            P(),
            P(("rep", "fsdp"), None),
            P(None, "fsdp", None),
            P(None, "fsdp", None),
            P(None, "fsdp", None),
            P(None, "fsdp", None),
            P(None, "fsdp", None),
            P(None, "fsdp", None),
            P(None, "fsdp", None),
            P(None, "fsdp", None),
            P(None, "fsdp", None),
            P(None, "fsdp", None),
            P(None, "fsdp", None),
            P(None, "fsdp", None),
            P(None, None, "fsdp"),
            P(None, None, "fsdp"),
            P(None, None, "fsdp"),
        ),
        out_specs=(
            P(("rep", "fsdp"), None),
            P(("rep", "fsdp"), None),
            P(),
            P(None, "fsdp", None),
            P(None, "fsdp", None),
            P(None, "fsdp", None),
            P(None, "fsdp", None),
            P(None, "fsdp", None),
            P(None, "fsdp", None),
            P(None, "fsdp", None),
            P(None, "fsdp", None),
            P(None, "fsdp", None),
            P(None, "fsdp", None),
            P(None, "fsdp", None),
            P(None, "fsdp", None),
            P(None, None, "fsdp"),
            P(None, None, "fsdp"),
            P(None, None, "fsdp"),
        ),
        check_vma=False,
    )
```

profile of v0, /device:TPU:0, one launch (start us, length us, event | category | flops | bytes accessed | tf_op | source)
XLA Modules:
  0.0 2044.5 jit_solution(3030323596174665837)
XLA Ops:
  20.9 17.8 all-gather.2
  39.0 10.9 slice_reduce_fusion.5
  50.0 15.8 all-gather.7
  66.2 10.9 slice_reduce_fusion.1
  88.3 86.7 %all-gather.50.cloned.1.call-done = bf16[1,768,6144]{2,1,0:T(8,128)(2,1)} async-done(((bf16[1,96,6144]{2,1,0:T(8,128)(2,1)}), bf16[1,768,6144]{2,1,0:T(8,128)(2,1)}) %all-gather.50.cloned.1.call-update) | async-done | bytes 9437200 | tf_op jit(solution)/shard_map/all_gather | solution.py:220
  183.0 7.8 multiply_convert_fusion.1
  190.8 36.4 %all-gather.52.cloned.1.call-done = bf16[1,3072,768]{2,1,0:T(8,128)(2,1)} async-done(((bf16[1,384,768]{2,1,0:T(8,128)(2,1)}), bf16[1,3072,768]{2,1,0:T(8,128)(2,1)}) %all-gather.52.cloned.1.call-update) | async-done | bytes 4718608 | tf_op jit(solution)/shard_map/all_gather | solution.py:221
  231.8 37.8 %all-gather.54.cloned.1.call-done = bf16[1,768,2304]{2,1,0:T(8,128)(2,1)} async-done(((bf16[1,96,2304]{2,1,0:T(8,128)(2,1)}), bf16[1,768,2304]{2,1,0:T(8,128)(2,1)}) %all-gather.54.cloned.1.call-update) | async-done | bytes 3538960 | tf_op jit(solution)/shard_map/all_gather | solution.py:218
  284.7 8.5 all-gather.56.cloned.1.call-done
  297.7 88.3 %all-gather.58.cloned.1.call-done = bf16[1,768,6144]{2,1,0:T(8,128)(2,1)} async-done(((bf16[1,96,6144]{2,1,0:T(8,128)(2,1)}), bf16[1,768,6144]{2,1,0:T(8,128)(2,1)}) %all-gather.58.cloned.1.call-update) | async-done | bytes 9437200 | tf_op jit(solution)/shard_map/all_gather | solution.py:220
  386.0 5.5 fusion.2
  394.2 7.8 multiply_convert_fusion
  402.1 36.4 %all-gather.60.cloned.1.call-done = bf16[1,3072,768]{2,1,0:T(8,128)(2,1)} async-done(((bf16[1,384,768]{2,1,0:T(8,128)(2,1)}), bf16[1,3072,768]{2,1,0:T(8,128)(2,1)}) %all-gather.60.cloned.1.call-update) | async-done | bytes 4718608 | tf_op jit(solution)/shard_map/all_gather | solution.py:221
  445.7 7.8 add_convert_fusion.1
  453.6 9.0 multiply_reduce_fusion.4
  484.7 8.2 add_convert_fusion
  501.7 5.6 fusion.85
  526.5 6.3 fusion.136
  534.2 6.2 fusion.137
  541.5 11.1 fusion.45
  554.1 10.7 fusion.44
  570.7 57.2 %reduce-scatter.24.cloned.1.call-done = f32[96,2304]{1,0:T(8,128)} async-done(((f32[768,2304]{1,0:T(8,128)}), f32[96,2304]{1,0:T(8,128)}) %reduce-scatter.24.cloned.1.call-update) | async-done | bytes 884752 | tf_op jit(solution)/shard_map/reduce_scatter | solution.py:243
  627.9 77.8 %reduce-scatter.22.cloned.1.call-done = f32[96,2304]{1,0:T(8,128)} async-done(((f32[768,2304]{1,0:T(8,128)}), f32[96,2304]{1,0:T(8,128)}) %reduce-scatter.22.cloned.1.call-update) | async-done | bytes 884752 | tf_op jit(solution)/shard_map/reduce_scatter | solution.py:243
  714.5 91.4 %reduce-scatter.38.cloned.1.call-done = f32[384,768]{1,0:T(8,128)} async-done(((f32[3072,768]{1,0:T(8,128)}), f32[384,768]{1,0:T(8,128)}) %reduce-scatter.38.cloned.1.call-update) | async-done | bytes 1179664 | tf_op jit(solution)/shard_map/reduce_scatter | solution.py:246
  805.9 100.1 %reduce-scatter.36.cloned.1.call-done = f32[384,768]{1,0:T(8,128)} async-done(((f32[3072,768]{1,0:T(8,128)}), f32[384,768]{1,0:T(8,128)}) %reduce-scatter.36.cloned.1.call-update) | async-done | bytes 1179664 | tf_op jit(solution)/shard_map/reduce_scatter | solution.py:246
  910.8 183.7 %reduce-scatter.32.cloned.1.call-done = f32[96,6144]{1,0:T(8,128)} async-done(((f32[768,6144]{1,0:T(8,128)}), f32[96,6144]{1,0:T(8,128)}) %reduce-scatter.32.cloned.1.call-update) | async-done | bytes 2359312 | tf_op jit(solution)/shard_map/reduce_scatter | solution.py:245
  1094.5 188.6 %reduce-scatter.30.cloned.1.call-done = f32[96,6144]{1,0:T(8,128)} async-done(((f32[768,6144]{1,0:T(8,128)}), f32[96,6144]{1,0:T(8,128)}) %reduce-scatter.30.cloned.1.call-update) | async-done | bytes 2359312 | tf_op jit(solution)/shard_map/reduce_scatter | solution.py:245
  1290.0 24.8 %reduce-scatter.46.cloned.1.call-done = f32[96,4]{1,0:T(8,128)} async-done(((f32[768,4]{1,0:T(8,128)}), f32[96,4]{1,0:T(8,128)}) %reduce-scatter.46.cloned.1.call-update) | async-done | bytes 1552
  1315.6 30.8 %reduce-scatter.44.cloned.1.call-done = f32[96,4]{1,0:T(8,128)} async-done(((f32[768,4]{1,0:T(8,128)}), f32[96,4]{1,0:T(8,128)}) %reduce-scatter.44.cloned.1.call-update) | async-done | bytes 1552
  1347.3 10.2 all-reduce.1
  1358.7 15.5 reduce-scatter.42.cloned.1.call-done
  1376.1 39.0 %reduce-scatter.40.cloned.1.call-done = f32[576,192]{1,0:T(8,128)} async-done(((f32[2304,192]{1,0:T(8,128)}), f32[576,192]{1,0:T(8,128)}) %reduce-scatter.40.cloned.1.call-update) | async-done | bytes 442384
  1418.8 74.0 %all-reduce.4.cloned.1.call-done = f32[2,384,768]{1,0,2:T(2,128)} async-done(((f32[2,384,768]{1,0,2:T(2,128)}), f32[2,384,768]{1,0,2:T(2,128)}) %all-reduce.4.cloned.1.call-update) | async-done | bytes 2359312
  1495.2 58.6 %reduce-scatter.34.cloned.1.call-done = f32[2,96,1536]{2,1,0:T(8,128)} async-done(((f32[2,96,6144]{2,1,0:T(8,128)}), f32[2,96,1536]{2,1,0:T(8,128)}) %reduce-scatter.34.cloned.1.call-update) | async-done | bytes 1179664 | tf_op jit(solution)/shard_map/reduce_scatter | solution.py:258
  1557.9 39.4 %psum.7 = f32[]{:T(128)} all-reduce(f32[]{:T(128)S(6)} %add.335), channel_id=1, replica_groups=mesh['rep'=4,'fsdp'=8] {'rep','fsdp'}, use_global_device_ids=true, to_apply=%region_50.51 | all-reduce | flops 1 | bytes 8 | tf_op jit(solution)/shard_map/psum | solution.py:265
  1631.9 15.3 all_gather.98
  1648.4 16.5 all_gather.99
  1666.3 13.1 all_gather.100
  1681.1 9.0 all_gather.107
  1690.8 6.5 all_gather.108
  1697.9 8.6 all_gather.109
  1715.3 13.3 all-gather.32.cloned.1.call-done
  1732.8 35.8 %all-gather.40.cloned.1.call-done = f32[2,384,768]{1,0,2:T(2,128)} async-done(((f32[2,384,192]{1,0,2:T(2,128)}), f32[2,384,768]{1,0,2:T(2,128)}) %all-gather.40.cloned.1.call-update) | async-done | bytes 2359312 | tf_op jit(solution)/shard_map/all_gather | solution.py:329
  1773.9 34.0 %all-gather.42.cloned.1.call-done = f32[2,384,768]{1,0,2:T(2,128)} async-done(((f32[2,384,192]{1,0,2:T(2,128)}), f32[2,384,768]{1,0,2:T(2,128)}) %all-gather.42.cloned.1.call-update) | async-done | bytes 2359312 | tf_op jit(solution)/shard_map/all_gather | solution.py:330
  1813.3 34.2 %all-gather.44.cloned.1.call-done = f32[2,384,768]{1,0,2:T(2,128)} async-done(((f32[2,384,192]{1,0,2:T(2,128)}), f32[2,384,768]{1,0,2:T(2,128)}) %all-gather.44.cloned.1.call-update) | async-done | bytes 2359312 | tf_op jit(solution)/shard_map/all_gather | solution.py:331
  1852.8 54.4 %all-gather.34.cloned.1.call-done = f32[2,96,6144]{2,1,0:T(8,128)} async-done(((f32[2,96,1536]{2,1,0:T(8,128)}), f32[2,96,6144]{2,1,0:T(8,128)}) %all-gather.34.cloned.1.call-update) | async-done | bytes 4718608 | tf_op jit(solution)/shard_map/all_gather | solution.py:326
  1907.1 59.5 %all-gather.36.cloned.1.call-done = f32[2,96,6144]{2,1,0:T(8,128)} async-done(((f32[2,96,1536]{2,1,0:T(8,128)}), f32[2,96,6144]{2,1,0:T(8,128)}) %all-gather.36.cloned.1.call-update) | async-done | bytes 4718608 | tf_op jit(solution)/shard_map/all_gather | solution.py:327
  1966.6 59.1 %all-gather.38.cloned.1.call-done = f32[2,96,6144]{2,1,0:T(8,128)} async-done(((f32[2,96,1536]{2,1,0:T(8,128)}), f32[2,96,6144]{2,1,0:T(8,128)}) %all-gather.38.cloned.1.call-update) | async-done | bytes 4718608 | tf_op jit(solution)/shard_map/all_gather | solution.py:328
  (464 shorter events, 236.2 us)
Async XLA Ops:
  7.2 70.1 %all-gather.46.cloned.1.call-start = ((), (), s32[]{:S(2)}) async-start(), calls=%async_computation.31 | async-start | bytes 3981312 | tf_op jit(solution)/shard_map/all_gather | solution.py:218
  9.9 76.1 %all-gather.48.cloned.1.call-start = ((), (), s32[]{:S(2)}) async-start(), calls=%async_computation.32 | async-start | bytes 1327104 | tf_op jit(solution)/shard_map/all_gather | solution.py:219
  10.7 164.2 %all-gather.50.cloned.1.call-start = ((), (), s32[]{:S(2)}) async-start(), calls=%async_computation.33 | async-start | bytes 10616832 | tf_op jit(solution)/shard_map/all_gather | solution.py:220
  15.1 212.1 %all-gather.52.cloned.1.call-start = ((), (), s32[]{:S(2)}) async-start(), calls=%async_computation.34 | async-start | bytes 5308416 | tf_op jit(solution)/shard_map/all_gather | solution.py:221
  17.2 252.4 %all-gather.54.cloned.1.call-start = ((), (), s32[]{:S(2)}) async-start(), calls=%async_computation.35 | async-start | bytes 3981312 | tf_op jit(solution)/shard_map/all_gather | solution.py:218
  17.8 275.5 %all-gather.56.cloned.1.call-start = ((), (), s32[]{:S(2)}) async-start(), calls=%async_computation.36 | async-start | bytes 1327104 | tf_op jit(solution)/shard_map/all_gather | solution.py:219
  18.4 367.6 %all-gather.58.cloned.1.call-start = ((), (), s32[]{:S(2)}) async-start(), calls=%async_computation.37 | async-start | bytes 10616832 | tf_op jit(solution)/shard_map/all_gather | solution.py:220
  19.1 419.3 %all-gather.60.cloned.1.call-start = ((), (), s32[]{:S(2)}) async-start(), calls=%async_computation.38 | async-start | bytes 5308416 | tf_op jit(solution)/shard_map/all_gather | solution.py:221
  19.9 547.8 %reduce-scatter.28.cloned.1.call-start = ((), (), s32[]{:S(2)}) async-start(), calls=%async_computation.16 | async-start | bytes 2654208 | tf_op jit(solution)/shard_map/reduce_scatter | solution.py:244
  20.0 57.3 %copy-start.93 = (pred[256]{0:T(512)(128)(4,1)}, pred[256]{0:T(512)(128)(4,1)S(1)}, u32[]{:S(2)}) copy-start(pred[256]{0:T(512)(128)(4,1)S(1)} %broadcast_compare_fusion) | copy-start | bytes 772
  20.5 56.8 %copy-start.61 = (f32[768]{0:T(1024)}, f32[768]{0:T(1024)S(1)}, u32[]{:S(2)}) copy-start(f32[768]{0:T(1024)S(1)} %convert_element_type.198) | copy-start | bytes 9220
  20.9 56.5 %copy-start.42 = (bf16[256,768]{1,0:T(8,128)(2,1)S(1)}, bf16[256,768]{1,0:T(8,128)(2,1)}, u32[]{:S(2)}) copy-start(bf16[256,768]{1,0:T(8,128)(2,1)} %param.19) | copy-start | bytes 1179652
  88.0 139.2 %copy-start.2 = (f32[256,768]{1,0:T(8,128)}, f32[256,768]{1,0:T(8,128)S(1)}, u32[]{:S(2)}) copy-start(f32[256,768]{1,0:T(8,128)S(1)} %get-tuple-element.145) | copy-start | bytes 2359300
  88.0 92.2 %copy-start.50 = (f32[256]{0:T(256)}, f32[256]{0:T(256)S(1)}, u32[]{:S(2)}) copy-start(f32[256]{0:T(256)S(1)} %broadcast_multiply_fusion.4) | copy-start | bytes 3076
  88.2 92.0 %copy-start.72 = (f32[256]{0:T(256)}, f32[256]{0:T(256)S(1)}, u32[]{:S(2)}) copy-start(f32[256]{0:T(256)S(1)} %multiply_reduce_fusion.14) | copy-start | bytes 3076
  88.3 92.0 %copy-start.56 = (f32[256]{0:T(256)}, f32[256]{0:T(256)S(1)}, u32[]{:S(2)}) copy-start(f32[256]{0:T(256)S(1)} %fusion.128) | copy-start | bytes 3076
  231.5 42.3 %copy-start.7 = (f32[256,768]{1,0:T(8,128)}, f32[256,768]{1,0:T(8,128)S(1)}, u32[]{:S(2)}) copy-start(f32[256,768]{1,0:T(8,128)S(1)} %get-tuple-element.147) | copy-start | bytes 2359300
  231.5 42.3 %copy-start.64 = (f32[256]{0:T(256)}, f32[256]{0:T(256)S(1)}, u32[]{:S(2)}) copy-start(f32[256]{0:T(256)S(1)} %broadcast_multiply_fusion.3) | copy-start | bytes 3076
  231.8 42.1 %copy-start.74 = (f32[256]{0:T(256)}, f32[256]{0:T(256)S(1)}, u32[]{:S(2)}) copy-start(f32[256]{0:T(256)S(1)} %multiply_reduce_fusion.13) | copy-start | bytes 3076
  231.8 42.1 %copy-start.67 = (f32[256]{0:T(256)}, f32[256]{0:T(256)S(1)}, u32[]{:S(2)}) copy-start(f32[256]{0:T(256)S(1)} %fusion.129) | copy-start | bytes 3076
  444.4 9.1 slice-start.7
  453.6 9.0 copy-start.77
  453.6 10.2 copy-start.40
  475.6 92.0 %reduce-scatter.26.cloned.1.call-start = ((), (), s32[]{:S(2)}) async-start(), calls=%async_computation.15 | async-start | bytes 2654208 | tf_op jit(solution)/shard_map/reduce_scatter | solution.py:244
  483.4 9.5 slice-start.4
  483.7 9.1 copy-start.33
  483.7 9.1 copy-start.85
  501.6 126.3 %reduce-scatter.24.cloned.1.call-start = ((), (), s32[]{:S(2)}) async-start(), calls=%async_computation.14 | async-start | bytes 7962624 | tf_op jit(solution)/shard_map/reduce_scatter | solution.py:243
  507.3 198.4 %reduce-scatter.22.cloned.1.call-start = ((), (), s32[]{:S(2)}) async-start(), calls=%async_computation.13 | async-start | bytes 7962624 | tf_op jit(solution)/shard_map/reduce_scatter | solution.py:243
  525.1 280.8 %reduce-scatter.38.cloned.1.call-start = ((), (), s32[]{:S(2)}) async-start(), calls=%async_computation.21 | async-start | bytes 10616832 | tf_op jit(solution)/shard_map/reduce_scatter | solution.py:246
  532.8 373.1 %reduce-scatter.36.cloned.1.call-start = ((), (), s32[]{:S(2)}) async-start(), calls=%async_computation.20 | async-start | bytes 10616832 | tf_op jit(solution)/shard_map/reduce_scatter | solution.py:246
  540.4 554.1 %reduce-scatter.32.cloned.1.call-start = ((), (), s32[]{:S(2)}) async-start(), calls=%async_computation.18 | async-start | bytes 21233664 | tf_op jit(solution)/shard_map/reduce_scatter | solution.py:245
  552.7 730.4 %reduce-scatter.30.cloned.1.call-start = ((), (), s32[]{:S(2)}) async-start(), calls=%async_computation.17 | async-start | bytes 21233664 | tf_op jit(solution)/shard_map/reduce_scatter | solution.py:245
  564.8 749.9 %reduce-scatter.46.cloned.1.call-start = ((), (), s32[]{:S(2)}) async-start(), calls=%async_computation.42 | async-start | bytes 442368
  566.5 779.9 %reduce-scatter.44.cloned.1.call-start = ((), (), s32[]{:S(2)}) async-start(), calls=%async_computation.41 | async-start | bytes 442368
  567.6 806.6 %reduce-scatter.42.cloned.1.call-start = ((), (), s32[]{:S(2)}) async-start(), calls=%async_computation.40 | async-start | bytes 983040
  570.6 844.5 %reduce-scatter.40.cloned.1.call-start = ((), (), s32[]{:S(2)}) async-start(), calls=%async_computation.39 | async-start | bytes 2949120
  714.4 778.5 %all-reduce.4.cloned.1.call-start = ((), (), s32[]{:S(2)}) async-start(), calls=%async_computation.43 | async-start | bytes 4718592
  910.8 643.0 %reduce-scatter.34.cloned.1.call-start = ((), (), s32[]{:S(2)}) async-start(), calls=%async_computation.19 | async-start | bytes 5898240 | tf_op jit(solution)/shard_map/reduce_scatter | solution.py:258
  1288.1 419.0 %all-gather.28.cloned.1.call-start = ((), (), s32[]{:S(2)}) async-start(), calls=%async_computation.22 | async-start | bytes 2949120 | tf_op jit(solution)/shard_map/all_gather | solution.py:320
  1602.9 108.3 %all-gather.30.cloned.1.call-start = ((), (), s32[]{:S(2)}) async-start(), calls=%async_computation.23 | async-start | bytes 2949120 | tf_op jit(solution)/shard_map/all_gather | solution.py:321
  1604.0 124.7 %all-gather.32.cloned.1.call-start = ((), (), s32[]{:S(2)}) async-start(), calls=%async_computation.24 | async-start | bytes 2949120 | tf_op jit(solution)/shard_map/all_gather | solution.py:322
  1605.1 163.5 %all-gather.40.cloned.1.call-start = ((), (), s32[]{:S(2)}) async-start(), calls=%async_computation.28 | async-start | bytes 2949120 | tf_op jit(solution)/shard_map/all_gather | solution.py:329
  1615.3 192.7 %all-gather.42.cloned.1.call-start = ((), (), s32[]{:S(2)}) async-start(), calls=%async_computation.29 | async-start | bytes 2949120 | tf_op jit(solution)/shard_map/all_gather | solution.py:330
  1617.7 229.8 %all-gather.44.cloned.1.call-start = ((), (), s32[]{:S(2)}) async-start(), calls=%async_computation.30 | async-start | bytes 2949120 | tf_op jit(solution)/shard_map/all_gather | solution.py:331
  1619.1 288.0 %all-gather.34.cloned.1.call-start = ((), (), s32[]{:S(2)}) async-start(), calls=%async_computation.25 | async-start | bytes 5898240 | tf_op jit(solution)/shard_map/all_gather | solution.py:326
  1623.6 343.1 %all-gather.36.cloned.1.call-start = ((), (), s32[]{:S(2)}) async-start(), calls=%async_computation.26 | async-start | bytes 5898240 | tf_op jit(solution)/shard_map/all_gather | solution.py:327
  1624.2 401.6 %all-gather.38.cloned.1.call-start = ((), (), s32[]{:S(2)}) async-start(), calls=%async_computation.27 | async-start | bytes 5898240 | tf_op jit(solution)/shard_map/all_gather | solution.py:328
  (96 other events, 321.1 us)
Sparse Core Ops, SparseCore 0:
  10.2 47.5 all-gather.45
  60.0 22.2 all-gather.47
  84.5 90.3 all-gather.49
  177.0 50.1 all-gather.51
  229.3 40.3 all-gather.53
  271.7 21.5 all-gather.55
  295.5 90.4 all-gather.57
  388.2 50.1 all-gather.59
  475.8 35.0 reduce-scatter.27
  513.6 35.3 reduce-scatter.25
  551.3 76.4 reduce-scatter.23
  630.1 75.5 reduce-scatter.21
  708.0 97.8 reduce-scatter.37
  808.0 97.8 reduce-scatter.35
  908.1 186.3 reduce-scatter.31
  1096.7 186.3 reduce-scatter.29
  1285.7 28.9 reduce-scatter.45
  1317.5 28.8 reduce-scatter.43
  1349.9 24.2 reduce-scatter.41
  1377.7 37.3 reduce-scatter.39
  1418.8 74.0 all-reduce.3
  1496.7 57.0 reduce-scatter.33
  1603.0 40.7 all-gather.27
  1646.2 42.5 all-gather.29
  1691.4 37.2 all-gather.31
  1731.1 37.4 all-gather.39
  1770.5 37.4 all-gather.41
  1809.9 37.4 all-gather.43
  1850.0 57.0 all-gather.33
  1909.5 57.0 all-gather.35
  1968.6 57.0 all-gather.37
where the time goes:
time: 2050 us; the launch traced here: 2040 us
  waiting for transfers between devices  1530 us (75%)
  blocking collectives  152 us (7%)
  local copies, waits for them, and re-layouts  146 us (7%)
  matrix products  133 us (6%)
  other arithmetic  59.2 us (3%)
  between operations  22.3 us (1%)
    reduce_scatter x2, waiting for transfers between devices, body(): lax.psum_scatter(local_grads[2], 'fsdp', scatter_dimension=0, tiled=True)  372 us
    reduce_scatter x2, waiting for transfers between devices, body(): lax.psum_scatter(local_grads[3], 'fsdp', scatter_dimension=0, tiled=True)  191 us
    unnamed x36, waiting for transfers between devices  188 us
    all_gather x2, waiting for transfers between devices, body(): lax.all_gather(w_gu[layer_index].astype(jnp.bfloat16), 'fsdp', axis=0, ti...  175 us
    reduce_scatter x2, waiting for transfers between devices, body(): lax.psum_scatter(local_grads[0], 'fsdp', scatter_dimension=0, tiled=True)  135 us
    unnamed x258, local copies, waits for them, and re-layouts  81 us
    all_gather x2, waiting for transfers between devices, body(): lax.all_gather(w_down[layer_index].astype(jnp.bfloat16), 'fsdp', axis=0,...  72.8 us
    all_gather x1, waiting for transfers between devices, body(): lax.all_gather(new_gu[1], 'rep', axis=2, tiled=True)  59.5 us
  transfers between devices with their start and end apart: 31, of which 25 were waited for; matrix products, arithmetic and copies ran while one was open for 13% of the time, Pallas kernels for 0%

commit v1 on v0

--- a/solution.py
+++ b/solution.py
@@ -1,6 +1,8 @@
 import jax
 import jax.numpy as jnp
 from jax import lax
+from jax.experimental import pallas as pl
+from jax.experimental.pallas import tpu as pltpu
 from jax.sharding import PartitionSpec as P
 
 D = 768
@@ -181,9 +183,218 @@
     return (weight, first_moment, second_moment)
 
 
-def rep_share(values_in, share_dim, share_index, share_count):
-    width = values_in.shape[share_dim] // share_count
-    return lax.dynamic_slice_in_dim(values_in, share_index * width, width, share_dim)
+both_axes = ("rep", "fsdp")
+
+
+def pairs_of(move):
+    found = []
+    for rep in range(4):
+        for shard in range(8):
+            target = move(rep // 2, rep % 2, shard // 2, shard % 2)
+            if target is not None:
+                to_y, to_x, to_z, to_c = target
+                found.append((rep * 8 + shard, (to_y * 2 + to_x) * 8 + to_z * 2 + to_c))
+    return found
+
+
+FLIP_CORE = pairs_of(lambda y, x, z, c: (y, x, z, 1 - c))
+FLIP_X = pairs_of(lambda y, x, z, c: (y, 1 - x, z, c))
+FLIP_Y = pairs_of(lambda y, x, z, c: (1 - y, x, z, c))
+FLIP_FIRST = pairs_of(lambda y, x, z, c: (y, 1 - x, z, c) if c == 0 else (1 - y, x, z, c))
+FLIP_SECOND = pairs_of(lambda y, x, z, c: (1 - y, x, z, c) if c == 0 else (y, 1 - x, z, c))
+Z_MATE = pairs_of(lambda y, x, z, c: (y, x, z ^ 1, c))
+Z_CROSS = pairs_of(lambda y, x, z, c: (y, x, 3 - z, c))
+Z_MIDDLE = pairs_of(lambda y, x, z, c: (y, x, 3 - z, c) if z in (1, 2) else None)
+Z_OUTWARD = pairs_of(lambda y, x, z, c: (y, x, z ^ 1, c) if z in (1, 2) else None)
+Z_INWARD = pairs_of(lambda y, x, z, c: (y, x, z ^ 1, c) if z in (0, 3) else None)
+
+
+def send(values, pairs):
+    return lax.ppermute(values, both_axes, pairs)
+
+
+def place():
+    rep = lax.axis_index("rep")
+    shard = lax.axis_index("fsdp")
+    y, x, z, c = rep // 2, rep % 2, shard // 2, shard % 2
+    first = jnp.where(c == 0, x, y)
+    second = jnp.where(c == 0, y, x)
+    return (z, c, first, second)
+
+
+def pick(values, index, axis):
+    return lax.dynamic_index_in_dim(values, index, axis, keepdims=False)
+
+
+def in_order(mine, other, bit):
+    return lax.dynamic_slice_in_dim(jnp.stack([mine, other, mine]), bit, 2, 0)
+
+
+def gather_chunk(own):
+    z, c, first, second = place()
+    quarter = pick(own, 2 * first + second, 0)
+    mate = send(quarter, Z_MATE)
+    pair = in_order(quarter, mate, z % 2)
+    got_middle = send(pair, Z_MIDDLE)
+    got_outward = send(got_middle, Z_OUTWARD)
+    inner = (z == 1) | (z == 2)
+    other = jnp.where(inner, got_middle, got_outward)
+    three = jnp.concatenate([mate[None], other])
+    six = jnp.stack([three, send(three, FLIP_SECOND)])
+    far = send(six, FLIP_FIRST)
+    return (own, six, far, send(own, FLIP_CORE), send(six, FLIP_CORE), send(far, FLIP_CORE))
+
+
+def assemble(pieces, kind):
+    count = pieces[0].shape[1]
+    rows = pieces[0].shape[2]
+    shapes = {
+        "attend": ((8 * rows, 3 * D), (8 * rows, D)),
+        "gate_up": ((8 * rows, 2 * FF),),
+        "down": ((8 * 4 * rows, D),),
+    }[kind]
+
+    def kernel(*refs):
+        in_refs, out_refs, sem = refs[:6], refs[6:-1], refs[-1]
+        z, c, first, second = place()
+        low = jnp.where(z < 2, 2, 0)
+        others = (z ^ 1, low, low + 1)
+
+        def copy(source, quarter, block, shard):
+            row = pl.multiple_of(shard * rows, rows)
+            if kind == "attend":
+
+                @pl.when(quarter < 3)
+                def _():
+                    column = pl.multiple_of(quarter * D, D)
+                    target = out_refs[0].at[pl.ds(row, rows), pl.ds(column, D)]
+                    pltpu.make_async_copy(source, target, sem).start()
+
+                @pl.when(quarter == 3)
+                def _():
+                    target = out_refs[1].at[pl.ds(row, rows), :]
+                    pltpu.make_async_copy(source, target, sem).start()
+
+            elif kind == "gate_up":
+                column = pl.multiple_of((quarter + 4 * block) * D, D)
+                target = out_refs[0].at[pl.ds(row, rows), pl.ds(column, D)]
+                pltpu.make_async_copy(source, target, sem).start()
+            else:
+                row = pl.multiple_of((shard * 4 + quarter) * rows, rows)
+                target = out_refs[0].at[pl.ds(row, rows), :]
+                pltpu.make_async_copy(source, target, sem).start()
+
+        for side in range(2):
+            own, six, far = in_refs[3 * side : 3 * side + 3]
+            core = c if side == 0 else 1 - c
+            high, little = (first, second) if side == 0 else (second, first)
+            for block in range(count):
+                for quarter in range(4):
+                    copy(own.at[quarter, block], jnp.int32(quarter), block, 2 * z + core)
+                for turn in range(2):
+                    unit = little if turn == 0 else 1 - little
+                    for step in range(3):
+                        shard = 2 * others[step] + core
+                        copy(six.at[turn, step, block], 2 * high + unit, block, shard)
+                        copy(far.at[turn, step, block], 2 * (1 - high) + unit, block, shard)
+        for out_ref in out_refs:
+            pltpu.make_async_copy(out_ref, out_ref, sem).wait()
+
+    return pl.pallas_call(
+        kernel,
+        out_shape=tuple(jax.ShapeDtypeStruct(shape, jnp.bfloat16) for shape in shapes),
+        in_specs=[pl.BlockSpec(memory_space=pl.ANY)] * 6,
+        out_specs=tuple(pl.BlockSpec(memory_space=pltpu.VMEM) for _ in shapes),
+        scratch_shapes=[pltpu.SemaphoreType.DMA],
+        compiler_params=pltpu.CompilerParams(vmem_limit_bytes=24 * 2**20),
+        name="assemble_" + kind,
+    )(*pieces)
+
+
+def add_low(left, right):
+    return (left.astype(jnp.float32) + right.astype(jnp.float32)).astype(jnp.bfloat16)
+
+
+def scatter_chunk(parts):
+    z, c, first, second = place()
+    count, rows = parts.shape[1], parts.shape[3]
+    parts = parts.reshape(2, 2, count, 4, 2, rows, D)
+    got = send(pick(parts, 1 - c, 4), FLIP_CORE)
+    parts = add_low(pick(parts, c, 4), got)
+    got = send(pick(parts, 1 - first, 0), FLIP_FIRST)
+    parts = add_low(pick(parts, first, 0), got)
+    parts = parts.reshape(2, count, 2, 2, rows, D)
+    theirs = pick(parts, 1 - z // 2, 2)
+    mine = pick(parts, z // 2, 2)
+    theirs = add_low(theirs, send(theirs, Z_INWARD))
+    mine = add_low(mine, send(theirs, Z_MIDDLE))
+    got = send(pick(mine, 1 - z % 2, 2), Z_MATE)
+    mine = add_low(pick(mine, z % 2, 2), got)
+    got = send(pick(mine, 1 - second, 0), FLIP_SECOND)
+    return add_low(pick(mine, second, 0), got)
+
+
+def spread_chunk(quarter):
+    z, c, first, second = place()
+    row = in_order(quarter, send(quarter, FLIP_SECOND), second)
+    whole = in_order(row, send(row, FLIP_FIRST), first)
+    return whole.reshape((4,) + quarter.shape)
+
+
+def sum_all(value):
+    for pairs in (FLIP_CORE, FLIP_X, FLIP_Y, Z_MATE, Z_CROSS):
+        value = value + send(value, pairs)
+    return value
+
+
+def by_neighbours():
+    return lax.axis_size("rep") == 4 and lax.axis_size("fsdp") == 8
+
+
+def gather_layer(w_qkv, w_out, w_gu, w_down):
+    low = [weight.astype(jnp.bfloat16) for weight in (w_qkv, w_out, w_gu, w_down)]
+    if not by_neighbours():
+        return tuple(lax.all_gather(weight, "fsdp", axis=0, tiled=True) for weight in low)
+    rows = w_qkv.shape[0]
+    attend = jnp.stack([low[0][:, :D], low[0][:, D : 2 * D], low[0][:, 2 * D :], low[1]])
+    gate_up = low[2].reshape(rows, 2, 4, D).transpose(2, 1, 0, 3)
+    down = low[3].reshape(4, 1, rows, D)
+    weight_qkv, weight_out = assemble(gather_chunk(attend[:, None]), "attend")
+    (weight_gu,) = assemble(gather_chunk(gate_up), "gate_up")
+    (weight_down,) = assemble(gather_chunk(down), "down")
+    return (weight_qkv, weight_out, weight_gu, weight_down)
+
+
+def reduce_layer(grad_qkv, grad_out, grad_gu, grad_down):
+    if not by_neighbours():
+        sums = []
+        squares = jnp.float32(0.0)
+        for grad in (grad_qkv, grad_out, grad_gu, grad_down):
+            part = lax.psum_scatter(grad, "fsdp", scatter_dimension=0, tiled=True)
+            part = lax.psum(part, "rep")
+            squares = squares + jnp.sum(part * part) / lax.axis_size("rep")
+            sums.append(part)
+        return (tuple(sums), squares)
+    rows = grad_qkv.shape[0] // 8
+    grad_qkv, grad_out, grad_gu, grad_down = (
+        grad.astype(jnp.bfloat16) for grad in (grad_qkv, grad_out, grad_gu, grad_down)
+    )
+    attend = jnp.stack(
+        [grad_qkv[:, :D], grad_qkv[:, D : 2 * D], grad_qkv[:, 2 * D :], grad_out]
+    ).reshape(4, 1, 8, rows, D)
+    gate_up = grad_gu.reshape(8, rows, 2, 4, D).transpose(3, 2, 0, 1, 4)
+    down = grad_down.reshape(8, 4, rows, D).transpose(1, 0, 2, 3)[:, None]
+    squares = jnp.float32(0.0)
+    sums = []
+    for chunk in (down, gate_up, attend):
+        quarter = scatter_chunk(chunk)
+        wide = quarter.astype(jnp.float32)
+        squares = squares + jnp.sum(wide * wide)
+        sums.append(spread_chunk(quarter))
+    down, gate_up, attend = sums
+    grad_qkv = jnp.concatenate([attend[0, 0], attend[1, 0], attend[2, 0]], axis=1)
+    grad_gu = gate_up.transpose(2, 1, 0, 3).reshape(rows, 2 * FF)
+    return ((grad_qkv, attend[3, 0], grad_gu, down.reshape(4 * rows, D)), squares)
 
 
 def body(
@@ -212,148 +423,46 @@
     hidden = jnp.where(
         masked, mask_embedding.astype(jnp.float32)[None, :], tokens_in.astype(jnp.float32)
     )
+    norm_low = lax.all_gather(norm_params.astype(jnp.bfloat16), "fsdp", axis=2, tiled=True)
     kept_list = []
-    for layer_index in range(layer_count):
-        weights = (
-            lax.all_gather(w_qkv[layer_index].astype(jnp.bfloat16), "fsdp", axis=0, tiled=True),
-            lax.all_gather(w_out[layer_index].astype(jnp.bfloat16), "fsdp", axis=0, tiled=True),
-            lax.all_gather(w_gu[layer_index].astype(jnp.bfloat16), "fsdp", axis=0, tiled=True),
-            lax.all_gather(w_down[layer_index].astype(jnp.bfloat16), "fsdp", axis=0, tiled=True),
-            lax.all_gather(
-                norm_params[layer_index].astype(jnp.bfloat16), "fsdp", axis=1, tiled=True
-            ),
-        )
+    weight_list = []
+    for layer in range(layer_count):
+        weights = gather_layer(w_qkv[layer], w_out[layer], w_gu[layer], w_down[layer])
+        weights = weights + (norm_low[layer],)
         hidden, kept_state = forward_layer(hidden, weights)
         kept_list.append(kept_state)
+        weight_list.append(weights)
     activations = hidden.astype(jnp.bfloat16)
     grad_hidden = out_cotangent.astype(jnp.float32) * masked_flags[:, None].astype(jnp.float32)
-    shard_list = [None] * layer_count
-    for layer_index in reversed(range(layer_count)):
-        weights = (
-            lax.all_gather(w_qkv[layer_index].astype(jnp.bfloat16), "fsdp", axis=0, tiled=True),
-            lax.all_gather(w_out[layer_index].astype(jnp.bfloat16), "fsdp", axis=0, tiled=True),
-            lax.all_gather(w_gu[layer_index].astype(jnp.bfloat16), "fsdp", axis=0, tiled=True),
-            lax.all_gather(w_down[layer_index].astype(jnp.bfloat16), "fsdp", axis=0, tiled=True),
-            lax.all_gather(
-                norm_params[layer_index].astype(jnp.bfloat16), "fsdp", axis=1, tiled=True
-            ),
+    grad_list = [None] * layer_count
+    norm_list = [None] * layer_count
+    squares = jnp.float32(0.0)
+    for layer in reversed(range(layer_count)):
+        grad_hidden, local_grads = backward_layer(
+            grad_hidden, weight_list[layer], kept_list[layer]
         )
-        grad_hidden, local_grads = backward_layer(grad_hidden, weights, kept_list[layer_index])
-        shard_list[layer_index] = (
-            lax.psum_scatter(local_grads[0], "fsdp", scatter_dimension=0, tiled=True),
-            lax.psum_scatter(local_grads[1], "fsdp", scatter_dimension=0, tiled=True),
-            lax.psum_scatter(local_grads[2], "fsdp", scatter_dimension=0, tiled=True),
-            lax.psum_scatter(local_grads[3], "fsdp", scatter_dimension=0, tiled=True),
-            lax.psum_scatter(local_grads[4], "fsdp", scatter_dimension=1, tiled=True),
-        )
-    shards = tuple(
-        (
-            jnp.stack([shard_list[layer_index][kind_index] for layer_index in range(layer_count)])
-            for kind_index in range(5)
-        )
-    )
-    reduced = (
-        lax.psum_scatter(shards[0], "rep", scatter_dimension=2, tiled=True),
-        lax.psum_scatter(shards[1], "rep", scatter_dimension=2, tiled=True),
-        lax.psum_scatter(shards[2], "rep", scatter_dimension=2, tiled=True),
-        lax.psum_scatter(shards[3], "rep", scatter_dimension=2, tiled=True),
-        lax.psum_scatter(shards[4], "rep", scatter_dimension=1, tiled=True),
-    )
-    squares = jnp.float32(0.0)
-    for piece_grad in reduced:
-        squares = squares + jnp.sum(piece_grad * piece_grad)
-    total_squares = lax.psum(squares, ("rep", "fsdp"))
-    grad_norm = jnp.sqrt(total_squares)
+        grad_list[layer], part = reduce_layer(*local_grads[:4])
+        squares = squares + part
+        norm_list[layer] = local_grads[4]
+    grad_norms = lax.psum(jnp.stack(norm_list), both_axes)
+    total = sum_all(squares) if by_neighbours() else lax.psum(squares, both_axes)
+    grad_norm = jnp.sqrt(total + jnp.sum(grad_norms * grad_norms))
     factor = clip_norm / jnp.maximum(grad_norm, clip_norm)
-    rep_index = lax.axis_index("rep")
-    rep_count = lax.axis_size("rep")
-
-    def owned(values_in, share_dim):
-        return rep_share(values_in, share_dim, rep_index, rep_count)
-
-    new_qkv = adam_step(
-        owned(w_qkv, 2),
-        owned(m_qkv, 2),
-        owned(v_qkv, 2),
-        reduced[0],
-        factor,
-        rate_matrix,
-        decay_matrix,
-    )
-    new_out = adam_step(
-        owned(w_out, 2),
-        owned(m_out, 2),
-        owned(v_out, 2),
-        reduced[1],
-        factor,
-        rate_matrix,
-        decay_matrix,
-    )
-    new_gu = adam_step(
-        owned(w_gu, 2),
-        owned(m_gu, 2),
-        owned(v_gu, 2),
-        reduced[2],
-        factor,
-        rate_matrix,
-        decay_matrix,
-    )
-    new_down = adam_step(
-        owned(w_down, 2),
-        owned(m_down, 2),
-        owned(v_down, 2),
-        reduced[3],
-        factor,
-        rate_matrix,
-        decay_matrix,
-    )
-    new_norm = adam_step(
-        owned(norm_params, 1),
-        owned(m_norms, 1),
-        owned(v_norms, 1),
-        reduced[4],
-        factor,
-        rate_norm,
-        0.0,
-    )
-    updated = (
-        lax.all_gather(new_qkv[0], "rep", axis=2, tiled=True),
-        lax.all_gather(new_qkv[1], "rep", axis=2, tiled=True),
-        lax.all_gather(new_qkv[2], "rep", axis=2, tiled=True),
-        lax.all_gather(new_out[0], "rep", axis=2, tiled=True),
-        lax.all_gather(new_out[1], "rep", axis=2, tiled=True),
-        lax.all_gather(new_out[2], "rep", axis=2, tiled=True),
-        lax.all_gather(new_gu[0], "rep", axis=2, tiled=True),
-        lax.all_gather(new_gu[1], "rep", axis=2, tiled=True),
-        lax.all_gather(new_gu[2], "rep", axis=2, tiled=True),
-        lax.all_gather(new_down[0], "rep", axis=2, tiled=True),
-        lax.all_gather(new_down[1], "rep", axis=2, tiled=True),
-        lax.all_gather(new_down[2], "rep", axis=2, tiled=True),
-        lax.all_gather(new_norm[0], "rep", axis=1, tiled=True),
-        lax.all_gather(new_norm[1], "rep", axis=1, tiled=True),
-        lax.all_gather(new_norm[2], "rep", axis=1, tiled=True),
-    )
+    width = norm_params.shape[2]
+    grad_norms = lax.dynamic_slice_in_dim(grad_norms, lax.axis_index("fsdp") * width, width, 2)
+    states = (
+        (w_qkv, m_qkv, v_qkv),
+        (w_out, m_out, v_out),
+        (w_gu, m_gu, v_gu),
+        (w_down, m_down, v_down),
+    )
+    updated = []
+    for kind, state in enumerate(states):
+        gradient = jnp.stack([grads[kind] for grads in grad_list]).astype(jnp.float32)
+        updated += adam_step(*state, gradient, factor, rate_matrix, decay_matrix)
+    updated += adam_step(norm_params, m_norms, v_norms, grad_norms, factor, rate_norm, 0.0)
     input_grad = jnp.where(masked, 0.0, grad_hidden)
-    return (
-        activations,
-        input_grad,
-        grad_norm,
-        updated[0],
-        updated[1],
-        updated[2],
-        updated[3],
-        updated[4],
-        updated[5],
-        updated[6],
-        updated[7],
-        updated[8],
-        updated[9],
-        updated[10],
-        updated[11],
-        updated[12],
-        updated[13],
-        updated[14],
-    )
+    return (activations, input_grad, grad_norm, *updated)
 
 
 def solution(mesh):

time: 2050 us -> 882 us (0.43)
  waiting for transfers between devices: 1530 us -> 206 us
  starting transfers between devices: 1.45 us -> 146 us
  other arithmetic: 59.2 us -> 129 us
  blocking collectives: 152 us -> 86.1 us
  matrix products: 133 us -> 69.8 us
  local copies, waits for them, and re-layouts: 146 us -> 201 us
    reduce_scatter x9 -> x0, waiting for transfers between devices: 757 us -> none  [the longest x2 372 us: body(): lax.psum_scatter(local_grads[2], 'fsdp', scatter_dimension=0, tiled=True)]
    all_gather x17 -> x0, waiting for transfers between devices: 585 us -> none  [the longest x2 175 us: body(): lax.all_gather(w_gu[layer_index].astype(jnp.bfloat16), 'fsdp', axis=0, ti...]
    ppermute x0 -> x101, waiting for transfers between devices: none -> 206 us  [send(): return lax.ppermute(values, both_axes, pairs)]
    unnamed x36 -> x0, waiting for transfers between devices: 188 us -> none
    ppermute x0 -> x101, starting transfers between devices: none -> 146 us  [send(): return lax.ppermute(values, both_axes, pairs)]
    reshape x0 -> x4, local copies, waits for them, and re-layouts: none -> 69.7 us  [the longest x2 39.1 us: scatter_chunk(): parts = parts.reshape(2, 2, count, 4, 2, rows, D)]
    all_gather x8 -> x1, blocking collectives: 103 us -> 48.1 us  [body(): lax.all_gather(norm_params.astype(jnp.bfloat16), 'fsdp', axis=2, tiled=True)]
    unnamed x258 -> x414, local copies, waits for them, and re-layouts: 81 us -> 26.6 us
  transfers between devices with their start and end apart: 31 -> 101, of which waited for: 25 -> 35; matrix products, arithmetic and copies ran while one was open for 13% -> 31% of each run, Pallas kernels for 0% -> 2%
where the time goes in v1:
time: 882 us; the launch traced here: 872 us
  waiting for transfers between devices  206 us (23%)
  local copies, waits for them, and re-layouts  201 us (23%)
  starting transfers between devices  146 us (17%)
  other arithmetic  129 us (15%)
  blocking collectives  86.1 us (10%)
  matrix products  69.8 us (8%)
  Pallas kernels  20 us (2%)
  between operations  13.4 us (2%)
    ppermute x101, waiting for transfers between devices, send(): return lax.ppermute(values, both_axes, pairs)  206 us
    ppermute x101, starting transfers between devices, send(): return lax.ppermute(values, both_axes, pairs)  146 us
    all_gather x1, blocking collectives, body(): lax.all_gather(norm_params.astype(jnp.bfloat16), 'fsdp', axis=2, tiled=True)  48.1 us
    reshape x2, local copies, waits for them, and re-layouts, scatter_chunk(): parts = parts.reshape(2, 2, count, 4, 2, rows, D)  39.1 us
    psum x1, blocking collectives, body(): grad_norms = lax.psum(jnp.stack(norm_list), both_axes)  38 us
    convert_element_type x30, other arithmetic, add_low(): (left.astype(jnp.float32) + right.astype(jnp.float32)).astype(jnp.bfloat16)  31.5 us
    reshape x2, local copies, waits for them, and re-layouts, reduce_layer(): gate_up = grad_gu.reshape(8, rows, 2, 4, D).transpose(3, 2, 0, 1, 4)  30.6 us
    dynamic_slice x12, local copies, waits for them, and re-layouts, pick(): return lax.dynamic_index_in_dim(values, index, axis, keepdims=False)  29.2 us
  transfers between devices with their start and end apart: 101, of which 35 were waited for; matrix products, arithmetic and copies ran while one was open for 31% of the time, Pallas kernels for 2%

profile of v1, /device:TPU:0, one launch (start us, length us, event | category | flops | bytes accessed | tf_op | source)
XLA Modules:
  0.0 871.9 jit_solution(478483858550496847)
XLA Ops:
  47.2 48.1 %all_gather.3 = bf16[2,4,768]{1,0,2:T(2,128)(2,1)S(1)} all-gather(bf16[2,4,96]{1,0,2:T(2,128)(2,1)S(1)} %copy.432), channel_id=1, replica_groups=mesh['rep'=4,'fsdp'=8] {'fsdp'}, dimensions={2}, use_global_device_ids=true | all-gather | bytes 13824 | tf_op jit(solution)/shard_map/all_gather | solution.py:426
  102.2 5.1 collective-permute-done.42
  107.2 6.3 collective-permute-done.26
  115.6 10.6 %collective-permute-done.10 = bf16[2,2,96,768]{3,2,1,0:T(8,128)(2,1)S(1)} collective-permute-done((bf16[2,2,96,768]{3,2,1,0:T(8,128)(2,1)}, bf16[2,2,96,768]{3,2,1,0:T(8,128)(2,1)S(1)}, u32[]{:S(2)}, u32[]{:S(2)}) %collective-permute-start.10) | collective-permute-done | bytes 589856 | tf_op jit(solution)/shard_map/ppermute | solution.py:213
  127.7 10.6 %collective-permute-done.34 = bf16[2,2,96,768]{3,2,1,0:T(8,128)(2,1)S(1)} collective-permute-done((bf16[2,2,96,768]{3,2,1,0:T(8,128)(2,1)}, bf16[2,2,96,768]{3,2,1,0:T(8,128)(2,1)S(1)}, u32[]{:S(2)}, u32[]{:S(2)}) %collective-permute-start.34) | collective-permute-done | bytes 589856 | tf_op jit(solution)/shard_map/ppermute | solution.py:213
  150.7 19.0 %collective-permute-done.27 = bf16[3,1,96,768]{3,2,0,1:T(8,128)(2,1)S(1)} collective-permute-done((bf16[3,1,96,768]{3,2,0,1:T(8,128)(2,1)S(1)}, bf16[3,1,96,768]{3,2,0,1:T(8,128)(2,1)S(1)}, u32[]{:S(2)}, u32[]{:S(2)}) %collective-permute-start.27) | collective-permute-done | bytes 442400 | tf_op jit(solution)/shard_map/ppermute | solution.py:213
  175.8 10.8 %slice_reduce_fusion.1 = (f32[768]{0:T(1024)}, f32[768]{0:T(1024)}, f32[768]{0:T(1024)S(1)}, f32[768]{0:T(1024)S(1)}) fusion(f32[1,4,768]{1,0,2:T(1,128)S(1)} %get-tuple-element.162), kind=kLoop, calls=%fused_computation.362 | loop fusion | bytes 24576 | tf_op jit(solution)/shard_map/slice | solution.py:94
  194.9 11.2 %slice_reduce_fusion.5 = (f32[768]{0:T(1024)}, f32[768]{0:T(1024)}, f32[768]{0:T(1024)S(1)}, f32[768]{0:T(1024)S(1)}) fusion(f32[1,4,768]{1,0,2:T(1,128)S(1)} %get-tuple-element.163), kind=kLoop, calls=%fused_computation.367 | loop fusion | bytes 24576 | tf_op jit(solution)/shard_map/slice | solution.py:94
  223.7 6.4 collective-permute-done.28
  245.5 5.3 assemble_down.2
  256.0 3.9 assemble_down.3
  261.0 3.7 collective-permute-done.36.refs_2_
  270.1 7.7 multiply_convert_fusion.1
  296.0 6.9 multiply_convert_fusion
  311.4 9.1 %multiply_reduce_fusion.3 = (f32[768]{0:T(1024)}, f32[256]{0:T(256)S(1)}, f32[768]{0:T(1024)}, f32[256,768]{1,0:T(8,128)S(1)}) fusion(f32[256,768]{1,0:T(8,128)S(1)} %copy-done.52, f32[256]{0:T(256)S(1)} %fusion.145, f32[256]{0:T(256)S(1)} %broadcast_multiply_fusion.2, f32[768]{0:T(1024)S(1)} %get-tuple-element.41, ...), kind=kOutput, calls=%fused_computation.251 | convolution fusion | flops 2424174848 | bytes 14955520 | tf_op jit(solution)/shard_map/dot_general | solution.py:50
  364.4 10.1 %convolution_convert_fusion = bf16[768,6144]{1,0:T(8,128)(2,1)} fusion(bf16[256,3072]{1,0:T(8,128)(2,1)} %copy-done.70, bf16[256,3072]{1,0:T(8,128)(2,1)} %copy-done.69, f32[256,768]{1,0:T(8,128)S(1)} %copy-done.50, f32[768]{0:T(1024)S(1)} %get-tuple-element.44, f32[768]{0:T(1024)S(1)} %get-tuple-element.45, f32[256]{0:T(256)S(1)} %copy-done.135, ...), kind=kOutput, calls=%fused_computation | convolution fusion | flops 2427912192 | bytes 13377536 | tf_op jit(solution)/shard_map/dot_general | solution.py:44
  374.6 5.5 convolution_convert_fusion.1
  398.0 15.3 %reshape.727 = bf16[8,96,2,4,768]{4,3,2,1,0:T(4,128)(2,1)} reshape(bf16[768,6144]{1,0:T(8,128)(2,1)} %convolution_convert_fusion) | data formatting | bytes 18874368 | tf_op jit(solution)/shard_map/reshape | solution.py:385
  413.3 19.3 %reshape.728 = bf16[2,2,2,4,2,96,768]{6,1,0,2,5,4,3:T(2,128)(2,1)} reshape(bf16[4,2,8,96,768]{4,0,1,3,2:T(4,128)(2,1)} %bitcast.558) | data formatting | bytes 18874368 | tf_op jit(solution)/shard_map/reshape | solution.py:321
  432.6 8.9 %constant_dynamic-slice_fusion.4 = (bf16[2,2,2,4,1,96,768]{6,1,0,2,5,4,3:T(2,128)(2,1)}, bf16[2,2,2,4,1,96,768]{6,1,0,2,5,4,3:T(2,128)(2,1)S(1)}) fusion(bf16[2,2,2,4,2,96,768]{6,1,0,2,5,4,3:T(2,128)(2,1)} %reshape.728, s32[]{:T(128)S(6)} %select_n.392, s32[]{:T(128)S(6)} %select_n.393), kind=kLoop, calls=%fused_computation.453 | loop fusion | bytes 18874376 | tf_op jit(solution)/shard_map/jit(dynamic_index_in_dim)/dynamic_slice | solution.py:226
  445.1 15.3 %reshape.721 = bf16[8,96,2,4,768]{4,3,2,1,0:T(4,128)(2,1)} reshape(bf16[768,6144]{1,0:T(8,128)(2,1)} %convolution_convert_fusion.1) | data formatting | bytes 18874368 | tf_op jit(solution)/shard_map/reshape | solution.py:385
  460.4 19.8 %reshape.722 = bf16[2,2,2,4,2,96,768]{6,1,0,2,5,4,3:T(2,128)(2,1)} reshape(bf16[4,2,8,96,768]{4,0,1,3,2:T(4,128)(2,1)} %bitcast.559) | data formatting | bytes 18874368 | tf_op jit(solution)/shard_map/reshape | solution.py:321
  480.2 8.8 %constant_dynamic-slice_fusion.8 = (bf16[2,2,2,4,1,96,768]{6,1,0,2,5,4,3:T(2,128)(2,1)}, bf16[2,2,2,4,1,96,768]{6,1,0,2,5,4,3:T(2,128)(2,1)S(1)}) fusion(bf16[2,2,2,4,2,96,768]{6,1,0,2,5,4,3:T(2,128)(2,1)} %reshape.722, s32[]{:T(128)S(6)} %select_n.392, s32[]{:T(128)S(6)} %select_n.393), kind=kLoop, calls=%fused_computation.457 | loop fusion | bytes 18874376 | tf_op jit(solution)/shard_map/jit(dynamic_index_in_dim)/dynamic_slice | solution.py:226
  493.0 38.0 %psum.7 = f32[2,4,768]{2,1,0:T(4,128)} all-reduce(f32[2,4,768]{2,1,0:T(4,128)} %pad_maximum_fusion.32), channel_id=1, replica_groups=mesh['rep'=4,'fsdp'=8] {'rep','fsdp'}, use_global_device_ids=true, to_apply=%region_36.37 | all-reduce | flops 6144 | bytes 49152 | tf_op jit(solution)/shard_map/psum | solution.py:447
  550.4 4.6 collective-permute-done.61
  558.3 9.4 %collective-permute-done.79 = bf16[2,1,4,96,768]{4,3,2,0,1:T(8,128)(2,1)S(1)} collective-permute-done((bf16[2,1,4,96,768]{4,3,2,0,1:T(8,128)(2,1)S(1)}, bf16[2,1,4,96,768]{4,3,2,0,1:T(8,128)(2,1)S(1)}, u32[]{:S(2)}, u32[]{:S(2)}) %collective-permute-start.79) | collective-permute-done | bytes 1179680 | tf_op jit(solution)/shard_map/ppermute | solution.py:213
  567.7 4.3 collective-permute-start.62
  573.2 7.1 collective-permute-done.67
  580.3 4.3 collective-permute-start.80
  585.0 8.0 collective-permute-done.49
  592.9 4.3 collective-permute-start.68
  602.5 8.3 collective-permute-done.68
  613.3 9.4 %collective-permute-done.50 = bf16[2,1,2,96,768]{4,3,0,2,1:T(8,128)(2,1)S(1)} collective-permute-done((bf16[2,1,2,96,768]{4,3,0,2,1:T(8,128)(2,1)S(1)}, bf16[2,1,2,96,768]{4,3,0,2,1:T(8,128)(2,1)S(1)}, u32[]{:S(2)}, u32[]{:S(2)}) %collective-permute-start.50) | collective-permute-done | bytes 589856 | tf_op jit(solution)/shard_map/ppermute | solution.py:213
  626.9 4.0 fusion
  633.9 3.8 fusion.1
  640.1 5.5 collective-permute-start.64
  648.2 6.7 collective-permute-start.70
  660.5 5.7 collective-permute-done.70
  686.1 13.4 %collective-permute-done.55 = bf16[2,2,4,96,768]{4,3,1,0,2:T(8,128)(2,1)S(1)} collective-permute-done((bf16[2,2,4,96,768]{4,3,1,0,2:T(8,128)(2,1)S(1)}, bf16[2,2,4,96,768]{4,3,1,0,2:T(8,128)(2,1)S(1)}, u32[]{:S(2)}, u32[]{:S(2)}) %collective-permute-start.55) | collective-permute-done | bytes 2359328 | tf_op jit(solution)/shard_map/ppermute | solution.py:213
  699.5 7.4 collective-permute-start.74
  714.1 19.1 %collective-permute-done.74 = bf16[2,2,2,96,768]{4,3,1,0,2:T(8,128)(2,1)S(1)} collective-permute-done((bf16[2,2,2,96,768]{4,3,1,0,2:T(8,128)(2,1)S(1)}, bf16[2,2,2,96,768]{4,3,1,0,2:T(8,128)(2,1)S(1)}, u32[]{:S(2)}, u32[]{:S(2)}) %collective-permute-start.74) | collective-permute-done | bytes 1179680 | tf_op jit(solution)/shard_map/ppermute | solution.py:213
  734.5 20.9 %collective-permute-done.56 = bf16[2,2,2,96,768]{4,3,1,0,2:T(8,128)(2,1)S(1)} collective-permute-done((bf16[2,2,2,96,768]{4,3,1,0,2:T(8,128)(2,1)S(1)}, bf16[2,2,2,96,768]{4,3,1,0,2:T(8,128)(2,1)S(1)}, u32[]{:S(2)}, u32[]{:S(2)}) %collective-permute-start.56) | collective-permute-done | bytes 1179680 | tf_op jit(solution)/shard_map/ppermute | solution.py:213
  759.3 4.4 collective-permute-start.76
  764.0 21.5 %collective-permute-start.58 = (bf16[2,2,96,768]{3,2,1,0:T(8,128)(2,1)S(1)}, bf16[2,2,96,768]{3,2,1,0:T(8,128)(2,1)S(1)}, u32[]{:S(2)}, u32[]{:S(2)}) collective-permute-start(bf16[2,2,96,768]{3,2,1,0:T(8,128)(2,1)S(1)} %dynamic-slice_bitcast_fusion.14), channel_id=1, source_target_pairs={{0,2},{1,3},{2,0},{3,1},{4,6},{5,7},{6,4},{7,5},{8,10},{9,11},{10,... | collective-permute-start | bytes 1769480 | tf_op jit(solution)/shard_map/ppermute | solution.py:213
  787.4 7.9 collective-permute-done.58
  828.9 5.7 multiply_subtract_fusion.2
  834.6 4.2 multiply_subtract_fusion.1
  860.4 10.1 %multiply_subtract_fusion = (f32[2,96,6144]{2,1,0:T(8,128)}, f32[2,96,6144]{2,1,0:T(8,128)}, f32[2,96,6144]{2,1,0:T(8,128)}) fusion(f32[2,96,6144]{2,1,0:T(8,128)} %param.29, f32[]{:T(128)S(6)} %div.260, bf16[1,96,6144]{2,1,0:T(8,128)(2,1)S(1)} %stack_reshape.7, bf16[1,96,6144]{2,1,0:T(8,128)(2,1)S(1)} %stack_reshape.6, f32[2,96,6144]{2,1,0:T(8,128)} %param.30, ...), kind=kLoop, calls=%fused_computation.32 | loop fusion | flops 21233664 | bytes 30670852 | tf_op jit(solution)/shard_map/sub | solution.py:180
  (853 shorter events, 353.1 us)
Async XLA Ops:
  3.3 28.2 %collective-permute-start.40 = (bf16[1,96,768]{2,1,0:T(8,128)(2,1)}, bf16[1,96,768]{2,1,0:T(8,128)(2,1)}, u32[]{:S(2)}, u32[]{:S(2)}) collective-permute-start(bf16[1,96,768]{2,1,0:T(8,128)(2,1)} %fusion.235), channel_id=1, source_target_pairs={{0,2},{1,3},{2,0},{3,1},{4,6},{5,7},{6,4},{7,5},{8,10},{9,11},{10,... | collective-permute-start | bytes 442376 | tf_op jit(solution)/shard_map/ppermute | solution.py:213
  9.1 30.6 %collective-permute-start.24 = (bf16[1,96,768]{2,1,0:T(8,128)(2,1)}, bf16[1,96,768]{2,1,0:T(8,128)(2,1)}, u32[]{:S(2)}, u32[]{:S(2)}) collective-permute-start(bf16[1,96,768]{2,1,0:T(8,128)(2,1)} %constant_dynamic-slice_fusion.10), channel_id=1, source_target_pairs={{0,2},{1,3},{2,0},{3,1},{4,6},{5,7},{6,4},{7,5},{8,10},{9,11},{10,... | collective-permute-start | bytes 442376 | tf_op jit(solution)/shard_map/ppermute | solution.py:213
  37.9 61.4 %collective-permute-start.9 = (bf16[2,2,96,768]{3,2,1,0:T(8,128)(2,1)S(1)}, bf16[2,2,96,768]{3,2,1,0:T(8,128)(2,1)}, u32[]{:S(2)}, u32[]{:S(2)}) collective-permute-start(bf16[2,2,96,768]{3,2,1,0:T(8,128)(2,1)S(1)} %fusion.94), channel_id=1, source_target_pairs={{2,4},{3,5},{4,2},{5,3},{10,12},{11,13},{12,10},{13,11},{18,20},{1... | collective-permute-start | bytes 1769480 | tf_op jit(solution)/shard_map/ppermute | solution.py:213
  39.7 60.9 %collective-permute-start.33 = (bf16[2,2,96,768]{3,2,1,0:T(8,128)(2,1)S(1)}, bf16[2,2,96,768]{3,2,1,0:T(8,128)(2,1)}, u32[]{:S(2)}, u32[]{:S(2)}) collective-permute-start(bf16[2,2,96,768]{3,2,1,0:T(8,128)(2,1)S(1)} %fusion.92), channel_id=1, source_target_pairs={{2,4},{3,5},{4,2},{5,3},{10,12},{11,13},{12,10},{13,11},{18,20},{1... | collective-permute-start | bytes 1769480 | tf_op jit(solution)/shard_map/ppermute | solution.py:213
  43.0 52.3 %collective-permute-start.25 = (bf16[2,1,96,768]{3,2,0,1:T(8,128)(2,1)}, bf16[2,1,96,768]{3,2,0,1:T(8,128)(2,1)}, u32[]{:S(2)}, u32[]{:S(2)}) collective-permute-start(bf16[2,1,96,768]{3,2,0,1:T(8,128)(2,1)} %fusion.126), channel_id=1, source_target_pairs={{2,4},{3,5},{4,2},{5,3},{10,12},{11,13},{12,10},{13,11},{18,20},{1... | collective-permute-start | bytes 884744 | tf_op jit(solution)/shard_map/ppermute | solution.py:213
  44.4 52.2 %collective-permute-start.18 = (bf16[2,1,96,768]{3,2,0,1:T(8,128)(2,1)}, bf16[2,1,96,768]{3,2,0,1:T(8,128)(2,1)}, u32[]{:S(2)}, u32[]{:S(2)}) collective-permute-start(bf16[2,1,96,768]{3,2,0,1:T(8,128)(2,1)} %collective-permute-done.17), channel_id=1, source_target_pairs={{2,0},{3,1},{4,6},{5,7},{10,8},{11,9},{12,14},{13,15},{18,16},{19,... | collective-permute-start | bytes 884744 | tf_op jit(solution)/shard_map/ppermute | solution.py:213
  45.7 53.2 %collective-permute-start.2 = (bf16[2,1,96,768]{3,2,1,0:T(8,128)(2,1)S(1)}, bf16[2,1,96,768]{3,2,1,0:T(8,128)(2,1)S(1)}, u32[]{:S(2)}, u32[]{:S(2)}) collective-permute-start(bf16[2,1,96,768]{3,2,1,0:T(8,128)(2,1)S(1)} %collective-permute-done.1), channel_id=1, source_target_pairs={{2,0},{3,1},{4,6},{5,7},{10,8},{11,9},{12,14},{13,15},{18,16},{19,... | collective-permute-start | bytes 884744 | tf_op jit(solution)/shard_map/ppermute | solution.py:213
  98.9 42.1 %collective-permute-start.21 = (bf16[4,1,96,768]{3,2,0,1:T(8,128)(2,1)S(1)}, bf16[4,1,96,768]{3,2,0,1:T(8,128)(2,1)S(1)}, u32[]{:S(2)}, u32[]{:S(2)}) collective-permute-start(bf16[4,1,96,768]{3,2,0,1:T(8,128)(2,1)S(1)} %bitcast.545), channel_id=1, source_target_pairs={{0,1},{1,0},{2,3},{3,2},{4,5},{5,4},{6,7},{7,6},{8,9},{9,8},{10,11... | collective-permute-start | bytes 1769480 | tf_op jit(solution)/shard_map/ppermute | solution.py:213
  100.7 37.6 %collective-permute-start.34 = (bf16[2,2,96,768]{3,2,1,0:T(8,128)(2,1)}, bf16[2,2,96,768]{3,2,1,0:T(8,128)(2,1)S(1)}, u32[]{:S(2)}, u32[]{:S(2)}) collective-permute-start(bf16[2,2,96,768]{3,2,1,0:T(8,128)(2,1)} %collective-permute-done.33), channel_id=1, source_target_pairs={{2,0},{3,1},{4,6},{5,7},{10,8},{11,9},{12,14},{13,15},{18,16},{19,... | collective-permute-start | bytes 1769480 | tf_op jit(solution)/shard_map/ppermute | solution.py:213
  107.2 41.4 %collective-permute-start.45 = (bf16[4,1,96,768]{3,2,0,1:T(8,128)(2,1)S(1)}, bf16[4,1,96,768]{3,2,0,1:T(8,128)(2,1)S(1)}, u32[]{:S(2)}, u32[]{:S(2)}) collective-permute-start(bf16[4,1,96,768]{3,2,0,1:T(8,128)(2,1)S(1)} %bitcast.541), channel_id=1, source_target_pairs={{0,1},{1,0},{2,3},{3,2},{4,5},{5,4},{6,7},{7,6},{8,9},{9,8},{10,11... | collective-permute-start | bytes 1769480 | tf_op jit(solution)/shard_map/ppermute | solution.py:213
  113.5 35.6 %collective-permute-start.29 = (bf16[4,1,96,768]{3,2,0,1:T(8,128)(2,1)}, bf16[4,1,96,768]{3,2,0,1:T(8,128)(2,1)S(1)}, u32[]{:S(2)}, u32[]{:S(2)}) collective-permute-start(bf16[4,1,96,768]{3,2,0,1:T(8,128)(2,1)} %get-tuple-element.145), channel_id=1, source_target_pairs={{0,1},{1,0},{2,3},{3,2},{4,5},{5,4},{6,7},{7,6},{8,9},{9,8},{10,11... | collective-permute-start | bytes 1769480 | tf_op jit(solution)/shard_map/ppermute | solution.py:213
  141.1 34.7 %collective-permute-start.11 = (bf16[3,2,96,768]{3,2,1,0:T(8,128)(2,1)S(1)}, bf16[3,2,96,768]{3,2,1,0:T(8,128)(2,1)S(1)}, u32[]{:S(2)}, u32[]{:S(2)}) collective-permute-start(bf16[3,2,96,768]{3,2,1,0:T(8,128)(2,1)S(1)} %get-tuple-element.128), channel_id=1, source_target_pairs={{0,16},{1,9},{2,18},{3,11},{4,20},{5,13},{6,22},{7,15},{8,24},{9,1... | collective-permute-start | bytes 2654216 | tf_op jit(solution)/shard_map/ppermute | solution.py:213
  142.6 27.0 %collective-permute-start.27 = (bf16[3,1,96,768]{3,2,0,1:T(8,128)(2,1)S(1)}, bf16[3,1,96,768]{3,2,0,1:T(8,128)(2,1)S(1)}, u32[]{:S(2)}, u32[]{:S(2)}) collective-permute-start(bf16[3,1,96,768]{3,2,0,1:T(8,128)(2,1)S(1)} %get-tuple-element.158), channel_id=1, source_target_pairs={{0,16},{1,9},{2,18},{3,11},{4,20},{5,13},{6,22},{7,15},{8,24},{9,1... | collective-permute-start | bytes 1327112 | tf_op jit(solution)/shard_map/ppermute | solution.py:213
  146.6 26.9 %collective-permute-start.5 = (bf16[4,1,96,768]{3,2,0,1:T(8,128)(2,1)S(1)}, bf16[4,1,96,768]{3,2,0,1:T(8,128)(2,1)S(1)}, u32[]{:S(2)}, u32[]{:S(2)}) collective-permute-start(bf16[4,1,96,768]{3,2,0,1:T(8,128)(2,1)S(1)} %copy-done.117), channel_id=1, source_target_pairs={{0,1},{1,0},{2,3},{3,2},{4,5},{5,4},{6,7},{7,6},{8,9},{9,8},{10,11... | collective-permute-start | bytes 1769480 | tf_op jit(solution)/shard_map/ppermute | solution.py:213
  148.7 39.8 %collective-permute-start.22 = (bf16[2,3,1,96,768]{4,3,1,2,0:T(8,128)(2,1)S(1)}, bf16[2,3,1,96,768]{4,3,1,2,0:T(8,128)(2,1)S(1)}, u32[]{:S(2)}, u32[]{:S(2)}) collective-permute-start(bf16[2,3,1,96,768]{4,3,1,2,0:T(8,128)(2,1)S(1)} %get-tuple-element.121), channel_id=1, source_target_pairs={{0,1},{1,0},{2,3},{3,2},{4,5},{5,4},{6,7},{7,6},{8,9},{9,8},{10,11... | collective-permute-start | bytes 2654216 | tf_op jit(solution)/shard_map/ppermute | solution.py:213
  149.2 41.7 %collective-permute-start.20 = (bf16[2,3,1,96,768]{4,3,1,2,0:T(8,128)(2,1)S(1)}, bf16[2,3,1,96,768]{4,3,1,2,0:T(8,128)(2,1)}, u32[]{:S(2)}, u32[]{:S(2)}) collective-permute-start(bf16[2,3,1,96,768]{4,3,1,2,0:T(8,128)(2,1)S(1)} %get-tuple-element.121), channel_id=1, source_target_pairs={{0,8},{1,17},{2,10},{3,19},{4,12},{5,21},{6,14},{7,23},{8,0},{9,25... | collective-permute-start | bytes 2654216 | tf_op jit(solution)/shard_map/ppermute | solution.py:213
  190.8 51.8 %collective-permute-start.12 = (bf16[2,3,2,96,768]{4,3,2,1,0:T(8,128)(2,1)S(1)}, bf16[2,3,2,96,768]{4,3,2,1,0:T(8,128)(2,1)}, u32[]{:S(2)}, u32[]{:S(2)}) collective-permute-start(bf16[2,3,2,96,768]{4,3,2,1,0:T(8,128)(2,1)S(1)} %pad_maximum_fusion.9.refs_1_), channel_id=1, source_target_pairs={{0,8},{1,17},{2,10},{3,19},{4,12},{5,21},{6,14},{7,23},{8,0},{9,25... | collective-permute-start | bytes 5308424 | tf_op jit(solution)/shard_map/ppermute | solution.py:213
  193.1 36.9 %collective-permute-start.28 = (bf16[2,3,1,96,768]{4,3,1,2,0:T(8,128)(2,1)}, bf16[2,3,1,96,768]{4,3,1,2,0:T(8,128)(2,1)}, u32[]{:S(2)}, u32[]{:S(2)}) collective-permute-start(bf16[2,3,1,96,768]{4,3,1,2,0:T(8,128)(2,1)} %get-tuple-element.129), channel_id=1, source_target_pairs={{0,8},{1,17},{2,10},{3,19},{4,12},{5,21},{6,14},{7,23},{8,0},{9,25... | collective-permute-start | bytes 2654216 | tf_op jit(solution)/shard_map/ppermute | solution.py:213
  208.1 33.5 %collective-permute-start.46 = (bf16[2,3,1,96,768]{4,3,2,1,0:T(8,128)(2,1)}, bf16[2,3,1,96,768]{4,3,2,1,0:T(8,128)(2,1)}, u32[]{:S(2)}, u32[]{:S(2)}) collective-permute-start(bf16[2,3,1,96,768]{4,3,2,1,0:T(8,128)(2,1)} %pad_maximum_fusion.23.refs_1_), channel_id=1, source_target_pairs={{0,1},{1,0},{2,3},{3,2},{4,5},{5,4},{6,7},{7,6},{8,9},{9,8},{10,11... | collective-permute-start | bytes 2654216 | tf_op jit(solution)/shard_map/ppermute | solution.py:213
  211.0 30.5 %collective-permute-start.44 = (bf16[2,3,1,96,768]{4,3,2,1,0:T(8,128)(2,1)}, bf16[2,3,1,96,768]{4,3,2,1,0:T(8,128)(2,1)}, u32[]{:S(2)}, u32[]{:S(2)}) collective-permute-start(bf16[2,3,1,96,768]{4,3,2,1,0:T(8,128)(2,1)} %pad_maximum_fusion.23.refs_1_), channel_id=1, source_target_pairs={{0,8},{1,17},{2,10},{3,19},{4,12},{5,21},{6,14},{7,23},{8,0},{9,25... | collective-permute-start | bytes 2654216 | tf_op jit(solution)/shard_map/ppermute | solution.py:213
  212.2 29.9 %collective-permute-start.23 = (bf16[2,3,1,96,768]{4,3,1,2,0:T(8,128)(2,1)}, bf16[2,3,1,96,768]{4,3,1,2,0:T(8,128)(2,1)}, u32[]{:S(2)}, u32[]{:S(2)}) collective-permute-start(bf16[2,3,1,96,768]{4,3,1,2,0:T(8,128)(2,1)} %collective-permute-done.20), channel_id=1, source_target_pairs={{0,1},{1,0},{2,3},{3,2},{4,5},{5,4},{6,7},{7,6},{8,9},{9,8},{10,11... | collective-permute-start | bytes 2654216 | tf_op jit(solution)/shard_map/ppermute | solution.py:213
  255.4 34.4 %collective-permute-start.37 = (bf16[4,2,96,768]{3,2,1,0:T(8,128)(2,1)}, bf16[4,2,96,768]{3,2,1,0:T(8,128)(2,1)}, u32[]{:S(2)}, u32[]{:S(2)}) collective-permute-start(bf16[4,2,96,768]{3,2,1,0:T(8,128)(2,1)} %bitcast.440.clone.2.refs_0_), channel_id=1, source_target_pairs={{0,1},{1,0},{2,3},{3,2},{4,5},{5,4},{6,7},{7,6},{8,9},{9,8},{10,11... | collective-permute-start | bytes 3538952 | tf_op jit(solution)/shard_map/ppermute | solution.py:213
  260.8 29.0 %collective-permute-start.38 = (bf16[2,3,2,96,768]{4,3,2,1,0:T(8,128)(2,1)S(1)}, bf16[2,3,2,96,768]{4,3,2,1,0:T(8,128)(2,1)}, u32[]{:S(2)}, u32[]{:S(2)}) collective-permute-start(bf16[2,3,2,96,768]{4,3,2,1,0:T(8,128)(2,1)S(1)} %pad_maximum_fusion.10.refs_1_), channel_id=1, source_target_pairs={{0,1},{1,0},{2,3},{3,2},{4,5},{5,4},{6,7},{7,6},{8,9},{9,8},{10,11... | collective-permute-start | bytes 5308424 | tf_op jit(solution)/shard_map/ppermute | solution.py:213
  395.4 139.9 %collective-permute-start.60 = (bf16[2,2,1,4,96,768]{5,4,3,1,0,2:T(8,128)(2,1)}, bf16[2,2,1,4,96,768]{5,4,3,1,0,2:T(8,128)(2,1)}, u32[]{:S(2)}, u32[]{:S(2)}) collective-permute-start(bf16[2,2,1,4,96,768]{5,4,3,1,0,2:T(8,128)(2,1)} %dynamic-slice_bitcast_fusion.3), channel_id=1, source_target_pairs={{0,1},{1,0},{2,3},{3,2},{4,5},{5,4},{6,7},{7,6},{8,9},{9,8},{10,11... | collective-permute-start | bytes 7077896 | tf_op jit(solution)/shard_map/ppermute | solution.py:213
  395.8 142.6 %collective-permute-start.78 = (bf16[2,2,1,4,96,768]{5,4,3,1,0,2:T(8,128)(2,1)}, bf16[2,2,1,4,96,768]{5,4,3,1,0,2:T(8,128)(2,1)}, u32[]{:S(2)}, u32[]{:S(2)}) collective-permute-start(bf16[2,2,1,4,96,768]{5,4,3,1,0,2:T(8,128)(2,1)} %dynamic-slice_bitcast_fusion), channel_id=1, source_target_pairs={{0,1},{1,0},{2,3},{3,2},{4,5},{5,4},{6,7},{7,6},{8,9},{9,8},{10,11... | collective-permute-start | bytes 7077896 | tf_op jit(solution)/shard_map/ppermute | solution.py:213
  395.9 147.4 %collective-permute-start.66 = (bf16[2,2,1,4,96,768]{5,4,1,0,3,2:T(8,128)(2,1)}, bf16[2,2,1,4,96,768]{5,4,1,0,3,2:T(8,128)(2,1)}, u32[]{:S(2)}, u32[]{:S(2)}) collective-permute-start(bf16[2,2,1,4,96,768]{5,4,1,0,3,2:T(8,128)(2,1)} %dynamic-slice_bitcast_fusion.2), channel_id=1, source_target_pairs={{0,1},{1,0},{2,3},{3,2},{4,5},{5,4},{6,7},{7,6},{8,9},{9,8},{10,11... | collective-permute-start | bytes 7077896 | tf_op jit(solution)/shard_map/ppermute | solution.py:213
  397.9 148.3 %collective-permute-start.48 = (bf16[2,2,1,4,96,768]{5,4,1,0,3,2:T(8,128)(2,1)}, bf16[2,2,1,4,96,768]{5,4,1,0,3,2:T(8,128)(2,1)}, u32[]{:S(2)}, u32[]{:S(2)}) collective-permute-start(bf16[2,2,1,4,96,768]{5,4,1,0,3,2:T(8,128)(2,1)} %dynamic-slice_bitcast_fusion.5), channel_id=1, source_target_pairs={{0,1},{1,0},{2,3},{3,2},{4,5},{5,4},{6,7},{7,6},{8,9},{9,8},{10,11... | collective-permute-start | bytes 7077896 | tf_op jit(solution)/shard_map/ppermute | solution.py:213
  444.7 180.5 %collective-permute-start.72 = (bf16[2,2,2,4,96,768]{5,4,2,1,3,0:T(8,128)(2,1)}, bf16[2,2,2,4,96,768]{5,4,2,1,3,0:T(8,128)(2,1)}, u32[]{:S(2)}, u32[]{:S(2)}) collective-permute-start(bf16[2,2,2,4,96,768]{5,4,2,1,3,0:T(8,128)(2,1)} %bitcast.527), channel_id=1, source_target_pairs={{0,1},{1,0},{2,3},{3,2},{4,5},{5,4},{6,7},{7,6},{8,9},{9,8},{10,11... | collective-permute-start | bytes 14155784 | tf_op jit(solution)/shard_map/ppermute | solution.py:213
  535.2 97.3 %collective-permute-start.54 = (bf16[2,2,2,4,96,768]{5,4,2,1,3,0:T(8,128)(2,1)}, bf16[2,2,2,4,96,768]{5,4,2,1,3,0:T(8,128)(2,1)}, u32[]{:S(2)}, u32[]{:S(2)}) collective-permute-start(bf16[2,2,2,4,96,768]{5,4,2,1,3,0:T(8,128)(2,1)} %bitcast.594), channel_id=1, source_target_pairs={{0,1},{1,0},{2,3},{3,2},{4,5},{5,4},{6,7},{7,6},{8,9},{9,8},{10,11... | collective-permute-start | bytes 14155784 | tf_op jit(solution)/shard_map/ppermute | solution.py:213
  546.3 34.0 %collective-permute-start.67 = (bf16[2,1,4,96,768]{4,3,0,2,1:T(8,128)(2,1)S(1)}, bf16[2,1,4,96,768]{4,3,0,2,1:T(8,128)(2,1)S(1)}, u32[]{:S(2)}, u32[]{:S(2)}) collective-permute-start(bf16[2,1,4,96,768]{4,3,0,2,1:T(8,128)(2,1)S(1)} %dynamic-slice_bitcast_fusion.8), channel_id=1, source_target_pairs={{0,8},{1,17},{2,10},{3,19},{4,12},{5,21},{6,14},{7,23},{8,0},{9,25... | collective-permute-start | bytes 3538952 | tf_op jit(solution)/shard_map/ppermute | solution.py:213
  555.0 37.9 %collective-permute-start.49 = (bf16[2,1,4,96,768]{4,3,0,2,1:T(8,128)(2,1)S(1)}, bf16[2,1,4,96,768]{4,3,0,2,1:T(8,128)(2,1)S(1)}, u32[]{:S(2)}, u32[]{:S(2)}) collective-permute-start(bf16[2,1,4,96,768]{4,3,0,2,1:T(8,128)(2,1)S(1)} %dynamic-slice_bitcast_fusion.11), channel_id=1, source_target_pairs={{0,8},{1,17},{2,10},{3,19},{4,12},{5,21},{6,14},{7,23},{8,0},{9,25... | collective-permute-start | bytes 3538952 | tf_op jit(solution)/shard_map/ppermute | solution.py:213
  567.7 30.0 %collective-permute-start.62 = (bf16[2,1,2,96,768]{4,3,0,2,1:T(8,128)(2,1)S(1)}, bf16[2,1,2,96,768]{4,3,0,2,1:T(8,128)(2,1)S(1)}, u32[]{:S(2)}, u32[]{:S(2)}) collective-permute-start(bf16[2,1,2,96,768]{4,3,0,2,1:T(8,128)(2,1)S(1)} %bitcast.625), channel_id=1, source_target_pairs={{0,2},{1,3},{6,4},{7,5},{8,10},{9,11},{14,12},{15,13},{16,18},{17,... | collective-permute-start | bytes 1769480 | tf_op jit(solution)/shard_map/ppermute | solution.py:213
  600.0 37.9 %collective-permute-start.63 = (bf16[2,1,2,96,768]{4,3,0,2,1:T(8,128)(2,1)}, bf16[2,1,2,96,768]{4,3,0,2,1:T(8,128)(2,1)}, u32[]{:S(2)}, u32[]{:S(2)}) collective-permute-start(bf16[2,1,2,96,768]{4,3,0,2,1:T(8,128)(2,1)} %add_convert_fusion.6), channel_id=1, source_target_pairs={{2,4},{3,5},{4,2},{5,3},{10,12},{11,13},{12,10},{13,11},{18,20},{1... | collective-permute-start | bytes 1769480 | tf_op jit(solution)/shard_map/ppermute | solution.py:213
  610.9 29.2 %collective-permute-start.81 = (bf16[2,1,2,96,768]{4,3,0,2,1:T(8,128)(2,1)}, bf16[2,1,2,96,768]{4,3,0,2,1:T(8,128)(2,1)}, u32[]{:S(2)}, u32[]{:S(2)}) collective-permute-start(bf16[2,1,2,96,768]{4,3,0,2,1:T(8,128)(2,1)} %add_convert_fusion.4), channel_id=1, source_target_pairs={{2,4},{3,5},{4,2},{5,3},{10,12},{11,13},{12,10},{13,11},{18,20},{1... | collective-permute-start | bytes 1769480 | tf_op jit(solution)/shard_map/ppermute | solution.py:213
  632.5 51.9 %collective-permute-start.73 = (bf16[2,2,4,96,768]{4,3,1,0,2:T(8,128)(2,1)}, bf16[2,2,4,96,768]{4,3,1,0,2:T(8,128)(2,1)S(1)}, u32[]{:S(2)}, u32[]{:S(2)}) collective-permute-start(bf16[2,2,4,96,768]{4,3,1,0,2:T(8,128)(2,1)} %dynamic-slice_bitcast_fusion.1), channel_id=1, source_target_pairs={{0,8},{1,17},{2,10},{3,19},{4,12},{5,21},{6,14},{7,23},{8,0},{9,25... | collective-permute-start | bytes 7077896 | tf_op jit(solution)/shard_map/ppermute | solution.py:213
  638.0 61.5 %collective-permute-start.55 = (bf16[2,2,4,96,768]{4,3,1,0,2:T(8,128)(2,1)S(1)}, bf16[2,2,4,96,768]{4,3,1,0,2:T(8,128)(2,1)S(1)}, u32[]{:S(2)}, u32[]{:S(2)}) collective-permute-start(bf16[2,2,4,96,768]{4,3,1,0,2:T(8,128)(2,1)S(1)} %dynamic-slice_bitcast_fusion.4), channel_id=1, source_target_pairs={{0,8},{1,17},{2,10},{3,19},{4,12},{5,21},{6,14},{7,23},{8,0},{9,25... | collective-permute-start | bytes 7077896 | tf_op jit(solution)/shard_map/ppermute | solution.py:213
  676.7 31.0 %collective-permute-start.89 = (bf16[1,96,768]{2,1,0:T(8,128)(2,1)S(1)}, bf16[1,96,768]{2,1,0:T(8,128)(2,1)S(1)}, u32[]{:S(2)}, u32[]{:S(2)}) collective-permute-start(bf16[1,96,768]{2,1,0:T(8,128)(2,1)S(1)} %get-tuple-element.62), channel_id=1, source_target_pairs={{0,16},{1,9},{2,18},{3,11},{4,20},{5,13},{6,22},{7,15},{8,24},{9,1... | collective-permute-start | bytes 442376 | tf_op jit(solution)/shard_map/ppermute | solution.py:213
  679.9 29.5 %collective-permute-start.97 = (bf16[1,96,768]{2,1,0:T(8,128)(2,1)S(1)}, bf16[1,96,768]{2,1,0:T(8,128)(2,1)S(1)}, u32[]{:S(2)}, u32[]{:S(2)}) collective-permute-start(bf16[1,96,768]{2,1,0:T(8,128)(2,1)S(1)} %get-tuple-element.66), channel_id=1, source_target_pairs={{0,16},{1,9},{2,18},{3,11},{4,20},{5,13},{6,22},{7,15},{8,24},{9,1... | collective-permute-start | bytes 442376 | tf_op jit(solution)/shard_map/ppermute | solution.py:213
  683.1 28.3 %collective-permute-start.99 = (bf16[1,96,768]{2,1,0:T(8,128)(2,1)S(1)}, bf16[1,96,768]{2,1,0:T(8,128)(2,1)S(1)}, u32[]{:S(2)}, u32[]{:S(2)}) collective-permute-start(bf16[1,96,768]{2,1,0:T(8,128)(2,1)S(1)} %get-tuple-element.72), channel_id=1, source_target_pairs={{0,16},{1,9},{2,18},{3,11},{4,20},{5,13},{6,22},{7,15},{8,24},{9,1... | collective-permute-start | bytes 442376 | tf_op jit(solution)/shard_map/ppermute | solution.py:213
  684.4 27.9 %collective-permute-start.92 = (bf16[2,1,96,768]{3,2,0,1:T(8,128)(2,1)S(1)}, bf16[2,1,96,768]{3,2,0,1:T(8,128)(2,1)S(1)}, u32[]{:S(2)}, u32[]{:S(2)}) collective-permute-start(bf16[2,1,96,768]{3,2,0,1:T(8,128)(2,1)S(1)} %fusion.120), channel_id=1, source_target_pairs={{0,8},{1,17},{2,10},{3,19},{4,12},{5,21},{6,14},{7,23},{8,0},{9,25... | collective-permute-start | bytes 884744 | tf_op jit(solution)/shard_map/ppermute | solution.py:213
  699.5 33.7 %collective-permute-start.74 = (bf16[2,2,2,96,768]{4,3,1,0,2:T(8,128)(2,1)S(1)}, bf16[2,2,2,96,768]{4,3,1,0,2:T(8,128)(2,1)S(1)}, u32[]{:S(2)}, u32[]{:S(2)}) collective-permute-start(bf16[2,2,2,96,768]{4,3,1,0,2:T(8,128)(2,1)S(1)} %dynamic-slice_bitcast_fusion.7), channel_id=1, source_target_pairs={{0,2},{1,3},{6,4},{7,5},{8,10},{9,11},{14,12},{15,13},{16,18},{17,... | collective-permute-start | bytes 3538952 | tf_op jit(solution)/shard_map/ppermute | solution.py:213
  707.7 47.7 %collective-permute-start.56 = (bf16[2,2,2,96,768]{4,3,1,0,2:T(8,128)(2,1)S(1)}, bf16[2,2,2,96,768]{4,3,1,0,2:T(8,128)(2,1)S(1)}, u32[]{:S(2)}, u32[]{:S(2)}) collective-permute-start(bf16[2,2,2,96,768]{4,3,1,0,2:T(8,128)(2,1)S(1)} %dynamic-slice_bitcast_fusion.10), channel_id=1, source_target_pairs={{0,2},{1,3},{6,4},{7,5},{8,10},{9,11},{14,12},{15,13},{16,18},{17,... | collective-permute-start | bytes 3538952 | tf_op jit(solution)/shard_map/ppermute | solution.py:213
  711.3 75.0 %collective-permute-start.98 = (bf16[2,1,96,768]{3,2,0,1:T(8,128)(2,1)S(1)}, bf16[2,1,96,768]{3,2,0,1:T(8,128)(2,1)S(1)}, u32[]{:S(2)}, u32[]{:S(2)}) collective-permute-start(bf16[2,1,96,768]{3,2,0,1:T(8,128)(2,1)S(1)} %fusion.118), channel_id=1, source_target_pairs={{0,8},{1,17},{2,10},{3,19},{4,12},{5,21},{6,14},{7,23},{8,0},{9,25... | collective-permute-start | bytes 884744 | tf_op jit(solution)/shard_map/ppermute | solution.py:213
  712.2 84.0 %collective-permute-start.100 = (bf16[2,1,96,768]{3,2,0,1:T(8,128)(2,1)S(1)}, bf16[2,1,96,768]{3,2,0,1:T(8,128)(2,1)S(1)}, u32[]{:S(2)}, u32[]{:S(2)}) collective-permute-start(bf16[2,1,96,768]{3,2,0,1:T(8,128)(2,1)S(1)} %fusion.116), channel_id=1, source_target_pairs={{0,8},{1,17},{2,10},{3,19},{4,12},{5,21},{6,14},{7,23},{8,0},{9,25... | collective-permute-start | bytes 884744 | tf_op jit(solution)/shard_map/ppermute | solution.py:213
  759.3 27.4 %collective-permute-start.76 = (bf16[2,2,96,768]{3,2,1,0:T(8,128)(2,1)S(1)}, bf16[2,2,96,768]{3,2,1,0:T(8,128)(2,1)S(1)}, u32[]{:S(2)}, u32[]{:S(2)}) collective-permute-start(bf16[2,2,96,768]{3,2,1,0:T(8,128)(2,1)S(1)} %dynamic-slice_bitcast_fusion.12), channel_id=1, source_target_pairs={{0,2},{1,3},{2,0},{3,1},{4,6},{5,7},{6,4},{7,5},{8,10},{9,11},{10,... | collective-permute-start | bytes 1769480 | tf_op jit(solution)/shard_map/ppermute | solution.py:213
  764.0 31.2 %collective-permute-start.58 = (bf16[2,2,96,768]{3,2,1,0:T(8,128)(2,1)S(1)}, bf16[2,2,96,768]{3,2,1,0:T(8,128)(2,1)S(1)}, u32[]{:S(2)}, u32[]{:S(2)}) collective-permute-start(bf16[2,2,96,768]{3,2,1,0:T(8,128)(2,1)S(1)} %dynamic-slice_bitcast_fusion.14), channel_id=1, source_target_pairs={{0,2},{1,3},{2,0},{3,1},{4,6},{5,7},{6,4},{7,5},{8,10},{9,11},{10,... | collective-permute-start | bytes 1769480 | tf_op jit(solution)/shard_map/ppermute | solution.py:213
  797.3 43.1 %collective-permute-start.93 = (bf16[2,96,768]{2,1,0:T(8,128)(2,1)S(1)}, bf16[2,96,768]{2,1,0:T(8,128)(2,1)}, u32[]{:S(2)}, u32[]{:S(2)}) collective-permute-start(bf16[2,96,768]{2,1,0:T(8,128)(2,1)S(1)} %get-tuple-element.64), channel_id=1, source_target_pairs={{0,16},{1,9},{2,18},{3,11},{4,20},{5,13},{6,22},{7,15},{8,24},{9,1... | collective-permute-start | bytes 884744 | tf_op jit(solution)/shard_map/ppermute | solution.py:213
  808.0 33.7 %collective-permute-start.95 = (bf16[2,96,768]{2,1,0:T(8,128)(2,1)S(1)}, bf16[2,96,768]{2,1,0:T(8,128)(2,1)}, u32[]{:S(2)}, u32[]{:S(2)}) collective-permute-start(bf16[2,96,768]{2,1,0:T(8,128)(2,1)S(1)} %get-tuple-element.70), channel_id=1, source_target_pairs={{0,16},{1,9},{2,18},{3,11},{4,20},{5,13},{6,22},{7,15},{8,24},{9,1... | collective-permute-start | bytes 884744 | tf_op jit(solution)/shard_map/ppermute | solution.py:213
  (260 other events, 2295.9 us)

commit v2 on v1

--- a/solution.py
+++ b/solution.py
@@ -123,17 +123,14 @@
     _, pull_two = jax.vjp(layer_norm, residual_two, norm_set[2], norm_set[3])
     grad_two, gain_two, shift_two = pull_two(grad_result)
     branch_low = grad_two.astype(jnp.bfloat16)
-    grad_down = outer_sum(product_low, branch_low)
     product_grad = back_product(branch_low, weight_down).astype(jnp.bfloat16).astype(jnp.float32)
     _, pull_gate = jax.vjp(gelu_gate, gate_up[:, :FF], gate_up[:, FF:])
     grad_gate, grad_up = pull_gate(product_grad)
     gate_up_low = jnp.concatenate([grad_gate, grad_up], axis=1).astype(jnp.bfloat16)
-    grad_gu = outer_sum(normed_low, gate_up_low)
     grad_normed = grad_two + back_product(gate_up_low, weight_gu)
     _, pull_one = jax.vjp(layer_norm, residual_one, norm_set[0], norm_set[1])
     grad_one, gain_one, shift_one = pull_one(grad_normed)
     attend_low = grad_one.astype(jnp.bfloat16)
-    grad_out_weight = outer_sum(mixture_low, attend_low)
     mixture_grad = (
         back_product(attend_low, weight_out)
         .astype(jnp.bfloat16)
@@ -165,10 +162,15 @@
         .reshape(inputs_low.shape[0], 3 * D)
         .astype(jnp.bfloat16)
     )
-    grad_qkv = outer_sum(inputs_low, qkv_grad)
     grad_input = grad_one + back_product(qkv_grad, weight_qkv)
     grad_norms = jnp.stack([gain_one, shift_one, gain_two, shift_two])
-    return (grad_input, (grad_qkv, grad_out_weight, grad_gu, grad_down, grad_norms))
+    factors = (
+        (inputs_low, qkv_grad),
+        (mixture_low, attend_low),
+        (normed_low, gate_up_low),
+        (product_low, branch_low),
+    )
+    return (grad_input, factors, grad_norms)
 
 
 def adam_step(weight, first_moment, second_moment, gradient, factor, step_rate, decay_rate):
@@ -184,16 +186,15 @@
 
 
 both_axes = ("rep", "fsdp")
+HALF = D // 2
 
 
 def pairs_of(move):
     found = []
     for rep in range(4):
         for shard in range(8):
-            target = move(rep // 2, rep % 2, shard // 2, shard % 2)
-            if target is not None:
-                to_y, to_x, to_z, to_c = target
-                found.append((rep * 8 + shard, (to_y * 2 + to_x) * 8 + to_z * 2 + to_c))
+            to_y, to_x, to_z, to_c = move(rep // 2, rep % 2, shard // 2, shard % 2)
+            found.append((rep * 8 + shard, (to_y * 2 + to_x) * 8 + to_z * 2 + to_c))
     return found
 
 
@@ -202,11 +203,9 @@
 FLIP_Y = pairs_of(lambda y, x, z, c: (1 - y, x, z, c))
 FLIP_FIRST = pairs_of(lambda y, x, z, c: (y, 1 - x, z, c) if c == 0 else (1 - y, x, z, c))
 FLIP_SECOND = pairs_of(lambda y, x, z, c: (1 - y, x, z, c) if c == 0 else (y, 1 - x, z, c))
-Z_MATE = pairs_of(lambda y, x, z, c: (y, x, z ^ 1, c))
-Z_CROSS = pairs_of(lambda y, x, z, c: (y, x, 3 - z, c))
-Z_MIDDLE = pairs_of(lambda y, x, z, c: (y, x, 3 - z, c) if z in (1, 2) else None)
-Z_OUTWARD = pairs_of(lambda y, x, z, c: (y, x, z ^ 1, c) if z in (1, 2) else None)
-Z_INWARD = pairs_of(lambda y, x, z, c: (y, x, z ^ 1, c) if z in (0, 3) else None)
+Z_ONE = pairs_of(lambda y, x, z, c: (y, x, z ^ 1, c))
+Z_TWO = pairs_of(lambda y, x, z, c: (y, x, z ^ 2, c))
+Z_THREE = pairs_of(lambda y, x, z, c: (y, x, z ^ 3, c))
 
 
 def send(values, pairs):
@@ -222,27 +221,32 @@
     return (z, c, first, second)
 
 
-def pick(values, index, axis):
-    return lax.dynamic_index_in_dim(values, index, axis, keepdims=False)
-
-
-def in_order(mine, other, bit):
-    return lax.dynamic_slice_in_dim(jnp.stack([mine, other, mine]), bit, 2, 0)
+def place_array():
+    return jnp.stack(place()).astype(jnp.int32)
+
+
+def by_neighbours():
+    return lax.axis_size("rep") == 4 and lax.axis_size("fsdp") == 8
+
+
+def whole(array):
+    zeros = (0,) * array.ndim
+    return pl.BlockSpec(array.shape, lambda *_: zeros)
+
+
+def kernel_cost(flops, bytes_accessed):
+    return pl.CostEstimate(flops=flops, bytes_accessed=bytes_accessed, transcendentals=0)
 
 
 def gather_chunk(own):
     z, c, first, second = place()
-    quarter = pick(own, 2 * first + second, 0)
-    mate = send(quarter, Z_MATE)
-    pair = in_order(quarter, mate, z % 2)
-    got_middle = send(pair, Z_MIDDLE)
-    got_outward = send(got_middle, Z_OUTWARD)
-    inner = (z == 1) | (z == 2)
-    other = jnp.where(inner, got_middle, got_outward)
-    three = jnp.concatenate([mate[None], other])
-    six = jnp.stack([three, send(three, FLIP_SECOND)])
-    far = send(six, FLIP_FIRST)
-    return (own, six, far, send(own, FLIP_CORE), send(six, FLIP_CORE), send(far, FLIP_CORE))
+    quarter = lax.dynamic_index_in_dim(own, 2 * first + second, 0, keepdims=False)
+    near = jnp.stack([send(quarter, Z_ONE), send(quarter, Z_TWO), send(quarter, Z_THREE)])
+    across = send(near, FLIP_SECOND)
+    far = send(near, FLIP_FIRST)
+    corner = send(across, FLIP_FIRST)
+    pieces = (own, near, across, far, corner)
+    return pieces + tuple(send(piece, FLIP_CORE) for piece in pieces)
 
 
 def assemble(pieces, kind):
@@ -255,10 +259,8 @@
     }[kind]
 
     def kernel(*refs):
-        in_refs, out_refs, sem = refs[:6], refs[6:-1], refs[-1]
+        in_refs, out_refs, sem = refs[:10], refs[10:-1], refs[-1]
         z, c, first, second = place()
-        low = jnp.where(z < 2, 2, 0)
-        others = (z ^ 1, low, low + 1)
 
         def copy(source, quarter, block, shard):
             row = pl.multiple_of(shard * rows, rows)
@@ -285,70 +287,429 @@
                 pltpu.make_async_copy(source, target, sem).start()
 
         for side in range(2):
-            own, six, far = in_refs[3 * side : 3 * side + 3]
+            own, near, across, far, corner = in_refs[5 * side : 5 * side + 5]
             core = c if side == 0 else 1 - c
-            high, little = (first, second) if side == 0 else (second, first)
+            high, low = (first, second) if side == 0 else (second, first)
             for block in range(count):
                 for quarter in range(4):
                     copy(own.at[quarter, block], jnp.int32(quarter), block, 2 * z + core)
-                for turn in range(2):
-                    unit = little if turn == 0 else 1 - little
-                    for step in range(3):
-                        shard = 2 * others[step] + core
-                        copy(six.at[turn, step, block], 2 * high + unit, block, shard)
-                        copy(far.at[turn, step, block], 2 * (1 - high) + unit, block, shard)
+                for step in range(3):
+                    shard = 2 * (z ^ (step + 1)) + core
+                    copy(near.at[step, block], 2 * high + low, block, shard)
+                    copy(across.at[step, block], 2 * high + 1 - low, block, shard)
+                    copy(far.at[step, block], 2 * (1 - high) + low, block, shard)
+                    copy(corner.at[step, block], 2 * (1 - high) + 1 - low, block, shard)
         for out_ref in out_refs:
             pltpu.make_async_copy(out_ref, out_ref, sem).wait()
 
     return pl.pallas_call(
         kernel,
         out_shape=tuple(jax.ShapeDtypeStruct(shape, jnp.bfloat16) for shape in shapes),
-        in_specs=[pl.BlockSpec(memory_space=pl.ANY)] * 6,
+        in_specs=[pl.BlockSpec(memory_space=pl.ANY)] * 10,
         out_specs=tuple(pl.BlockSpec(memory_space=pltpu.VMEM) for _ in shapes),
         scratch_shapes=[pltpu.SemaphoreType.DMA],
         compiler_params=pltpu.CompilerParams(vmem_limit_bytes=24 * 2**20),
+        cost_estimate=kernel_cost(0, 2 * 2 * 8 * 4 * count * rows * D),
         name="assemble_" + kind,
     )(*pieces)
 
 
-def add_low(left, right):
-    return (left.astype(jnp.float32) + right.astype(jnp.float32)).astype(jnp.bfloat16)
-
-
-def scatter_chunk(parts):
-    z, c, first, second = place()
-    count, rows = parts.shape[1], parts.shape[3]
-    parts = parts.reshape(2, 2, count, 4, 2, rows, D)
-    got = send(pick(parts, 1 - c, 4), FLIP_CORE)
-    parts = add_low(pick(parts, c, 4), got)
-    got = send(pick(parts, 1 - first, 0), FLIP_FIRST)
-    parts = add_low(pick(parts, first, 0), got)
-    parts = parts.reshape(2, count, 2, 2, rows, D)
-    theirs = pick(parts, 1 - z // 2, 2)
-    mine = pick(parts, z // 2, 2)
-    theirs = add_low(theirs, send(theirs, Z_INWARD))
-    mine = add_low(mine, send(theirs, Z_MIDDLE))
-    got = send(pick(mine, 1 - z % 2, 2), Z_MATE)
-    mine = add_low(pick(mine, z % 2, 2), got)
-    got = send(pick(mine, 1 - second, 0), FLIP_SECOND)
-    return add_low(pick(mine, second, 0), got)
-
-
-def spread_chunk(quarter):
-    z, c, first, second = place()
-    row = in_order(quarter, send(quarter, FLIP_SECOND), second)
-    whole = in_order(row, send(row, FLIP_FIRST), first)
-    return whole.reshape((4,) + quarter.shape)
+def gather_norms(norm_params):
+    width = norm_params.shape[2]
+    own = norm_params.astype(jnp.bfloat16).reshape(8, width)
+    mine = jnp.stack([own, send(own, Z_ONE), send(own, Z_TWO), send(own, Z_THREE)])
+    parts = jnp.stack([mine, send(mine, FLIP_CORE)]).astype(jnp.float32)
+
+    def kernel(place_ref, parts_ref, out_ref):
+        z, c = place_ref[0], place_ref[1]
+        for shard in range(8):
+            values = parts_ref[(shard % 2) ^ c, (shard // 2) ^ z]
+            out_ref[:, shard * width : (shard + 1) * width] = values
+
+    return pl.pallas_call(
+        kernel,
+        out_shape=jax.ShapeDtypeStruct((8, 8 * width), jnp.float32),
+        in_specs=[
+            pl.BlockSpec(memory_space=pltpu.SMEM),
+            pl.BlockSpec(memory_space=pltpu.VMEM),
+        ],
+        out_specs=pl.BlockSpec(memory_space=pltpu.VMEM),
+        name="norm_columns",
+    )(place_array(), parts)
+
+
+def chip_product(left, right, left_other, right_other):
+    dims = (((0,), (0,)), ((), ()))
+    return lax.dot_general(
+        left, right, dims, preferred_element_type=jnp.float32
+    ) + lax.dot_general(left_other, right_other, dims, preferred_element_type=jnp.float32)
+
+
+def turn(step, where):
+    first, second = where[2], where[3]
+    return 2 * (first ^ (1 - step // 2)) + (second ^ (1 - step % 2))
+
+
+def store_rows(out_ref, product, z, rows):
+    for chip in range(4):
+        piece = product[chip * 2 * rows : (chip + 1) * 2 * rows]
+        out_ref[0, chip ^ z, 0] = piece.reshape(2, rows, HALF).astype(jnp.bfloat16)
+
+
+def grad_attend(inputs, inputs_other, qkv, qkv_other, mixed, mixed_other, out, out_other):
+    tokens = inputs.shape[0]
+    rows = D // 8
+
+    def kernel(where, a, a2, g, g2, o, o2, b, b2, sent, kept):
+        step = pl.program_id(0)
+        quarter = turn(step, where)
+
+        def put(product):
+            @pl.when(step < 2)
+            def _():
+                store_rows(sent, product, where[0], rows)
+
+            @pl.when(step >= 2)
+            def _():
+                store_rows(kept, product, where[0], rows)
+
+        @pl.when(quarter < 3)
+        def _():
+            put(chip_product(a[...], g[...], a2[...], g2[...]))
+
+        @pl.when(quarter == 3)
+        def _():
+            put(chip_product(o[...], b[...], o2[...], b2[...]))
+
+    def own_column(step, where):
+        return (0, 2 * jnp.minimum(turn(step, where), 2) + where[1])
+
+    def other_column(step, where):
+        return (0, jnp.minimum(turn(step, where), 2))
+
+    shape = (2, 4, 1, 2, rows, HALF)
+    block = (1, 4, 1, 2, rows, HALF)
+    return pl.pallas_call(
+        kernel,
+        out_shape=(jax.ShapeDtypeStruct(shape, jnp.bfloat16),) * 2,
+        grid_spec=pltpu.PrefetchScalarGridSpec(
+            num_scalar_prefetch=1,
+            grid=(4,),
+            in_specs=[
+                whole(inputs),
+                whole(inputs_other),
+                pl.BlockSpec((tokens, HALF), own_column),
+                pl.BlockSpec((tokens, HALF), other_column),
+                whole(mixed),
+                whole(mixed_other),
+                pl.BlockSpec((tokens, HALF), lambda step, where: (0, where[1])),
+                whole(out_other),
+            ],
+            out_specs=[
+                pl.BlockSpec(block, lambda step, where: (jnp.minimum(step, 1), 0, 0, 0, 0, 0)),
+                pl.BlockSpec(
+                    block, lambda step, where: (jnp.maximum(step, 2) - 2, 0, 0, 0, 0, 0)
+                ),
+            ],
+        ),
+        compiler_params=pltpu.CompilerParams(vmem_limit_bytes=32 * 2**20),
+        cost_estimate=kernel_cost(2 * 2 * tokens * 2 * D * D, 2 * D * 2 * D + 12 * tokens * D),
+        name="grad_attend",
+    )(place_array(), inputs, inputs_other, qkv, qkv_other, mixed, mixed_other, out, out_other)
+
+
+def grad_gate_up(inputs, inputs_other, grads, grads_other):
+    tokens = inputs.shape[0]
+    rows = D // 8
+
+    def kernel(where, a, a2, g, g2, sent, kept):
+        step = pl.program_id(0)
+        product = chip_product(a[...], g[...], a2[...], g2[...])
+
+        @pl.when(step < 4)
+        def _():
+            store_rows(sent, product, where[0], rows)
+
+        @pl.when(step >= 4)
+        def _():
+            store_rows(kept, product, where[0], rows)
+
+    def column(step, where):
+        return (step % 2) * 4 + turn(step // 2, where)
+
+    shape = (2, 4, 2, 2, rows, HALF)
+    block = (1, 4, 1, 2, rows, HALF)
+
+    def sent_at(step, where):
+        held = jnp.minimum(step, 3)
+        return (held // 2, 0, held % 2, 0, 0, 0)
+
+    def kept_at(step, where):
+        held = jnp.maximum(step, 4) - 4
+        return (held // 2, 0, held % 2, 0, 0, 0)
+
+    return pl.pallas_call(
+        kernel,
+        out_shape=(jax.ShapeDtypeStruct(shape, jnp.bfloat16),) * 2,
+        grid_spec=pltpu.PrefetchScalarGridSpec(
+            num_scalar_prefetch=1,
+            grid=(8,),
+            in_specs=[
+                whole(inputs),
+                whole(inputs_other),
+                pl.BlockSpec(
+                    (tokens, HALF), lambda step, where: (0, 2 * column(step, where) + where[1])
+                ),
+                pl.BlockSpec((tokens, HALF), lambda step, where: (0, column(step, where))),
+            ],
+            out_specs=[pl.BlockSpec(block, sent_at), pl.BlockSpec(block, kept_at)],
+        ),
+        compiler_params=pltpu.CompilerParams(vmem_limit_bytes=32 * 2**20),
+        cost_estimate=kernel_cost(2 * 2 * tokens * D * FF, 2 * D * FF + 8 * tokens * FF),
+        name="grad_gate_up",
+    )(place_array(), inputs, inputs_other, grads, grads_other)
+
+
+def grad_down(inputs, inputs_other, grads, grads_other):
+    tokens = inputs.shape[0]
+    rows = FF // 32
+
+    def kernel(where, a, a2, g, g2, sent, kept):
+        product = chip_product(a[...], g[...], a2[...], g2[...])
+        product = product.astype(jnp.bfloat16).reshape(2, 4, rows, HALF)
+        for quarter in range(4):
+            away = (quarter // 2) ^ where[2]
+            spot = 1 - ((quarter % 2) ^ where[3])
+
+            @pl.when(away == 1)
+            def _():
+                sent[spot, 0, 0] = product[:, quarter]
+
+            @pl.when(away == 0)
+            def _():
+                kept[spot, 0, 0] = product[:, quarter]
+
+    def chip_columns(step, where):
+        return (0, step ^ where[0])
+
+    shape = (2, 4, 1, 2, rows, HALF)
+    spec = pl.BlockSpec((2, 1, 1, 2, rows, HALF), lambda step, where: (0, step, 0, 0, 0, 0))
+    return pl.pallas_call(
+        kernel,
+        out_shape=(jax.ShapeDtypeStruct(shape, jnp.bfloat16),) * 2,
+        grid_spec=pltpu.PrefetchScalarGridSpec(
+            num_scalar_prefetch=1,
+            grid=(4,),
+            in_specs=[
+                pl.BlockSpec((tokens, FF // 4), chip_columns),
+                pl.BlockSpec((tokens, FF // 4), chip_columns),
+                pl.BlockSpec((tokens, HALF), lambda step, where: (0, where[1])),
+                whole(grads_other),
+            ],
+            out_specs=[spec, spec],
+        ),
+        compiler_params=pltpu.CompilerParams(vmem_limit_bytes=32 * 2**20),
+        cost_estimate=kernel_cost(2 * 2 * tokens * FF * HALF, 2 * FF * HALF + 8 * tokens * FF),
+        name="grad_down",
+    )(place_array(), inputs, inputs_other, grads, grads_other)
+
+
+def add_halves(kept, got):
+    def kernel(kept_ref, got_ref, sent_ref, left_ref):
+        for place_at, out_ref in ((0, sent_ref), (1, left_ref)):
+            total = kept_ref[place_at].astype(jnp.float32) + got_ref[place_at].astype(jnp.float32)
+            out_ref[...] = total.astype(jnp.bfloat16)
+
+    rest = kept.shape[3:]
+    count = kept.shape[2]
+    spec_in = pl.BlockSpec((2, 1, count) + rest, lambda step: (0, step, 0, 0, 0, 0))
+    spec_out = pl.BlockSpec((1, count) + rest, lambda step: (step, 0, 0, 0, 0))
+    return pl.pallas_call(
+        kernel,
+        grid=(4,),
+        out_shape=(jax.ShapeDtypeStruct(kept.shape[1:], jnp.bfloat16),) * 2,
+        in_specs=[spec_in] * 2,
+        out_specs=[spec_out] * 2,
+        compiler_params=pltpu.CompilerParams(vmem_limit_bytes=32 * 2**20),
+        cost_estimate=kernel_cost(kept.size, 6 * kept.size),
+        name="add_halves",
+    )(kept, got)
+
+
+def add_chips(left, got):
+    def kernel(left_ref, got_ref, *out_refs):
+        for chip, out_ref in enumerate(out_refs):
+            total = left_ref[chip].astype(jnp.float32) + got_ref[chip].astype(jnp.float32)
+            out_ref[...] = total.astype(jnp.bfloat16)
+
+    return pl.pallas_call(
+        kernel,
+        out_shape=(jax.ShapeDtypeStruct(left.shape[1:], jnp.bfloat16),) * 4,
+        in_specs=[pl.BlockSpec(memory_space=pltpu.VMEM)] * 2,
+        out_specs=[pl.BlockSpec(memory_space=pltpu.VMEM)] * 4,
+        compiler_params=pltpu.CompilerParams(vmem_limit_bytes=32 * 2**20),
+        cost_estimate=kernel_cost(left.size, 6 * left.size),
+        name="add_chips",
+    )(left, got)
+
+
+def add_last(parts):
+    count, _, rows, width = parts[0].shape
+
+    def kernel(where, *refs):
+        part_refs, (mine, theirs, squares) = refs[:4], refs[4:]
+        total = jnp.zeros((8, width), jnp.float32)
+        for block in range(count):
+            for core in range(2):
+                value = part_refs[0][block, core].astype(jnp.float32)
+                for part_ref in part_refs[1:]:
+                    value = value + part_ref[block, core].astype(jnp.float32)
+                low = value.astype(jnp.bfloat16)
+                value = low.astype(jnp.float32)
+                total = total + jnp.sum((value * value).reshape(rows // 8, 8, width), axis=0)
+
+                @pl.when(where[1] == core)
+                def _():
+                    mine[block] = low
+
+                @pl.when(where[1] != core)
+                def _():
+                    theirs[block] = low
+
+        squares[...] = total
+
+    shape = jax.ShapeDtypeStruct((count, rows, width), jnp.bfloat16)
+    vmem = pl.BlockSpec(memory_space=pltpu.VMEM)
+    return pl.pallas_call(
+        kernel,
+        out_shape=(shape, shape, jax.ShapeDtypeStruct((8, width), jnp.float32)),
+        in_specs=[pl.BlockSpec(memory_space=pltpu.SMEM)] + [vmem] * 4,
+        out_specs=[vmem] * 3,
+        compiler_params=pltpu.CompilerParams(vmem_limit_bytes=32 * 2**20),
+        cost_estimate=kernel_cost(4 * parts[0].size, 10 * parts[0].size),
+        name="add_last",
+    )(place_array(), *parts)
+
+
+def reduce_chunk(sent, kept):
+    away, left = add_halves(kept, send(sent, FLIP_FIRST))
+    parts = add_chips(left, send(away, FLIP_SECOND))
+    parts = (
+        parts[0],
+        send(parts[1], Z_ONE),
+        send(parts[2], Z_TWO),
+        send(parts[3], Z_THREE),
+    )
+    mine, theirs, squares = add_last(parts)
+    pair = jnp.stack([mine, send(theirs, FLIP_CORE)])
+    across = send(pair, FLIP_SECOND)
+    far = send(pair, FLIP_FIRST)
+    return ((pair, across, far, send(across, FLIP_FIRST)), squares)
+
+
+def other_half(grads, c):
+    tokens, width = grads.shape
+    blocks = grads.reshape(tokens, width // D, 2, HALF)
+    chosen = jnp.where(c == 0, blocks[:, :, 1], blocks[:, :, 0])
+    return chosen.reshape(tokens, width // 2)
+
+
+def reduce_layer(factors):
+    (inputs, qkv), (mixed, out), (normed, gate_up), (product, branch) = factors
+    c = place()[1]
+    rest = tuple(send(other_half(grads, c), FLIP_CORE) for grads in (qkv, out, gate_up, branch))
+    qkv_other, out_other, gate_up_other, branch_other = rest
+    down = grad_down(product, send(product, FLIP_CORE), branch, branch_other)
+    wide = grad_gate_up(normed, send(normed, FLIP_CORE), gate_up, gate_up_other)
+    attend = grad_attend(
+        inputs,
+        send(inputs, FLIP_CORE),
+        qkv,
+        qkv_other,
+        mixed,
+        send(mixed, FLIP_CORE),
+        out,
+        out_other,
+    )
+    down, squares_down = reduce_chunk(*down)
+    wide, squares_wide = reduce_chunk(*wide)
+    attend, squares_attend = reduce_chunk(*attend)
+    return (attend, wide, down, squares_down + squares_wide + squares_attend)
+
+
+def adam_blocks(weight, first_moment, second_moment, layers, factor, kind):
+    layer_count, rows_all, width = weight.shape
+    rows = layers[0][0].shape[2]
+    blocks = (rows_all // rows) * (width // D)
+    by_rows = rows_all // rows
+
+    def kernel(where, factor_ref, w, m, v, *refs):
+        piece_refs, outs = refs[: 4 * layer_count], refs[4 * layer_count :]
+        layer = pl.program_id(0)
+        block = pl.program_id(1)
+        c, first, second = where[1], where[2], where[3]
+        if kind == "gate_up":
+            quarter, index = block % 4, block // 4
+        elif kind == "out":
+            quarter, index = 3, 0
+        else:
+            quarter, index = block, 0
+        for half in range(2):
+            other = c ^ half
+            swapped = other == 1
+            high, low = quarter // 2, quarter % 2
+            flip_first = first ^ jnp.where(swapped, low, high)
+            flip_second = second ^ jnp.where(swapped, high, low)
+            number = 2 * flip_first + flip_second
+            columns = slice(half * HALF, (half + 1) * HALF)
+
+            def pick_piece(at):
+                values = [piece_refs[4 * at + turn][other, index] for turn in range(4)]
+                low_pair = jnp.where(number % 2 == 0, values[0], values[1])
+                high_pair = jnp.where(number % 2 == 0, values[2], values[3])
+                return jnp.where(number // 2 == 0, low_pair, high_pair).astype(jnp.float32)
+
+            gradient = pick_piece(0)
+            for at in range(1, layer_count):
+                gradient = jnp.where(layer == at, pick_piece(at), gradient)
+            results = adam_step(
+                w[0, :, columns],
+                m[0, :, columns],
+                v[0, :, columns],
+                gradient,
+                factor_ref[0],
+                rate_matrix,
+                decay_matrix,
+            )
+            for out, result in zip(outs, results):
+                out[0, :, columns] = result
+
+    def at(layer, block, where):
+        return (layer, block, 0) if by_rows > 1 else (layer, 0, block)
+
+    state = pl.BlockSpec((1, rows, D), at)
+    pieces = [piece for layer in layers for piece in layer]
+    return pl.pallas_call(
+        kernel,
+        out_shape=(jax.ShapeDtypeStruct(weight.shape, jnp.float32),) * 3,
+        grid_spec=pltpu.PrefetchScalarGridSpec(
+            num_scalar_prefetch=1,
+            grid=(layer_count, blocks),
+            in_specs=[pl.BlockSpec(memory_space=pltpu.SMEM)]
+            + [state] * 3
+            + [whole(piece) for piece in pieces],
+            out_specs=[state] * 3,
+        ),
+        compiler_params=pltpu.CompilerParams(vmem_limit_bytes=32 * 2**20),
+        cost_estimate=kernel_cost(20 * weight.size, 24 * weight.size),
+        name="adam_" + kind,
+    )(place_array(), factor.reshape(1), weight, first_moment, second_moment, *pieces)
 
 
 def sum_all(value):
-    for pairs in (FLIP_CORE, FLIP_X, FLIP_Y, Z_MATE, Z_CROSS):
+    for pairs in (FLIP_CORE, FLIP_X, FLIP_Y, Z_ONE, Z_TWO):
         value = value + send(value, pairs)
     return value
-
-
-def by_neighbours():
-    return lax.axis_size("rep") == 4 and lax.axis_size("fsdp") == 8
 
 
 def gather_layer(w_qkv, w_out, w_gu, w_down):
@@ -365,36 +726,50 @@
     return (weight_qkv, weight_out, weight_gu, weight_down)
 
 
-def reduce_layer(grad_qkv, grad_out, grad_gu, grad_down):
-    if not by_neighbours():
-        sums = []
-        squares = jnp.float32(0.0)
-        for grad in (grad_qkv, grad_out, grad_gu, grad_down):
-            part = lax.psum_scatter(grad, "fsdp", scatter_dimension=0, tiled=True)
-            part = lax.psum(part, "rep")
-            squares = squares + jnp.sum(part * part) / lax.axis_size("rep")
-            sums.append(part)
-        return (tuple(sums), squares)
-    rows = grad_qkv.shape[0] // 8
-    grad_qkv, grad_out, grad_gu, grad_down = (
-        grad.astype(jnp.bfloat16) for grad in (grad_qkv, grad_out, grad_gu, grad_down)
-    )
-    attend = jnp.stack(
-        [grad_qkv[:, :D], grad_qkv[:, D : 2 * D], grad_qkv[:, 2 * D :], grad_out]
-    ).reshape(4, 1, 8, rows, D)
-    gate_up = grad_gu.reshape(8, rows, 2, 4, D).transpose(3, 2, 0, 1, 4)
-    down = grad_down.reshape(8, 4, rows, D).transpose(1, 0, 2, 3)[:, None]
-    squares = jnp.float32(0.0)
-    sums = []
-    for chunk in (down, gate_up, attend):
-        quarter = scatter_chunk(chunk)
-        wide = quarter.astype(jnp.float32)
-        squares = squares + jnp.sum(wide * wide)
-        sums.append(spread_chunk(quarter))
-    down, gate_up, attend = sums
-    grad_qkv = jnp.concatenate([attend[0, 0], attend[1, 0], attend[2, 0]], axis=1)
-    grad_gu = gate_up.transpose(2, 1, 0, 3).reshape(rows, 2 * FF)
-    return ((grad_qkv, attend[3, 0], grad_gu, down.reshape(4 * rows, D)), squares)
+def update(states, norm_state, factors, norm_list):
+    layer_count = len(factors)
+    norm_grads = jnp.concatenate(norm_list)
+    width = norm_state[0].shape[2]
+    if by_neighbours():
+        reduced = [None] * layer_count
+        squares = jnp.zeros((8, HALF), jnp.float32)
+        for layer in reversed(range(layer_count)):
+            *reduced[layer], part = reduce_layer(factors[layer])
+            squares = squares + part
+        rows = norm_grads.shape[0]
+        packed = jnp.concatenate([norm_grads, jnp.pad(squares, ((0, 0), (0, D - HALF)))])
+        packed = sum_all(packed)
+        norm_grads = packed[:rows]
+        total = jnp.sum(packed[rows:])
+    else:
+        total = jnp.float32(0.0)
+        reduced = []
+        for layer in range(layer_count):
+            sums = []
+            for left, right in factors[layer]:
+                part = outer_sum(left, right)
+                part = lax.psum_scatter(part, "fsdp", scatter_dimension=0, tiled=True)
+                part = lax.psum(part, "rep")
+                total = total + jnp.sum(part * part)
+                sums.append(part)
+            reduced.append(sums)
+        total = lax.psum(total, "fsdp")
+        norm_grads = lax.psum(norm_grads, both_axes)
+    grad_norm = jnp.sqrt(total + jnp.sum(norm_grads * norm_grads))
+    factor = clip_norm / jnp.maximum(grad_norm, clip_norm)
+    updated = []
+    for kind, state in enumerate(states):
+        if by_neighbours():
+            chunk, name = ((0, "qkv"), (0, "out"), (1, "gate_up"), (2, "down"))[kind]
+            layers = [pieces[chunk] for pieces in reduced]
+            updated += adam_blocks(*state, layers, factor, name)
+        else:
+            gradient = jnp.stack([sums[kind] for sums in reduced])
+            updated += adam_step(*state, gradient, factor, rate_matrix, decay_matrix)
+    norm_grads = norm_grads.reshape(layer_count, -1, D)
+    norm_grads = lax.dynamic_slice_in_dim(norm_grads, lax.axis_index("fsdp") * width, width, 2)
+    updated += adam_step(*norm_state, norm_grads, factor, rate_norm, 0.0)
+    return (grad_norm, updated)
 
 
 def body(
@@ -423,44 +798,34 @@
     hidden = jnp.where(
         masked, mask_embedding.astype(jnp.float32)[None, :], tokens_in.astype(jnp.float32)
     )
-    norm_low = lax.all_gather(norm_params.astype(jnp.bfloat16), "fsdp", axis=2, tiled=True)
+    if by_neighbours():
+        norm_all = gather_norms(norm_params).reshape(layer_count, 4, D)
+    else:
+        norm_all = lax.all_gather(norm_params.astype(jnp.bfloat16), "fsdp", axis=2, tiled=True)
     kept_list = []
     weight_list = []
     for layer in range(layer_count):
         weights = gather_layer(w_qkv[layer], w_out[layer], w_gu[layer], w_down[layer])
-        weights = weights + (norm_low[layer],)
+        weights = weights + (norm_all[layer],)
         hidden, kept_state = forward_layer(hidden, weights)
         kept_list.append(kept_state)
         weight_list.append(weights)
     activations = hidden.astype(jnp.bfloat16)
     grad_hidden = out_cotangent.astype(jnp.float32) * masked_flags[:, None].astype(jnp.float32)
-    grad_list = [None] * layer_count
+    factor_list = [None] * layer_count
     norm_list = [None] * layer_count
-    squares = jnp.float32(0.0)
     for layer in reversed(range(layer_count)):
-        grad_hidden, local_grads = backward_layer(
+        grad_hidden, factor_list[layer], norm_list[layer] = backward_layer(
             grad_hidden, weight_list[layer], kept_list[layer]
         )
-        grad_list[layer], part = reduce_layer(*local_grads[:4])
-        squares = squares + part
-        norm_list[layer] = local_grads[4]
-    grad_norms = lax.psum(jnp.stack(norm_list), both_axes)
-    total = sum_all(squares) if by_neighbours() else lax.psum(squares, both_axes)
-    grad_norm = jnp.sqrt(total + jnp.sum(grad_norms * grad_norms))
-    factor = clip_norm / jnp.maximum(grad_norm, clip_norm)
-    width = norm_params.shape[2]
-    grad_norms = lax.dynamic_slice_in_dim(grad_norms, lax.axis_index("fsdp") * width, width, 2)
     states = (
         (w_qkv, m_qkv, v_qkv),
         (w_out, m_out, v_out),
         (w_gu, m_gu, v_gu),
         (w_down, m_down, v_down),
     )
-    updated = []
-    for kind, state in enumerate(states):
-        gradient = jnp.stack([grads[kind] for grads in grad_list]).astype(jnp.float32)
-        updated += adam_step(*state, gradient, factor, rate_matrix, decay_matrix)
-    updated += adam_step(norm_params, m_norms, v_norms, grad_norms, factor, rate_norm, 0.0)
+    norm_state = (norm_params, m_norms, v_norms)
+    grad_norm, updated = update(states, norm_state, factor_list, norm_list)
     input_grad = jnp.where(masked, 0.0, grad_hidden)
     return (activations, input_grad, grad_norm, *updated)
 

time: 882 us -> 807 us (0.915)
  Pallas kernels: 20 us -> 108 us
  blocking collectives: 86.1 us -> 0 us
  other arithmetic: 129 us -> 70.9 us
  local copies, waits for them, and re-layouts: 201 us -> 177 us
  waiting for transfers between devices: 206 us -> 219 us
  matrix products: 69.8 us -> 60 us
  starting transfers between devices: 146 us -> 155 us
    pallas_call x0 -> x29, Pallas kernels: none -> 84.5 us  [the longest x4 26.7 us: adam_blocks(): pl.pallas_call(kernel, out_shape=(jax.ShapeDtypeStruct(weight.shape, jnp....]
    reshape x4 -> x1, local copies, waits for them, and re-layouts: 69.7 us -> 1.35 us  [update(): norm_grads = norm_grads.reshape(layer_count, -1, D)]
    unnamed x414 -> x548, local copies, waits for them, and re-layouts: 26.6 us -> 86 us
    all_gather x1 -> x0, blocking collectives: 48.1 us -> none  [body(): lax.all_gather(norm_params.astype(jnp.bfloat16), 'fsdp', axis=2, tiled=True)]
    psum x1 -> x0, blocking collectives: 38 us -> none  [body(): grad_norms = lax.psum(jnp.stack(norm_list), both_axes)]
    dynamic_slice x12 -> x0, local copies, waits for them, and re-layouts: 29.2 us -> none  [pick(): return lax.dynamic_index_in_dim(values, index, axis, keepdims=False)]
    convert_element_type x32 -> x10, other arithmetic: 32.1 us -> 3.52 us  [the longest x2 2.07 us: forward_layer(): inputs_low = hidden.astype(jnp.bfloat16)]
    concatenate x0 -> x9, local copies, waits for them, and re-layouts: none -> 24.5 us  [the longest x8 24.5 us: backward_layer(): jnp.concatenate([grad_gate, grad_up], axis=1).astype(jnp.bfloat16)]
  transfers between devices with their start and end apart: 101 -> 145, of which waited for: 35 -> 39; matrix products, arithmetic and copies ran while one was open for 31% -> 30% of each run, Pallas kernels for 2% -> 12%
where the time goes in v2:
time: 807 us; the launch traced here: 797 us
  waiting for transfers between devices  219 us (27%)
  local copies, waits for them, and re-layouts  177 us (22%)
  starting transfers between devices  155 us (19%)
  Pallas kernels  108 us (13%)
  other arithmetic  70.9 us (9%)
  matrix products  60 us (7%)
    ppermute x145, waiting for transfers between devices, send(): return lax.ppermute(values, both_axes, pairs)  219 us
    ppermute x145, starting transfers between devices, send(): return lax.ppermute(values, both_axes, pairs)  155 us
    unnamed x548, local copies, waits for them, and re-layouts  86 us
    dot_general x8, matrix products, back_product(): lax.dot_general(gradient, weight, (((1,), (1,)), ((), ())), preferred_ele...  27.7 us
    pallas_call x4, Pallas kernels, adam_blocks(): pl.pallas_call(kernel, out_shape=(jax.ShapeDtypeStruct(weight.shape, jnp....  26.7 us
    concatenate x8, local copies, waits for them, and re-layouts, backward_layer(): jnp.concatenate([grad_gate, grad_up], axis=1).astype(jnp.bfloat16)  24.5 us
    pallas_call x6, Pallas kernels, assemble(): pl.pallas_call(kernel, out_shape=tuple((jax.ShapeDtypeStruct(shape, jnp.b...  23.5 us
    pallas_call x2, Pallas kernels, grad_gate_up(): pl.pallas_call(kernel, out_shape=(jax.ShapeDtypeStruct(shape, jnp.bfloat1...  19.2 us
  transfers between devices with their start and end apart: 145, of which 39 were waited for; matrix products, arithmetic and copies ran while one was open for 30% of the time, Pallas kernels for 12%

profile of v2, /device:TPU:0, one launch (start us, length us, event | category | flops | bytes accessed | tf_op | source)
XLA Modules:
  0.0 796.8 jit_solution(12559463474014366732)
XLA Ops:
  9.0 3.9 collective-permute-start.13
  22.9 3.8 collective-permute-start.38
  27.2 5.0 collective-permute-done.1
  34.6 8.4 %collective-permute-start.60 = (bf16[1,96,768]{2,1,0:T(8,128)(2,1)}, bf16[1,96,768]{2,1,0:T(8,128)(2,1)}, u32[]{:S(2)}, u32[]{:S(2)}) collective-permute-start(bf16[1,96,768]{2,1,0:T(8,128)(2,1)} %dynamic-slice_bitcast_fusion.2), channel_id=1, source_target_pairs={{0,4},{1,5},{2,6},{3,7},{4,0},{5,1},{6,2},{7,3},{8,12},{9,13},{10,... | collective-permute-start | bytes 442376 | tf_op jit(solution)/shard_map/ppermute | solution.py:212
  54.5 19.3 %collective-permute-done.61 = bf16[1,96,768]{2,1,0:T(8,128)(2,1)S(1)} collective-permute-done((bf16[1,96,768]{2,1,0:T(8,128)(2,1)}, bf16[1,96,768]{2,1,0:T(8,128)(2,1)S(1)}, u32[]{:S(2)}, u32[]{:S(2)}) %collective-permute-start.61) | collective-permute-done | bytes 147488 | tf_op jit(solution)/shard_map/ppermute | solution.py:212
  73.8 13.1 %collective-permute-start.16 = (bf16[2,96,768]{2,1,0:T(8,128)(2,1)S(1)}, bf16[2,96,768]{2,1,0:T(8,128)(2,1)}, u32[]{:S(2)}, u32[]{:S(2)}) collective-permute-start(bf16[2,96,768]{2,1,0:T(8,128)(2,1)S(1)} %dynamic-slice_bitcast_fusion.1), channel_id=1, source_target_pairs={{0,4},{1,5},{2,6},{3,7},{4,0},{5,1},{6,2},{7,3},{8,12},{9,13},{10,... | collective-permute-start | bytes 884744 | tf_op jit(solution)/shard_map/ppermute | solution.py:212
  93.2 14.3 %collective-permute-done.16 = bf16[2,96,768]{2,1,0:T(8,128)(2,1)} collective-permute-done((bf16[2,96,768]{2,1,0:T(8,128)(2,1)S(1)}, bf16[2,96,768]{2,1,0:T(8,128)(2,1)}, u32[]{:S(2)}, u32[]{:S(2)}) %collective-permute-start.16) | collective-permute-done | bytes 294944 | tf_op jit(solution)/shard_map/ppermute | solution.py:212
  115.7 5.5 collective-permute-done.3.refs_2_
  196.6 9.1 %collective-permute-done.19.refs_3_ = bf16[3,2,96,768]{3,2,1,0:T(8,128)(2,1)} collective-permute-done((bf16[3,2,96,768]{3,2,1,0:T(8,128)(2,1)}, bf16[3,2,96,768]{3,2,1,0:T(8,128)(2,1)}, u32[]{:S(2)}, u32[]{:S(2)}) %collective-permute-start.19) | collective-permute-done | bytes 884768 | tf_op jit(solution)/shard_map/ppermute | solution.py:212
  209.5 5.8 collective-permute-done.20.refs_4_
  228.0 6.1 assemble_down.2
  234.3 5.1 assemble_down.3
  253.4 7.8 multiply_convert_fusion.1
  288.0 7.6 multiply_convert_fusion
  305.5 5.0 concatenate.33
  310.5 5.5 concatenate.34
  316.0 4.0 pad_maximum_fusion.g
  321.0 8.1 %multiply_reduce_fusion.3 = (f32[768]{0:T(1024)}, f32[256]{0:T(256)S(1)}, f32[768]{0:T(1024)}, f32[256,768]{1,0:T(8,128)S(1)}) fusion(f32[256,768]{1,0:T(8,128)S(1)} %copy-done.144, f32[256]{0:T(256)S(1)} %copy-done.231, f32[256]{0:T(256)S(1)} %copy-done.220, f32[768]{0:T(1024)S(1)} %copy-done.213, bf16[768,6144]{1,0:T(8,128)(2,1)} %copy-done.1, ...), kind=kOutput, calls=%fused_computation.108 | convolution fusion | flops 2424174848 | bytes 14955520 | tf_op jit(solution)/shard_map/dot_general | solution.py:50
  349.3 5.2 concatenate.36
  354.4 5.0 concatenate.37
  359.4 3.9 pad_maximum_fusion.1.g
  364.3 8.3 %multiply_reduce_fusion.5 = (f32[768]{0:T(1024)}, f32[256]{0:T(256)S(1)}, f32[768]{0:T(1024)}, f32[256,768]{1,0:T(8,128)S(1)}) fusion(f32[256,768]{1,0:T(8,128)S(1)} %copy-done.139, f32[256]{0:T(256)S(1)} %copy-done.226, f32[256]{0:T(256)S(1)} %copy-done.215, f32[768]{0:T(1024)S(1)} %copy-done.208, bf16[768,6144]{1,0:T(8,128)(2,1)} %copy-done, ...), kind=kOutput, calls=%fused_computation.110 | convolution fusion | flops 2424174848 | bytes 14955520 | tf_op jit(solution)/shard_map/dot_general | solution.py:50
  443.8 9.7 %grad_gate_up.2 = (bf16[2,4,2,2,96,384]{5,4,3,2,1,0:T(8,128)(2,1)}, bf16[2,4,2,2,96,384]{5,4,3,2,1,0:T(8,128)(2,1)S(1)}) custom-call(s32[4]{0:T(128)S(1)} %copy-done.118, bf16[256,768]{1,0:T(8,128)(2,1)S(1)} %fusion.34.a, bf16[256,768]{1,0:T(8,128)(2,1)S(1)} %collective-permute-done.77.a2, bf16[256,6144]{1,0:T(8,128)(2,1)S(1)} %copy-done.8, ...), custom_call_target="tpu_custom_call" | custom-call | flops 2415919104 | bytes 11010048 | tf_op jit(solution)/shard_map/grad_gate_up/pallas_call | solution.py:451
  457.0 9.6 %grad_gate_up.3 = (bf16[2,4,2,2,96,384]{5,4,3,2,1,0:T(8,128)(2,1)}, bf16[2,4,2,2,96,384]{5,4,3,2,1,0:T(8,128)(2,1)S(1)}) custom-call(s32[4]{0:T(128)S(1)} %copy-done.118, bf16[256,768]{1,0:T(8,128)(2,1)S(1)} %copy-done.36, bf16[256,768]{1,0:T(8,128)(2,1)} %collective-permute-done.100.a2, bf16[256,6144]{1,0:T(8,128)(2,1)S(1)} %copy-done.9, ...), custom_call_target="tpu_custom_call" | custom-call | flops 2415919104 | bytes 11010048 | tf_op jit(solution)/shard_map/grad_gate_up/pallas_call | solution.py:451
  477.1 5.8 grad_attend.2
  490.6 5.3 grad_attend.3
  496.8 5.2 grad_down.2
  503.4 5.2 grad_down.3
  508.6 13.2 %collective-permute-done.88.got_ref = bf16[2,4,1,2,96,384]{5,4,3,2,1,0:T(8,128)(2,1)} collective-permute-done((bf16[2,4,1,2,96,384]{5,4,3,2,1,0:T(8,128)(2,1)}, bf16[2,4,1,2,96,384]{5,4,3,2,1,0:T(8,128)(2,1)}, u32[]{:S(2)}, u32[]{:S(2)}) %collective-permute-start.88) | collective-permute-done | bytes 1179680 | tf_op jit(solution)/shard_map/ppermute | solution.py:212
  530.1 10.6 %collective-permute-done.111.got_ref = bf16[2,4,1,2,96,384]{5,4,3,2,1,0:T(8,128)(2,1)S(1)} collective-permute-done((bf16[2,4,1,2,96,384]{5,4,3,2,1,0:T(8,128)(2,1)S(1)}, bf16[2,4,1,2,96,384]{5,4,3,2,1,0:T(8,128)(2,1)S(1)}, u32[]{:S(2)}, u32[]{:S(2)}) %collective-permute-start.111) | collective-permute-done | bytes 1179680 | tf_op jit(solution)/shard_map/ppermute | solution.py:212
  546.3 19.7 %collective-permute-done.72.got_ref = bf16[2,4,1,2,96,384]{5,4,3,2,1,0:T(8,128)(2,1)S(1)} collective-permute-done((bf16[2,4,1,2,96,384]{5,4,3,2,1,0:T(8,128)(2,1)S(1)}, bf16[2,4,1,2,96,384]{5,4,3,2,1,0:T(8,128)(2,1)S(1)}, u32[]{:S(2)}, u32[]{:S(2)}) %collective-permute-start.72) | collective-permute-done | bytes 1179680 | tf_op jit(solution)/shard_map/ppermute | solution.py:212
  568.8 22.4 %collective-permute-done.95.got_ref = bf16[2,4,1,2,96,384]{5,4,3,2,1,0:T(8,128)(2,1)S(1)} collective-permute-done((bf16[2,4,1,2,96,384]{5,4,3,2,1,0:T(8,128)(2,1)S(1)}, bf16[2,4,1,2,96,384]{5,4,3,2,1,0:T(8,128)(2,1)S(1)}, u32[]{:S(2)}, u32[]{:S(2)}) %collective-permute-start.95) | collective-permute-done | bytes 1179680 | tf_op jit(solution)/shard_map/ppermute | solution.py:212
  600.9 7.6 collective-permute-done.91.refs_2_
  611.3 5.9 collective-permute-done.92.refs_3_
  620.0 6.3 collective-permute-done.113.refs_1_
  635.0 4.3 collective-permute-done.74.refs_1_
  639.3 5.9 collective-permute-done.75.refs_2_
  645.5 5.3 collective-permute-done.76.refs_3_
  650.9 4.8 collective-permute-start.82
  655.7 3.9 collective-permute-start.83
  659.5 14.7 %collective-permute-done.98.refs_2_ = bf16[1,2,96,384]{3,2,1,0:T(8,128)(2,1)S(1)} collective-permute-done((bf16[1,2,96,384]{3,2,1,0:T(8,128)(2,1)S(1)}, bf16[1,2,96,384]{3,2,1,0:T(8,128)(2,1)S(1)}, u32[]{:S(2)}, u32[]{:S(2)}) %collective-permute-start.98) | collective-permute-done | bytes 147488 | tf_op jit(solution)/shard_map/ppermute | solution.py:212
  683.2 6.8 collective-permute-done.82.refs_2_
  690.9 10.8 %collective-permute-done.105.refs_2_ = bf16[2,2,96,384]{3,2,1,0:T(8,128)(2,1)S(1)} collective-permute-done((bf16[2,2,96,384]{3,2,1,0:T(8,128)(2,1)S(1)}, bf16[2,2,96,384]{3,2,1,0:T(8,128)(2,1)S(1)}, u32[]{:S(2)}, u32[]{:S(2)}) %collective-permute-start.105) | collective-permute-done | bytes 294944 | tf_op jit(solution)/shard_map/ppermute | solution.py:212
  714.1 3.7 collective-permute-start.119
  732.2 4.7 fusion.20
  761.0 4.9 adam_qkv.1
  772.0 6.7 adam_down.1
  782.5 12.9 %adam_gate_up.1 = (f32[2,96,6144]{2,1,0:T(8,128)}, f32[2,96,6144]{2,1,0:T(8,128)}, f32[2,96,6144]{2,1,0:T(8,128)}) custom-call(s32[4]{0:T(128)S(1)} %copy-done.118, f32[1]{0:T(128)} %bitcast.85.factor_ref, f32[2,96,6144]{2,1,0:T(8,128)S(1)} %bitcast.260, f32[2,96,6144]{2,1,0:T(8,128)S(1)} %bitcast.270, f32[2,96,6144]{2,1,0:T(8,128)S(1)} %copy-done.7, ...), custom_call_target="tpu_custom_call" | custom-call | flops 23592960 | bytes 28311552 | tf_op jit(solution)/shard_map/adam_gate_up/pallas_call | solution.py:692
  (1028 shorter events, 414.1 us)
Async XLA Ops:
  48.1 40.0 %collective-permute-start.48 = (bf16[2,96,768]{2,1,0:T(8,128)(2,1)}, bf16[2,96,768]{2,1,0:T(8,128)(2,1)S(1)}, u32[]{:S(2)}, u32[]{:S(2)}) collective-permute-start(bf16[2,96,768]{2,1,0:T(8,128)(2,1)} %dynamic-slice_bitcast_fusion), channel_id=1, source_target_pairs={{0,2},{1,3},{2,0},{3,1},{4,6},{5,7},{6,4},{7,5},{8,10},{9,11},{10,... | collective-permute-start | bytes 884744 | tf_op jit(solution)/shard_map/ppermute | solution.py:212
  48.2 41.5 %collective-permute-start.49 = (bf16[2,96,768]{2,1,0:T(8,128)(2,1)}, bf16[2,96,768]{2,1,0:T(8,128)(2,1)S(1)}, u32[]{:S(2)}, u32[]{:S(2)}) collective-permute-start(bf16[2,96,768]{2,1,0:T(8,128)(2,1)} %dynamic-slice_bitcast_fusion), channel_id=1, source_target_pairs={{0,4},{1,5},{2,6},{3,7},{4,0},{5,1},{6,2},{7,3},{8,12},{9,13},{10,... | collective-permute-start | bytes 884744 | tf_op jit(solution)/shard_map/ppermute | solution.py:212
  50.4 40.8 %collective-permute-start.50 = (bf16[2,96,768]{2,1,0:T(8,128)(2,1)}, bf16[2,96,768]{2,1,0:T(8,128)(2,1)S(1)}, u32[]{:S(2)}, u32[]{:S(2)}) collective-permute-start(bf16[2,96,768]{2,1,0:T(8,128)(2,1)} %dynamic-slice_bitcast_fusion), channel_id=1, source_target_pairs={{0,6},{1,7},{2,4},{3,5},{4,2},{5,3},{6,0},{7,1},{8,14},{9,15},{10,... | collective-permute-start | bytes 884744 | tf_op jit(solution)/shard_map/ppermute | solution.py:212
  54.5 36.7 %collective-permute-start.15 = (bf16[2,96,768]{2,1,0:T(8,128)(2,1)S(1)}, bf16[2,96,768]{2,1,0:T(8,128)(2,1)S(1)}, u32[]{:S(2)}, u32[]{:S(2)}) collective-permute-start(bf16[2,96,768]{2,1,0:T(8,128)(2,1)S(1)} %dynamic-slice_bitcast_fusion.1), channel_id=1, source_target_pairs={{0,2},{1,3},{2,0},{3,1},{4,6},{5,7},{6,4},{7,5},{8,10},{9,11},{10,... | collective-permute-start | bytes 884744 | tf_op jit(solution)/shard_map/ppermute | solution.py:212
  73.8 33.7 %collective-permute-start.16 = (bf16[2,96,768]{2,1,0:T(8,128)(2,1)S(1)}, bf16[2,96,768]{2,1,0:T(8,128)(2,1)}, u32[]{:S(2)}, u32[]{:S(2)}) collective-permute-start(bf16[2,96,768]{2,1,0:T(8,128)(2,1)S(1)} %dynamic-slice_bitcast_fusion.1), channel_id=1, source_target_pairs={{0,4},{1,5},{2,6},{3,7},{4,0},{5,1},{6,2},{7,3},{8,12},{9,13},{10,... | collective-permute-start | bytes 884744 | tf_op jit(solution)/shard_map/ppermute | solution.py:212
  159.8 29.6 %collective-permute-start.18 = (bf16[3,2,96,768]{3,2,1,0:T(8,128)(2,1)}, bf16[3,2,96,768]{3,2,1,0:T(8,128)(2,1)}, u32[]{:S(2)}, u32[]{:S(2)}) collective-permute-start(bf16[3,2,96,768]{3,2,1,0:T(8,128)(2,1)} %pad_maximum_fusion.6.refs_1_), channel_id=1, source_target_pairs={{0,16},{1,9},{2,18},{3,11},{4,20},{5,13},{6,22},{7,15},{8,24},{9,1... | collective-permute-start | bytes 2654216 | tf_op jit(solution)/shard_map/ppermute | solution.py:212
  177.3 28.5 %collective-permute-start.19 = (bf16[3,2,96,768]{3,2,1,0:T(8,128)(2,1)}, bf16[3,2,96,768]{3,2,1,0:T(8,128)(2,1)}, u32[]{:S(2)}, u32[]{:S(2)}) collective-permute-start(bf16[3,2,96,768]{3,2,1,0:T(8,128)(2,1)} %pad_maximum_fusion.6.refs_1_), channel_id=1, source_target_pairs={{0,8},{1,17},{2,10},{3,19},{4,12},{5,21},{6,14},{7,23},{8,0},{9,25... | collective-permute-start | bytes 2654216 | tf_op jit(solution)/shard_map/ppermute | solution.py:212
  206.2 38.9 %collective-permute-start.21 = (bf16[4,2,96,768]{3,2,1,0:T(8,128)(2,1)S(1)}, bf16[4,2,96,768]{3,2,1,0:T(8,128)(2,1)}, u32[]{:S(2)}, u32[]{:S(2)}) collective-permute-start(bf16[4,2,96,768]{3,2,1,0:T(8,128)(2,1)S(1)} %bitcast.263), channel_id=1, source_target_pairs={{0,1},{1,0},{2,3},{3,2},{4,5},{5,4},{6,7},{7,6},{8,9},{9,8},{10,11... | collective-permute-start | bytes 3538952 | tf_op jit(solution)/shard_map/ppermute | solution.py:212
  207.2 38.5 %collective-permute-start.23 = (bf16[3,2,96,768]{3,2,1,0:T(8,128)(2,1)}, bf16[3,2,96,768]{3,2,1,0:T(8,128)(2,1)}, u32[]{:S(2)}, u32[]{:S(2)}) collective-permute-start(bf16[3,2,96,768]{3,2,1,0:T(8,128)(2,1)} %collective-permute-done.18.refs_2_), channel_id=1, source_target_pairs={{0,1},{1,0},{2,3},{3,2},{4,5},{5,4},{6,7},{7,6},{8,9},{9,8},{10,11... | collective-permute-start | bytes 2654216 | tf_op jit(solution)/shard_map/ppermute | solution.py:212
  207.6 37.7 %collective-permute-start.53 = (bf16[3,2,96,768]{3,2,1,0:T(8,128)(2,1)}, bf16[3,2,96,768]{3,2,1,0:T(8,128)(2,1)}, u32[]{:S(2)}, u32[]{:S(2)}) collective-permute-start(bf16[3,2,96,768]{3,2,1,0:T(8,128)(2,1)} %collective-permute-done.51.refs_2_), channel_id=1, source_target_pairs={{0,8},{1,17},{2,10},{3,19},{4,12},{5,21},{6,14},{7,23},{8,0},{9,25... | collective-permute-start | bytes 2654216 | tf_op jit(solution)/shard_map/ppermute | solution.py:212
  209.2 36.6 %collective-permute-start.24 = (bf16[3,2,96,768]{3,2,1,0:T(8,128)(2,1)}, bf16[3,2,96,768]{3,2,1,0:T(8,128)(2,1)}, u32[]{:S(2)}, u32[]{:S(2)}) collective-permute-start(bf16[3,2,96,768]{3,2,1,0:T(8,128)(2,1)} %collective-permute-done.19.refs_3_), channel_id=1, source_target_pairs={{0,1},{1,0},{2,3},{3,2},{4,5},{5,4},{6,7},{7,6},{8,9},{9,8},{10,11... | collective-permute-start | bytes 2654216 | tf_op jit(solution)/shard_map/ppermute | solution.py:212
  215.2 30.9 %collective-permute-start.25 = (bf16[3,2,96,768]{3,2,1,0:T(8,128)(2,1)}, bf16[3,2,96,768]{3,2,1,0:T(8,128)(2,1)}, u32[]{:S(2)}, u32[]{:S(2)}) collective-permute-start(bf16[3,2,96,768]{3,2,1,0:T(8,128)(2,1)} %collective-permute-done.20.refs_4_), channel_id=1, source_target_pairs={{0,1},{1,0},{2,3},{3,2},{4,5},{5,4},{6,7},{7,6},{8,9},{9,8},{10,11... | collective-permute-start | bytes 2654216 | tf_op jit(solution)/shard_map/ppermute | solution.py:212
  245.1 35.3 %collective-permute-start.54 = (bf16[4,2,96,768]{3,2,1,0:T(8,128)(2,1)S(1)}, bf16[4,2,96,768]{3,2,1,0:T(8,128)(2,1)}, u32[]{:S(2)}, u32[]{:S(2)}) collective-permute-start(bf16[4,2,96,768]{3,2,1,0:T(8,128)(2,1)S(1)} %bitcast.261), channel_id=1, source_target_pairs={{0,1},{1,0},{2,3},{3,2},{4,5},{5,4},{6,7},{7,6},{8,9},{9,8},{10,11... | collective-permute-start | bytes 3538952 | tf_op jit(solution)/shard_map/ppermute | solution.py:212
  245.3 34.7 %collective-permute-start.55 = (bf16[3,2,96,768]{3,2,1,0:T(8,128)(2,1)S(1)}, bf16[3,2,96,768]{3,2,1,0:T(8,128)(2,1)}, u32[]{:S(2)}, u32[]{:S(2)}) collective-permute-start(bf16[3,2,96,768]{3,2,1,0:T(8,128)(2,1)S(1)} %pad_maximum_fusion.7.refs_1_), channel_id=1, source_target_pairs={{0,1},{1,0},{2,3},{3,2},{4,5},{5,4},{6,7},{7,6},{8,9},{9,8},{10,11... | collective-permute-start | bytes 2654216 | tf_op jit(solution)/shard_map/ppermute | solution.py:212
  245.6 34.9 %collective-permute-start.56 = (bf16[3,2,96,768]{3,2,1,0:T(8,128)(2,1)}, bf16[3,2,96,768]{3,2,1,0:T(8,128)(2,1)}, u32[]{:S(2)}, u32[]{:S(2)}) collective-permute-start(bf16[3,2,96,768]{3,2,1,0:T(8,128)(2,1)} %collective-permute-done.51.refs_2_), channel_id=1, source_target_pairs={{0,1},{1,0},{2,3},{3,2},{4,5},{5,4},{6,7},{7,6},{8,9},{9,8},{10,11... | collective-permute-start | bytes 2654216 | tf_op jit(solution)/shard_map/ppermute | solution.py:212
  245.8 35.1 %collective-permute-start.57 = (bf16[3,2,96,768]{3,2,1,0:T(8,128)(2,1)}, bf16[3,2,96,768]{3,2,1,0:T(8,128)(2,1)}, u32[]{:S(2)}, u32[]{:S(2)}) collective-permute-start(bf16[3,2,96,768]{3,2,1,0:T(8,128)(2,1)} %collective-permute-done.52.refs_3_), channel_id=1, source_target_pairs={{0,1},{1,0},{2,3},{3,2},{4,5},{5,4},{6,7},{7,6},{8,9},{9,8},{10,11... | collective-permute-start | bytes 2654216 | tf_op jit(solution)/shard_map/ppermute | solution.py:212
  246.2 34.8 %collective-permute-start.58 = (bf16[3,2,96,768]{3,2,1,0:T(8,128)(2,1)}, bf16[3,2,96,768]{3,2,1,0:T(8,128)(2,1)}, u32[]{:S(2)}, u32[]{:S(2)}) collective-permute-start(bf16[3,2,96,768]{3,2,1,0:T(8,128)(2,1)} %collective-permute-done.53.refs_4_), channel_id=1, source_target_pairs={{0,1},{1,0},{2,3},{3,2},{4,5},{5,4},{6,7},{7,6},{8,9},{9,8},{10,11... | collective-permute-start | bytes 2654216 | tf_op jit(solution)/shard_map/ppermute | solution.py:212
  280.0 136.4 %collective-permute-start.107 = (bf16[256,768]{1,0:T(8,128)(2,1)}, bf16[256,768]{1,0:T(8,128)(2,1)}, u32[]{:S(2)}, u32[]{:S(2)}) collective-permute-start(bf16[256,768]{1,0:T(8,128)(2,1)} %fusion.31.a), channel_id=1, source_target_pairs={{0,1},{1,0},{2,3},{3,2},{4,5},{5,4},{6,7},{7,6},{8,9},{9,8},{10,11... | collective-permute-start | bytes 1179656 | tf_op jit(solution)/shard_map/ppermute | solution.py:212
  280.4 136.8 %collective-permute-start.100 = (bf16[256,768]{1,0:T(8,128)(2,1)S(1)}, bf16[256,768]{1,0:T(8,128)(2,1)}, u32[]{:S(2)}, u32[]{:S(2)}) collective-permute-start(bf16[256,768]{1,0:T(8,128)(2,1)S(1)} %copy-done.35), channel_id=1, source_target_pairs={{0,1},{1,0},{2,3},{3,2},{4,5},{5,4},{6,7},{7,6},{8,9},{9,8},{10,11... | collective-permute-start | bytes 1179656 | tf_op jit(solution)/shard_map/ppermute | solution.py:212
  280.6 137.0 %collective-permute-start.109 = (bf16[256,768]{1,0:T(8,128)(2,1)}, bf16[256,768]{1,0:T(8,128)(2,1)}, u32[]{:S(2)}, u32[]{:S(2)}) collective-permute-start(bf16[256,768]{1,0:T(8,128)(2,1)} %copy.130.o), channel_id=1, source_target_pairs={{0,1},{1,0},{2,3},{3,2},{4,5},{5,4},{6,7},{7,6},{8,9},{9,8},{10,11... | collective-permute-start | bytes 1179656 | tf_op jit(solution)/shard_map/ppermute | solution.py:212
  389.9 52.0 %collective-permute-start.78 = (bf16[256,3072]{1,0:T(8,128)(2,1)}, bf16[256,3072]{1,0:T(8,128)(2,1)}, u32[]{:S(2)}, u32[]{:S(2)}) collective-permute-start(bf16[256,3072]{1,0:T(8,128)(2,1)} %bitcast.133), channel_id=1, source_target_pairs={{0,1},{1,0},{2,3},{3,2},{4,5},{5,4},{6,7},{7,6},{8,9},{9,8},{10,11... | collective-permute-start | bytes 4718600 | tf_op jit(solution)/shard_map/ppermute | solution.py:212
  408.7 46.0 %collective-permute-start.101 = (bf16[256,3072]{1,0:T(8,128)(2,1)}, bf16[256,3072]{1,0:T(8,128)(2,1)}, u32[]{:S(2)}, u32[]{:S(2)}) collective-permute-start(bf16[256,3072]{1,0:T(8,128)(2,1)} %bitcast.140), channel_id=1, source_target_pairs={{0,1},{1,0},{2,3},{3,2},{4,5},{5,4},{6,7},{7,6},{8,9},{9,8},{10,11... | collective-permute-start | bytes 4718600 | tf_op jit(solution)/shard_map/ppermute | solution.py:212
  437.1 29.4 %collective-permute-start.85 = (bf16[256,1152]{1,0:T(8,128)(2,1)}, bf16[256,1152]{1,0:T(8,128)(2,1)}, u32[]{:S(2)}, u32[]{:S(2)}) collective-permute-start(bf16[256,1152]{1,0:T(8,128)(2,1)} %copy.109), channel_id=1, source_target_pairs={{0,1},{1,0},{2,3},{3,2},{4,5},{5,4},{6,7},{7,6},{8,9},{9,8},{10,11... | collective-permute-start | bytes 1769480 | tf_op jit(solution)/shard_map/ppermute | solution.py:212
  441.4 54.5 %collective-permute-start.70 = (bf16[256,3072]{1,0:T(8,128)(2,1)}, bf16[256,3072]{1,0:T(8,128)(2,1)}, u32[]{:S(2)}, u32[]{:S(2)}) collective-permute-start(bf16[256,3072]{1,0:T(8,128)(2,1)} %get-tuple-element.215.a), channel_id=1, source_target_pairs={{0,1},{1,0},{2,3},{3,2},{4,5},{5,4},{6,7},{7,6},{8,9},{9,8},{10,11... | collective-permute-start | bytes 4718600 | tf_op jit(solution)/shard_map/ppermute | solution.py:212
  441.9 60.2 %collective-permute-start.93 = (bf16[256,3072]{1,0:T(8,128)(2,1)}, bf16[256,3072]{1,0:T(8,128)(2,1)}, u32[]{:S(2)}, u32[]{:S(2)}) collective-permute-start(bf16[256,3072]{1,0:T(8,128)(2,1)} %get-tuple-element.217.a), channel_id=1, source_target_pairs={{0,1},{1,0},{2,3},{3,2},{4,5},{5,4},{6,7},{7,6},{8,9},{9,8},{10,11... | collective-permute-start | bytes 4718600 | tf_op jit(solution)/shard_map/ppermute | solution.py:212
  454.3 28.6 %collective-permute-start.108 = (bf16[256,1152]{1,0:T(8,128)(2,1)}, bf16[256,1152]{1,0:T(8,128)(2,1)}, u32[]{:S(2)}, u32[]{:S(2)}) collective-permute-start(bf16[256,1152]{1,0:T(8,128)(2,1)} %copy.124), channel_id=1, source_target_pairs={{0,1},{1,0},{2,3},{3,2},{4,5},{5,4},{6,7},{7,6},{8,9},{9,8},{10,11... | collective-permute-start | bytes 1769480 | tf_op jit(solution)/shard_map/ppermute | solution.py:212
  454.7 70.6 %collective-permute-start.79 = (bf16[2,4,2,2,96,384]{5,4,3,2,1,0:T(8,128)(2,1)}, bf16[2,4,2,2,96,384]{5,4,3,2,1,0:T(8,128)(2,1)}, u32[]{:S(2)}, u32[]{:S(2)}) collective-permute-start(bf16[2,4,2,2,96,384]{5,4,3,2,1,0:T(8,128)(2,1)} %get-tuple-element.114), channel_id=1, source_target_pairs={{0,8},{1,17},{2,10},{3,19},{4,12},{5,21},{6,14},{7,23},{8,0},{9,25... | collective-permute-start | bytes 7077896 | tf_op jit(solution)/shard_map/ppermute | solution.py:212
  466.5 76.5 %collective-permute-start.102 = (bf16[2,4,2,2,96,384]{5,4,3,2,1,0:T(8,128)(2,1)}, bf16[2,4,2,2,96,384]{5,4,3,2,1,0:T(8,128)(2,1)}, u32[]{:S(2)}, u32[]{:S(2)}) collective-permute-start(bf16[2,4,2,2,96,384]{5,4,3,2,1,0:T(8,128)(2,1)} %get-tuple-element.141), channel_id=1, source_target_pairs={{0,8},{1,17},{2,10},{3,19},{4,12},{5,21},{6,14},{7,23},{8,0},{9,25... | collective-permute-start | bytes 7077896 | tf_op jit(solution)/shard_map/ppermute | solution.py:212
  482.9 38.9 %collective-permute-start.88 = (bf16[2,4,1,2,96,384]{5,4,3,2,1,0:T(8,128)(2,1)}, bf16[2,4,1,2,96,384]{5,4,3,2,1,0:T(8,128)(2,1)}, u32[]{:S(2)}, u32[]{:S(2)}) collective-permute-start(bf16[2,4,1,2,96,384]{5,4,3,2,1,0:T(8,128)(2,1)} %get-tuple-element.123), channel_id=1, source_target_pairs={{0,8},{1,17},{2,10},{3,19},{4,12},{5,21},{6,14},{7,23},{8,0},{9,25... | collective-permute-start | bytes 3538952 | tf_op jit(solution)/shard_map/ppermute | solution.py:212
  496.0 44.7 %collective-permute-start.111 = (bf16[2,4,1,2,96,384]{5,4,3,2,1,0:T(8,128)(2,1)S(1)}, bf16[2,4,1,2,96,384]{5,4,3,2,1,0:T(8,128)(2,1)S(1)}, u32[]{:S(2)}, u32[]{:S(2)}) collective-permute-start(bf16[2,4,1,2,96,384]{5,4,3,2,1,0:T(8,128)(2,1)S(1)} %get-tuple-element.150), channel_id=1, source_target_pairs={{0,8},{1,17},{2,10},{3,19},{4,12},{5,21},{6,14},{7,23},{8,0},{9,25... | collective-permute-start | bytes 3538952 | tf_op jit(solution)/shard_map/ppermute | solution.py:212
  502.1 63.9 %collective-permute-start.72 = (bf16[2,4,1,2,96,384]{5,4,3,2,1,0:T(8,128)(2,1)S(1)}, bf16[2,4,1,2,96,384]{5,4,3,2,1,0:T(8,128)(2,1)S(1)}, u32[]{:S(2)}, u32[]{:S(2)}) collective-permute-start(bf16[2,4,1,2,96,384]{5,4,3,2,1,0:T(8,128)(2,1)S(1)} %get-tuple-element.105), channel_id=1, source_target_pairs={{0,8},{1,17},{2,10},{3,19},{4,12},{5,21},{6,14},{7,23},{8,0},{9,25... | collective-permute-start | bytes 3538952 | tf_op jit(solution)/shard_map/ppermute | solution.py:212
  521.8 69.4 %collective-permute-start.95 = (bf16[2,4,1,2,96,384]{5,4,3,2,1,0:T(8,128)(2,1)S(1)}, bf16[2,4,1,2,96,384]{5,4,3,2,1,0:T(8,128)(2,1)S(1)}, u32[]{:S(2)}, u32[]{:S(2)}) collective-permute-start(bf16[2,4,1,2,96,384]{5,4,3,2,1,0:T(8,128)(2,1)S(1)} %get-tuple-element.132), channel_id=1, source_target_pairs={{0,8},{1,17},{2,10},{3,19},{4,12},{5,21},{6,14},{7,23},{8,0},{9,25... | collective-permute-start | bytes 3538952 | tf_op jit(solution)/shard_map/ppermute | solution.py:212
  525.4 42.9 %collective-permute-start.89 = (bf16[4,1,2,96,384]{4,3,2,1,0:T(8,128)(2,1)S(1)}, bf16[4,1,2,96,384]{4,3,2,1,0:T(8,128)(2,1)S(1)}, u32[]{:S(2)}, u32[]{:S(2)}) collective-permute-start(bf16[4,1,2,96,384]{4,3,2,1,0:T(8,128)(2,1)S(1)} %get-tuple-element.125), channel_id=1, source_target_pairs={{0,16},{1,9},{2,18},{3,11},{4,20},{5,13},{6,22},{7,15},{8,24},{9,1... | collective-permute-start | bytes 1769480 | tf_op jit(solution)/shard_map/ppermute | solution.py:212
  540.7 89.3 %collective-permute-start.80 = (bf16[4,2,2,96,384]{4,3,2,1,0:T(8,128)(2,1)S(1)}, bf16[4,2,2,96,384]{4,3,2,1,0:T(8,128)(2,1)S(1)}, u32[]{:S(2)}, u32[]{:S(2)}) collective-permute-start(bf16[4,2,2,96,384]{4,3,2,1,0:T(8,128)(2,1)S(1)} %get-tuple-element.116), channel_id=1, source_target_pairs={{0,16},{1,9},{2,18},{3,11},{4,20},{5,13},{6,22},{7,15},{8,24},{9,1... | collective-permute-start | bytes 3538952 | tf_op jit(solution)/shard_map/ppermute | solution.py:212
  543.0 52.3 %collective-permute-start.112 = (bf16[4,1,2,96,384]{4,3,2,1,0:T(8,128)(2,1)S(1)}, bf16[4,1,2,96,384]{4,3,2,1,0:T(8,128)(2,1)S(1)}, u32[]{:S(2)}, u32[]{:S(2)}) collective-permute-start(bf16[4,1,2,96,384]{4,3,2,1,0:T(8,128)(2,1)S(1)} %get-tuple-element.152), channel_id=1, source_target_pairs={{0,16},{1,9},{2,18},{3,11},{4,20},{5,13},{6,22},{7,15},{8,24},{9,1... | collective-permute-start | bytes 1769480 | tf_op jit(solution)/shard_map/ppermute | solution.py:212
  565.9 79.3 %collective-permute-start.103 = (bf16[4,2,2,96,384]{4,3,2,1,0:T(8,128)(2,1)S(1)}, bf16[4,2,2,96,384]{4,3,2,1,0:T(8,128)(2,1)S(1)}, u32[]{:S(2)}, u32[]{:S(2)}) collective-permute-start(bf16[4,2,2,96,384]{4,3,2,1,0:T(8,128)(2,1)S(1)} %get-tuple-element.143), channel_id=1, source_target_pairs={{0,16},{1,9},{2,18},{3,11},{4,20},{5,13},{6,22},{7,15},{8,24},{9,1... | collective-permute-start | bytes 3538952 | tf_op jit(solution)/shard_map/ppermute | solution.py:212
  568.2 51.5 %collective-permute-start.73 = (bf16[4,1,2,96,384]{4,3,2,1,0:T(8,128)(2,1)S(1)}, bf16[4,1,2,96,384]{4,3,2,1,0:T(8,128)(2,1)S(1)}, u32[]{:S(2)}, u32[]{:S(2)}) collective-permute-start(bf16[4,1,2,96,384]{4,3,2,1,0:T(8,128)(2,1)S(1)} %get-tuple-element.107), channel_id=1, source_target_pairs={{0,16},{1,9},{2,18},{3,11},{4,20},{5,13},{6,22},{7,15},{8,24},{9,1... | collective-permute-start | bytes 1769480 | tf_op jit(solution)/shard_map/ppermute | solution.py:212
  595.3 35.8 %collective-permute-start.96 = (bf16[4,1,2,96,384]{4,3,2,1,0:T(8,128)(2,1)S(1)}, bf16[4,1,2,96,384]{4,3,2,1,0:T(8,128)(2,1)S(1)}, u32[]{:S(2)}, u32[]{:S(2)}) collective-permute-start(bf16[4,1,2,96,384]{4,3,2,1,0:T(8,128)(2,1)S(1)} %get-tuple-element.134), channel_id=1, source_target_pairs={{0,16},{1,9},{2,18},{3,11},{4,20},{5,13},{6,22},{7,15},{8,24},{9,1... | collective-permute-start | bytes 1769480 | tf_op jit(solution)/shard_map/ppermute | solution.py:212
  631.1 46.4 %collective-permute-start.81 = (bf16[2,2,96,384]{3,2,1,0:T(8,128)(2,1)S(1)}, bf16[2,2,96,384]{3,2,1,0:T(8,128)(2,1)S(1)}, u32[]{:S(2)}, u32[]{:S(2)}) collective-permute-start(bf16[2,2,96,384]{3,2,1,0:T(8,128)(2,1)S(1)} %get-tuple-element.118), channel_id=1, source_target_pairs={{0,2},{1,3},{2,0},{3,1},{4,6},{5,7},{6,4},{7,5},{8,10},{9,11},{10,... | collective-permute-start | bytes 884744 | tf_op jit(solution)/shard_map/ppermute | solution.py:212
  645.2 29.0 %collective-permute-start.98 = (bf16[1,2,96,384]{3,2,1,0:T(8,128)(2,1)S(1)}, bf16[1,2,96,384]{3,2,1,0:T(8,128)(2,1)S(1)}, u32[]{:S(2)}, u32[]{:S(2)}) collective-permute-start(bf16[1,2,96,384]{3,2,1,0:T(8,128)(2,1)S(1)} %get-tuple-element.137), channel_id=1, source_target_pairs={{0,4},{1,5},{2,6},{3,7},{4,0},{5,1},{6,2},{7,3},{8,12},{9,13},{10,... | collective-permute-start | bytes 442376 | tf_op jit(solution)/shard_map/ppermute | solution.py:212
  645.2 29.0 %collective-permute-start.99 = (bf16[1,2,96,384]{3,2,1,0:T(8,128)(2,1)S(1)}, bf16[1,2,96,384]{3,2,1,0:T(8,128)(2,1)S(1)}, u32[]{:S(2)}, u32[]{:S(2)}) collective-permute-start(bf16[1,2,96,384]{3,2,1,0:T(8,128)(2,1)S(1)} %get-tuple-element.138), channel_id=1, source_target_pairs={{0,6},{1,7},{2,4},{3,5},{4,2},{5,3},{6,0},{7,1},{8,14},{9,15},{10,... | collective-permute-start | bytes 442376 | tf_op jit(solution)/shard_map/ppermute | solution.py:212
  650.9 39.2 %collective-permute-start.82 = (bf16[2,2,96,384]{3,2,1,0:T(8,128)(2,1)S(1)}, bf16[2,2,96,384]{3,2,1,0:T(8,128)(2,1)S(1)}, u32[]{:S(2)}, u32[]{:S(2)}) collective-permute-start(bf16[2,2,96,384]{3,2,1,0:T(8,128)(2,1)S(1)} %get-tuple-element.119), channel_id=1, source_target_pairs={{0,4},{1,5},{2,6},{3,7},{4,0},{5,1},{6,2},{7,3},{8,12},{9,13},{10,... | collective-permute-start | bytes 884744 | tf_op jit(solution)/shard_map/ppermute | solution.py:212
  655.7 34.4 %collective-permute-start.83 = (bf16[2,2,96,384]{3,2,1,0:T(8,128)(2,1)S(1)}, bf16[2,2,96,384]{3,2,1,0:T(8,128)(2,1)S(1)}, u32[]{:S(2)}, u32[]{:S(2)}) collective-permute-start(bf16[2,2,96,384]{3,2,1,0:T(8,128)(2,1)S(1)} %get-tuple-element.120), channel_id=1, source_target_pairs={{0,6},{1,7},{2,4},{3,5},{4,2},{5,3},{6,0},{7,1},{8,14},{9,15},{10,... | collective-permute-start | bytes 884744 | tf_op jit(solution)/shard_map/ppermute | solution.py:212
  737.0 29.0 %collective-permute-start.140 = (bf16[2,1,96,384]{3,2,1,0:T(8,128)(2,1)}, bf16[2,1,96,384]{3,2,1,0:T(8,128)(2,1)}, u32[]{:S(2)}, u32[]{:S(2)}) collective-permute-start(bf16[2,1,96,384]{3,2,1,0:T(8,128)(2,1)} %collective-permute-done.138.refs_1_), channel_id=1, source_target_pairs={{0,8},{1,17},{2,10},{3,19},{4,12},{5,21},{6,14},{7,23},{8,0},{9,25... | collective-permute-start | bytes 442376 | tf_op jit(solution)/shard_map/ppermute | solution.py:212
  738.6 41.5 %collective-permute-start.135 = (bf16[2,2,96,384]{3,2,1,0:T(8,128)(2,1)S(1)}, bf16[2,2,96,384]{3,2,1,0:T(8,128)(2,1)}, u32[]{:S(2)}, u32[]{:S(2)}) collective-permute-start(bf16[2,2,96,384]{3,2,1,0:T(8,128)(2,1)S(1)} %pad_maximum_fusion.15.refs_4_), channel_id=1, source_target_pairs={{0,8},{1,17},{2,10},{3,19},{4,12},{5,21},{6,14},{7,23},{8,0},{9,25... | collective-permute-start | bytes 884744 | tf_op jit(solution)/shard_map/ppermute | solution.py:212
  740.4 39.7 %collective-permute-start.131 = (bf16[2,2,96,384]{3,2,1,0:T(8,128)(2,1)}, bf16[2,2,96,384]{3,2,1,0:T(8,128)(2,1)}, u32[]{:S(2)}, u32[]{:S(2)}) collective-permute-start(bf16[2,2,96,384]{3,2,1,0:T(8,128)(2,1)} %pad_maximum_fusion.14.refs_0_), channel_id=1, source_target_pairs={{0,8},{1,17},{2,10},{3,19},{4,12},{5,21},{6,14},{7,23},{8,0},{9,25... | collective-permute-start | bytes 884744 | tf_op jit(solution)/shard_map/ppermute | solution.py:212
  741.3 38.8 %collective-permute-start.136 = (bf16[2,2,96,384]{3,2,1,0:T(8,128)(2,1)}, bf16[2,2,96,384]{3,2,1,0:T(8,128)(2,1)}, u32[]{:S(2)}, u32[]{:S(2)}) collective-permute-start(bf16[2,2,96,384]{3,2,1,0:T(8,128)(2,1)} %collective-permute-done.134.refs_5_), channel_id=1, source_target_pairs={{0,8},{1,17},{2,10},{3,19},{4,12},{5,21},{6,14},{7,23},{8,0},{9,25... | collective-permute-start | bytes 884744 | tf_op jit(solution)/shard_map/ppermute | solution.py:212
  743.3 36.8 %collective-permute-start.132 = (bf16[2,2,96,384]{3,2,1,0:T(8,128)(2,1)}, bf16[2,2,96,384]{3,2,1,0:T(8,128)(2,1)}, u32[]{:S(2)}, u32[]{:S(2)}) collective-permute-start(bf16[2,2,96,384]{3,2,1,0:T(8,128)(2,1)} %collective-permute-done.130.refs_1_), channel_id=1, source_target_pairs={{0,8},{1,17},{2,10},{3,19},{4,12},{5,21},{6,14},{7,23},{8,0},{9,25... | collective-permute-start | bytes 884744 | tf_op jit(solution)/shard_map/ppermute | solution.py:212
  (362 other events, 4422.9 us)

commit v3 on v1

v3 whole, which is shorter than its diff:
```python
import jax
import jax.numpy as jnp
from jax import lax
from jax.experimental import pallas as pl
from jax.experimental.pallas import tpu as pltpu
from jax.sharding import PartitionSpec as P

D = 768
HEADS = 12
HEAD_DIM = 64
FF = 3072
SEQ_LEN = 128
STEP = 10
HALF = D // 2
PAIR = 2 * HEAD_DIM


beta_first = 0.9
beta_second = 0.999
adam_eps = 1e-08
clip_norm = 1.0
rate_matrix = 0.03
rate_norm = 0.5
decay_matrix = 0.01
norm_eps = 1e-05
low_type = jnp.bfloat16
wide_type = jnp.float32
both_axes = ("rep", "fsdp")


def pairs_of(move):
    found = []
    for rep in range(4):
        for shard in range(8):
            to_y, to_x, to_z, to_c = move(rep // 2, rep % 2, shard // 2, shard % 2)
            found.append((rep * 8 + shard, (to_y * 2 + to_x) * 8 + to_z * 2 + to_c))
    return found


FLIP_CORE = pairs_of(lambda y, x, z, c: (y, x, z, 1 - c))
FLIP_X = pairs_of(lambda y, x, z, c: (y, 1 - x, z, c))
FLIP_Y = pairs_of(lambda y, x, z, c: (1 - y, x, z, c))
FLIP_FIRST = pairs_of(lambda y, x, z, c: (y, 1 - x, z, c) if c == 0 else (1 - y, x, z, c))
FLIP_SECOND = pairs_of(lambda y, x, z, c: (1 - y, x, z, c) if c == 0 else (y, 1 - x, z, c))
Z_ONE = pairs_of(lambda y, x, z, c: (y, x, z ^ 1, c))
Z_TWO = pairs_of(lambda y, x, z, c: (y, x, z ^ 2, c))
Z_THREE = pairs_of(lambda y, x, z, c: (y, x, z ^ 3, c))


def send(values, pairs):
    return lax.ppermute(values, both_axes, pairs)


def place():
    rep = lax.axis_index("rep")
    shard = lax.axis_index("fsdp")
    y, x, z, c = rep // 2, rep % 2, shard // 2, shard % 2
    first = jnp.where(c == 0, x, y)
    second = jnp.where(c == 0, y, x)
    return (z, c, first, second)


def by_neighbours():
    return lax.axis_size("rep") == 4 and lax.axis_size("fsdp") == 8


def run(
    kernel, name, where, args, in_specs, outs, out_specs, grid=(1,), scratch=(), after=(), reuse=None
):
    first_out = 1 + len(args) + len(after)

    def body_of(*refs):
        kernel(*refs[: 1 + len(args)], *refs[first_out:])

    return pl.pallas_call(
        body_of,
        out_shape=[jax.ShapeDtypeStruct(shape, dtype) for shape, dtype in outs],
        grid_spec=pltpu.PrefetchScalarGridSpec(
            num_scalar_prefetch=1,
            grid=grid,
            in_specs=list(in_specs) + [pl.BlockSpec(memory_space=pl.ANY)] * len(after),
            out_specs=list(out_specs),
            scratch_shapes=list(scratch),
        ),
        input_output_aliases={1 + at: out for at, out in (reuse or {}).items()},
        compiler_params=pltpu.CompilerParams(vmem_limit_bytes=40 * 2**20),
        cost_estimate=pl.CostEstimate(flops=1000, bytes_accessed=1000, transcendentals=0),
        name=name,
    )(where, *args, *after)


class Chain:
    def __init__(self, where):
        self.where = where
        self.last = ()

    def __call__(self, call, *args):
        results = call(*args, self.where, self.last)
        self.last = (min(results, key=lambda array: array.size),)
        return results

    def wait(self, *arrays):
        self.last += arrays


def full(shape):
    zeros = (0,) * len(shape)
    return pl.BlockSpec(shape, lambda *_: zeros)


def fulls(arrays):
    return [full(array.shape) for array in arrays]


def dot(left, right):
    return jnp.dot(left, right, preferred_element_type=wide_type)


def dot_right(left, right):
    return lax.dot_general(
        left, right, (((1,), (1,)), ((), ())), preferred_element_type=wide_type
    )


def dot_left(left, right):
    return lax.dot_general(
        left, right, (((0,), (0,)), ((), ())), preferred_element_type=wide_type
    )


def spread_of(values):
    center = values - jnp.mean(values, axis=-1, keepdims=True)
    variance = jnp.mean(center * center, axis=-1, keepdims=True)
    scale = lax.rsqrt(variance + norm_eps)
    return (center * scale, scale)


def norm_back(grad, values, gain):
    unit, scale = spread_of(values)
    inner = grad * gain
    mean_inner = jnp.mean(inner, axis=-1, keepdims=True)
    mean_product = jnp.mean(inner * unit, axis=-1, keepdims=True)
    grad_values = scale * (inner - mean_inner - unit * mean_product)
    return (
        grad_values,
        jnp.sum(grad * unit, axis=0, keepdims=True),
        jnp.sum(grad, axis=0, keepdims=True),
    )


def put_theirs(out_ref, at, block, core):
    @pl.when(core == 0)
    def _():
        out_ref[at] = block[:, HALF:]

    @pl.when(core != 0)
    def _():
        out_ref[at] = block[:, :HALF]


def head_tools():
    lane = lax.broadcasted_iota(jnp.int32, (1, PAIR), 1)
    masks = ((lane < HEAD_DIM).astype(low_type), (lane >= HEAD_DIM).astype(low_type))
    rows = lax.broadcasted_iota(jnp.int32, (SEQ_LEN, SEQ_LEN), 0)
    columns = lax.broadcasted_iota(jnp.int32, (SEQ_LEN, SEQ_LEN), 1)
    distance = jnp.abs(rows - columns).astype(wide_type)
    return (masks, distance, columns)


def head_slope(head):
    return 2.0 ** (-8.0 * (head + 1.0) / HEADS)


def attend_forward(hidden, weight_qkv, weight_out, norms, layer, where, after=()):
    tokens = hidden.shape[0]

    def kernel(where, h, wq, wo, n, trio, qkv, log_total, residual, normed):
        low = h[...].astype(low_type)
        trio[0] = low
        for part in range(3):
            columns = slice(part * D, (part + 1) * D)
            qkv[:, columns] = dot(low, wq[:, columns]).astype(low_type)
        masks, distance, lanes = head_tools()
        for sequence in range(tokens // SEQ_LEN):
            rows = slice(sequence * SEQ_LEN, (sequence + 1) * SEQ_LEN)
            logs = jnp.zeros((SEQ_LEN, SEQ_LEN), wide_type)
            for pair in range(HEADS // 2):
                query, key, value = (
                    qkv[rows, part * D + pair * PAIR : part * D + (pair + 1) * PAIR]
                    for part in range(3)
                )
                mixture = jnp.zeros((SEQ_LEN, PAIR), wide_type)
                for side in range(2):
                    head = 2 * pair + side
                    scores = dot_right(query * masks[side], key) * HEAD_DIM ** (-0.5)
                    scores = scores - head_slope(head) * distance
                    summit = jnp.max(scores, axis=-1, keepdims=True)
                    powers = jnp.exp(scores - summit)
                    total = jnp.sum(powers, axis=-1, keepdims=True)
                    logs = jnp.where(lanes == head, summit + jnp.log(total), logs)
                    attention = (powers * (1.0 / total)).astype(low_type)
                    mixture = mixture + dot(attention, value * masks[side])
                trio[1, rows, pair * PAIR : (pair + 1) * PAIR] = mixture.astype(low_type)
            log_total[rows, :] = logs
        total = h[...] + dot(trio[1], wo[...])
        residual[...] = total
        unit, _ = spread_of(total)
        result = unit * n[4 * layer : 4 * layer + 1] + n[4 * layer + 1 : 4 * layer + 2]
        normed[...] = result
        trio[2] = result.astype(low_type)

    args = (hidden, weight_qkv, weight_out, norms)
    outs = [
        ((3, tokens, D), low_type),
        ((tokens, 3 * D), low_type),
        ((tokens, SEQ_LEN), wide_type),
        ((tokens, D), wide_type),
        ((tokens, D), wide_type),
    ]
    specs = [full(shape) for shape, _ in outs]
    return run(kernel, "attend_forward", where, args, fulls(args), outs, specs, after=after)


def gate_forward(trio, weight_gu, where, after=()):
    tokens = trio.shape[1]

    def kernel(where, a, wg, wu, product, slopes):
        gate = dot(a[0], wg[...])
        up = dot(a[0], wu[...])
        bell = 0.5 * (1.0 + lax.erf(gate * 0.5**0.5))
        curve = gate * bell
        product[...] = (curve * up).astype(low_type)
        density = jnp.exp(-0.5 * gate * gate) * 0.3989422804014327
        slopes[0] = (up * (bell + gate * density)).astype(low_type)
        slopes[1] = curve.astype(low_type)

    return run(
        kernel,
        "gate_forward",
        where,
        (trio, weight_gu, weight_gu),
        [
            pl.BlockSpec((1, tokens, D), lambda step, where: (2, 0, 0)),
            pl.BlockSpec((D, D), lambda step, where: (0, step)),
            pl.BlockSpec((D, D), lambda step, where: (0, step + FF // D)),
        ],
        [((tokens, FF), low_type), ((2, tokens, FF), low_type)],
        [
            pl.BlockSpec((tokens, D), lambda step, where: (0, step)),
            pl.BlockSpec((2, tokens, D), lambda step, where: (0, 0, step)),
        ],
        grid=(FF // D,),
        after=after,
    )


def down_forward(product, weight_down, normed, norms, layer, where, after=()):
    tokens = normed.shape[0]

    def kernel(where, x, w, h, n, residual, result):
        step = pl.program_id(0)

        @pl.when(step == 0)
        def _():
            residual[...] = h[...]

        residual[...] += dot(x[...], w[...])

        @pl.when(step == FF // D - 1)
        def _():
            unit, _ = spread_of(residual[...])
            result[...] = unit * n[4 * layer + 2 : 4 * layer + 3] + n[4 * layer + 3 : 4 * layer + 4]

    return run(
        kernel,
        "down_forward",
        where,
        (product, weight_down, normed, norms),
        [
            pl.BlockSpec((tokens, D), lambda step, where: (0, step)),
            pl.BlockSpec((D, D), lambda step, where: (step, 0)),
            full(normed.shape),
            full(norms.shape),
        ],
        [((tokens, D), wide_type)] * 2,
        [full((tokens, D))] * 2,
        grid=(FF // D,),
        after=after,
    )


def feed_backward(grad, residual_two, residual_one, slopes, weights, norms, layer, where, after=()):
    _, weight_out, weight_gu, weight_down = weights
    tokens = grad.shape[0]
    last = FF // D - 1

    def kernel(where, g, r2, r1, s, wd, wg, wu, wo, n, *refs):
        gates, theirs, branch, grad_one, attend, mixed, grad_norms, total = refs
        step = pl.program_id(0)
        core = where[1]

        def norm_row(at):
            return n[4 * layer + at : 4 * layer + at + 1]

        @pl.when(step == 0)
        def _():
            grad_two, gain, shift = norm_back(g[...], r2[...], norm_row(2))
            total[...] = grad_two
            low = grad_two.astype(low_type)
            branch[...] = low
            put_theirs(theirs, (slice(None), slice(8 * HALF, 9 * HALF)), low, core)
            grad_norms[2:3] = gain
            grad_norms[3:4] = shift

        grad_product = dot_right(branch[...], wd[...]).astype(low_type).astype(wide_type)
        for side, weight in ((0, wg), (1, wu)):
            low = (grad_product * s[side].astype(wide_type)).astype(low_type)
            gates[side] = low
            column = pl.multiple_of((4 * side + step) * HALF, HALF)
            put_theirs(theirs, (slice(None), pl.ds(column, HALF)), low, core)
            total[...] += dot_right(low, weight[...])

        @pl.when(step == last)
        def _():
            one, gain, shift = norm_back(total[...], r1[...], norm_row(0))
            grad_one[...] = one
            low = one.astype(low_type)
            attend[...] = low
            put_theirs(theirs, (slice(None), slice(9 * HALF, 10 * HALF)), low, core)
            mixed[...] = dot_right(low, wo[...]).astype(low_type)
            grad_norms[0:1] = gain
            grad_norms[1:2] = shift

    def columns(step, where):
        return (0, 0, step)

    outs = [
        ((2, tokens, FF), low_type),
        ((tokens, 10 * HALF), low_type),
        ((tokens, D), low_type),
        ((tokens, D), wide_type),
        ((tokens, D), low_type),
        ((tokens, D), low_type),
        ((4, D), wide_type),
    ]
    return run(
        kernel,
        "feed_backward",
        where,
        (
            grad,
            residual_two,
            residual_one,
            slopes,
            weight_down,
            weight_gu,
            weight_gu,
            weight_out,
            norms,
        ),
        [
            full(grad.shape),
            full(grad.shape),
            full(grad.shape),
            pl.BlockSpec((2, tokens, D), columns),
            pl.BlockSpec((D, D), lambda step, where: (step, 0)),
            pl.BlockSpec((D, D), lambda step, where: (0, step)),
            pl.BlockSpec((D, D), lambda step, where: (0, step + FF // D)),
            full(weight_out.shape),
            full(norms.shape),
        ],
        outs,
        [
            pl.BlockSpec((2, tokens, D), columns),
        ]
        + [full(shape) for shape, _ in outs[1:]],
        grid=(FF // D,),
        scratch=[pltpu.VMEM((tokens, D), wide_type)],
        after=after,
    )


def attend_backward(grad_mixed, qkv, log_total, grad_one, weight_qkv, where, after=()):
    tokens = grad_mixed.shape[0]

    def kernel(where, g, x, logs, one, wq, grads, theirs, result):
        masks, distance, lanes = head_tools()
        for sequence in range(tokens // SEQ_LEN):
            rows = slice(sequence * SEQ_LEN, (sequence + 1) * SEQ_LEN)
            all_logs = logs[rows, :]
            for pair in range(HEADS // 2):
                columns = [
                    slice(part * D + pair * PAIR, part * D + (pair + 1) * PAIR)
                    for part in range(3)
                ]
                query, key, value = (x[rows, column] for column in columns)
                grad = g[rows, columns[0]]
                sums = [jnp.zeros((SEQ_LEN, PAIR), wide_type) for _ in range(3)]
                for side in range(2):
                    head = 2 * pair + side
                    mask = masks[side]
                    scores = dot_right(query * mask, key) * HEAD_DIM ** (-0.5)
                    scores = scores - head_slope(head) * distance
                    attention = jnp.exp(scores - all_logs[:, head : head + 1])
                    grad_side = grad * mask
                    grad_attention = dot_right(grad_side, value)
                    sums[2] += dot_left(attention.astype(low_type), grad_side)
                    weighted = attention * grad_attention
                    inner = jnp.sum(weighted, axis=-1, keepdims=True)
                    grad_scores = (weighted - attention * inner).astype(low_type)
                    sums[0] += dot(grad_scores, key * mask)
                    sums[1] += dot_left(grad_scores, query * mask)
                for column, total, scale in zip(
                    columns, sums, (HEAD_DIM ** (-0.5), HEAD_DIM ** (-0.5), 1.0)
                ):
                    grads[rows, column] = (total * scale).astype(low_type)
        total = one[...]
        for part in range(3):
            block = grads[:, part * D : (part + 1) * D]
            total = total + dot_right(block, wq[:, part * D : (part + 1) * D])
            at = (slice(None), slice(part * HALF, (part + 1) * HALF))
            put_theirs(theirs, at, block, where[1])
        result[...] = total

    args = (grad_mixed, qkv, log_total, grad_one, weight_qkv)
    outs = [
        ((tokens, 3 * D), low_type),
        ((tokens, 3 * HALF), low_type),
        ((tokens, D), wide_type),
    ]
    specs = [full(shape) for shape, _ in outs]
    return run(kernel, "attend_backward", where, args, fulls(args), outs, specs, after=after)


KINDS = ("attend", "gate_up", "down")
BLOCKS = {"attend": 1, "gate_up": 2, "down": 1}


NORM_ROWS = 16


def own_chunks(chunks, weights, norm_params, where, after=()):
    rows = weights[0].shape[1]
    more = 0 if norm_params is None else NORM_ROWS
    counts = [BLOCKS[kind] for kind, _ in chunks]
    names = {"attend": (0, 1), "gate_up": (2,), "down": (3,)}
    used = [(at, layer) for kind, layer in chunks for at in names[kind]]

    def kernel(where, *refs):
        matrix = dict(zip(used, refs))
        owns, quarters = refs[len(args) : -1], refs[-1]
        start = 0
        if more:
            quarters[:, rows:] = jnp.zeros((sum(counts), more, D), low_type)
            count, width = norm_params.shape
            quarters[0, rows : rows + count, :width] = refs[len(used)][...].astype(low_type)
        for (kind, layer), own, count in zip(chunks, owns, counts):
            if kind == "attend":
                for part in range(3):
                    values = matrix[0, layer][0, :, part * D : (part + 1) * D]
                    own[part, 0] = values.astype(low_type)
                own[3, 0] = matrix[1, layer][0].astype(low_type)
            elif kind == "gate_up":
                for block in range(8):
                    values = matrix[2, layer][0, :, block * D : (block + 1) * D]
                    own[block % 4, block // 4] = values.astype(low_type)
            else:
                for block in range(4):
                    values = matrix[3, layer][0, block * rows : (block + 1) * rows, :]
                    own[block, 0] = values.astype(low_type)
            quarters[start : start + count, :rows] = own[2 * where[2] + where[3]]
            start += count

    def at_layer(layer):
        return lambda step, where: (layer, 0, 0)

    args = [weights[at] for at, _ in used]
    specs = [
        pl.BlockSpec((1,) + weights[at].shape[1:], at_layer(layer)) for at, layer in used
    ]
    if more:
        args.append(norm_params)
        specs.append(full(norm_params.shape))
    outs = [((4, count, rows, D), low_type) for count in counts]
    outs.append(((sum(counts), rows + more, D), low_type))
    out_specs = [full(shape) for shape, _ in outs]
    return run(kernel, "own_chunks", where, args, specs, outs, out_specs, after=after)


def stack_chips(arrived, rows, where, after=()):
    count = arrived[0].shape[0]
    more = arrived[0].shape[1] - rows

    def kernel(where, *refs):
        out, rest = refs[3:]
        for spot in range(3):
            out[spot] = refs[spot][:, :rows]
            if more:
                rest[spot] = refs[spot][0, rows:, :SEQ_LEN]

    shape = (3, count, rows, D)
    rest = (3, max(more, NORM_ROWS), SEQ_LEN)
    outs = [(shape, low_type), (rest, low_type)]
    specs = [full(shape), full(rest)]
    return run(kernel, "stack_chips", where, arrived, fulls(arrived), outs, specs, after=after)


def stack_two(one, two, where, after=()):
    def kernel(where, one, two, out, token, sem):
        copies = [
            pltpu.make_async_copy(one, out.at[0], sem.at[0]),
            pltpu.make_async_copy(two, out.at[1], sem.at[1]),
        ]
        for copy in copies:
            copy.start()
        for copy in copies:
            copy.wait()

    shape = (2,) + one.shape
    return run(
        kernel,
        "stack_two",
        where,
        (one, two),
        [pl.BlockSpec(memory_space=pl.ANY)] * 2,
        [(shape, low_type), ((8, 128), low_type)],
        [full(shape), full((8, 128))],
        scratch=[pltpu.SemaphoreType.DMA((2,))],
        after=after,
    )


def pack(owns, six, far, where, after=()):
    counts = [own.shape[1] for own in owns]
    total, rows = sum(counts), owns[0].shape[2]
    number = len(owns) + 4

    def kernel(where, *refs):
        in_refs, (six_ref, far_ref, out, token, sem) = refs[: len(owns)], refs[len(owns) :]
        moves = []
        begin = 0
        for ref, count in zip(in_refs, counts):
            moves.append((ref, out.at[pl.ds(0, 4), pl.ds(begin, count)]))
            begin += count
        for index in range(4):
            ref = (six_ref, far_ref)[index // 2]
            moves.append((ref.at[index % 2], out.at[pl.ds(4 + 3 * index, 3)]))
        copies = [
            pltpu.make_async_copy(*move, sem.at[index]) for index, move in enumerate(moves)
        ]
        for copy in copies:
            copy.start()
        for copy in copies:
            copy.wait()

    shape = (16, total, rows, D)
    return run(
        kernel,
        "pack",
        where,
        (*owns, six, far),
        [pl.BlockSpec(memory_space=pl.ANY)] * (len(owns) + 2),
        [(shape, low_type), ((8, 128), low_type)],
        [full(shape), full((8, 128))],
        scratch=[pltpu.SemaphoreType.DMA((number,))],
        after=after,
    )


def assemble(pieces, kind, begin, where, after=()):
    count = pieces[0].shape[1]
    rows = pieces[0].shape[2]
    shapes = {
        "attend": ((8 * rows, 3 * D), (8 * rows, D)),
        "gate_up": ((8 * rows, 2 * FF),),
        "down": ((8 * 4 * rows, D),),
    }[kind]

    def kernel(where, *refs):
        own_ref, six_ref, far_ref, packed = refs[:4]
        out_refs, sem = refs[4:-1], refs[-1]
        mine = (own_ref, six_ref.at[0], six_ref.at[1], far_ref.at[0], far_ref.at[1])
        others = (packed, *(packed.at[pl.ds(at, 3)] for at in (4, 7, 10, 13)))
        z, c, first, second = (where[at] for at in range(4))

        def copy(source, quarter, block, shard):
            row = pl.multiple_of(shard * rows, rows)
            if kind == "attend":

                @pl.when(quarter < 3)
                def _():
                    column = pl.multiple_of(quarter * D, D)
                    target = out_refs[0].at[pl.ds(row, rows), pl.ds(column, D)]
                    pltpu.make_async_copy(source, target, sem).start()

                @pl.when(quarter == 3)
                def _():
                    target = out_refs[1].at[pl.ds(row, rows), :]
                    pltpu.make_async_copy(source, target, sem).start()

            elif kind == "gate_up":
                column = pl.multiple_of((quarter + 4 * block) * D, D)
                target = out_refs[0].at[pl.ds(row, rows), pl.ds(column, D)]
                pltpu.make_async_copy(source, target, sem).start()
            else:
                row = pl.multiple_of((shard * 4 + quarter) * rows, rows)
                target = out_refs[0].at[pl.ds(row, rows), :]
                pltpu.make_async_copy(source, target, sem).start()

        for side in range(2):
            own, near, across, far, corner = mine if side == 0 else others
            own_begin = 0 if side == 0 else begin
            core = c if side == 0 else 1 - c
            high, low = (first, second) if side == 0 else (second, first)
            for block in range(count):
                for quarter in range(4):
                    copy(
                        own.at[quarter, own_begin + block], jnp.int32(quarter), block, 2 * z + core
                    )
                for step in range(3):
                    shard = 2 * (z ^ (step + 1)) + core
                    copy(near.at[step, begin + block], 2 * high + low, block, shard)
                    copy(across.at[step, begin + block], 2 * high + 1 - low, block, shard)
                    copy(far.at[step, begin + block], 2 * (1 - high) + low, block, shard)
                    copy(corner.at[step, begin + block], 2 * (1 - high) + 1 - low, block, shard)
        for out_ref in out_refs:
            pltpu.make_async_copy(out_ref, out_ref, sem).wait()

    return run(
        kernel,
        "assemble_" + kind,
        where,
        pieces,
        [pl.BlockSpec(memory_space=pl.ANY)] * 4,
        [(shape, low_type) for shape in shapes],
        [pl.BlockSpec(memory_space=pltpu.VMEM) for _ in shapes],
        scratch=[pltpu.SemaphoreType.DMA],
        after=after,
    )


def norm_columns(near, other, norm_params, where, after=()):
    count, width = norm_params.shape

    def kernel(where, own_ref, near_ref, other_ref, out_ref):
        for shard in range(8):
            side = (shard % 2) ^ where[1]
            chip = (shard // 2) ^ where[0]
            here = near_ref[jnp.maximum(chip, 1) - 1, :count, :width].astype(wide_type)
            here = jnp.where(chip == 0, own_ref[...].astype(low_type).astype(wide_type), here)
            there = other_ref[chip, :count, :width].astype(wide_type)
            out_ref[:, shard * width : (shard + 1) * width] = jnp.where(side == 0, here, there)

    args = (norm_params, near, other)
    outs = [((count, 8 * width), wide_type)]
    specs = [full(outs[0][0])]
    return run(kernel, "norm_columns", where, args, fulls(args), outs, specs, after=after)


def turn(step, where):
    first, second = where[2], where[3]
    return 2 * (first ^ (1 - step // 2)) + (second ^ (1 - step % 2))


def fill_left(left, values, values_other):
    tokens = values.shape[0]
    left[:, :tokens] = values.T
    left[:, tokens:] = values_other.T


def chip_dot(left, right, right_other):
    tokens = right.shape[0]
    return dot(left[:, :tokens], right) + dot(left[:, tokens:], right_other)


def store_rows(out_ref, product, z, rows):
    for chip in range(4):
        piece = product[chip * 2 * rows : (chip + 1) * 2 * rows]
        out_ref[0, chip ^ z, 0] = piece.reshape(2, rows, HALF).astype(low_type)


def trio_part(tokens, part):
    return pl.BlockSpec((1, tokens, D), lambda step, where: (part, 0, 0))


def grad_attend(trio, trio_other, qkv, qkv_other, out, feed_other, filled, where, after=()):
    tokens = out.shape[0]
    rows = D // 8

    def kernel(where, a, a2, o, o2, g, g2, b, b2, _, __, sent, kept, left_a, left_o):
        step = pl.program_id(0)
        quarter = turn(step, where)

        @pl.when(step == 0)
        def _():
            fill_left(left_a, a[0], a2[0])
            fill_left(left_o, o[0], o2[0])

        def put(product):
            @pl.when(step < 2)
            def _():
                store_rows(sent, product, where[0], rows)

            @pl.when(step >= 2)
            def _():
                store_rows(kept, product, where[0], rows)

        @pl.when(quarter < 3)
        def _():
            put(chip_dot(left_a, g[...], g2[...]))

        @pl.when(quarter == 3)
        def _():
            put(chip_dot(left_o, b[...], b2[...]))

    def own_column(step, where):
        return (0, 2 * jnp.minimum(turn(step, where), 2) + where[1])

    def other_column(step, where):
        return (0, jnp.minimum(turn(step, where), 2))

    shape = (2, 4, 2, 2, rows, HALF)
    block = (1, 4, 1, 2, rows, HALF)
    return run(
        kernel,
        "grad_attend",
        where,
        (trio, trio_other, trio, trio_other, qkv, qkv_other, out, feed_other, *filled),
        [
            trio_part(tokens, 0),
            trio_part(tokens, 0),
            trio_part(tokens, 1),
            trio_part(tokens, 1),
            pl.BlockSpec((tokens, HALF), own_column),
            pl.BlockSpec((tokens, HALF), other_column),
            pl.BlockSpec((tokens, HALF), lambda step, where: (0, where[1])),
            pl.BlockSpec((tokens, HALF), lambda step, where: (0, 9)),
        ]
        + [pl.BlockSpec(memory_space=pl.ANY)] * 2,
        [(shape, low_type)] * 2,
        [
            pl.BlockSpec(block, lambda step, where: (jnp.minimum(step, 1), 0, 1, 0, 0, 0)),
            pl.BlockSpec(block, lambda step, where: (jnp.maximum(step, 2) - 2, 0, 1, 0, 0, 0)),
        ],
        grid=(4,),
        scratch=[pltpu.VMEM((D, 2 * tokens), low_type)] * 2,
        after=after,
        reuse={8: 0, 9: 1},
    )


def grad_gate_up(trio, trio_other, grads, feed_other, where, after=()):
    tokens = trio.shape[1]
    rows = D // 8

    def kernel(where, a, a2, g, g2, sent, kept, left):
        step = pl.program_id(0)

        @pl.when(step == 0)
        def _():
            fill_left(left, a[0], a2[0])

        product = chip_dot(left, g[0], g2[...])

        @pl.when(step < 4)
        def _():
            store_rows(sent, product, where[0], rows)

        @pl.when(step >= 4)
        def _():
            store_rows(kept, product, where[0], rows)

    def own_column(step, where):
        return (step % 2, 0, 2 * turn(step // 2, where) + where[1])

    def other_column(step, where):
        return (0, 4 * (step % 2) + turn(step // 2, where))

    def sent_at(step, where):
        held = jnp.minimum(step, 3)
        return (held // 2, 0, held % 2, 0, 0, 0)

    def kept_at(step, where):
        held = jnp.maximum(step, 4) - 4
        return (held // 2, 0, held % 2, 0, 0, 0)

    shape = (2, 4, 2, 2, rows, HALF)
    block = (1, 4, 1, 2, rows, HALF)
    return run(
        kernel,
        "grad_gate_up",
        where,
        (trio, trio_other, grads, feed_other),
        [
            trio_part(tokens, 2),
            trio_part(tokens, 2),
            pl.BlockSpec((1, tokens, HALF), own_column),
            pl.BlockSpec((tokens, HALF), other_column),
        ],
        [(shape, low_type)] * 2,
        [pl.BlockSpec(block, sent_at), pl.BlockSpec(block, kept_at)],
        grid=(8,),
        scratch=[pltpu.VMEM((D, 2 * tokens), low_type)],
        after=after,
    )


def grad_down(inputs, inputs_other, grads, feed_other, where, after=()):
    tokens = inputs.shape[0]
    rows = FF // 32

    def kernel(where, a, a2, g, g2, sent, kept, left):
        fill_left(left, a[...], a2[...])
        product = chip_dot(left, g[...], g2[...])
        product = product.astype(low_type).reshape(2, 4, rows, HALF)
        for quarter in range(4):
            away = (quarter // 2) ^ where[2]
            spot = 1 - ((quarter % 2) ^ where[3])

            @pl.when(away == 1)
            def _():
                sent[spot, 0, 0] = product[:, quarter]

            @pl.when(away == 0)
            def _():
                kept[spot, 0, 0] = product[:, quarter]

    def chip_columns(step, where):
        return (0, step ^ where[0])

    shape = (2, 4, 2, 2, rows, HALF)
    spec = pl.BlockSpec((2, 1, 1, 2, rows, HALF), lambda step, where: (0, step, 0, 0, 0, 0))
    return run(
        kernel,
        "grad_down",
        where,
        (inputs, inputs_other, grads, feed_other),
        [
            pl.BlockSpec((tokens, FF // 4), chip_columns),
            pl.BlockSpec((tokens, FF // 4), chip_columns),
            pl.BlockSpec((tokens, HALF), lambda step, where: (0, where[1])),
            pl.BlockSpec((tokens, HALF), lambda step, where: (0, 8)),
        ],
        [(shape, low_type)] * 2,
        [spec, spec],
        grid=(4,),
        scratch=[pltpu.VMEM((FF // 4, 2 * tokens), low_type)],
        after=after,
    )


def add_halves(kept, got, where, after=()):
    def kernel(where, kept_ref, got_ref, sent_ref, left_ref):
        for spot, out_ref in ((0, sent_ref), (1, left_ref)):
            total = kept_ref[spot].astype(wide_type) + got_ref[spot].astype(wide_type)
            out_ref[...] = total.astype(low_type)

    rest = kept.shape[2:]
    spec_in = pl.BlockSpec((2, 1) + rest, lambda step, where: (0, step, 0, 0, 0, 0))
    spec_out = pl.BlockSpec((1,) + rest, lambda step, where: (step, 0, 0, 0, 0))
    outs = [(kept.shape[1:], low_type)] * 2
    return run(
        kernel,
        "add_halves",
        where,
        (kept, got),
        [spec_in] * 2,
        outs,
        [spec_out] * 2,
        grid=(4,),
        after=after,
    )


def add_chips(sums, where, after=()):
    args = [array for both in sums for array in both]
    counts = [left.shape[1] for left, _ in sums]
    rest = sums[0][0].shape[2:]

    def kernel(where, *refs):
        in_refs, out_refs = refs[: len(args)], refs[len(args) :]
        start = 0
        for index, count in enumerate(counts):
            left_ref, got_ref = in_refs[2 * index : 2 * index + 2]
            for chip, out_ref in enumerate(out_refs):
                total = left_ref[chip].astype(wide_type) + got_ref[chip].astype(wide_type)
                out_ref[start : start + count] = total.astype(low_type)
            start += count

    outs = [((sum(counts),) + rest, low_type)] * 4
    specs = [full(shape) for shape, _ in outs]
    return run(kernel, "add_chips", where, args, fulls(args), outs, specs, after=after)


def add_last(parts, where, after=()):
    count, _, rows, width = parts[0].shape

    def kernel(where, *refs):
        part_refs, (total, squares) = refs[:4], refs[4:]
        added = jnp.zeros((8, width), wide_type)
        for block in range(count):
            for core in range(2):
                value = part_refs[0][block, core].astype(wide_type)
                for part_ref in part_refs[1:]:
                    value = value + part_ref[block, core].astype(wide_type)
                low = value.astype(low_type)
                total[block, core] = low
                value = low.astype(wide_type)
                added = added + jnp.sum((value * value).reshape(rows // 8, 8, width), axis=0)
        squares[...] = added

    outs = [(parts[0].shape, low_type), ((8, width), wide_type)]
    specs = [full(shape) for shape, _ in outs]
    return run(kernel, "add_last", where, parts, fulls(parts), outs, specs, after=after)


def pack_replicas(row, far, where, after=()):
    def kernel(where, row, far, out, token, sem):
        copies = [
            pltpu.make_async_copy(row, out.at[pl.ds(0, 2)], sem.at[0]),
            pltpu.make_async_copy(far, out.at[pl.ds(2, 2)], sem.at[1]),
        ]
        for copy in copies:
            copy.start()
        for copy in copies:
            copy.wait()

    shape = (4,) + row.shape[1:]
    return run(
        kernel,
        "pack_replicas",
        where,
        (row, far),
        [pl.BlockSpec(memory_space=pl.ANY)] * 2,
        [(shape, low_type), ((8, 128), low_type)],
        [full(shape), full((8, 128))],
        scratch=[pltpu.SemaphoreType.DMA((2,))],
        after=after,
    )


def adam_step(weight, first_moment, second_moment, gradient, factor, step_rate, decay_rate):
    gradient = gradient * factor
    first_moment = beta_first * first_moment + (1.0 - beta_first) * gradient
    second_moment = beta_second * second_moment + (1.0 - beta_second) * gradient * gradient
    first_hat = first_moment / (1.0 - beta_first**STEP)
    second_hat = second_moment / (1.0 - beta_second**STEP)
    weight = weight - step_rate * (
        first_hat / (jnp.sqrt(second_hat) + adam_eps) + decay_rate * weight
    )
    return (weight, first_moment, second_moment)


def adam_blocks(weight, first_moment, second_moment, layers, factor, kind, where):
    layer_count, rows_all, width = weight.shape
    rows = layers[0][0][0].shape[-2]
    blocks = (rows_all // rows) * (width // D)
    by_rows = rows_all // rows
    pieces = [piece for layer, _ in layers for piece in layer]

    def kernel(where, factor_ref, w, m, v, *refs):
        piece_refs, outs = refs[: len(pieces)], refs[len(pieces) :]
        layer = pl.program_id(0)
        block = pl.program_id(1)
        c, first, second = where[1], where[2], where[3]
        if kind == "gate_up":
            quarter, index = block % 4, block // 4
        elif kind == "out":
            quarter, index = 3, 0
        else:
            quarter, index = block, 0
        high, low = quarter // 2, quarter % 2
        for at in range(layer_count):
            own, swapped = piece_refs[2 * at : 2 * at + 2]
            start = layers[at][1]

            @pl.when(layer == at)
            def _():
                mine = own[2 * (first ^ high) + (second ^ low), start + index, c]
                theirs = swapped[2 * (second ^ high) + (first ^ low), start + index, c]
                mine, theirs = mine.astype(wide_type), theirs.astype(wide_type)
                for half in range(2):
                    columns = slice(half * HALF, (half + 1) * HALF)
                    results = adam_step(
                        w[0, :, columns],
                        m[0, :, columns],
                        v[0, :, columns],
                        jnp.where(c == half, mine, theirs),
                        factor_ref[0],
                        rate_matrix,
                        decay_matrix,
                    )
                    for out, result in zip(outs, results):
                        out[0, :, columns] = result

    def at(layer, block, where):
        return (layer, block, 0) if by_rows > 1 else (layer, 0, block)

    state = pl.BlockSpec((1, rows, D), at)
    return run(
        kernel,
        "adam_" + kind,
        where,
        (factor.reshape(1), weight, first_moment, second_moment, *pieces),
        [pl.BlockSpec(memory_space=pltpu.SMEM)] + [state] * 3 + fulls(pieces),
        [(weight.shape, wide_type)] * 3,
        [state] * 3,
        grid=(layer_count, blocks),
    )


def sum_all(value):
    for pairs in (FLIP_CORE, FLIP_X, FLIP_Y, Z_ONE, Z_TWO):
        value = value + send(value, pairs)
    return value


def keep_attend(results):
    names = ("trio", "qkv", "logs", "residual_one", "normed")
    return dict(zip(names, results))


def forward(hidden, weight_list, norms, where):
    kept_list = []
    for layer, weights in enumerate(weight_list):
        kept = keep_attend(attend_forward(hidden, *weights[:2], norms, layer, where))
        kept["product"], kept["slopes"] = gate_forward(kept["trio"], weights[2], where)
        kept["residual_two"], hidden = down_forward(
            kept["product"], weights[3], kept["normed"], norms, layer, where
        )
        kept_list.append(kept)
    return (hidden, kept_list)


def forward_neighbours(hidden, states, norm_params, chain):
    layer_count = states[0].shape[0]
    norm_params = norm_params.reshape(8, -1)
    rows = states[0].shape[1]
    kept_list = [None] * layer_count
    weight_list = [()] * layer_count
    groups = [(("attend", 0),)]
    for layer in range(layer_count):
        groups.append((("gate_up", layer),))
        if layer < layer_count - 1:
            groups.append((("down", layer), ("attend", layer + 1)))
    groups.append((("down", layer_count - 1),))
    owns, started, near, across, six, far, other, weights = ({} for _ in range(8))
    norms = []

    def start(at):
        more = norm_params if at == 0 else None
        *owns[at], quarters = chain(own_chunks, groups[at], states, more)
        started[at] = [send(quarters, move) for move in (Z_ONE, Z_TWO, Z_THREE)]

    def spread(at):
        near[at], rest = chain(stack_chips, started[at], rows)
        across[at] = send(near[at], FLIP_SECOND)
        if at == 0:
            count, width = norm_params.shape
            own = jnp.pad(
                norm_params.astype(low_type), ((0, NORM_ROWS - count), (0, SEQ_LEN - width))
            )
            other_rest = send(jnp.concatenate([own[None], rest]), FLIP_CORE)
            norms.extend((rest, other_rest))

    def spread_on(at):
        six[at], _ = chain(stack_two, near[at], across[at])
        far[at] = send(six[at], FLIP_FIRST)

    def swap(at):
        whole, _ = chain(pack, owns[at], six[at], far[at])
        other[at] = send(whole, FLIP_CORE)

    def lay_out(at):
        begin = 0
        if at == 0:
            norms[:] = chain(norm_columns, *norms, norm_params)
        for (kind, layer), own in zip(groups[at], owns[at]):
            weights[kind, layer] = chain(assemble, (own, six[at], far[at], other[at]), kind, begin)
            weight_list[layer] += tuple(weights[kind, layer])
            begin += BLOCKS[kind]

    def compute(at, hidden):
        for kind, layer in groups[at]:
            args = weights[kind, layer]
            if kind == "attend":
                results = chain(attend_forward, hidden, *args, norms[0], layer)
                kept_list[layer] = keep_attend(results)
                continue
            kept = kept_list[layer]
            if kind == "gate_up":
                kept["product"], kept["slopes"] = chain(gate_forward, kept["trio"], *args)
            else:
                kept["residual_two"], hidden = chain(
                    down_forward, kept["product"], *args, kept["normed"], norms[0], layer
                )
        return hidden

    last = len(groups) - 1
    start(0)
    spread(0)
    start(1)
    spread_on(0)
    for at in range(len(groups)):
        if at < last:
            spread(at + 1)
        if at + 2 <= last:
            start(at + 2)
        swap(at)
        lay_out(at)
        if at < last:
            spread_on(at + 1)
        hidden = compute(at, hidden)
    return (hidden, weight_list, kept_list, norms[0])


def gather_weights(states):
    return [
        tuple(
            lax.all_gather(weight[layer].astype(low_type), "fsdp", axis=0, tiled=True)
            for weight in states
        )
        for layer in range(states[0].shape[0])
    ]


def backward(grad, weights, kept, norms, layer, where):
    gates, _, branch, grad_one, attend, grad_mixed, grad_norms = feed_backward(
        grad, kept["residual_two"], kept["residual_one"], kept["slopes"], weights, norms, layer, where
    )
    grad_qkv, _, grad = attend_backward(
        grad_mixed, kept["qkv"], kept["logs"], grad_one, weights[0], where
    )
    gate_up = jnp.concatenate([gates[0], gates[1]], axis=1)
    factors = (
        (kept["trio"][0], grad_qkv),
        (kept["trio"][1], attend),
        (kept["trio"][2], gate_up),
        (kept["product"], branch),
    )
    return (grad, factors, grad_norms)


def backward_neighbours(grad, weight_list, kept_list, norms, chain):
    layer_count = len(weight_list)
    norm_list = [None] * layer_count
    pieces = [[None] * 4 for _ in range(layer_count)]
    squares = []
    sums = [{} for _ in range(layer_count)]

    def feed(layer, grad):
        kept = kept_list[layer]
        gates, theirs, branch, grad_one, attend, grad_mixed, norm_list[layer] = chain(
            feed_backward,
            grad,
            kept["residual_two"],
            kept["residual_one"],
            kept["slopes"],
            weight_list[layer],
            norms,
            layer,
        )
        return dict(
            gates=gates,
            feed_other=send(theirs, FLIP_CORE),
            branch=branch,
            grad_one=grad_one,
            attend=attend,
            grad_mixed=grad_mixed,
        )

    def attention(layer, made):
        kept = kept_list[layer]
        made["qkv"], theirs, grad = chain(
            attend_backward,
            made["grad_mixed"],
            kept["qkv"],
            kept["logs"],
            made["grad_one"],
            weight_list[layer][0],
        )
        made["qkv_other"] = send(theirs, FLIP_CORE)
        return grad

    def product_wide(layer, made):
        kept = kept_list[layer]
        sent, held = chain(
            grad_gate_up, kept["trio"], kept["trio_other"], made["gates"], made["feed_other"]
        )
        sums[layer]["wide"] = (held, send(sent, FLIP_FIRST))

    def product_rest(layer, made):
        kept = kept_list[layer]
        other = made["feed_other"]
        filled = chain(grad_down, kept["product"], kept["product_other"], made["branch"], other)
        qkv, qkv_other = made["qkv"], made["qkv_other"]
        trio, trio_other = kept["trio"], kept["trio_other"]
        sent, held = chain(
            grad_attend, trio, trio_other, qkv, qkv_other, made["attend"], other, filled
        )
        sums[layer]["rest"] = (held, send(sent, FLIP_FIRST))

    def halves(layer, name):
        away, left = chain(add_halves, *sums[layer][name])
        sums[layer][name] = (left, send(away, FLIP_SECOND))

    def chips(layer, names):
        own, *parts = chain(add_chips, [sums[layer][name] for name in names])
        moves = (Z_ONE, Z_TWO, Z_THREE)
        return [own] + [send(part, move) for part, move in zip(parts, moves)]

    def share(parts):
        total, part = chain(add_last, parts)
        squares.append(part)
        return (total, send(total, FLIP_SECOND))

    def share_on(found):
        row, _ = chain(stack_two, *found)
        return (row, send(row, FLIP_FIRST))

    def swap(layer, names, found):
        mine, _ = chain(pack_replicas, *found)
        found = (mine, send(mine, FLIP_CORE))
        order = {"wide": (("gate_up", (2,)),), "rest": (("down", (3,)), ("attend", (0, 1)))}
        start = 0
        for name in names:
            for kind, indices in order[name]:
                for index in indices:
                    pieces[layer][index] = (found, start)
                start += BLOCKS[kind]

    for kept in kept_list:
        for name in ("trio", "product"):
            kept[name + "_other"] = send(kept[name], FLIP_CORE)
    made = feed(layer_count - 1, grad)
    for kept in kept_list:
        chain.wait(kept["trio_other"], kept["product_other"])
    for layer in reversed(range(layer_count)):
        product_wide(layer, made)
        if layer < layer_count - 1:
            halves(layer + 1, "rest")
        grad = attention(layer, made)
        if layer > 0:
            product_rest(layer, made)
            made = feed(layer - 1, grad)
            halves(layer, "wide")
    both = ("wide", "rest")
    earlier = layer_count - 1
    parts = chips(earlier, both)
    product_rest(0, made)
    halves(0, "wide")
    found = share(parts)
    halves(0, "rest")
    parts = chips(0, ("wide",))
    found = share_on(found)
    swap(earlier, both, found)
    found = share(parts)
    parts = chips(0, ("rest",))
    found = share_on(found)
    swap(0, ("wide",), found)
    found = share(parts)
    found = share_on(found)
    swap(0, ("rest",), found)
    return (grad, norm_list, pieces, sum(squares))


def body(
    tokens_in,
    masked_flags,
    mask_embedding,
    out_cotangent,
    w_qkv,
    m_qkv,
    v_qkv,
    w_out,
    m_out,
    v_out,
    w_gu,
    m_gu,
    v_gu,
    w_down,
    m_down,
    v_down,
    norm_params,
    m_norms,
    v_norms,
):
    layer_count = w_qkv.shape[0]
    masked = masked_flags[:, None] == 1
    where = jnp.stack(place()).astype(jnp.int32)
    hidden = jnp.where(masked, mask_embedding.astype(wide_type)[None, :], tokens_in.astype(wide_type))
    grad = out_cotangent.astype(wide_type) * masked_flags[:, None].astype(wide_type)
    chain = Chain(where)
    matrices = (w_qkv, w_out, w_gu, w_down)
    if by_neighbours():
        hidden, weight_list, kept, norms = forward_neighbours(hidden, matrices, norm_params, chain)
    else:
        norms = lax.all_gather(norm_params.astype(low_type), "fsdp", axis=2, tiled=True)
        norms = norms.astype(wide_type).reshape(-1, D)
        weight_list = gather_weights(matrices)
        hidden, kept = forward(hidden, weight_list, norms, where)
    activations = hidden.astype(low_type)
    states = (
        (w_qkv, m_qkv, v_qkv),
        (w_out, m_out, v_out),
        (w_gu, m_gu, v_gu),
        (w_down, m_down, v_down),
    )
    if by_neighbours():
        grad, norm_list, pieces, squares = backward_neighbours(
            grad, weight_list, kept, norms, chain
        )
        norm_grads = jnp.concatenate(norm_list)
        rows = norm_grads.shape[0]
        packed = jnp.concatenate([norm_grads, jnp.pad(squares, ((0, 0), (0, D - HALF)))])
        packed = sum_all(packed)
        norm_grads = packed[:rows]
        total = jnp.sum(packed[rows:])
    else:
        norm_list = [None] * layer_count
        sums = [None] * layer_count
        total = wide_type(0.0)
        for layer in reversed(range(layer_count)):
            grad, factors, norm_list[layer] = backward(
                grad, weight_list[layer], kept[layer], norms, layer, where
            )
            sums[layer] = []
            for left, right in factors:
                part = dot_left(left, right)
                part = lax.psum_scatter(part, "fsdp", scatter_dimension=0, tiled=True)
                part = lax.psum(part, "rep")
                total = total + jnp.sum(part * part)
                sums[layer].append(part)
        total = lax.psum(total, "fsdp")
        norm_grads = lax.psum(jnp.concatenate(norm_list), both_axes)
    grad_norm = jnp.sqrt(total + jnp.sum(norm_grads * norm_grads))
    factor = clip_norm / jnp.maximum(grad_norm, clip_norm)
    updated = []
    for kind, state in enumerate(states):
        if by_neighbours():
            name = ("qkv", "out", "gate_up", "down")[kind]
            layers = [layer[kind] for layer in pieces]
            updated += adam_blocks(*state, layers, factor, name, where)
        else:
            gradient = jnp.stack([layer[kind] for layer in sums])
            updated += adam_step(*state, gradient, factor, rate_matrix, decay_matrix)
    width = norm_params.shape[2]
    norm_grads = norm_grads.reshape(layer_count, -1, D)
    norm_grads = lax.dynamic_slice_in_dim(norm_grads, lax.axis_index("fsdp") * width, width, 2)
    updated += adam_step(norm_params, m_norms, v_norms, norm_grads, factor, rate_norm, 0.0)
    input_grad = jnp.where(masked, 0.0, grad)
    return (activations, input_grad, grad_norm, *updated)


def solution(mesh):
    return jax.shard_map(
        body,
        mesh=mesh,
        in_specs=(
            P(("rep", "fsdp"), None),
            P(("rep", "fsdp")),
            P(),
            P(("rep", "fsdp"), None),
            P(None, "fsdp", None),
            P(None, "fsdp", None),
            P(None, "fsdp", None),
            P(None, "fsdp", None),
            P(None, "fsdp", None),
            P(None, "fsdp", None),
            P(None, "fsdp", None),
            P(None, "fsdp", None),
            P(None, "fsdp", None),
            P(None, "fsdp", None),
            P(None, "fsdp", None),
            P(None, "fsdp", None),
            P(None, None, "fsdp"),
            P(None, None, "fsdp"),
            P(None, None, "fsdp"),
        ),
        out_specs=(
            P(("rep", "fsdp"), None),
            P(("rep", "fsdp"), None),
            P(),
            P(None, "fsdp", None),
            P(None, "fsdp", None),
            P(None, "fsdp", None),
            P(None, "fsdp", None),
            P(None, "fsdp", None),
            P(None, "fsdp", None),
            P(None, "fsdp", None),
            P(None, "fsdp", None),
            P(None, "fsdp", None),
            P(None, "fsdp", None),
            P(None, "fsdp", None),
            P(None, "fsdp", None),
            P(None, None, "fsdp"),
            P(None, None, "fsdp"),
            P(None, None, "fsdp"),
        ),
        check_vma=False,
    )
```

time: 882 us -> 660 us (0.75)
  Pallas kernels: 20 us -> 233 us
  local copies, waits for them, and re-layouts: 201 us -> 70.7 us
  other arithmetic: 129 us -> 8.56 us
  blocking collectives: 86.1 us -> 0 us
  matrix products: 69.8 us -> 0 us
  starting transfers between devices: 146 us -> 91.2 us
  waiting for transfers between devices: 206 us -> 248 us
    pallas_call x6 -> x63, Pallas kernels: 20 us -> 233 us  [run(): pl.pallas_call(body_of, out_shape=[jax.ShapeDtypeStruct(shape, dtype) for...]
    reshape x16 -> x1, local copies, waits for them, and re-layouts: 82.2 us -> 1.36 us  [body(): norm_grads = norm_grads.reshape(layer_count, -1, D)]
    dot_general x36 -> x0, matrix products: 69.8 us -> none  [the longest x8 24.4 us: outer_sum(): lax.dot_general(left_rows, right_rows, (((0,), (0,)), ((), ())), preferre...]
    ppermute x101 -> x70, starting transfers between devices: 146 us -> 91.2 us  [send(): return lax.ppermute(values, both_axes, pairs)]
    all_gather x1 -> x0, blocking collectives: 48.1 us -> none  [body(): lax.all_gather(norm_params.astype(jnp.bfloat16), 'fsdp', axis=2, tiled=True)]
    convert_element_type x39 -> x4, other arithmetic: 48.7 us -> 1.93 us  [the longest x1 1.92 us: body(): activations = hidden.astype(low_type)]
    unnamed x414 -> x206, local copies, waits for them, and re-layouts: 26.6 us -> 69.3 us
    another operation x51 -> x1, other arithmetic: 42 us -> 0.08 us  [body(): where = jnp.stack(place()).astype(jnp.int32)]
  transfers between devices with their start and end apart: 101 -> 70, of which waited for: 35 -> 34; matrix products, arithmetic and copies ran while one was open for 31% -> 2% of each run, Pallas kernels for 2% -> 24%
where the time goes in v3:
time: 660 us; the launch traced here: 656 us
  waiting for transfers between devices  248 us (38%)
  Pallas kernels  233 us (35%)
  starting transfers between devices  91.2 us (14%)
  local copies, waits for them, and re-layouts  70.7 us (11%)
  other arithmetic  8.56 us (1%)
    ppermute x70, waiting for transfers between devices, send(): return lax.ppermute(values, both_axes, pairs)  248 us
    pallas_call x63, Pallas kernels, run(): pl.pallas_call(body_of, out_shape=[jax.ShapeDtypeStruct(shape, dtype) for...  233 us
    ppermute x70, starting transfers between devices, send(): return lax.ppermute(values, both_axes, pairs)  91.2 us
    unnamed x206, local copies, waits for them, and re-layouts  69.3 us
  transfers between devices with their start and end apart: 70, of which 34 were waited for; matrix products, arithmetic and copies ran while one was open for 2% of the time, Pallas kernels for 24%

profile of v3, /device:TPU:0, one launch (start us, length us, event | category | flops | bytes accessed | tf_op | source)
XLA Modules:
  0.0 656.2 jit_solution(18400663656683055164)
XLA Ops:
  10.3 4.5 collective-permute-done.refs_1_
  14.8 8.5 %collective-permute-done.1.refs_2_ = bf16[1,112,768]{2,1,0:T(8,128)(2,1)S(1)} collective-permute-done((bf16[1,112,768]{2,1,0:T(8,128)(2,1)S(1)}, bf16[1,112,768]{2,1,0:T(8,128)(2,1)S(1)}, u32[]{:S(2)}, u32[]{:S(2)}) %collective-permute-start.1) | collective-permute-done | bytes 172064 | tf_op jit(solution)/shard_map/ppermute | solution.py:51
  40.2 6.5 collective-permute-done.5.refs_1_
  46.7 13.9 %collective-permute-done.6.refs_2_ = bf16[2,96,768]{2,1,0:T(8,128)(2,1)S(1)} collective-permute-done((bf16[2,96,768]{2,1,0:T(8,128)(2,1)S(1)}, bf16[2,96,768]{2,1,0:T(8,128)(2,1)S(1)}, u32[]{:S(2)}, u32[]{:S(2)}) %collective-permute-start.6) | collective-permute-done | bytes 294944 | tf_op jit(solution)/shard_map/ppermute | solution.py:51
  72.4 5.2 collective-permute-done.10.refs_2_
  86.6 6.8 %attend_forward.2 = (bf16[3,256,768]{2,1,0:T(8,128)(2,1)S(1)}, bf16[256,2304]{1,0:T(8,128)(2,1)S(1)}, f32[256,128]{1,0:T(8,128)S(1)}, f32[256,768]{1,0:T(8,128)S(1)}, f32[256,768]{1,0:T(8,128)S(1)}) custom-call(s32[4]{0:T(128)S(1)} %pad_add_fusion.refs_0_, f32[256,768]{1,0:T(8,128)S(1)} %convert_select_fusion.refs_1_, ...), custom_call_target="tpu_custom_call" | custom-call | flops 1000 | bytes 1000 | tf_op jit(solution)/shard_map/attend_forward/pallas_call | solution.py:75
  94.4 13.1 %collective-permute-done.13.refs_2_ = bf16[2,96,768]{2,1,0:T(8,128)(2,1)S(1)} collective-permute-done((bf16[2,96,768]{2,1,0:T(8,128)(2,1)}, bf16[2,96,768]{2,1,0:T(8,128)(2,1)S(1)}, u32[]{:S(2)}, u32[]{:S(2)}) %collective-permute-start.13) | collective-permute-done | bytes 294944 | tf_op jit(solution)/shard_map/ppermute | solution.py:51
  112.1 7.3 %collective-permute-done.15.refs_4_ = bf16[16,2,96,768]{3,2,1,0:T(8,128)(2,1)S(1)} collective-permute-done((bf16[16,2,96,768]{3,2,1,0:T(8,128)(2,1)S(1)}, bf16[16,2,96,768]{3,2,1,0:T(8,128)(2,1)S(1)}, u32[]{:S(2)}, u32[]{:S(2)}) %collective-permute-start.15) | collective-permute-done | bytes 4718624 | tf_op jit(solution)/shard_map/ppermute | solution.py:51
  119.4 5.4 assemble_gate_up.2.refs_3_.refs_2_.refs_6_.refs_7_
  130.0 4.9 collective-permute-start.18
  137.5 6.8 %gate_forward.2 = (bf16[256,3072]{1,0:T(8,128)(2,1)S(1)}, bf16[2,256,3072]{2,1,0:T(8,128)(2,1)S(1)}) custom-call(s32[4]{0:T(128)S(1)} %pad_add_fusion.refs_0_, bf16[3,256,768]{2,1,0:T(8,128)(2,1)S(1)} %get-tuple-element.177.refs_1_.refs_3_, bf16[768,6144]{1,0:T(8,128)(2,1)} %assemble_gate_up.2.refs_3_.refs_2_.refs_6_.refs_7_, ...), custom_call_target="tpu_custom_call" | custom-call | flops 1000 | bytes 1000 | tf_op jit(solution)/shard_map/gate_forward/pallas_call | solution.py:75
  147.6 10.8 %collective-permute-done.19.refs_2_ = bf16[2,96,768]{2,1,0:T(8,128)(2,1)S(1)} collective-permute-done((bf16[2,96,768]{2,1,0:T(8,128)(2,1)S(1)}, bf16[2,96,768]{2,1,0:T(8,128)(2,1)S(1)}, u32[]{:S(2)}, u32[]{:S(2)}) %collective-permute-start.19) | collective-permute-done | bytes 294944 | tf_op jit(solution)/shard_map/ppermute | solution.py:51
  162.7 6.3 collective-permute-done.21.refs_4_
  169.0 6.7 %assemble_down.2.refs_5_.refs_2_ = bf16[3072,768]{1,0:T(8,128)(2,1)S(1)} custom-call(s32[4]{0:T(128)S(1)} %pad_add_fusion.refs_0_, bf16[4,1,96,768]{3,2,1,0:T(8,128)(2,1)S(1)} %get-tuple-element.188.refs_1_, bf16[2,3,2,96,768]{4,3,2,1,0:T(8,128)(2,1)S(1)} %get-tuple-element.189.refs_3_.refs_2_, ...), custom_call_target="tpu_custom_call" | custom-call | flops 1000 | bytes 1000 | tf_op jit(solution)/shard_map/assemble_down/pallas_call | solution.py:75
  178.0 14.8 %assemble_attend.3 = (bf16[768,2304]{1,0:T(8,128)(2,1)S(1)}, bf16[768,768]{1,0:T(8,128)(2,1)S(1)}) custom-call(s32[4]{0:T(128)S(1)} %pad_add_fusion.refs_0_, bf16[4,1,96,768]{3,2,1,0:T(8,128)(2,1)S(1)} %get-tuple-element.190.refs_2_.refs_1_, bf16[2,3,2,96,768]{4,3,2,1,0:T(8,128)(2,1)S(1)} %get-tuple-element.189.refs_3_.refs_2_, ...), custom_call_target="tpu_custom_call" | custom-call | flops 1000 | bytes 1000 | tf_op jit(solution)/shard_map/assemble_attend/pallas_call | solution.py:75
  196.0 6.6 collective-permute-start.24
  210.5 6.8 %attend_forward.3 = (bf16[3,256,768]{2,1,0:T(8,128)(2,1)S(1)}, bf16[256,2304]{1,0:T(8,128)(2,1)S(1)}, f32[256,128]{1,0:T(8,128)S(1)}, f32[256,768]{1,0:T(8,128)S(1)}, f32[256,768]{1,0:T(8,128)S(1)}) custom-call(s32[4]{0:T(128)S(1)} %pad_add_fusion.refs_0_, f32[256,768]{1,0:T(8,128)S(1)} %get-tuple-element.199.refs_1_, bf16[768,2304]{1,0:T(8,128)(2,1)S(1)} %copy-done.15, ...), custom_call_target="tpu_custom_call" | custom-call | flops 1000 | bytes 1000 | tf_op jit(solution)/shard_map/attend_forward/pallas_call | solution.py:75
  221.3 7.2 %collective-permute-done.27.refs_4_ = bf16[16,2,96,768]{3,2,1,0:T(8,128)(2,1)S(1)} collective-permute-done((bf16[16,2,96,768]{3,2,1,0:T(8,128)(2,1)S(1)}, bf16[16,2,96,768]{3,2,1,0:T(8,128)(2,1)S(1)}, u32[]{:S(2)}, u32[]{:S(2)}) %collective-permute-start.27) | collective-permute-done | bytes 4718624 | tf_op jit(solution)/shard_map/ppermute | solution.py:51
  233.0 5.4 assemble_gate_up.3.refs_3_.refs_2_.refs_6_.refs_7_
  243.8 6.8 %gate_forward.3 = (bf16[256,3072]{1,0:T(8,128)(2,1)S(1)}, bf16[2,256,3072]{2,1,0:T(8,128)(2,1)S(1)}) custom-call(s32[4]{0:T(128)S(1)} %pad_add_fusion.refs_0_, bf16[3,256,768]{2,1,0:T(8,128)(2,1)S(1)} %get-tuple-element.202.refs_1_.refs_3_, bf16[768,6144]{1,0:T(8,128)(2,1)} %assemble_gate_up.3.refs_3_.refs_2_.refs_6_.refs_7_, ...), custom_call_target="tpu_custom_call" | custom-call | flops 1000 | bytes 1000 | tf_op jit(solution)/shard_map/gate_forward/pallas_call | solution.py:75
  250.6 5.7 collective-permute-done.29.refs_3_
  265.7 6.7 %assemble_down.3.refs_2_.refs_5_ = bf16[3072,768]{1,0:T(8,128)(2,1)S(1)} custom-call(s32[4]{0:T(128)S(1)} %pad_add_fusion.refs_0_, bf16[4,1,96,768]{3,2,1,0:T(8,128)(2,1)S(1)} %get-tuple-element.212.refs_1_, bf16[2,3,1,96,768]{4,3,2,1,0:T(8,128)(2,1)S(1)} %get-tuple-element.213.refs_2_, bf16[2,3,1,96,768]{4,3,2,1,0:T(8,128)(2,1)S(1)} %collective-permute-done.29.refs_3_, ...), custom_call_target="tpu_custom_call" | custom-call | flops 1000 | bytes 1000 | tf_op jit(solution)/shard_map/assemble_down/pallas_call | solution.py:75
  277.7 12.2 %feed_backward.2 = (bf16[2,256,3072]{2,1,0:T(8,128)(2,1)S(1)}, bf16[256,3840]{1,0:T(8,128)(2,1)S(1)}, bf16[256,768]{1,0:T(8,128)(2,1)S(1)}, f32[256,768]{1,0:T(8...) custom-call(s32[4]{0:T(128)S(1)} %pad_add_fusion.refs_0_, ...), custom_call_target="tpu_custom_call" | custom-call | flops 1000 | bytes 1000 | tf_op jit(solution)/shard_map/feed_backward/pallas_call | solution.py:75
  292.8 9.0 %collective-permute-done.33.refs_6_.refs_2_.refs_4_ = bf16[3,256,768]{2,1,0:T(8,128)(2,1)S(1)} collective-permute-done((bf16[3,256,768]{2,1,0:T(8,128)(2,1)S(1)}, bf16[3,256,768]{2,1,0:T(8,128)(2,1)S(1)}, u32[]{:S(2)}, u32[]{:S(2)}) %collective-permute-start.33) | collective-permute-done | bytes 1179680 | tf_op jit(solution)/shard_map/ppermute | solution.py:51
  303.5 9.5 %grad_gate_up.2 = (bf16[2,4,2,2,96,384]{5,4,3,2,1,0:T(8,128)(2,1)}, bf16[2,4,2,2,96,384]{5,4,3,2,1,0:T(8,128)(2,1)S(1)}) custom-call(s32[4]{0:T(128)S(1)} %pad_add_fusion.refs_0_, bf16[3,256,768]{2,1,0:T(8,128)(2,1)S(1)} %get-tuple-element.202.refs_1_.refs_3_, bf16[3,256,768]{2,1,0:T(8,128)(2,1)S(1)} %collective-permute-done.31.refs_2_.refs_8_.refs_4_, ...), custom_call_target="tpu_custom_call" | custom-call | flops 1000 | bytes 1000 | tf_op jit(solution)/shard_map/grad_gate_up/pallas_call | solution.py:75
  317.7 7.2 %attend_backward.2 = (bf16[256,2304]{1,0:T(8,128)(2,1)S(1)}, bf16[256,1152]{1,0:T(8,128)(2,1)S(1)}, f32[256,768]{1,0:T(8,128)S(1)}) custom-call(s32[4]{0:T(128)S(1)} %pad_add_fusion.refs_0_, bf16[256,768]{1,0:T(8,128)(2,1)S(1)} %get-tuple-element.221.refs_1_, bf16[256,2304]{1,0:T(8,128)(2,1)S(1)} %copy-done.69, f32[256,128]{1,0:T(8,128)S(1)} %copy-done.82, ...), custom_call_target="tpu_custom_call" | custom-call | flops 1000 | bytes 1000 | tf_op jit(solution)/shard_map/attend_backward/pallas_call | solution.py:75
  325.7 4.4 grad_down.2
  344.2 14.0 %feed_backward.3 = (bf16[2,256,3072]{2,1,0:T(8,128)(2,1)S(1)}, bf16[256,3840]{1,0:T(8,128)(2,1)}, bf16[256,768]{1,0:T(8,128)(2,1)S(1)}, f32[256,768]{1,0:T(8,128...) custom-call(s32[4]{0:T(128)S(1)} %pad_add_fusion.refs_0_, ...), custom_call_target="tpu_custom_call" | custom-call | flops 1000 | bytes 1000 | tf_op jit(solution)/shard_map/feed_backward/pallas_call | solution.py:75
  359.9 4.4 add_halves.4
  367.9 7.6 %grad_gate_up.3 = (bf16[2,4,2,2,96,384]{5,4,3,2,1,0:T(8,128)(2,1)S(1)}, bf16[2,4,2,2,96,384]{5,4,3,2,1,0:T(8,128)(2,1)S(1)}) custom-call(s32[4]{0:T(128)S(1)} %pad_add_fusion.refs_0_, bf16[3,256,768]{2,1,0:T(8,128)(2,1)S(1)} %get-tuple-element.177.refs_1_.refs_3_, bf16[3,256,768]{2,1,0:T(8,128)(2,1)S(1)} %collective-permute-done.33.refs_6_.refs_2_.refs_4_, ...), custom_call_target="tpu_custom_call" | custom-call | flops 1000 | bytes 1000 | tf_op jit(solution)/shard_map/grad_gate_up/pallas_call | solution.py:75
  375.5 14.9 %collective-permute-done.37.refs_2_ = bf16[2,4,2,2,96,384]{5,4,3,2,1,0:T(8,128)(2,1)} collective-permute-done((bf16[2,4,2,2,96,384]{5,4,3,2,1,0:T(8,128)(2,1)S(1)}, bf16[2,4,2,2,96,384]{5,4,3,2,1,0:T(8,128)(2,1)}, u32[]{:S(2)}, u32[]{:S(2)}) %collective-permute-start.37) | collective-permute-done | bytes 2359328 | tf_op jit(solution)/shard_map/ppermute | solution.py:51
  390.4 4.7 add_halves.5
  398.6 8.2 %attend_backward.3 = (bf16[256,2304]{1,0:T(8,128)(2,1)S(1)}, bf16[256,1152]{1,0:T(8,128)(2,1)}, f32[256,768]{1,0:T(8,128)S(1)}) custom-call(s32[4]{0:T(128)S(1)} %pad_add_fusion.refs_0_, bf16[256,768]{1,0:T(8,128)(2,1)S(1)} %get-tuple-element.238.refs_1_, bf16[256,2304]{1,0:T(8,128)(2,1)S(1)} %copy-done.67, ...), custom_call_target="tpu_custom_call" | custom-call | flops 1000 | bytes 1000 | tf_op jit(solution)/shard_map/attend_backward/pallas_call | solution.py:75
  407.8 17.5 %collective-permute-done.41.refs_4_ = bf16[4,2,2,96,384]{4,3,2,1,0:T(8,128)(2,1)} collective-permute-done((bf16[4,2,2,96,384]{4,3,2,1,0:T(8,128)(2,1)}, bf16[4,2,2,96,384]{4,3,2,1,0:T(8,128)(2,1)}, u32[]{:S(2)}, u32[]{:S(2)}) %collective-permute-start.41) | collective-permute-done | bytes 1179680 | tf_op jit(solution)/shard_map/ppermute | solution.py:51
  447.0 5.6 collective-permute-start.42
  457.4 13.4 %collective-permute-done.42.refs_2_ = bf16[4,2,96,384]{3,2,1,0:T(8,128)(2,1)S(1)} collective-permute-done((bf16[4,2,96,384]{3,2,1,0:T(8,128)(2,1)S(1)}, bf16[4,2,96,384]{3,2,1,0:T(8,128)(2,1)S(1)}, u32[]{:S(2)}, u32[]{:S(2)}) %collective-permute-start.42) | collective-permute-done | bytes 589856 | tf_op jit(solution)/shard_map/ppermute | solution.py:51
  470.8 22.2 %collective-permute-done.43.refs_3_ = bf16[4,2,96,384]{3,2,1,0:T(8,128)(2,1)S(1)} collective-permute-done((bf16[4,2,96,384]{3,2,1,0:T(8,128)(2,1)S(1)}, bf16[4,2,96,384]{3,2,1,0:T(8,128)(2,1)S(1)}, u32[]{:S(2)}, u32[]{:S(2)}) %collective-permute-start.43) | collective-permute-done | bytes 589856 | tf_op jit(solution)/shard_map/ppermute | solution.py:51
  498.3 11.9 %collective-permute-done.52.refs_2_ = bf16[4,2,96,384]{3,2,1,0:T(8,128)(2,1)S(1)} collective-permute-done((bf16[4,2,96,384]{3,2,1,0:T(8,128)(2,1)S(1)}, bf16[4,2,96,384]{3,2,1,0:T(8,128)(2,1)S(1)}, u32[]{:S(2)}, u32[]{:S(2)}) %collective-permute-start.52) | collective-permute-done | bytes 589856 | tf_op jit(solution)/shard_map/ppermute | solution.py:51
  520.9 9.6 %collective-permute-done.53.refs_2_ = bf16[2,4,2,96,384]{4,3,2,1,0:T(8,128)(2,1)S(1)} collective-permute-done((bf16[2,4,2,96,384]{4,3,2,1,0:T(8,128)(2,1)S(1)}, bf16[2,4,2,96,384]{4,3,2,1,0:T(8,128)(2,1)S(1)}, u32[]{:S(2)}, u32[]{:S(2)}) %collective-permute-start.53) | collective-permute-done | bytes 1179680 | tf_op jit(solution)/shard_map/ppermute | solution.py:51
  535.0 8.0 %collective-permute-done.58.refs_2_ = bf16[2,2,96,384]{3,2,1,0:T(8,128)(2,1)S(1)} collective-permute-done((bf16[2,2,96,384]{3,2,1,0:T(8,128)(2,1)S(1)}, bf16[2,2,96,384]{3,2,1,0:T(8,128)(2,1)S(1)}, u32[]{:S(2)}, u32[]{:S(2)}) %collective-permute-start.58) | collective-permute-done | bytes 294944 | tf_op jit(solution)/shard_map/ppermute | solution.py:51
  544.2 5.7 collective-permute-start.55
  557.7 6.1 collective-permute-done.56.refs_3_
  565.3 9.2 %collective-permute-done.65.refs_2_ = bf16[2,2,96,384]{3,2,1,0:T(8,128)(2,1)S(1)} collective-permute-done((bf16[2,2,96,384]{3,2,1,0:T(8,128)(2,1)S(1)}, bf16[2,2,96,384]{3,2,1,0:T(8,128)(2,1)S(1)}, u32[]{:S(2)}, u32[]{:S(2)}) %collective-permute-start.65) | collective-permute-done | bytes 294944 | tf_op jit(solution)/shard_map/ppermute | solution.py:51
  575.9 9.3 %collective-permute-done.66.refs_2_ = bf16[2,2,2,96,384]{4,3,2,1,0:T(8,128)(2,1)S(1)} collective-permute-done((bf16[2,2,2,96,384]{4,3,2,1,0:T(8,128)(2,1)S(1)}, bf16[2,2,2,96,384]{4,3,2,1,0:T(8,128)(2,1)S(1)}, u32[]{:S(2)}, u32[]{:S(2)}) %collective-permute-start.66) | collective-permute-done | bytes 589856 | tf_op jit(solution)/shard_map/ppermute | solution.py:51
  618.5 17.3 %adam_gate_up.1 = (f32[2,96,6144]{2,1,0:T(8,128)}, f32[2,96,6144]{2,1,0:T(8,128)}, f32[2,96,6144]{2,1,0:T(8,128)}) custom-call(s32[4]{0:T(128)S(1)} %pad_add_fusion.refs_0_, f32[1]{0:T(128)} %bitcast.6.refs_1_, f32[2,96,6144]{2,1,0:T(8,128)S(1)} %copy-done.6, f32[2,96,6144]{2,1,0:T(8,128)} %refs_3_.8, f32[2,96,6144]{2,1,0:T(8,128)} %refs_4_.6, ...), custom_call_target="tpu_custom_call" | custom-call | flops 1000 | bytes 1000 | tf_op jit(solution)/shard_map/adam_gate_up/pallas_call | solution.py:75
  635.9 6.8 %adam_qkv.1 = (f32[2,96,2304]{2,1,0:T(8,128)}, f32[2,96,2304]{2,1,0:T(8,128)}, f32[2,96,2304]{2,1,0:T(8,128)}) custom-call(s32[4]{0:T(128)S(1)} %pad_add_fusion.refs_0_, f32[1]{0:T(128)} %bitcast.6.refs_1_, f32[2,96,2304]{2,1,0:T(8,128)S(1)} %copy-done.11, f32[2,96,2304]{2,1,0:T(8,128)S(1)} %copy-done.62, f32[2,96,2304]{2,1,0:T(8,128)S(1)} %copy-done.63, ...), custom_call_target="tpu_custom_call" | custom-call | flops 1000 | bytes 1000 | tf_op jit(solution)/shard_map/adam_qkv/pallas_call | solution.py:75
  642.7 4.4 adam_out.1
  647.2 7.7 %adam_down.1 = (f32[2,384,768]{2,1,0:T(8,128)}, f32[2,384,768]{2,1,0:T(8,128)}, f32[2,384,768]{2,1,0:T(8,128)}) custom-call(s32[4]{0:T(128)S(1)} %pad_add_fusion.refs_0_, f32[1]{0:T(128)} %bitcast.6.refs_1_, f32[2,384,768]{2,1,0:T(8,128)S(1)} %copy-done.8, f32[2,384,768]{2,1,0:T(8,128)S(1)} %copy-done.56, f32[2,384,768]{2,1,0:T(8,128)S(1)} %copy-done.57, ...), custom_call_target="tpu_custom_call" | custom-call | flops 1000 | bytes 1000 | tf_op jit(solution)/shard_map/adam_down/pallas_call | solution.py:75
  (383 shorter events, 234.0 us)
Async XLA Ops:
  7.7 15.6 %collective-permute-start.1 = (bf16[1,112,768]{2,1,0:T(8,128)(2,1)S(1)}, bf16[1,112,768]{2,1,0:T(8,128)(2,1)S(1)}, u32[]{:S(2)}, u32[]{:S(2)}) collective-permute-start(bf16[1,112,768]{2,1,0:T(8,128)(2,1)S(1)} %get-tuple-element.163.refs_4_), channel_id=1, source_target_pairs={{0,4},{1,5},{2,6},{3,7},{4,0},{5,1},{6,2},{7,3},{8,12},{9,13},{10,... | collective-permute-start | bytes 516104 | tf_op jit(solution)/shard_map/ppermute | solution.py:51
  10.3 13.0 %collective-permute-start.2 = (bf16[1,112,768]{2,1,0:T(8,128)(2,1)S(1)}, bf16[1,112,768]{2,1,0:T(8,128)(2,1)S(1)}, u32[]{:S(2)}, u32[]{:S(2)}) collective-permute-start(bf16[1,112,768]{2,1,0:T(8,128)(2,1)S(1)} %get-tuple-element.163.refs_4_), channel_id=1, source_target_pairs={{0,6},{1,7},{2,4},{3,5},{4,2},{5,3},{6,0},{7,1},{8,14},{9,15},{10,... | collective-permute-start | bytes 516104 | tf_op jit(solution)/shard_map/ppermute | solution.py:51
  33.3 29.4 %collective-permute-start.4 = (bf16[2,3,1,96,768]{4,3,2,1,0:T(8,128)(2,1)S(1)}, bf16[2,3,1,96,768]{4,3,2,1,0:T(8,128)(2,1)S(1)}, u32[]{:S(2)}, u32[]{:S(2)}) collective-permute-start(bf16[2,3,1,96,768]{4,3,2,1,0:T(8,128)(2,1)S(1)} %get-tuple-element.167.refs_2_), channel_id=1, source_target_pairs={{0,8},{1,17},{2,10},{3,19},{4,12},{5,21},{6,14},{7,23},{8,0},{9,25... | collective-permute-start | bytes 2654216 | tf_op jit(solution)/shard_map/ppermute | solution.py:51
  34.9 11.8 %collective-permute-start.5 = (bf16[2,96,768]{2,1,0:T(8,128)(2,1)S(1)}, bf16[2,96,768]{2,1,0:T(8,128)(2,1)S(1)}, u32[]{:S(2)}, u32[]{:S(2)}) collective-permute-start(bf16[2,96,768]{2,1,0:T(8,128)(2,1)S(1)} %get-tuple-element.166.refs_3_), channel_id=1, source_target_pairs={{0,2},{1,3},{2,0},{3,1},{4,6},{5,7},{6,4},{7,5},{8,10},{9,11},{10,... | collective-permute-start | bytes 884744 | tf_op jit(solution)/shard_map/ppermute | solution.py:51
  37.7 23.0 %collective-permute-start.6 = (bf16[2,96,768]{2,1,0:T(8,128)(2,1)S(1)}, bf16[2,96,768]{2,1,0:T(8,128)(2,1)S(1)}, u32[]{:S(2)}, u32[]{:S(2)}) collective-permute-start(bf16[2,96,768]{2,1,0:T(8,128)(2,1)S(1)} %get-tuple-element.166.refs_3_), channel_id=1, source_target_pairs={{0,4},{1,5},{2,6},{3,7},{4,0},{5,1},{6,2},{7,3},{8,12},{9,13},{10,... | collective-permute-start | bytes 884744 | tf_op jit(solution)/shard_map/ppermute | solution.py:51
  38.7 22.0 %collective-permute-start.7 = (bf16[2,96,768]{2,1,0:T(8,128)(2,1)S(1)}, bf16[2,96,768]{2,1,0:T(8,128)(2,1)S(1)}, u32[]{:S(2)}, u32[]{:S(2)}) collective-permute-start(bf16[2,96,768]{2,1,0:T(8,128)(2,1)S(1)} %get-tuple-element.166.refs_3_), channel_id=1, source_target_pairs={{0,6},{1,7},{2,4},{3,5},{4,2},{5,3},{6,0},{7,1},{8,14},{9,15},{10,... | collective-permute-start | bytes 884744 | tf_op jit(solution)/shard_map/ppermute | solution.py:51
  64.5 13.1 %collective-permute-start.10 = (bf16[3,2,96,768]{3,2,1,0:T(8,128)(2,1)S(1)}, bf16[3,2,96,768]{3,2,1,0:T(8,128)(2,1)S(1)}, u32[]{:S(2)}, u32[]{:S(2)}) collective-permute-start(bf16[3,2,96,768]{3,2,1,0:T(8,128)(2,1)S(1)} %get-tuple-element.175.refs_1_), channel_id=1, source_target_pairs={{0,16},{1,9},{2,18},{3,11},{4,20},{5,13},{6,22},{7,15},{8,24},{9,1... | collective-permute-start | bytes 2654216 | tf_op jit(solution)/shard_map/ppermute | solution.py:51
  78.5 31.3 %collective-permute-start.11 = (bf16[2,3,2,96,768]{4,3,2,1,0:T(8,128)(2,1)S(1)}, bf16[2,3,2,96,768]{4,3,2,1,0:T(8,128)(2,1)S(1)}, u32[]{:S(2)}, u32[]{:S(2)}) collective-permute-start(bf16[2,3,2,96,768]{4,3,2,1,0:T(8,128)(2,1)S(1)} %get-tuple-element.179.refs_2_), channel_id=1, source_target_pairs={{0,8},{1,17},{2,10},{3,19},{4,12},{5,21},{6,14},{7,23},{8,0},{9,25... | collective-permute-start | bytes 5308424 | tf_op jit(solution)/shard_map/ppermute | solution.py:51
  79.6 14.8 %collective-permute-start.12 = (bf16[2,96,768]{2,1,0:T(8,128)(2,1)}, bf16[2,96,768]{2,1,0:T(8,128)(2,1)S(1)}, u32[]{:S(2)}, u32[]{:S(2)}) collective-permute-start(bf16[2,96,768]{2,1,0:T(8,128)(2,1)} %get-tuple-element.170.refs_4_), channel_id=1, source_target_pairs={{0,2},{1,3},{2,0},{3,1},{4,6},{5,7},{6,4},{7,5},{8,10},{9,11},{10,... | collective-permute-start | bytes 884744 | tf_op jit(solution)/shard_map/ppermute | solution.py:51
  83.8 23.7 %collective-permute-start.13 = (bf16[2,96,768]{2,1,0:T(8,128)(2,1)}, bf16[2,96,768]{2,1,0:T(8,128)(2,1)S(1)}, u32[]{:S(2)}, u32[]{:S(2)}) collective-permute-start(bf16[2,96,768]{2,1,0:T(8,128)(2,1)} %get-tuple-element.170.refs_4_), channel_id=1, source_target_pairs={{0,4},{1,5},{2,6},{3,7},{4,0},{5,1},{6,2},{7,3},{8,12},{9,13},{10,... | collective-permute-start | bytes 884744 | tf_op jit(solution)/shard_map/ppermute | solution.py:51
  84.9 22.6 %collective-permute-start.14 = (bf16[2,96,768]{2,1,0:T(8,128)(2,1)}, bf16[2,96,768]{2,1,0:T(8,128)(2,1)S(1)}, u32[]{:S(2)}, u32[]{:S(2)}) collective-permute-start(bf16[2,96,768]{2,1,0:T(8,128)(2,1)} %get-tuple-element.170.refs_4_), channel_id=1, source_target_pairs={{0,6},{1,7},{2,4},{3,5},{4,2},{5,3},{6,0},{7,1},{8,14},{9,15},{10,... | collective-permute-start | bytes 884744 | tf_op jit(solution)/shard_map/ppermute | solution.py:51
  111.5 13.3 %collective-permute-start.16 = (bf16[3,2,96,768]{3,2,1,0:T(8,128)(2,1)S(1)}, bf16[3,2,96,768]{3,2,1,0:T(8,128)(2,1)S(1)}, u32[]{:S(2)}, u32[]{:S(2)}) collective-permute-start(bf16[3,2,96,768]{3,2,1,0:T(8,128)(2,1)S(1)} %get-tuple-element.185.refs_1_), channel_id=1, source_target_pairs={{0,16},{1,9},{2,18},{3,11},{4,20},{5,13},{6,22},{7,15},{8,24},{9,1... | collective-permute-start | bytes 2654216 | tf_op jit(solution)/shard_map/ppermute | solution.py:51
  129.4 30.2 %collective-permute-start.17 = (bf16[2,3,2,96,768]{4,3,2,1,0:T(8,128)(2,1)S(1)}, bf16[2,3,2,96,768]{4,3,2,1,0:T(8,128)(2,1)S(1)}, u32[]{:S(2)}, u32[]{:S(2)}) collective-permute-start(bf16[2,3,2,96,768]{4,3,2,1,0:T(8,128)(2,1)S(1)} %get-tuple-element.189.refs_3_.refs_2_), channel_id=1, source_target_pairs={{0,8},{1,17},{2,10},{3,19},{4,12},{5,21},{6,14},{7,23},{8,0},{9,25... | collective-permute-start | bytes 5308424 | tf_op jit(solution)/shard_map/ppermute | solution.py:51
  130.0 17.5 %collective-permute-start.18 = (bf16[2,96,768]{2,1,0:T(8,128)(2,1)S(1)}, bf16[2,96,768]{2,1,0:T(8,128)(2,1)S(1)}, u32[]{:S(2)}, u32[]{:S(2)}) collective-permute-start(bf16[2,96,768]{2,1,0:T(8,128)(2,1)S(1)} %get-tuple-element.182.refs_4_), channel_id=1, source_target_pairs={{0,2},{1,3},{2,0},{3,1},{4,6},{5,7},{6,4},{7,5},{8,10},{9,11},{10,... | collective-permute-start | bytes 884744 | tf_op jit(solution)/shard_map/ppermute | solution.py:51
  134.9 23.5 %collective-permute-start.19 = (bf16[2,96,768]{2,1,0:T(8,128)(2,1)S(1)}, bf16[2,96,768]{2,1,0:T(8,128)(2,1)S(1)}, u32[]{:S(2)}, u32[]{:S(2)}) collective-permute-start(bf16[2,96,768]{2,1,0:T(8,128)(2,1)S(1)} %get-tuple-element.182.refs_4_), channel_id=1, source_target_pairs={{0,4},{1,5},{2,6},{3,7},{4,0},{5,1},{6,2},{7,3},{8,12},{9,13},{10,... | collective-permute-start | bytes 884744 | tf_op jit(solution)/shard_map/ppermute | solution.py:51
  136.0 22.4 %collective-permute-start.20 = (bf16[2,96,768]{2,1,0:T(8,128)(2,1)S(1)}, bf16[2,96,768]{2,1,0:T(8,128)(2,1)S(1)}, u32[]{:S(2)}, u32[]{:S(2)}) collective-permute-start(bf16[2,96,768]{2,1,0:T(8,128)(2,1)S(1)} %get-tuple-element.182.refs_4_), channel_id=1, source_target_pairs={{0,6},{1,7},{2,4},{3,5},{4,2},{5,3},{6,0},{7,1},{8,14},{9,15},{10,... | collective-permute-start | bytes 884744 | tf_op jit(solution)/shard_map/ppermute | solution.py:51
  161.1 33.4 %collective-permute-start.22 = (bf16[3,2,96,768]{3,2,1,0:T(8,128)(2,1)S(1)}, bf16[3,2,96,768]{3,2,1,0:T(8,128)(2,1)S(1)}, u32[]{:S(2)}, u32[]{:S(2)}) collective-permute-start(bf16[3,2,96,768]{3,2,1,0:T(8,128)(2,1)S(1)} %get-tuple-element.196.refs_1_), channel_id=1, source_target_pairs={{0,16},{1,9},{2,18},{3,11},{4,20},{5,13},{6,22},{7,15},{8,24},{9,1... | collective-permute-start | bytes 2654216 | tf_op jit(solution)/shard_map/ppermute | solution.py:51
  195.5 23.4 %collective-permute-start.23 = (bf16[2,3,2,96,768]{4,3,2,1,0:T(8,128)(2,1)S(1)}, bf16[2,3,2,96,768]{4,3,2,1,0:T(8,128)(2,1)S(1)}, u32[]{:S(2)}, u32[]{:S(2)}) collective-permute-start(bf16[2,3,2,96,768]{4,3,2,1,0:T(8,128)(2,1)S(1)} %get-tuple-element.204.refs_2_), channel_id=1, source_target_pairs={{0,8},{1,17},{2,10},{3,19},{4,12},{5,21},{6,14},{7,23},{8,0},{9,25... | collective-permute-start | bytes 5308424 | tf_op jit(solution)/shard_map/ppermute | solution.py:51
  196.0 22.3 %collective-permute-start.24 = (bf16[1,96,768]{2,1,0:T(8,128)(2,1)S(1)}, bf16[1,96,768]{2,1,0:T(8,128)(2,1)S(1)}, u32[]{:S(2)}, u32[]{:S(2)}) collective-permute-start(bf16[1,96,768]{2,1,0:T(8,128)(2,1)S(1)} %get-tuple-element.192.refs_5_), channel_id=1, source_target_pairs={{0,2},{1,3},{2,0},{3,1},{4,6},{5,7},{6,4},{7,5},{8,10},{9,11},{10,... | collective-permute-start | bytes 442376 | tf_op jit(solution)/shard_map/ppermute | solution.py:51
  202.6 15.8 %collective-permute-start.25 = (bf16[1,96,768]{2,1,0:T(8,128)(2,1)S(1)}, bf16[1,96,768]{2,1,0:T(8,128)(2,1)S(1)}, u32[]{:S(2)}, u32[]{:S(2)}) collective-permute-start(bf16[1,96,768]{2,1,0:T(8,128)(2,1)S(1)} %get-tuple-element.192.refs_5_), channel_id=1, source_target_pairs={{0,4},{1,5},{2,6},{3,7},{4,0},{5,1},{6,2},{7,3},{8,12},{9,13},{10,... | collective-permute-start | bytes 442376 | tf_op jit(solution)/shard_map/ppermute | solution.py:51
  203.6 14.7 %collective-permute-start.26 = (bf16[1,96,768]{2,1,0:T(8,128)(2,1)S(1)}, bf16[1,96,768]{2,1,0:T(8,128)(2,1)S(1)}, u32[]{:S(2)}, u32[]{:S(2)}) collective-permute-start(bf16[1,96,768]{2,1,0:T(8,128)(2,1)S(1)} %get-tuple-element.192.refs_5_), channel_id=1, source_target_pairs={{0,6},{1,7},{2,4},{3,5},{4,2},{5,3},{6,0},{7,1},{8,14},{9,15},{10,... | collective-permute-start | bytes 442376 | tf_op jit(solution)/shard_map/ppermute | solution.py:51
  220.6 17.8 %collective-permute-start.28 = (bf16[3,1,96,768]{3,2,1,0:T(8,128)(2,1)S(1)}, bf16[3,1,96,768]{3,2,1,0:T(8,128)(2,1)S(1)}, u32[]{:S(2)}, u32[]{:S(2)}) collective-permute-start(bf16[3,1,96,768]{3,2,1,0:T(8,128)(2,1)S(1)} %get-tuple-element.209.refs_1_), channel_id=1, source_target_pairs={{0,16},{1,9},{2,18},{3,11},{4,20},{5,13},{6,22},{7,15},{8,24},{9,1... | collective-permute-start | bytes 1327112 | tf_op jit(solution)/shard_map/ppermute | solution.py:51
  243.2 13.1 %collective-permute-start.29 = (bf16[2,3,1,96,768]{4,3,2,1,0:T(8,128)(2,1)S(1)}, bf16[2,3,1,96,768]{4,3,2,1,0:T(8,128)(2,1)S(1)}, u32[]{:S(2)}, u32[]{:S(2)}) collective-permute-start(bf16[2,3,1,96,768]{4,3,2,1,0:T(8,128)(2,1)S(1)} %get-tuple-element.213.refs_2_), channel_id=1, source_target_pairs={{0,8},{1,17},{2,10},{3,19},{4,12},{5,21},{6,14},{7,23},{8,0},{9,25... | collective-permute-start | bytes 2654216 | tf_op jit(solution)/shard_map/ppermute | solution.py:51
  291.6 11.9 %collective-permute-start.32 = (bf16[256,3840]{1,0:T(8,128)(2,1)S(1)}, bf16[256,3840]{1,0:T(8,128)(2,1)S(1)}, u32[]{:S(2)}, u32[]{:S(2)}) collective-permute-start(bf16[256,3840]{1,0:T(8,128)(2,1)S(1)} %get-tuple-element.225), channel_id=1, source_target_pairs={{0,1},{1,0},{2,3},{3,2},{4,5},{5,4},{6,7},{7,6},{8,9},{9,8},{10,11... | collective-permute-start | bytes 5898248 | tf_op jit(solution)/shard_map/ppermute | solution.py:51
  292.1 11.3 %collective-permute-start.35 = (bf16[256,3072]{1,0:T(8,128)(2,1)S(1)}, bf16[256,3072]{1,0:T(8,128)(2,1)S(1)}, u32[]{:S(2)}, u32[]{:S(2)}) collective-permute-start(bf16[256,3072]{1,0:T(8,128)(2,1)S(1)} %copy-done.18), channel_id=1, source_target_pairs={{0,1},{1,0},{2,3},{3,2},{4,5},{5,4},{6,7},{7,6},{8,9},{9,8},{10,11... | collective-permute-start | bytes 4718600 | tf_op jit(solution)/shard_map/ppermute | solution.py:51
  325.2 34.7 %collective-permute-start.39 = (bf16[2,4,2,2,96,384]{5,4,3,2,1,0:T(8,128)(2,1)}, bf16[2,4,2,2,96,384]{5,4,3,2,1,0:T(8,128)(2,1)}, u32[]{:S(2)}, u32[]{:S(2)}) collective-permute-start(bf16[2,4,2,2,96,384]{5,4,3,2,1,0:T(8,128)(2,1)} %get-tuple-element.227.refs_6_), channel_id=1, source_target_pairs={{0,8},{1,17},{2,10},{3,19},{4,12},{5,21},{6,14},{7,23},{8,0},{9,25... | collective-permute-start | bytes 7077896 | tf_op jit(solution)/shard_map/ppermute | solution.py:51
  341.5 48.9 %collective-permute-start.37 = (bf16[2,4,2,2,96,384]{5,4,3,2,1,0:T(8,128)(2,1)S(1)}, bf16[2,4,2,2,96,384]{5,4,3,2,1,0:T(8,128)(2,1)}, u32[]{:S(2)}, u32[]{:S(2)}) collective-permute-start(bf16[2,4,2,2,96,384]{5,4,3,2,1,0:T(8,128)(2,1)S(1)} %get-tuple-element.237.refs_10_), channel_id=1, source_target_pairs={{0,8},{1,17},{2,10},{3,19},{4,12},{5,21},{6,14},{7,23},{8,0},{9,25... | collective-permute-start | bytes 7077896 | tf_op jit(solution)/shard_map/ppermute | solution.py:51
  365.4 42.5 %collective-permute-start.40 = (bf16[4,2,2,96,384]{4,3,2,1,0:T(8,128)(2,1)}, bf16[4,2,2,96,384]{4,3,2,1,0:T(8,128)(2,1)}, u32[]{:S(2)}, u32[]{:S(2)}) collective-permute-start(bf16[4,2,2,96,384]{4,3,2,1,0:T(8,128)(2,1)} %get-tuple-element.246.refs_5_), channel_id=1, source_target_pairs={{0,16},{1,9},{2,18},{3,11},{4,20},{5,13},{6,22},{7,15},{8,24},{9,1... | collective-permute-start | bytes 3538952 | tf_op jit(solution)/shard_map/ppermute | solution.py:51
  396.1 29.2 %collective-permute-start.41 = (bf16[4,2,2,96,384]{4,3,2,1,0:T(8,128)(2,1)}, bf16[4,2,2,96,384]{4,3,2,1,0:T(8,128)(2,1)}, u32[]{:S(2)}, u32[]{:S(2)}) collective-permute-start(bf16[4,2,2,96,384]{4,3,2,1,0:T(8,128)(2,1)} %get-tuple-element.248.refs_6_), channel_id=1, source_target_pairs={{0,16},{1,9},{2,18},{3,11},{4,20},{5,13},{6,22},{7,15},{8,24},{9,1... | collective-permute-start | bytes 3538952 | tf_op jit(solution)/shard_map/ppermute | solution.py:51
  396.8 56.9 %collective-permute-start.45 = (bf16[2,4,2,2,96,384]{5,4,3,2,1,0:T(8,128)(2,1)S(1)}, bf16[2,4,2,2,96,384]{5,4,3,2,1,0:T(8,128)(2,1)S(1)}, u32[]{:S(2)}, u32[]{:S(2)}) collective-permute-start(bf16[2,4,2,2,96,384]{5,4,3,2,1,0:T(8,128)(2,1)S(1)} %get-tuple-element.247.refs_3_), channel_id=1, source_target_pairs={{0,8},{1,17},{2,10},{3,19},{4,12},{5,21},{6,14},{7,23},{8,0},{9,25... | collective-permute-start | bytes 7077896 | tf_op jit(solution)/shard_map/ppermute | solution.py:51
  407.8 29.1 %collective-permute-start.46 = (bf16[256,1152]{1,0:T(8,128)(2,1)}, bf16[256,1152]{1,0:T(8,128)(2,1)S(1)}, u32[]{:S(2)}, u32[]{:S(2)}) collective-permute-start(bf16[256,1152]{1,0:T(8,128)(2,1)} %get-tuple-element.258), channel_id=1, source_target_pairs={{0,1},{1,0},{2,3},{3,2},{4,5},{5,4},{6,7},{7,6},{8,9},{9,8},{10,11... | collective-permute-start | bytes 1769480 | tf_op jit(solution)/shard_map/ppermute | solution.py:51
  446.4 49.4 %collective-permute-start.48 = (bf16[2,4,2,2,96,384]{5,4,3,2,1,0:T(8,128)(2,1)S(1)}, bf16[2,4,2,2,96,384]{5,4,3,2,1,0:T(8,128)(2,1)S(1)}, u32[]{:S(2)}, u32[]{:S(2)}) collective-permute-start(bf16[2,4,2,2,96,384]{5,4,3,2,1,0:T(8,128)(2,1)S(1)} %get-tuple-element.263.refs_3_), channel_id=1, source_target_pairs={{0,8},{1,17},{2,10},{3,19},{4,12},{5,21},{6,14},{7,23},{8,0},{9,25... | collective-permute-start | bytes 7077896 | tf_op jit(solution)/shard_map/ppermute | solution.py:51
  447.0 23.8 %collective-permute-start.42 = (bf16[4,2,96,384]{3,2,1,0:T(8,128)(2,1)S(1)}, bf16[4,2,96,384]{3,2,1,0:T(8,128)(2,1)S(1)}, u32[]{:S(2)}, u32[]{:S(2)}) collective-permute-start(bf16[4,2,96,384]{3,2,1,0:T(8,128)(2,1)S(1)} %get-tuple-element.253), channel_id=1, source_target_pairs={{0,2},{1,3},{2,0},{3,1},{4,6},{5,7},{6,4},{7,5},{8,10},{9,11},{10,... | collective-permute-start | bytes 1769480 | tf_op jit(solution)/shard_map/ppermute | solution.py:51
  452.6 40.4 %collective-permute-start.43 = (bf16[4,2,96,384]{3,2,1,0:T(8,128)(2,1)S(1)}, bf16[4,2,96,384]{3,2,1,0:T(8,128)(2,1)S(1)}, u32[]{:S(2)}, u32[]{:S(2)}) collective-permute-start(bf16[4,2,96,384]{3,2,1,0:T(8,128)(2,1)S(1)} %get-tuple-element.254), channel_id=1, source_target_pairs={{0,4},{1,5},{2,6},{3,7},{4,0},{5,1},{6,2},{7,3},{8,12},{9,13},{10,... | collective-permute-start | bytes 1769480 | tf_op jit(solution)/shard_map/ppermute | solution.py:51
  455.4 42.1 %collective-permute-start.47 = (bf16[4,2,2,96,384]{4,3,2,1,0:T(8,128)(2,1)S(1)}, bf16[4,2,2,96,384]{4,3,2,1,0:T(8,128)(2,1)S(1)}, u32[]{:S(2)}, u32[]{:S(2)}) collective-permute-start(bf16[4,2,2,96,384]{4,3,2,1,0:T(8,128)(2,1)S(1)} %get-tuple-element.264.refs_5_), channel_id=1, source_target_pairs={{0,16},{1,9},{2,18},{3,11},{4,20},{5,13},{6,22},{7,15},{8,24},{9,1... | collective-permute-start | bytes 3538952 | tf_op jit(solution)/shard_map/ppermute | solution.py:51
  455.9 37.1 %collective-permute-start.44 = (bf16[4,2,96,384]{3,2,1,0:T(8,128)(2,1)S(1)}, bf16[4,2,96,384]{3,2,1,0:T(8,128)(2,1)S(1)}, u32[]{:S(2)}, u32[]{:S(2)}) collective-permute-start(bf16[4,2,96,384]{3,2,1,0:T(8,128)(2,1)S(1)} %get-tuple-element.255), channel_id=1, source_target_pairs={{0,6},{1,7},{2,4},{3,5},{4,2},{5,3},{6,0},{7,1},{8,14},{9,15},{10,... | collective-permute-start | bytes 1769480 | tf_op jit(solution)/shard_map/ppermute | solution.py:51
  494.0 16.3 %collective-permute-start.52 = (bf16[4,2,96,384]{3,2,1,0:T(8,128)(2,1)S(1)}, bf16[4,2,96,384]{3,2,1,0:T(8,128)(2,1)S(1)}, u32[]{:S(2)}, u32[]{:S(2)}) collective-permute-start(bf16[4,2,96,384]{3,2,1,0:T(8,128)(2,1)S(1)} %get-tuple-element.273.refs_1_), channel_id=1, source_target_pairs={{0,16},{1,9},{2,18},{3,11},{4,20},{5,13},{6,22},{7,15},{8,24},{9,1... | collective-permute-start | bytes 1769480 | tf_op jit(solution)/shard_map/ppermute | solution.py:51
  511.0 19.4 %collective-permute-start.53 = (bf16[2,4,2,96,384]{4,3,2,1,0:T(8,128)(2,1)S(1)}, bf16[2,4,2,96,384]{4,3,2,1,0:T(8,128)(2,1)S(1)}, u32[]{:S(2)}, u32[]{:S(2)}) collective-permute-start(bf16[2,4,2,96,384]{4,3,2,1,0:T(8,128)(2,1)S(1)} %get-tuple-element.274.refs_1_), channel_id=1, source_target_pairs={{0,8},{1,17},{2,10},{3,19},{4,12},{5,21},{6,14},{7,23},{8,0},{9,25... | collective-permute-start | bytes 3538952 | tf_op jit(solution)/shard_map/ppermute | solution.py:51
  512.6 21.5 %collective-permute-start.54 = (bf16[4,2,2,96,384]{4,3,2,1,0:T(8,128)(2,1)S(1)}, bf16[4,2,2,96,384]{4,3,2,1,0:T(8,128)(2,1)S(1)}, u32[]{:S(2)}, u32[]{:S(2)}) collective-permute-start(bf16[4,2,2,96,384]{4,3,2,1,0:T(8,128)(2,1)S(1)} %get-tuple-element.268.refs_3_), channel_id=1, source_target_pairs={{0,16},{1,9},{2,18},{3,11},{4,20},{5,13},{6,22},{7,15},{8,24},{9,1... | collective-permute-start | bytes 3538952 | tf_op jit(solution)/shard_map/ppermute | solution.py:51
  514.2 17.3 %collective-permute-start.49 = (bf16[2,2,96,384]{3,2,1,0:T(8,128)(2,1)S(1)}, bf16[2,2,96,384]{3,2,1,0:T(8,128)(2,1)S(1)}, u32[]{:S(2)}, u32[]{:S(2)}) collective-permute-start(bf16[2,2,96,384]{3,2,1,0:T(8,128)(2,1)S(1)} %get-tuple-element.270), channel_id=1, source_target_pairs={{0,2},{1,3},{2,0},{3,1},{4,6},{5,7},{6,4},{7,5},{8,10},{9,11},{10,... | collective-permute-start | bytes 884744 | tf_op jit(solution)/shard_map/ppermute | solution.py:51
  518.5 14.1 %collective-permute-start.50 = (bf16[2,2,96,384]{3,2,1,0:T(8,128)(2,1)S(1)}, bf16[2,2,96,384]{3,2,1,0:T(8,128)(2,1)S(1)}, u32[]{:S(2)}, u32[]{:S(2)}) collective-permute-start(bf16[2,2,96,384]{3,2,1,0:T(8,128)(2,1)S(1)} %get-tuple-element.271), channel_id=1, source_target_pairs={{0,4},{1,5},{2,6},{3,7},{4,0},{5,1},{6,2},{7,3},{8,12},{9,13},{10,... | collective-permute-start | bytes 884744 | tf_op jit(solution)/shard_map/ppermute | solution.py:51
  519.3 13.4 %collective-permute-start.51 = (bf16[2,2,96,384]{3,2,1,0:T(8,128)(2,1)S(1)}, bf16[2,2,96,384]{3,2,1,0:T(8,128)(2,1)S(1)}, u32[]{:S(2)}, u32[]{:S(2)}) collective-permute-start(bf16[2,2,96,384]{3,2,1,0:T(8,128)(2,1)S(1)} %get-tuple-element.272), channel_id=1, source_target_pairs={{0,6},{1,7},{2,4},{3,5},{4,2},{5,3},{6,0},{7,1},{8,14},{9,15},{10,... | collective-permute-start | bytes 884744 | tf_op jit(solution)/shard_map/ppermute | solution.py:51
  544.2 13.6 %collective-permute-start.55 = (bf16[2,2,96,384]{3,2,1,0:T(8,128)(2,1)S(1)}, bf16[2,2,96,384]{3,2,1,0:T(8,128)(2,1)S(1)}, u32[]{:S(2)}, u32[]{:S(2)}) collective-permute-start(bf16[2,2,96,384]{3,2,1,0:T(8,128)(2,1)S(1)} %get-tuple-element.280), channel_id=1, source_target_pairs={{0,2},{1,3},{2,0},{3,1},{4,6},{5,7},{6,4},{7,5},{8,10},{9,11},{10,... | collective-permute-start | bytes 884744 | tf_op jit(solution)/shard_map/ppermute | solution.py:51
  549.9 14.0 %collective-permute-start.56 = (bf16[2,2,96,384]{3,2,1,0:T(8,128)(2,1)S(1)}, bf16[2,2,96,384]{3,2,1,0:T(8,128)(2,1)S(1)}, u32[]{:S(2)}, u32[]{:S(2)}) collective-permute-start(bf16[2,2,96,384]{3,2,1,0:T(8,128)(2,1)S(1)} %get-tuple-element.281), channel_id=1, source_target_pairs={{0,4},{1,5},{2,6},{3,7},{4,0},{5,1},{6,2},{7,3},{8,12},{9,13},{10,... | collective-permute-start | bytes 884744 | tf_op jit(solution)/shard_map/ppermute | solution.py:51
  551.2 12.7 %collective-permute-start.57 = (bf16[2,2,96,384]{3,2,1,0:T(8,128)(2,1)S(1)}, bf16[2,2,96,384]{3,2,1,0:T(8,128)(2,1)S(1)}, u32[]{:S(2)}, u32[]{:S(2)}) collective-permute-start(bf16[2,2,96,384]{3,2,1,0:T(8,128)(2,1)S(1)} %get-tuple-element.282), channel_id=1, source_target_pairs={{0,6},{1,7},{2,4},{3,5},{4,2},{5,3},{6,0},{7,1},{8,14},{9,15},{10,... | collective-permute-start | bytes 884744 | tf_op jit(solution)/shard_map/ppermute | solution.py:51
  552.7 63.5 %collective-permute-start.68 = (bf16[4,4,2,96,384]{4,3,2,1,0:T(8,128)(2,1)S(1)}, bf16[4,4,2,96,384]{4,3,2,1,0:T(8,128)(2,1)}, u32[]{:S(2)}, u32[]{:S(2)}) collective-permute-start(bf16[4,4,2,96,384]{4,3,2,1,0:T(8,128)(2,1)S(1)} %get-tuple-element.292.refs_7_), channel_id=1, source_target_pairs={{0,1},{1,0},{2,3},{3,2},{4,5},{5,4},{6,7},{7,6},{8,9},{9,8},{10,11... | collective-permute-start | bytes 7077896 | tf_op jit(solution)/shard_map/ppermute | solution.py:51
  575.9 40.2 %collective-permute-start.69 = (bf16[4,2,2,96,384]{4,3,2,1,0:T(8,128)(2,1)}, bf16[4,2,2,96,384]{4,3,2,1,0:T(8,128)(2,1)}, u32[]{:S(2)}, u32[]{:S(2)}) collective-permute-start(bf16[4,2,2,96,384]{4,3,2,1,0:T(8,128)(2,1)} %get-tuple-element.299.refs_5_), channel_id=1, source_target_pairs={{0,1},{1,0},{2,3},{3,2},{4,5},{5,4},{6,7},{7,6},{8,9},{9,8},{10,11... | collective-permute-start | bytes 3538952 | tf_op jit(solution)/shard_map/ppermute | solution.py:51
  586.6 49.3 %collective-permute-start.67 = (bf16[4,2,2,96,384]{4,3,2,1,0:T(8,128)(2,1)S(1)}, bf16[4,2,2,96,384]{4,3,2,1,0:T(8,128)(2,1)}, u32[]{:S(2)}, u32[]{:S(2)}) collective-permute-start(bf16[4,2,2,96,384]{4,3,2,1,0:T(8,128)(2,1)S(1)} %get-tuple-element.291.refs_5_), channel_id=1, source_target_pairs={{0,1},{1,0},{2,3},{3,2},{4,5},{5,4},{6,7},{7,6},{8,9},{9,8},{10,11... | collective-permute-start | bytes 3538952 | tf_op jit(solution)/shard_map/ppermute | solution.py:51
  (124 other events, 979.6 us)

commit v4 on v3

--- a/solution.py
+++ b/solution.py
@@ -40,6 +40,7 @@
 FLIP_CORE = pairs_of(lambda y, x, z, c: (y, x, z, 1 - c))
 FLIP_X = pairs_of(lambda y, x, z, c: (y, 1 - x, z, c))
 FLIP_Y = pairs_of(lambda y, x, z, c: (1 - y, x, z, c))
+FLIP_XY = pairs_of(lambda y, x, z, c: (1 - y, 1 - x, z, c))
 FLIP_FIRST = pairs_of(lambda y, x, z, c: (y, 1 - x, z, c) if c == 0 else (1 - y, x, z, c))
 FLIP_SECOND = pairs_of(lambda y, x, z, c: (1 - y, x, z, c) if c == 0 else (y, 1 - x, z, c))
 Z_ONE = pairs_of(lambda y, x, z, c: (y, x, z ^ 1, c))
@@ -62,6 +63,34 @@
 
 def by_neighbours():
     return lax.axis_size("rep") == 4 and lax.axis_size("fsdp") == 8
+
+
+KERNEL_TIMES = {
+    "own_chunks": 1,
+    "stack_chips": 1.5,
+    "stack_two": 2,
+    "relay": 1,
+    "pack": 2.5,
+    "norm_columns": 1,
+    "assemble_attend": 3,
+    "assemble_gate_up": 6,
+    "assemble_down": 5,
+    "attend_forward": 7.5,
+    "gate_forward": 7,
+    "down_forward": 4,
+    "feed_backward": 13,
+    "attend_backward": 8,
+    "grad_gate_up": 9,
+    "grad_down": 5,
+    "grad_attend": 6,
+    "add_halves": 4,
+    "add_chips": 2.5,
+    "add_last": 2,
+    "pack_replicas": 2,
+    "adam_all": 30,
+}
+TIME_SCALE = 10.0
+VMEM_MIB = {"adam_all": 58}
 
 
 def run(
@@ -83,8 +112,10 @@
             scratch_shapes=list(scratch),
         ),
         input_output_aliases={1 + at: out for at, out in (reuse or {}).items()},
-        compiler_params=pltpu.CompilerParams(vmem_limit_bytes=40 * 2**20),
-        cost_estimate=pl.CostEstimate(flops=1000, bytes_accessed=1000, transcendentals=0),
+        compiler_params=pltpu.CompilerParams(vmem_limit_bytes=VMEM_MIB.get(name, 40) * 2**20),
+        cost_estimate=pl.CostEstimate(
+            flops=int(KERNEL_TIMES[name] * TIME_SCALE * 1e9), bytes_accessed=1000, transcendentals=0
+        ),
         name=name,
     )(where, *args, *after)
 
@@ -505,6 +536,25 @@
     return run(kernel, "stack_chips", where, arrived, fulls(arrived), outs, specs, after=after)
 
 
+def relay(values, where, after=()):
+    def kernel(where, x, out, token, sem):
+        copy = pltpu.make_async_copy(x, out, sem)
+        copy.start()
+        copy.wait()
+
+    return run(
+        kernel,
+        "relay",
+        where,
+        (values,),
+        [pl.BlockSpec(memory_space=pl.ANY)],
+        [(values.shape, low_type), ((8, 128), low_type)],
+        [full(values.shape), full((8, 128))],
+        scratch=[pltpu.SemaphoreType.DMA],
+        after=after,
+    )
+
+
 def stack_two(one, two, where, after=()):
     def kernel(where, one, two, out, token, sem):
         copies = [
@@ -943,75 +993,100 @@
     gradient = gradient * factor
     first_moment = beta_first * first_moment + (1.0 - beta_first) * gradient
     second_moment = beta_second * second_moment + (1.0 - beta_second) * gradient * gradient
-    first_hat = first_moment / (1.0 - beta_first**STEP)
-    second_hat = second_moment / (1.0 - beta_second**STEP)
+    first_hat = first_moment * (1.0 / (1.0 - beta_first**STEP))
+    second_hat = second_moment * (1.0 / (1.0 - beta_second**STEP))
     weight = weight - step_rate * (
         first_hat / (jnp.sqrt(second_hat) + adam_eps) + decay_rate * weight
     )
     return (weight, first_moment, second_moment)
 
 
-def adam_blocks(weight, first_moment, second_moment, layers, factor, kind, where):
-    layer_count, rows_all, width = weight.shape
-    rows = layers[0][0][0].shape[-2]
-    blocks = (rows_all // rows) * (width // D)
-    by_rows = rows_all // rows
-    pieces = [piece for layer, _ in layers for piece in layer]
-
-    def kernel(where, factor_ref, w, m, v, *refs):
-        piece_refs, outs = refs[: len(pieces)], refs[len(pieces) :]
-        layer = pl.program_id(0)
-        block = pl.program_id(1)
-        c, first, second = where[1], where[2], where[3]
-        if kind == "gate_up":
-            quarter, index = block % 4, block // 4
-        elif kind == "out":
-            quarter, index = 3, 0
-        else:
-            quarter, index = block, 0
-        high, low = quarter // 2, quarter % 2
-        for at in range(layer_count):
-            own, swapped = piece_refs[2 * at : 2 * at + 2]
-            start = layers[at][1]
-
-            @pl.when(layer == at)
+def adam_all(states, pieces, factor, where):
+    layer_count = len(pieces)
+    rows = states[0][0].shape[1]
+    sizes = [state[0].shape[1] * state[0].shape[2] // (rows * D) for state in states]
+    spans = []
+    begin = 0
+    for kind, size in enumerate(sizes):
+        spans.append((kind, begin, size))
+        begin += size
+
+    def quarter_of(kind, block):
+        return ((block, 0), (3, 0), (block % 4, block // 4), (block, 0))[kind]
+
+    def kernel(where, factor_ref, *refs):
+        step = pl.program_id(0)
+        in_refs, piece_refs = refs[: 3 * len(states)], refs[3 * len(states) : -3 * len(states)]
+        out_refs = refs[-3 * len(states) :]
+        for kind, start, size in spans:
+
+            @pl.when((step >= start) & (step < start + size))
             def _():
-                mine = own[2 * (first ^ high) + (second ^ low), start + index, c]
-                theirs = swapped[2 * (second ^ high) + (first ^ low), start + index, c]
-                mine, theirs = mine.astype(wide_type), theirs.astype(wide_type)
-                for half in range(2):
-                    columns = slice(half * HALF, (half + 1) * HALF)
-                    results = adam_step(
-                        w[0, :, columns],
-                        m[0, :, columns],
-                        v[0, :, columns],
-                        jnp.where(c == half, mine, theirs),
-                        factor_ref[0],
-                        rate_matrix,
-                        decay_matrix,
-                    )
-                    for out, result in zip(outs, results):
-                        out[0, :, columns] = result
-
-    def at(layer, block, where):
-        return (layer, block, 0) if by_rows > 1 else (layer, 0, block)
-
-    state = pl.BlockSpec((1, rows, D), at)
+                w, m, v = in_refs[3 * kind : 3 * kind + 3]
+                outs = out_refs[3 * kind : 3 * kind + 3]
+                for layer in range(layer_count):
+                    first = 2 * (kind * layer_count + layer)
+                    mine, theirs = (ref[0, 0, 0] for ref in piece_refs[first : first + 2])
+                    mine, theirs = mine.astype(wide_type), theirs.astype(wide_type)
+                    for half in range(2):
+                        columns = slice(half * HALF, (half + 1) * HALF)
+                        results = adam_step(
+                            w[layer, :, columns],
+                            m[layer, :, columns],
+                            v[layer, :, columns],
+                            jnp.where(where[1] == half, mine, theirs),
+                            factor_ref[0],
+                            rate_matrix,
+                            decay_matrix,
+                        )
+                        for out, result in zip(outs, results):
+                            out[layer, :, columns] = result
+
+    def state_spec(kind):
+        _, first, size = spans[kind]
+
+        def at(step, where):
+            block = jnp.clip(step - first, 0, size - 1)
+            return (0, block, 0) if kind == 3 else (0, 0, block)
+
+        return pl.BlockSpec((layer_count, rows, D), at)
+
+    def piece_spec(kind, start, size, place_at, side):
+        def at(step, where):
+            block = jnp.clip(step - start, 0, size - 1)
+            quarter, index = quarter_of(kind, block)
+            high, low = quarter // 2, quarter % 2
+            first, second = where[2], where[3]
+            if side == 1:
+                first, second = second, first
+            return (2 * (first ^ high) + (second ^ low), place_at + index, where[1], 0, 0)
+
+        return pl.BlockSpec((1, 1, 1, rows, HALF), at)
+
+    state_specs = [state_spec(kind) for kind in range(len(states)) for _ in range(3)]
+    piece_list, piece_specs = [], []
+    for kind, start, size in spans:
+        for layer in range(layer_count):
+            found, place_at = pieces[layer][kind]
+            for side in range(2):
+                piece_list.append(found[side])
+                piece_specs.append(piece_spec(kind, start, size, place_at, side))
     return run(
         kernel,
-        "adam_" + kind,
+        "adam_all",
         where,
-        (factor.reshape(1), weight, first_moment, second_moment, *pieces),
-        [pl.BlockSpec(memory_space=pltpu.SMEM)] + [state] * 3 + fulls(pieces),
-        [(weight.shape, wide_type)] * 3,
-        [state] * 3,
-        grid=(layer_count, blocks),
+        (factor.reshape(1), *(array for state in states for array in state), *piece_list),
+        [pl.BlockSpec(memory_space=pltpu.SMEM)] + state_specs + piece_specs,
+        [(array.shape, wide_type) for state in states for array in state],
+        state_specs,
+        grid=(begin,),
     )
 
 
 def sum_all(value):
-    for pairs in (FLIP_CORE, FLIP_X, FLIP_Y, Z_ONE, Z_TWO):
-        value = value + send(value, pairs)
+    value = value + send(value, FLIP_CORE)
+    for one, two, three in ((FLIP_X, FLIP_Y, FLIP_XY), (Z_ONE, Z_TWO, Z_THREE)):
+        value = (value + send(value, one)) + (send(value, two) + send(value, three))
     return value
 
 
@@ -1073,8 +1148,6 @@
 
     def lay_out(at):
         begin = 0
-        if at == 0:
-            norms[:] = chain(norm_columns, *norms, norm_params)
         for (kind, layer), own in zip(groups[at], owns[at]):
             weights[kind, layer] = chain(assemble, (own, six[at], far[at], other[at]), kind, begin)
             weight_list[layer] += tuple(weights[kind, layer])
@@ -1100,6 +1173,7 @@
     start(0)
     spread(0)
     start(1)
+    norms[:] = chain(norm_columns, *norms, norm_params)
     spread_on(0)
     for at in range(len(groups)):
         if at < last:
@@ -1107,9 +1181,9 @@
         if at + 2 <= last:
             start(at + 2)
         swap(at)
-        lay_out(at)
         if at < last:
             spread_on(at + 1)
+        lay_out(at)
         hidden = compute(at, hidden)
     return (hidden, weight_list, kept_list, norms[0])
 
@@ -1146,6 +1220,7 @@
     norm_list = [None] * layer_count
     pieces = [[None] * 4 for _ in range(layer_count)]
     squares = []
+    swapped = []
     sums = [{} for _ in range(layer_count)]
 
     def feed(layer, grad):
@@ -1204,30 +1279,30 @@
         away, left = chain(add_halves, *sums[layer][name])
         sums[layer][name] = (left, send(away, FLIP_SECOND))
 
-    def chips(layer, names):
-        own, *parts = chain(add_chips, [sums[layer][name] for name in names])
+    def chips(layer, name):
+        own, *parts = chain(add_chips, [sums[layer][name]])
         moves = (Z_ONE, Z_TWO, Z_THREE)
         return [own] + [send(part, move) for part, move in zip(parts, moves)]
 
-    def share(parts):
-        total, part = chain(add_last, parts)
+    def total(parts):
+        whole, part = chain(add_last, parts)
         squares.append(part)
-        return (total, send(total, FLIP_SECOND))
+        return whole
+
+    def share(whole):
+        ready, _ = chain(relay, whole)
+        return (whole, send(ready, FLIP_SECOND))
 
     def share_on(found):
         row, _ = chain(stack_two, *found)
         return (row, send(row, FLIP_FIRST))
 
-    def swap(layer, names, found):
+    def swap(layer, name, found):
         mine, _ = chain(pack_replicas, *found)
         found = (mine, send(mine, FLIP_CORE))
-        order = {"wide": (("gate_up", (2,)),), "rest": (("down", (3,)), ("attend", (0, 1)))}
-        start = 0
-        for name in names:
-            for kind, indices in order[name]:
-                for index in indices:
-                    pieces[layer][index] = (found, start)
-                start += BLOCKS[kind]
+        swapped.append(found[1])
+        for kind, at in ((2, 0),) if name == "wide" else ((3, 0), (0, 1), (1, 1)):
+            pieces[layer][kind] = (found, at)
 
     for kept in kept_list:
         for name in ("trio", "product"):
@@ -1235,32 +1310,45 @@
     made = feed(layer_count - 1, grad)
     for kept in kept_list:
         chain.wait(kept["trio_other"], kept["product_other"])
-    for layer in reversed(range(layer_count)):
-        product_wide(layer, made)
-        if layer < layer_count - 1:
-            halves(layer + 1, "rest")
-        grad = attention(layer, made)
-        if layer > 0:
-            product_rest(layer, made)
-            made = feed(layer - 1, grad)
-            halves(layer, "wide")
-    both = ("wide", "rest")
-    earlier = layer_count - 1
-    parts = chips(earlier, both)
-    product_rest(0, made)
-    halves(0, "wide")
-    found = share(parts)
-    halves(0, "rest")
-    parts = chips(0, ("wide",))
-    found = share_on(found)
-    swap(earlier, both, found)
-    found = share(parts)
-    parts = chips(0, ("rest",))
-    found = share_on(found)
-    swap(0, ("wide",), found)
-    found = share(parts)
-    found = share_on(found)
-    swap(0, ("rest",), found)
+    def settle():
+        chain.wait(*swapped)
+        swapped.clear()
+
+    layer = layer_count - 1
+    grad = attention(layer, made)
+    product_wide(layer, made)
+    product_rest(layer, made)
+    while layer > 0:
+        made = feed(layer - 1, grad)
+        halves(layer, "wide")
+        product_wide(layer - 1, made)
+        parts = chips(layer, "wide")
+        halves(layer, "rest")
+        wide = total(parts)
+        grad = attention(layer - 1, made)
+        product_rest(layer - 1, made)
+        parts = chips(layer, "rest")
+        halves(layer - 1, "wide")
+        rest = total(parts)
+        halves(layer - 1, "rest")
+        layer -= 1
+        parts = chips(layer, "wide")
+        shared = share(wide)
+        shared_rest = share(rest)
+        shared = share_on(shared)
+        wide = total(parts)
+        parts = chips(layer, "rest")
+        shared_rest = share_on(shared_rest)
+        shared_wide = share(wide)
+        swap(layer + 1, "wide", shared)
+        swap(layer + 1, "rest", shared_rest)
+        shared_wide = share_on(shared_wide)
+        rest = total(parts)
+        shared_rest = share(rest)
+        settle()
+        swap(layer, "wide", shared_wide)
+        shared_rest = share_on(shared_rest)
+        swap(layer, "rest", shared_rest)
     return (grad, norm_list, pieces, sum(squares))
 
 
@@ -1335,13 +1423,11 @@
         norm_grads = lax.psum(jnp.concatenate(norm_list), both_axes)
     grad_norm = jnp.sqrt(total + jnp.sum(norm_grads * norm_grads))
     factor = clip_norm / jnp.maximum(grad_norm, clip_norm)
-    updated = []
-    for kind, state in enumerate(states):
-        if by_neighbours():
-            name = ("qkv", "out", "gate_up", "down")[kind]
-            layers = [layer[kind] for layer in pieces]
-            updated += adam_blocks(*state, layers, factor, name, where)
-        else:
+    if by_neighbours():
+        updated = list(adam_all(states, pieces, factor, where))
+    else:
+        updated = []
+        for kind, state in enumerate(states):
             gradient = jnp.stack([layer[kind] for layer in sums])
             updated += adam_step(*state, gradient, factor, rate_matrix, decay_matrix)
     width = norm_params.shape[2]

time: 660 us -> 555 us (0.84)
  waiting for transfers between devices: 248 us -> 146 us
  local copies, waits for them, and re-layouts: 70.7 us -> 34.5 us
  starting transfers between devices: 91.2 us -> 119 us
    ppermute x70 -> x78, waiting for transfers between devices: 248 us -> 146 us  [send(): return lax.ppermute(values, both_axes, pairs)]
    unnamed x206 -> x188, local copies, waits for them, and re-layouts: 69.3 us -> 34.5 us
    ppermute x70 -> x78, starting transfers between devices: 91.2 us -> 119 us  [send(): return lax.ppermute(values, both_axes, pairs)]
    pallas_call x63 -> x68, Pallas kernels: 233 us -> 237 us  [run(): pl.pallas_call(body_of, out_shape=[jax.ShapeDtypeStruct(shape, dtype) for...]
  transfers between devices with their start and end apart: 70 -> 78, of which waited for: 34 -> 28; matrix products, arithmetic and copies ran while one was open for 2% -> 1% of each run, Pallas kernels for 24% -> 36%
where the time goes in v4:
time: 555 us; the launch traced here: 546 us
  Pallas kernels  237 us (43%)
  waiting for transfers between devices  146 us (26%)
  starting transfers between devices  119 us (21%)
  local copies, waits for them, and re-layouts  34.5 us (6%)
    pallas_call x68, Pallas kernels, run(): pl.pallas_call(body_of, out_shape=[jax.ShapeDtypeStruct(shape, dtype) for...  237 us
    ppermute x78, waiting for transfers between devices, send(): return lax.ppermute(values, both_axes, pairs)  146 us
    ppermute x78, starting transfers between devices, send(): return lax.ppermute(values, both_axes, pairs)  119 us
    unnamed x188, local copies, waits for them, and re-layouts  34.5 us
  transfers between devices with their start and end apart: 78, of which 28 were waited for; matrix products, arithmetic and copies ran while one was open for 1% of the time, Pallas kernels for 36%

profile of v4, /device:TPU:0, one launch (start us, length us, event | category | flops | bytes accessed | tf_op | source)
XLA Modules:
  0.0 545.6 jit_solution(17772463708602671145)
XLA Ops:
  10.3 4.5 collective-permute-done.refs_1_
  14.8 8.5 %collective-permute-done.1.refs_2_ = bf16[1,112,768]{2,1,0:T(8,128)(2,1)S(1)} collective-permute-done((bf16[1,112,768]{2,1,0:T(8,128)(2,1)S(1)}, bf16[1,112,768]{2,1,0:T(8,128)(2,1)S(1)}, u32[]{:S(2)}, u32[]{:S(2)}) %collective-permute-start.1) | collective-permute-done | bytes 172064 | tf_op jit(solution)/shard_map/ppermute | solution.py:52
  33.2 6.1 %collective-permute-done.3.refs_2_ = bf16[3,1,96,768]{3,2,1,0:T(8,128)(2,1)S(1)} collective-permute-done((bf16[3,1,96,768]{3,2,1,0:T(8,128)(2,1)S(1)}, bf16[3,1,96,768]{3,2,1,0:T(8,128)(2,1)S(1)}, u32[]{:S(2)}, u32[]{:S(2)}) %collective-permute-start.3) | collective-permute-done | bytes 442400 | tf_op jit(solution)/shard_map/ppermute | solution.py:52
  42.1 9.9 %collective-permute-done.7.refs_2_ = bf16[2,96,768]{2,1,0:T(8,128)(2,1)S(1)} collective-permute-done((bf16[2,96,768]{2,1,0:T(8,128)(2,1)S(1)}, bf16[2,96,768]{2,1,0:T(8,128)(2,1)S(1)}, u32[]{:S(2)}, u32[]{:S(2)}) %collective-permute-start.7) | collective-permute-done | bytes 294944 | tf_op jit(solution)/shard_map/ppermute | solution.py:52
  57.0 6.2 %collective-permute-start.12 = (bf16[2,96,768]{2,1,0:T(8,128)(2,1)S(1)}, bf16[2,96,768]{2,1,0:T(8,128)(2,1)S(1)}, u32[]{:S(2)}, u32[]{:S(2)}) collective-permute-start(bf16[2,96,768]{2,1,0:T(8,128)(2,1)S(1)} %get-tuple-element.188.refs_4_), channel_id=1, source_target_pairs={{0,2},{1,3},{2,0},{3,1},{4,6},{5,7},{6,4},{7,5},{8,10},{9,11},{10,... | collective-permute-start | bytes 884744 | tf_op jit(solution)/shard_map/ppermute | solution.py:52
  77.0 7.8 %attend_forward.2 = (bf16[3,256,768]{2,1,0:T(8,128)(2,1)}, bf16[256,2304]{1,0:T(8,128)(2,1)S(1)}, f32[256,128]{1,0:T(8,128)S(1)}, f32[256,768]{1,0:T(8,128)S(1)}, f32[256,768]{1,0:T(8,128)S(1)}) custom-call(s32[4]{0:T(128)S(1)} %pad_add_fusion.refs_0_, f32[256,768]{1,0:T(8,128)S(1)} %convert_select_fusion.refs_1_, bf16[768,2304]{1,0:T(8,128)(2,1)S(1)} %copy-done.37, ...), custom_call_target="tpu_custom_call" | custom-call | flops 74999996416 | bytes 1000 | tf_op jit(solution)/shard_map/attend_forward/pallas_call | solution.py:104
  92.5 6.1 %collective-permute-start.18 = (bf16[2,96,768]{2,1,0:T(8,128)(2,1)}, bf16[2,96,768]{2,1,0:T(8,128)(2,1)}, u32[]{:S(2)}, u32[]{:S(2)}) collective-permute-start(bf16[2,96,768]{2,1,0:T(8,128)(2,1)} %get-tuple-element.200.refs_4_), channel_id=1, source_target_pairs={{0,2},{1,3},{2,0},{3,1},{4,6},{5,7},{6,4},{7,5},{8,10},{9,11},{10,... | collective-permute-start | bytes 884744 | tf_op jit(solution)/shard_map/ppermute | solution.py:52
  107.7 5.4 assemble_gate_up.2.refs_2_.refs_3_.refs_4_.refs_6_.refs_7_
  113.1 7.6 %gate_forward.2 = (bf16[256,3072]{1,0:T(8,128)(2,1)}, bf16[2,256,3072]{2,1,0:T(8,128)(2,1)S(1)}) custom-call(s32[4]{0:T(128)S(1)} %pad_add_fusion.refs_0_, bf16[3,256,768]{2,1,0:T(8,128)(2,1)} %get-tuple-element.195.refs_1_.refs_3_, bf16[768,6144]{1,0:T(8,128)(2,1)} %assemble_gate_up.2.refs_2_.refs_3_.refs_4_.refs_6_.refs_7_, ...), custom_call_target="tpu_custom_call" | custom-call | flops 70000001024 | bytes 1000 | tf_op jit(solution)/shard_map/gate_forward/pallas_call | solution.py:104
  125.6 3.5 collective-permute-done.17.refs_4_.refs_3_
  133.4 6.1 %collective-permute-start.24 = (bf16[1,96,768]{2,1,0:T(8,128)(2,1)}, bf16[1,96,768]{2,1,0:T(8,128)(2,1)}, u32[]{:S(2)}, u32[]{:S(2)}) collective-permute-start(bf16[1,96,768]{2,1,0:T(8,128)(2,1)} %get-tuple-element.210.refs_5_), channel_id=1, source_target_pairs={{0,2},{1,3},{2,0},{3,1},{4,6},{5,7},{6,4},{7,5},{8,10},{9,11},{10,... | collective-permute-start | bytes 442376 | tf_op jit(solution)/shard_map/ppermute | solution.py:52
  148.6 4.5 assemble_down.2.refs_5_.refs_2_
  162.2 4.7 down_forward.2
  166.9 7.8 %attend_forward.3 = (bf16[3,256,768]{2,1,0:T(8,128)(2,1)}, bf16[256,2304]{1,0:T(8,128)(2,1)S(1)}, f32[256,128]{1,0:T(8,128)S(1)}, f32[256,768]{1,0:T(8,128)S(1)}, f32[256,768]{1,0:T(8,128)S(1)}) custom-call(s32[4]{0:T(128)S(1)} %pad_add_fusion.refs_0_, f32[256,768]{1,0:T(8,128)S(1)} %get-tuple-element.217.refs_1_, bf16[768,2304]{1,0:T(8,128)(2,1)S(1)} %copy-done.34, ...), custom_call_target="tpu_custom_call" | custom-call | flops 74999996416 | bytes 1000 | tf_op jit(solution)/shard_map/attend_forward/pallas_call | solution.py:104
  181.0 6.8 %collective-permute-done.28.refs_2_ = bf16[3,1,96,768]{3,2,1,0:T(8,128)(2,1)S(1)} collective-permute-done((bf16[3,1,96,768]{3,2,1,0:T(8,128)(2,1)S(1)}, bf16[3,1,96,768]{3,2,1,0:T(8,128)(2,1)S(1)}, u32[]{:S(2)}, u32[]{:S(2)}) %collective-permute-start.28) | collective-permute-done | bytes 442400 | tf_op jit(solution)/shard_map/ppermute | solution.py:52
  189.8 6.3 %assemble_gate_up.3.refs_2_.refs_3_.refs_4_.refs_6_.refs_7_ = bf16[768,6144]{1,0:T(8,128)(2,1)} custom-call(s32[4]{0:T(128)S(1)} %pad_add_fusion.refs_0_, bf16[4,2,96,768]{3,2,1,0:T(8,128)(2,1)S(1)} %get-tuple-element.221.refs_1_, bf16[2,3,2,96,768]{4,3,2,1,0:T(8,128)(2,1)} %get-tuple-element.222.refs_2_, ...), custom_call_target="tpu_custom_call" | custom-call | flops 60000002048 | bytes 1000 | tf_op jit(solution)/shard_map/assemble_gate_up/pallas_call | solution.py:104
  196.1 7.6 %gate_forward.3 = (bf16[256,3072]{1,0:T(8,128)(2,1)}, bf16[2,256,3072]{2,1,0:T(8,128)(2,1)S(1)}) custom-call(s32[4]{0:T(128)S(1)} %pad_add_fusion.refs_0_, bf16[3,256,768]{2,1,0:T(8,128)(2,1)} %get-tuple-element.220.refs_1_.refs_3_, bf16[768,6144]{1,0:T(8,128)(2,1)} %assemble_gate_up.3.refs_2_.refs_3_.refs_4_.refs_6_.refs_7_, ...), custom_call_target="tpu_custom_call" | custom-call | flops 70000001024 | bytes 1000 | tf_op jit(solution)/shard_map/gate_forward/pallas_call | solution.py:104
  206.7 4.1 collective-permute-done.30.refs_4_
  210.8 6.7 %assemble_down.3.refs_2_.refs_5_ = bf16[3072,768]{1,0:T(8,128)(2,1)S(1)} custom-call(s32[4]{0:T(128)S(1)} %pad_add_fusion.refs_0_, bf16[4,1,96,768]{3,2,1,0:T(8,128)(2,1)S(1)} %get-tuple-element.230.refs_1_, bf16[2,3,1,96,768]{4,3,2,1,0:T(8,128)(2,1)S(1)} %get-tuple-element.231.refs_2_, bf16[2,3,1,96,768]{4,3,2,1,0:T(8,128)(2,1)S(1)} %collective-permute-done.29.refs_3_, ...), custom_call_target="tpu_custom_call" | custom-call | flops 49999998976 | bytes 1000 | tf_op jit(solution)/shard_map/assemble_down/pallas_call | solution.py:104
  217.6 6.1 %down_forward.3 = (f32[256,768]{1,0:T(8,128)S(1)}, f32[256,768]{1,0:T(8,128)S(1)}) custom-call(s32[4]{0:T(128)S(1)} %pad_add_fusion.refs_0_, bf16[256,3072]{1,0:T(8,128)(2,1)} %get-tuple-element.229.refs_4_.refs_1_, bf16[3072,768]{1,0:T(8,128)(2,1)S(1)} %assemble_down.3.refs_2_.refs_5_, f32[256,768]{1,0:T(8,128)S(1)} %get-tuple-element.234.refs_3_, ...), custom_call_target="tpu_custom_call" | custom-call | flops 40000000000 | bytes 1000 | tf_op jit(solution)/shard_map/down_forward/pallas_call | solution.py:104
  223.8 12.7 %feed_backward.2 = (bf16[2,256,3072]{2,1,0:T(8,128)(2,1)S(1)}, bf16[256,3840]{1,0:T(8,128)(2,1)S(1)}, bf16[256,768]{1,0:T(8,128)(2,1)S(1)}, f32[256,768]{1,0:T(8...) custom-call(s32[4]{0:T(128)S(1)} %pad_add_fusion.refs_0_, ...), custom_call_target="tpu_custom_call" | custom-call | flops 130000003072 | bytes 1000 | tf_op jit(solution)/shard_map/feed_backward/pallas_call | solution.py:104
  240.3 7.3 %attend_backward.2 = (bf16[256,2304]{1,0:T(8,128)(2,1)S(1)}, bf16[256,1152]{1,0:T(8,128)(2,1)S(1)}, f32[256,768]{1,0:T(8,128)S(1)}) custom-call(s32[4]{0:T(128)S(1)} %pad_add_fusion.refs_0_, bf16[256,768]{1,0:T(8,128)(2,1)S(1)} %get-tuple-element.239.refs_1_, bf16[256,2304]{1,0:T(8,128)(2,1)S(1)} %copy-done.67, f32[256,128]{1,0:T(8,128)S(1)} %copy-done.55, ...), custom_call_target="tpu_custom_call" | custom-call | flops 80000000000 | bytes 1000 | tf_op jit(solution)/shard_map/attend_backward/pallas_call | solution.py:104
  249.9 9.3 %grad_gate_up.2 = (bf16[2,4,2,2,96,384]{5,4,3,2,1,0:T(8,128)(2,1)}, bf16[2,4,2,2,96,384]{5,4,3,2,1,0:T(8,128)(2,1)S(1)}) custom-call(s32[4]{0:T(128)S(1)} %pad_add_fusion.refs_0_, bf16[3,256,768]{2,1,0:T(8,128)(2,1)} %get-tuple-element.220.refs_1_.refs_3_, bf16[3,256,768]{2,1,0:T(8,128)(2,1)} %collective-permute-done.33.refs_9_.refs_2_.refs_4_, ...), custom_call_target="tpu_custom_call" | custom-call | flops 89999998976 | bytes 1000 | tf_op jit(solution)/shard_map/grad_gate_up/pallas_call | solution.py:104
  260.4 5.2 grad_down.2
  267.1 6.5 %grad_attend.2 = (bf16[2,4,2,2,96,384]{5,4,3,2,1,0:T(8,128)(2,1)}, bf16[2,4,2,2,96,384]{5,4,3,2,1,0:T(8,128)(2,1)S(1)}) custom-call(s32[4]{0:T(128)S(1)} %pad_add_fusion.refs_0_, bf16[3,256,768]{2,1,0:T(8,128)(2,1)} %get-tuple-element.220.refs_1_.refs_3_, ...), custom_call_target="tpu_custom_call", output_to_operand_aliasing={{0}: (9, {}), {1}: (10, {})} | custom-call | flops 60000002048 | bytes 1000 | tf_op jit(solution)/shard_map/grad_attend/pallas_call | solution.py:104
  276.9 12.8 %feed_backward.3 = (bf16[2,256,3072]{2,1,0:T(8,128)(2,1)S(1)}, bf16[256,3840]{1,0:T(8,128)(2,1)S(1)}, bf16[256,768]{1,0:T(8,128)(2,1)S(1)}, f32[256,768]{1,0:T(8...) custom-call(s32[4]{0:T(128)S(1)} %pad_add_fusion.refs_0_, ...), custom_call_target="tpu_custom_call" | custom-call | flops 130000003072 | bytes 1000 | tf_op jit(solution)/shard_map/feed_backward/pallas_call | solution.py:104
  298.8 9.3 %grad_gate_up.3 = (bf16[2,4,2,2,96,384]{5,4,3,2,1,0:T(8,128)(2,1)}, bf16[2,4,2,2,96,384]{5,4,3,2,1,0:T(8,128)(2,1)S(1)}) custom-call(s32[4]{0:T(128)S(1)} %pad_add_fusion.refs_0_, bf16[3,256,768]{2,1,0:T(8,128)(2,1)} %get-tuple-element.195.refs_1_.refs_3_, bf16[3,256,768]{2,1,0:T(8,128)(2,1)} %collective-permute-done.31.refs_7_.refs_2_.refs_4_, ...), custom_call_target="tpu_custom_call" | custom-call | flops 89999998976 | bytes 1000 | tf_op jit(solution)/shard_map/grad_gate_up/pallas_call | solution.py:104
  309.6 14.2 %collective-permute-done.38.refs_2_ = bf16[4,2,2,96,384]{4,3,2,1,0:T(8,128)(2,1)S(1)} collective-permute-done((bf16[4,2,2,96,384]{4,3,2,1,0:T(8,128)(2,1)S(1)}, bf16[4,2,2,96,384]{4,3,2,1,0:T(8,128)(2,1)S(1)}, u32[]{:S(2)}, u32[]{:S(2)}) %collective-permute-start.38) | collective-permute-done | bytes 1179680 | tf_op jit(solution)/shard_map/ppermute | solution.py:52
  324.7 5.7 %collective-permute-start.40 = (bf16[2,2,96,384]{3,2,1,0:T(8,128)(2,1)S(1)}, bf16[2,2,96,384]{3,2,1,0:T(8,128)(2,1)S(1)}, u32[]{:S(2)}, u32[]{:S(2)}) collective-permute-start(bf16[2,2,96,384]{3,2,1,0:T(8,128)(2,1)S(1)} %get-tuple-element.267), channel_id=1, source_target_pairs={{0,2},{1,3},{2,0},{3,1},{4,6},{5,7},{6,4},{7,5},{8,10},{9,11},{10,... | collective-permute-start | bytes 884744 | tf_op jit(solution)/shard_map/ppermute | solution.py:52
  332.9 4.6 add_halves.5
  339.3 3.5 collective-permute-done.40.refs_2_
  342.8 11.1 %collective-permute-done.41.refs_3_ = bf16[2,2,96,384]{3,2,1,0:T(8,128)(2,1)S(1)} collective-permute-done((bf16[2,2,96,384]{3,2,1,0:T(8,128)(2,1)S(1)}, bf16[2,2,96,384]{3,2,1,0:T(8,128)(2,1)S(1)}, u32[]{:S(2)}, u32[]{:S(2)}) %collective-permute-start.41) | collective-permute-done | bytes 294944 | tf_op jit(solution)/shard_map/ppermute | solution.py:52
  354.7 7.3 %attend_backward.3 = (bf16[256,2304]{1,0:T(8,128)(2,1)S(1)}, bf16[256,1152]{1,0:T(8,128)(2,1)S(1)}, f32[256,768]{1,0:T(8,128)S(1)}) custom-call(s32[4]{0:T(128)S(1)} %pad_add_fusion.refs_0_, bf16[256,768]{1,0:T(8,128)(2,1)S(1)} %copy-done.79, bf16[256,2304]{1,0:T(8,128)(2,1)S(1)} %copy-done.65, f32[256,128]{1,0:T(8,128)S(1)} %copy-done.53, ...), custom_call_target="tpu_custom_call" | custom-call | flops 80000000000 | bytes 1000 | tf_op jit(solution)/shard_map/attend_backward/pallas_call | solution.py:104
  362.1 5.2 grad_down.3
  368.4 5.7 %grad_attend.3 = (bf16[2,4,2,2,96,384]{5,4,3,2,1,0:T(8,128)(2,1)S(1)}, bf16[2,4,2,2,96,384]{5,4,3,2,1,0:T(8,128)(2,1)S(1)}) custom-call(s32[4]{0:T(128)S(1)} %pad_add_fusion.refs_0_, bf16[3,256,768]{2,1,0:T(8,128)(2,1)} %get-tuple-element.195.refs_1_.refs_3_, ...), custom_call_target="tpu_custom_call", output_to_operand_aliasing={{0}: (9, {}), {1}: (10, {})} | custom-call | flops 60000002048 | bytes 1000 | tf_op jit(solution)/shard_map/grad_attend/pallas_call | solution.py:104
  378.1 5.4 collective-permute-start.46
  391.0 5.6 %collective-permute-done.46.refs_2_ = bf16[2,2,96,384]{3,2,1,0:T(8,128)(2,1)S(1)} collective-permute-done((bf16[2,2,96,384]{3,2,1,0:T(8,128)(2,1)S(1)}, bf16[2,2,96,384]{3,2,1,0:T(8,128)(2,1)S(1)}, u32[]{:S(2)}, u32[]{:S(2)}) %collective-permute-start.46) | collective-permute-done | bytes 294944 | tf_op jit(solution)/shard_map/ppermute | solution.py:52
  396.6 10.3 %collective-permute-done.47.refs_3_ = bf16[2,2,96,384]{3,2,1,0:T(8,128)(2,1)S(1)} collective-permute-done((bf16[2,2,96,384]{3,2,1,0:T(8,128)(2,1)S(1)}, bf16[2,2,96,384]{3,2,1,0:T(8,128)(2,1)S(1)}, u32[]{:S(2)}, u32[]{:S(2)}) %collective-permute-start.47) | collective-permute-done | bytes 294944 | tf_op jit(solution)/shard_map/ppermute | solution.py:52
  407.7 6.5 %collective-permute-done.51.refs_2_ = bf16[2,4,2,2,96,384]{5,4,3,2,1,0:T(8,128)(2,1)S(1)} collective-permute-done((bf16[2,4,2,2,96,384]{5,4,3,2,1,0:T(8,128)(2,1)S(1)}, bf16[2,4,2,2,96,384]{5,4,3,2,1,0:T(8,128)(2,1)S(1)}, u32[]{:S(2)}, u32[]{:S(2)}) %collective-permute-start.51) | collective-permute-done | bytes 2359328 | tf_op jit(solution)/shard_map/ppermute | solution.py:52
  419.9 5.4 collective-permute-start.52
  429.4 7.0 %collective-permute-done.55.refs_2_ = bf16[2,2,96,384]{3,2,1,0:T(8,128)(2,1)S(1)} collective-permute-done((bf16[2,2,96,384]{3,2,1,0:T(8,128)(2,1)S(1)}, bf16[2,2,96,384]{3,2,1,0:T(8,128)(2,1)S(1)}, u32[]{:S(2)}, u32[]{:S(2)}) %collective-permute-start.55) | collective-permute-done | bytes 294944 | tf_op jit(solution)/shard_map/ppermute | solution.py:52
  440.4 8.4 %collective-permute-done.53.refs_3_ = bf16[2,2,96,384]{3,2,1,0:T(8,128)(2,1)S(1)} collective-permute-done((bf16[2,2,96,384]{3,2,1,0:T(8,128)(2,1)S(1)}, bf16[2,2,96,384]{3,2,1,0:T(8,128)(2,1)S(1)}, u32[]{:S(2)}, u32[]{:S(2)}) %collective-permute-start.53) | collective-permute-done | bytes 294944 | tf_op jit(solution)/shard_map/ppermute | solution.py:52
  450.5 5.0 collective-permute-start.57
  462.2 8.6 %collective-permute-done.62.refs_2_ = bf16[2,2,2,96,384]{4,3,2,1,0:T(8,128)(2,1)S(1)} collective-permute-done((bf16[2,2,2,96,384]{4,3,2,1,0:T(8,128)(2,1)S(1)}, bf16[2,2,2,96,384]{4,3,2,1,0:T(8,128)(2,1)S(1)}, u32[]{:S(2)}, u32[]{:S(2)}) %collective-permute-start.62) | collective-permute-done | bytes 589856 | tf_op jit(solution)/shard_map/ppermute | solution.py:52
  473.6 5.4 collective-permute-done.58.refs_3_
  493.8 5.1 collective-permute-done.75.refs_2_
  501.7 5.6 %collective-permute-start.69 = (f32[16,768]{1,0:T(8,128)S(1)}, f32[16,768]{1,0:T(8,128)S(1)}, u32[]{:S(2)}, u32[]{:S(2)}) collective-permute-start(f32[16,768]{1,0:T(8,128)S(1)} %add_add_fusion.1), channel_id=1, source_target_pairs={{0,4},{1,5},{2,6},{3,7},{4,0},{5,1},{6,2},{7,3},{8,12},{9,13},{10,... | collective-permute-start | bytes 147464 | tf_op jit(solution)/shard_map/ppermute | solution.py:52
  516.2 28.1 %adam_all.1 = (f32[2,96,2304]{2,1,0:T(8,128)}, f32[2,96,2304]{2,1,0:T(8,128)}, f32[2,96,2304]{2,1,0:T(8,128)}, f32[2,96,768]{2,1,0:T(8,128)}, f32[2,96,768]{2,1,...) custom-call(s32[4]{0:T(128)} %copy-done.13, ...), custom_call_target="tpu_custom_call" | custom-call | flops 299999985664 | bytes 1000 | tf_op jit(solution)/shard_map/adam_all/pallas_call | solution.py:104
  (385 shorter events, 187.6 us)
Async XLA Ops:
  7.7 15.6 %collective-permute-start.1 = (bf16[1,112,768]{2,1,0:T(8,128)(2,1)S(1)}, bf16[1,112,768]{2,1,0:T(8,128)(2,1)S(1)}, u32[]{:S(2)}, u32[]{:S(2)}) collective-permute-start(bf16[1,112,768]{2,1,0:T(8,128)(2,1)S(1)} %get-tuple-element.181.refs_4_), channel_id=1, source_target_pairs={{0,4},{1,5},{2,6},{3,7},{4,0},{5,1},{6,2},{7,3},{8,12},{9,13},{10,... | collective-permute-start | bytes 516104 | tf_op jit(solution)/shard_map/ppermute | solution.py:52
  25.7 16.4 %collective-permute-start.6 = (bf16[2,96,768]{2,1,0:T(8,128)(2,1)S(1)}, bf16[2,96,768]{2,1,0:T(8,128)(2,1)S(1)}, u32[]{:S(2)}, u32[]{:S(2)}) collective-permute-start(bf16[2,96,768]{2,1,0:T(8,128)(2,1)S(1)} %get-tuple-element.184.refs_4_), channel_id=1, source_target_pairs={{0,2},{1,3},{2,0},{3,1},{4,6},{5,7},{6,4},{7,5},{8,10},{9,11},{10,... | collective-permute-start | bytes 884744 | tf_op jit(solution)/shard_map/ppermute | solution.py:52
  28.5 23.4 %collective-permute-start.7 = (bf16[2,96,768]{2,1,0:T(8,128)(2,1)S(1)}, bf16[2,96,768]{2,1,0:T(8,128)(2,1)S(1)}, u32[]{:S(2)}, u32[]{:S(2)}) collective-permute-start(bf16[2,96,768]{2,1,0:T(8,128)(2,1)S(1)} %get-tuple-element.184.refs_4_), channel_id=1, source_target_pairs={{0,4},{1,5},{2,6},{3,7},{4,0},{5,1},{6,2},{7,3},{8,12},{9,13},{10,... | collective-permute-start | bytes 884744 | tf_op jit(solution)/shard_map/ppermute | solution.py:52
  29.5 22.4 %collective-permute-start.8 = (bf16[2,96,768]{2,1,0:T(8,128)(2,1)S(1)}, bf16[2,96,768]{2,1,0:T(8,128)(2,1)S(1)}, u32[]{:S(2)}, u32[]{:S(2)}) collective-permute-start(bf16[2,96,768]{2,1,0:T(8,128)(2,1)S(1)} %get-tuple-element.184.refs_4_), channel_id=1, source_target_pairs={{0,6},{1,7},{2,4},{3,5},{4,2},{5,3},{6,0},{7,1},{8,14},{9,15},{10,... | collective-permute-start | bytes 884744 | tf_op jit(solution)/shard_map/ppermute | solution.py:52
  57.0 27.8 %collective-permute-start.12 = (bf16[2,96,768]{2,1,0:T(8,128)(2,1)S(1)}, bf16[2,96,768]{2,1,0:T(8,128)(2,1)S(1)}, u32[]{:S(2)}, u32[]{:S(2)}) collective-permute-start(bf16[2,96,768]{2,1,0:T(8,128)(2,1)S(1)} %get-tuple-element.188.refs_4_), channel_id=1, source_target_pairs={{0,2},{1,3},{2,0},{3,1},{4,6},{5,7},{6,4},{7,5},{8,10},{9,11},{10,... | collective-permute-start | bytes 884744 | tf_op jit(solution)/shard_map/ppermute | solution.py:52
  63.2 23.4 %collective-permute-start.13 = (bf16[2,96,768]{2,1,0:T(8,128)(2,1)S(1)}, bf16[2,96,768]{2,1,0:T(8,128)(2,1)S(1)}, u32[]{:S(2)}, u32[]{:S(2)}) collective-permute-start(bf16[2,96,768]{2,1,0:T(8,128)(2,1)S(1)} %get-tuple-element.188.refs_4_), channel_id=1, source_target_pairs={{0,4},{1,5},{2,6},{3,7},{4,0},{5,1},{6,2},{7,3},{8,12},{9,13},{10,... | collective-permute-start | bytes 884744 | tf_op jit(solution)/shard_map/ppermute | solution.py:52
  64.3 22.4 %collective-permute-start.14 = (bf16[2,96,768]{2,1,0:T(8,128)(2,1)S(1)}, bf16[2,96,768]{2,1,0:T(8,128)(2,1)S(1)}, u32[]{:S(2)}, u32[]{:S(2)}) collective-permute-start(bf16[2,96,768]{2,1,0:T(8,128)(2,1)S(1)} %get-tuple-element.188.refs_4_), channel_id=1, source_target_pairs={{0,6},{1,7},{2,4},{3,5},{4,2},{5,3},{6,0},{7,1},{8,14},{9,15},{10,... | collective-permute-start | bytes 884744 | tf_op jit(solution)/shard_map/ppermute | solution.py:52
  66.6 22.6 %collective-permute-start.11 = (bf16[2,3,2,96,768]{4,3,2,1,0:T(8,128)(2,1)S(1)}, bf16[2,3,2,96,768]{4,3,2,1,0:T(8,128)(2,1)S(1)}, u32[]{:S(2)}, u32[]{:S(2)}) collective-permute-start(bf16[2,3,2,96,768]{4,3,2,1,0:T(8,128)(2,1)S(1)} %get-tuple-element.197.refs_2_), channel_id=1, source_target_pairs={{0,8},{1,17},{2,10},{3,19},{4,12},{5,21},{6,14},{7,23},{8,0},{9,25... | collective-permute-start | bytes 5308424 | tf_op jit(solution)/shard_map/ppermute | solution.py:52
  90.8 16.9 %collective-permute-start.15 = (bf16[16,2,96,768]{3,2,1,0:T(8,128)(2,1)S(1)}, bf16[16,2,96,768]{3,2,1,0:T(8,128)(2,1)S(1)}, u32[]{:S(2)}, u32[]{:S(2)}) collective-permute-start(bf16[16,2,96,768]{3,2,1,0:T(8,128)(2,1)S(1)} %get-tuple-element.201), channel_id=1, source_target_pairs={{0,1},{1,0},{2,3},{3,2},{4,5},{5,4},{6,7},{7,6},{8,9},{9,8},{10,11... | collective-permute-start | bytes 14155784 | tf_op jit(solution)/shard_map/ppermute | solution.py:52
  92.5 29.9 %collective-permute-start.18 = (bf16[2,96,768]{2,1,0:T(8,128)(2,1)}, bf16[2,96,768]{2,1,0:T(8,128)(2,1)}, u32[]{:S(2)}, u32[]{:S(2)}) collective-permute-start(bf16[2,96,768]{2,1,0:T(8,128)(2,1)} %get-tuple-element.200.refs_4_), channel_id=1, source_target_pairs={{0,2},{1,3},{2,0},{3,1},{4,6},{5,7},{6,4},{7,5},{8,10},{9,11},{10,... | collective-permute-start | bytes 884744 | tf_op jit(solution)/shard_map/ppermute | solution.py:52
  98.6 23.8 %collective-permute-start.19 = (bf16[2,96,768]{2,1,0:T(8,128)(2,1)}, bf16[2,96,768]{2,1,0:T(8,128)(2,1)}, u32[]{:S(2)}, u32[]{:S(2)}) collective-permute-start(bf16[2,96,768]{2,1,0:T(8,128)(2,1)} %get-tuple-element.200.refs_4_), channel_id=1, source_target_pairs={{0,4},{1,5},{2,6},{3,7},{4,0},{5,1},{6,2},{7,3},{8,12},{9,13},{10,... | collective-permute-start | bytes 884744 | tf_op jit(solution)/shard_map/ppermute | solution.py:52
  99.6 22.8 %collective-permute-start.20 = (bf16[2,96,768]{2,1,0:T(8,128)(2,1)}, bf16[2,96,768]{2,1,0:T(8,128)(2,1)}, u32[]{:S(2)}, u32[]{:S(2)}) collective-permute-start(bf16[2,96,768]{2,1,0:T(8,128)(2,1)} %get-tuple-element.200.refs_4_), channel_id=1, source_target_pairs={{0,6},{1,7},{2,4},{3,5},{4,2},{5,3},{6,0},{7,1},{8,14},{9,15},{10,... | collective-permute-start | bytes 884744 | tf_op jit(solution)/shard_map/ppermute | solution.py:52
  106.1 22.9 %collective-permute-start.17 = (bf16[2,3,2,96,768]{4,3,2,1,0:T(8,128)(2,1)}, bf16[2,3,2,96,768]{4,3,2,1,0:T(8,128)(2,1)}, u32[]{:S(2)}, u32[]{:S(2)}) collective-permute-start(bf16[2,3,2,96,768]{4,3,2,1,0:T(8,128)(2,1)} %get-tuple-element.207.refs_3_.refs_2_), channel_id=1, source_target_pairs={{0,8},{1,17},{2,10},{3,19},{4,12},{5,21},{6,14},{7,23},{8,0},{9,25... | collective-permute-start | bytes 5308424 | tf_op jit(solution)/shard_map/ppermute | solution.py:52
  131.7 16.9 %collective-permute-start.21 = (bf16[16,2,96,768]{3,2,1,0:T(8,128)(2,1)S(1)}, bf16[16,2,96,768]{3,2,1,0:T(8,128)(2,1)S(1)}, u32[]{:S(2)}, u32[]{:S(2)}) collective-permute-start(bf16[16,2,96,768]{3,2,1,0:T(8,128)(2,1)S(1)} %get-tuple-element.211), channel_id=1, source_target_pairs={{0,1},{1,0},{2,3},{3,2},{4,5},{5,4},{6,7},{7,6},{8,9},{9,8},{10,11... | collective-permute-start | bytes 14155784 | tf_op jit(solution)/shard_map/ppermute | solution.py:52
  133.4 41.4 %collective-permute-start.24 = (bf16[1,96,768]{2,1,0:T(8,128)(2,1)}, bf16[1,96,768]{2,1,0:T(8,128)(2,1)}, u32[]{:S(2)}, u32[]{:S(2)}) collective-permute-start(bf16[1,96,768]{2,1,0:T(8,128)(2,1)} %get-tuple-element.210.refs_5_), channel_id=1, source_target_pairs={{0,2},{1,3},{2,0},{3,1},{4,6},{5,7},{6,4},{7,5},{8,10},{9,11},{10,... | collective-permute-start | bytes 442376 | tf_op jit(solution)/shard_map/ppermute | solution.py:52
  139.5 35.3 %collective-permute-start.25 = (bf16[1,96,768]{2,1,0:T(8,128)(2,1)}, bf16[1,96,768]{2,1,0:T(8,128)(2,1)}, u32[]{:S(2)}, u32[]{:S(2)}) collective-permute-start(bf16[1,96,768]{2,1,0:T(8,128)(2,1)} %get-tuple-element.210.refs_5_), channel_id=1, source_target_pairs={{0,4},{1,5},{2,6},{3,7},{4,0},{5,1},{6,2},{7,3},{8,12},{9,13},{10,... | collective-permute-start | bytes 442376 | tf_op jit(solution)/shard_map/ppermute | solution.py:52
  140.5 34.3 %collective-permute-start.26 = (bf16[1,96,768]{2,1,0:T(8,128)(2,1)}, bf16[1,96,768]{2,1,0:T(8,128)(2,1)}, u32[]{:S(2)}, u32[]{:S(2)}) collective-permute-start(bf16[1,96,768]{2,1,0:T(8,128)(2,1)} %get-tuple-element.210.refs_5_), channel_id=1, source_target_pairs={{0,6},{1,7},{2,4},{3,5},{4,2},{5,3},{6,0},{7,1},{8,14},{9,15},{10,... | collective-permute-start | bytes 442376 | tf_op jit(solution)/shard_map/ppermute | solution.py:52
  147.0 29.5 %collective-permute-start.23 = (bf16[2,3,2,96,768]{4,3,2,1,0:T(8,128)(2,1)}, bf16[2,3,2,96,768]{4,3,2,1,0:T(8,128)(2,1)}, u32[]{:S(2)}, u32[]{:S(2)}) collective-permute-start(bf16[2,3,2,96,768]{4,3,2,1,0:T(8,128)(2,1)} %get-tuple-element.222.refs_2_), channel_id=1, source_target_pairs={{0,8},{1,17},{2,10},{3,19},{4,12},{5,21},{6,14},{7,23},{8,0},{9,25... | collective-permute-start | bytes 5308424 | tf_op jit(solution)/shard_map/ppermute | solution.py:52
  188.9 14.7 %collective-permute-start.29 = (bf16[2,3,1,96,768]{4,3,2,1,0:T(8,128)(2,1)S(1)}, bf16[2,3,1,96,768]{4,3,2,1,0:T(8,128)(2,1)S(1)}, u32[]{:S(2)}, u32[]{:S(2)}) collective-permute-start(bf16[2,3,1,96,768]{4,3,2,1,0:T(8,128)(2,1)S(1)} %get-tuple-element.231.refs_2_), channel_id=1, source_target_pairs={{0,8},{1,17},{2,10},{3,19},{4,12},{5,21},{6,14},{7,23},{8,0},{9,25... | collective-permute-start | bytes 2654216 | tf_op jit(solution)/shard_map/ppermute | solution.py:52
  205.6 32.7 %collective-permute-start.31 = (bf16[3,256,768]{2,1,0:T(8,128)(2,1)}, bf16[3,256,768]{2,1,0:T(8,128)(2,1)}, u32[]{:S(2)}, u32[]{:S(2)}) collective-permute-start(bf16[3,256,768]{2,1,0:T(8,128)(2,1)} %get-tuple-element.195.refs_1_.refs_3_), channel_id=1, source_target_pairs={{0,1},{1,0},{2,3},{3,2},{4,5},{5,4},{6,7},{7,6},{8,9},{9,8},{10,11... | collective-permute-start | bytes 3538952 | tf_op jit(solution)/shard_map/ppermute | solution.py:52
  206.2 32.2 %collective-permute-start.32 = (bf16[256,3072]{1,0:T(8,128)(2,1)}, bf16[256,3072]{1,0:T(8,128)(2,1)}, u32[]{:S(2)}, u32[]{:S(2)}) collective-permute-start(bf16[256,3072]{1,0:T(8,128)(2,1)} %get-tuple-element.205.refs_4_.refs_1_), channel_id=1, source_target_pairs={{0,1},{1,0},{2,3},{3,2},{4,5},{5,4},{6,7},{7,6},{8,9},{9,8},{10,11... | collective-permute-start | bytes 4718600 | tf_op jit(solution)/shard_map/ppermute | solution.py:52
  206.2 32.1 %collective-permute-start.33 = (bf16[3,256,768]{2,1,0:T(8,128)(2,1)}, bf16[3,256,768]{2,1,0:T(8,128)(2,1)}, u32[]{:S(2)}, u32[]{:S(2)}) collective-permute-start(bf16[3,256,768]{2,1,0:T(8,128)(2,1)} %get-tuple-element.220.refs_1_.refs_3_), channel_id=1, source_target_pairs={{0,1},{1,0},{2,3},{3,2},{4,5},{5,4},{6,7},{7,6},{8,9},{9,8},{10,11... | collective-permute-start | bytes 3538952 | tf_op jit(solution)/shard_map/ppermute | solution.py:52
  206.7 31.7 %collective-permute-start.34 = (bf16[256,3072]{1,0:T(8,128)(2,1)}, bf16[256,3072]{1,0:T(8,128)(2,1)}, u32[]{:S(2)}, u32[]{:S(2)}) collective-permute-start(bf16[256,3072]{1,0:T(8,128)(2,1)} %get-tuple-element.229.refs_4_.refs_1_), channel_id=1, source_target_pairs={{0,1},{1,0},{2,3},{3,2},{4,5},{5,4},{6,7},{7,6},{8,9},{9,8},{10,11... | collective-permute-start | bytes 4718600 | tf_op jit(solution)/shard_map/ppermute | solution.py:52
  247.6 19.5 %collective-permute-start.35 = (bf16[256,1152]{1,0:T(8,128)(2,1)S(1)}, bf16[256,1152]{1,0:T(8,128)(2,1)S(1)}, u32[]{:S(2)}, u32[]{:S(2)}) collective-permute-start(bf16[256,1152]{1,0:T(8,128)(2,1)S(1)} %get-tuple-element.247), channel_id=1, source_target_pairs={{0,1},{1,0},{2,3},{3,2},{4,5},{5,4},{6,7},{7,6},{8,9},{9,8},{10,11... | collective-permute-start | bytes 1769480 | tf_op jit(solution)/shard_map/ppermute | solution.py:52
  259.2 32.2 %collective-permute-start.37 = (bf16[2,4,2,2,96,384]{5,4,3,2,1,0:T(8,128)(2,1)}, bf16[2,4,2,2,96,384]{5,4,3,2,1,0:T(8,128)(2,1)}, u32[]{:S(2)}, u32[]{:S(2)}) collective-permute-start(bf16[2,4,2,2,96,384]{5,4,3,2,1,0:T(8,128)(2,1)} %get-tuple-element.252.refs_5_), channel_id=1, source_target_pairs={{0,8},{1,17},{2,10},{3,19},{4,12},{5,21},{6,14},{7,23},{8,0},{9,25... | collective-permute-start | bytes 7077896 | tf_op jit(solution)/shard_map/ppermute | solution.py:52
  275.0 57.9 %collective-permute-start.43 = (bf16[2,4,2,2,96,384]{5,4,3,2,1,0:T(8,128)(2,1)}, bf16[2,4,2,2,96,384]{5,4,3,2,1,0:T(8,128)(2,1)}, u32[]{:S(2)}, u32[]{:S(2)}) collective-permute-start(bf16[2,4,2,2,96,384]{5,4,3,2,1,0:T(8,128)(2,1)} %get-tuple-element.255.refs_10_), channel_id=1, source_target_pairs={{0,8},{1,17},{2,10},{3,19},{4,12},{5,21},{6,14},{7,23},{8,0},{9,25... | collective-permute-start | bytes 7077896 | tf_op jit(solution)/shard_map/ppermute | solution.py:52
  294.9 29.0 %collective-permute-start.38 = (bf16[4,2,2,96,384]{4,3,2,1,0:T(8,128)(2,1)S(1)}, bf16[4,2,2,96,384]{4,3,2,1,0:T(8,128)(2,1)S(1)}, u32[]{:S(2)}, u32[]{:S(2)}) collective-permute-start(bf16[4,2,2,96,384]{4,3,2,1,0:T(8,128)(2,1)S(1)} %get-tuple-element.262.refs_5_), channel_id=1, source_target_pairs={{0,16},{1,9},{2,18},{3,11},{4,20},{5,13},{6,22},{7,15},{8,24},{9,1... | collective-permute-start | bytes 3538952 | tf_op jit(solution)/shard_map/ppermute | solution.py:52
  308.1 77.9 %collective-permute-start.49 = (bf16[2,4,2,2,96,384]{5,4,3,2,1,0:T(8,128)(2,1)}, bf16[2,4,2,2,96,384]{5,4,3,2,1,0:T(8,128)(2,1)}, u32[]{:S(2)}, u32[]{:S(2)}) collective-permute-start(bf16[2,4,2,2,96,384]{5,4,3,2,1,0:T(8,128)(2,1)} %get-tuple-element.265.refs_3_), channel_id=1, source_target_pairs={{0,8},{1,17},{2,10},{3,19},{4,12},{5,21},{6,14},{7,23},{8,0},{9,25... | collective-permute-start | bytes 7077896 | tf_op jit(solution)/shard_map/ppermute | solution.py:52
  324.7 18.1 %collective-permute-start.40 = (bf16[2,2,96,384]{3,2,1,0:T(8,128)(2,1)S(1)}, bf16[2,2,96,384]{3,2,1,0:T(8,128)(2,1)S(1)}, u32[]{:S(2)}, u32[]{:S(2)}) collective-permute-start(bf16[2,2,96,384]{3,2,1,0:T(8,128)(2,1)S(1)} %get-tuple-element.267), channel_id=1, source_target_pairs={{0,2},{1,3},{2,0},{3,1},{4,6},{5,7},{6,4},{7,5},{8,10},{9,11},{10,... | collective-permute-start | bytes 884744 | tf_op jit(solution)/shard_map/ppermute | solution.py:52
  330.4 23.5 %collective-permute-start.41 = (bf16[2,2,96,384]{3,2,1,0:T(8,128)(2,1)S(1)}, bf16[2,2,96,384]{3,2,1,0:T(8,128)(2,1)S(1)}, u32[]{:S(2)}, u32[]{:S(2)}) collective-permute-start(bf16[2,2,96,384]{3,2,1,0:T(8,128)(2,1)S(1)} %get-tuple-element.268), channel_id=1, source_target_pairs={{0,4},{1,5},{2,6},{3,7},{4,0},{5,1},{6,2},{7,3},{8,12},{9,13},{10,... | collective-permute-start | bytes 884744 | tf_op jit(solution)/shard_map/ppermute | solution.py:52
  331.4 22.5 %collective-permute-start.42 = (bf16[2,2,96,384]{3,2,1,0:T(8,128)(2,1)S(1)}, bf16[2,2,96,384]{3,2,1,0:T(8,128)(2,1)S(1)}, u32[]{:S(2)}, u32[]{:S(2)}) collective-permute-start(bf16[2,2,96,384]{3,2,1,0:T(8,128)(2,1)S(1)} %get-tuple-element.269), channel_id=1, source_target_pairs={{0,6},{1,7},{2,4},{3,5},{4,2},{5,3},{6,0},{7,1},{8,14},{9,15},{10,... | collective-permute-start | bytes 884744 | tf_op jit(solution)/shard_map/ppermute | solution.py:52
  337.5 38.4 %collective-permute-start.44 = (bf16[4,2,2,96,384]{4,3,2,1,0:T(8,128)(2,1)}, bf16[4,2,2,96,384]{4,3,2,1,0:T(8,128)(2,1)}, u32[]{:S(2)}, u32[]{:S(2)}) collective-permute-start(bf16[4,2,2,96,384]{4,3,2,1,0:T(8,128)(2,1)} %get-tuple-element.271.refs_5_), channel_id=1, source_target_pairs={{0,16},{1,9},{2,18},{3,11},{4,20},{5,13},{6,22},{7,15},{8,24},{9,1... | collective-permute-start | bytes 3538952 | tf_op jit(solution)/shard_map/ppermute | solution.py:52
  374.1 40.2 %collective-permute-start.51 = (bf16[2,4,2,2,96,384]{5,4,3,2,1,0:T(8,128)(2,1)S(1)}, bf16[2,4,2,2,96,384]{5,4,3,2,1,0:T(8,128)(2,1)S(1)}, u32[]{:S(2)}, u32[]{:S(2)}) collective-permute-start(bf16[2,4,2,2,96,384]{5,4,3,2,1,0:T(8,128)(2,1)S(1)} %get-tuple-element.281.refs_3_), channel_id=1, source_target_pairs={{0,8},{1,17},{2,10},{3,19},{4,12},{5,21},{6,14},{7,23},{8,0},{9,25... | collective-permute-start | bytes 7077896 | tf_op jit(solution)/shard_map/ppermute | solution.py:52
  378.1 18.5 %collective-permute-start.46 = (bf16[2,2,96,384]{3,2,1,0:T(8,128)(2,1)S(1)}, bf16[2,2,96,384]{3,2,1,0:T(8,128)(2,1)S(1)}, u32[]{:S(2)}, u32[]{:S(2)}) collective-permute-start(bf16[2,2,96,384]{3,2,1,0:T(8,128)(2,1)S(1)} %get-tuple-element.283), channel_id=1, source_target_pairs={{0,2},{1,3},{2,0},{3,1},{4,6},{5,7},{6,4},{7,5},{8,10},{9,11},{10,... | collective-permute-start | bytes 884744 | tf_op jit(solution)/shard_map/ppermute | solution.py:52
  383.5 23.4 %collective-permute-start.47 = (bf16[2,2,96,384]{3,2,1,0:T(8,128)(2,1)S(1)}, bf16[2,2,96,384]{3,2,1,0:T(8,128)(2,1)S(1)}, u32[]{:S(2)}, u32[]{:S(2)}) collective-permute-start(bf16[2,2,96,384]{3,2,1,0:T(8,128)(2,1)S(1)} %get-tuple-element.284), channel_id=1, source_target_pairs={{0,4},{1,5},{2,6},{3,7},{4,0},{5,1},{6,2},{7,3},{8,12},{9,13},{10,... | collective-permute-start | bytes 884744 | tf_op jit(solution)/shard_map/ppermute | solution.py:52
  384.6 22.3 %collective-permute-start.48 = (bf16[2,2,96,384]{3,2,1,0:T(8,128)(2,1)S(1)}, bf16[2,2,96,384]{3,2,1,0:T(8,128)(2,1)S(1)}, u32[]{:S(2)}, u32[]{:S(2)}) collective-permute-start(bf16[2,2,96,384]{3,2,1,0:T(8,128)(2,1)S(1)} %get-tuple-element.285), channel_id=1, source_target_pairs={{0,6},{1,7},{2,4},{3,5},{4,2},{5,3},{6,0},{7,1},{8,14},{9,15},{10,... | collective-permute-start | bytes 884744 | tf_op jit(solution)/shard_map/ppermute | solution.py:52
  389.4 29.7 %collective-permute-start.50 = (bf16[4,2,2,96,384]{4,3,2,1,0:T(8,128)(2,1)S(1)}, bf16[4,2,2,96,384]{4,3,2,1,0:T(8,128)(2,1)S(1)}, u32[]{:S(2)}, u32[]{:S(2)}) collective-permute-start(bf16[4,2,2,96,384]{4,3,2,1,0:T(8,128)(2,1)S(1)} %get-tuple-element.287.refs_5_), channel_id=1, source_target_pairs={{0,16},{1,9},{2,18},{3,11},{4,20},{5,13},{6,22},{7,15},{8,24},{9,1... | collective-permute-start | bytes 3538952 | tf_op jit(solution)/shard_map/ppermute | solution.py:52
  416.0 33.7 %collective-permute-start.56 = (bf16[4,2,2,96,384]{4,3,2,1,0:T(8,128)(2,1)S(1)}, bf16[4,2,2,96,384]{4,3,2,1,0:T(8,128)(2,1)S(1)}, u32[]{:S(2)}, u32[]{:S(2)}) collective-permute-start(bf16[4,2,2,96,384]{4,3,2,1,0:T(8,128)(2,1)S(1)} %get-tuple-element.291.refs_3_), channel_id=1, source_target_pairs={{0,16},{1,9},{2,18},{3,11},{4,20},{5,13},{6,22},{7,15},{8,24},{9,1... | collective-permute-start | bytes 3538952 | tf_op jit(solution)/shard_map/ppermute | solution.py:52
  419.9 19.2 %collective-permute-start.52 = (bf16[2,2,96,384]{3,2,1,0:T(8,128)(2,1)S(1)}, bf16[2,2,96,384]{3,2,1,0:T(8,128)(2,1)S(1)}, u32[]{:S(2)}, u32[]{:S(2)}) collective-permute-start(bf16[2,2,96,384]{3,2,1,0:T(8,128)(2,1)S(1)} %get-tuple-element.293), channel_id=1, source_target_pairs={{0,2},{1,3},{2,0},{3,1},{4,6},{5,7},{6,4},{7,5},{8,10},{9,11},{10,... | collective-permute-start | bytes 884744 | tf_op jit(solution)/shard_map/ppermute | solution.py:52
  425.4 23.5 %collective-permute-start.53 = (bf16[2,2,96,384]{3,2,1,0:T(8,128)(2,1)S(1)}, bf16[2,2,96,384]{3,2,1,0:T(8,128)(2,1)S(1)}, u32[]{:S(2)}, u32[]{:S(2)}) collective-permute-start(bf16[2,2,96,384]{3,2,1,0:T(8,128)(2,1)S(1)} %get-tuple-element.294), channel_id=1, source_target_pairs={{0,4},{1,5},{2,6},{3,7},{4,0},{5,1},{6,2},{7,3},{8,12},{9,13},{10,... | collective-permute-start | bytes 884744 | tf_op jit(solution)/shard_map/ppermute | solution.py:52
  426.4 22.4 %collective-permute-start.54 = (bf16[2,2,96,384]{3,2,1,0:T(8,128)(2,1)S(1)}, bf16[2,2,96,384]{3,2,1,0:T(8,128)(2,1)S(1)}, u32[]{:S(2)}, u32[]{:S(2)}) collective-permute-start(bf16[2,2,96,384]{3,2,1,0:T(8,128)(2,1)S(1)} %get-tuple-element.295), channel_id=1, source_target_pairs={{0,6},{1,7},{2,4},{3,5},{4,2},{5,3},{6,0},{7,1},{8,14},{9,15},{10,... | collective-permute-start | bytes 884744 | tf_op jit(solution)/shard_map/ppermute | solution.py:52
  436.4 21.6 %collective-permute-start.60 = (bf16[2,2,96,384]{3,2,1,0:T(8,128)(2,1)S(1)}, bf16[2,2,96,384]{3,2,1,0:T(8,128)(2,1)S(1)}, u32[]{:S(2)}, u32[]{:S(2)}) collective-permute-start(bf16[2,2,96,384]{3,2,1,0:T(8,128)(2,1)S(1)} %get-tuple-element.309), channel_id=1, source_target_pairs={{0,16},{1,9},{2,18},{3,11},{4,20},{5,13},{6,22},{7,15},{8,24},{9,1... | collective-permute-start | bytes 884744 | tf_op jit(solution)/shard_map/ppermute | solution.py:52
  439.1 21.7 %collective-permute-start.63 = (bf16[2,2,2,96,384]{4,3,2,1,0:T(8,128)(2,1)S(1)}, bf16[2,2,2,96,384]{4,3,2,1,0:T(8,128)(2,1)S(1)}, u32[]{:S(2)}, u32[]{:S(2)}) collective-permute-start(bf16[2,2,2,96,384]{4,3,2,1,0:T(8,128)(2,1)S(1)} %get-tuple-element.313.refs_1_), channel_id=1, source_target_pairs={{0,8},{1,17},{2,10},{3,19},{4,12},{5,21},{6,14},{7,23},{8,0},{9,25... | collective-permute-start | bytes 1769480 | tf_op jit(solution)/shard_map/ppermute | solution.py:52
  450.5 23.1 %collective-permute-start.57 = (bf16[2,2,96,384]{3,2,1,0:T(8,128)(2,1)S(1)}, bf16[2,2,96,384]{3,2,1,0:T(8,128)(2,1)S(1)}, u32[]{:S(2)}, u32[]{:S(2)}) collective-permute-start(bf16[2,2,96,384]{3,2,1,0:T(8,128)(2,1)S(1)} %get-tuple-element.305), channel_id=1, source_target_pairs={{0,2},{1,3},{2,0},{3,1},{4,6},{5,7},{6,4},{7,5},{8,10},{9,11},{10,... | collective-permute-start | bytes 884744 | tf_op jit(solution)/shard_map/ppermute | solution.py:52
  455.5 23.5 %collective-permute-start.58 = (bf16[2,2,96,384]{3,2,1,0:T(8,128)(2,1)S(1)}, bf16[2,2,96,384]{3,2,1,0:T(8,128)(2,1)S(1)}, u32[]{:S(2)}, u32[]{:S(2)}) collective-permute-start(bf16[2,2,96,384]{3,2,1,0:T(8,128)(2,1)S(1)} %get-tuple-element.306), channel_id=1, source_target_pairs={{0,4},{1,5},{2,6},{3,7},{4,0},{5,1},{6,2},{7,3},{8,12},{9,13},{10,... | collective-permute-start | bytes 884744 | tf_op jit(solution)/shard_map/ppermute | solution.py:52
  456.6 22.4 %collective-permute-start.59 = (bf16[2,2,96,384]{3,2,1,0:T(8,128)(2,1)S(1)}, bf16[2,2,96,384]{3,2,1,0:T(8,128)(2,1)S(1)}, u32[]{:S(2)}, u32[]{:S(2)}) collective-permute-start(bf16[2,2,96,384]{3,2,1,0:T(8,128)(2,1)S(1)} %get-tuple-element.307), channel_id=1, source_target_pairs={{0,6},{1,7},{2,4},{3,5},{4,2},{5,3},{6,0},{7,1},{8,14},{9,15},{10,... | collective-permute-start | bytes 884744 | tf_op jit(solution)/shard_map/ppermute | solution.py:52
  493.8 22.5 %collective-permute-start.77 = (bf16[4,2,2,96,384]{4,3,2,1,0:T(8,128)(2,1)S(1)}, bf16[4,2,2,96,384]{4,3,2,1,0:T(8,128)(2,1)}, u32[]{:S(2)}, u32[]{:S(2)}) collective-permute-start(bf16[4,2,2,96,384]{4,3,2,1,0:T(8,128)(2,1)S(1)} %get-tuple-element.329.refs_22_), channel_id=1, source_target_pairs={{0,1},{1,0},{2,3},{3,2},{4,5},{5,4},{6,7},{7,6},{8,9},{9,8},{10,11... | collective-permute-start | bytes 3538952 | tf_op jit(solution)/shard_map/ppermute | solution.py:52
  500.8 15.4 %collective-permute-start.76 = (bf16[4,2,2,96,384]{4,3,2,1,0:T(8,128)(2,1)}, bf16[4,2,2,96,384]{4,3,2,1,0:T(8,128)(2,1)}, u32[]{:S(2)}, u32[]{:S(2)}) collective-permute-start(bf16[4,2,2,96,384]{4,3,2,1,0:T(8,128)(2,1)} %get-tuple-element.328.refs_14_.refs_18_.refs_26_), channel_id=1, source_target_pairs={{0,1},{1,0},{2,3},{3,2},{4,5},{5,4},{6,7},{7,6},{8,9},{9,8},{10,11... | collective-permute-start | bytes 3538952 | tf_op jit(solution)/shard_map/ppermute | solution.py:52
  (123 other events, 1334.3 us)

commit v5 on v4

--- a/solution.py
+++ b/solution.py
@@ -89,8 +89,8 @@
     "pack_replicas": 2,
     "adam_all": 30,
 }
-TIME_SCALE = 10.0
-VMEM_MIB = {"adam_all": 58}
+TIME_SCALE = 9.0
+VMEM_MIB = {"adam_all": 58, "gate_forward": 14, "feed_backward": 14, "assemble_gate_up": 14, "attend_forward": 14, "attend_backward": 14}
 
 
 def run(
@@ -112,7 +112,7 @@
             scratch_shapes=list(scratch),
         ),
         input_output_aliases={1 + at: out for at, out in (reuse or {}).items()},
-        compiler_params=pltpu.CompilerParams(vmem_limit_bytes=VMEM_MIB.get(name, 40) * 2**20),
+        compiler_params=pltpu.CompilerParams(vmem_limit_bytes=VMEM_MIB.get(name, 8) * 2**20),
         cost_estimate=pl.CostEstimate(
             flops=int(KERNEL_TIMES[name] * TIME_SCALE * 1e9), bytes_accessed=1000, transcendentals=0
         ),
@@ -1001,6 +1001,17 @@
     return (weight, first_moment, second_moment)
 
 
+def adam_scaled(weight, first_moment, second_moment, gradient, factor):
+    first_moment = beta_first * first_moment + ((1.0 - beta_first) * factor) * gradient
+    square = gradient * gradient
+    second_moment = beta_second * second_moment + ((1.0 - beta_second) * factor * factor) * square
+    second_hat = second_moment * (1.0 / (1.0 - beta_second**STEP))
+    root = second_hat * lax.rsqrt(second_hat) + adam_eps
+    step = (rate_matrix / (1.0 - beta_first**STEP)) * first_moment
+    weight = (1.0 - rate_matrix * decay_matrix) * weight - step / root
+    return (weight, first_moment, second_moment)
+
+
 def adam_all(states, pieces, factor, where):
     layer_count = len(pieces)
     rows = states[0][0].shape[1]
@@ -1030,14 +1041,12 @@
                     mine, theirs = mine.astype(wide_type), theirs.astype(wide_type)
                     for half in range(2):
                         columns = slice(half * HALF, (half + 1) * HALF)
-                        results = adam_step(
+                        results = adam_scaled(
                             w[layer, :, columns],
                             m[layer, :, columns],
                             v[layer, :, columns],
                             jnp.where(where[1] == half, mine, theirs),
                             factor_ref[0],
-                            rate_matrix,
-                            decay_matrix,
                         )
                         for out, result in zip(outs, results):
                             out[layer, :, columns] = result
@@ -1330,9 +1339,9 @@
         parts = chips(layer, "rest")
         halves(layer - 1, "wide")
         rest = total(parts)
-        halves(layer - 1, "rest")
         layer -= 1
         parts = chips(layer, "wide")
+        halves(layer, "rest")
         shared = share(wide)
         shared_rest = share(rest)
         shared = share_on(shared)

time: 555 us -> 525 us (0.946)
  local copies, waits for them, and re-layouts: 34.5 us -> 8.97 us
  waiting for transfers between devices: 146 us -> 169 us
  Pallas kernels: 237 us -> 221 us
  starting transfers between devices: 119 us -> 109 us
    unnamed x188 -> x128, local copies, waits for them, and re-layouts: 34.5 us -> 8.95 us
    ppermute x78, waiting for transfers between devices: 146 us -> 169 us  [send(): return lax.ppermute(values, both_axes, pairs)]
    pallas_call x68, Pallas kernels: 237 us -> 221 us  [run(): pl.pallas_call(body_of, out_shape=[jax.ShapeDtypeStruct(shape, dtype) for...]
    ppermute x78, starting transfers between devices: 119 us -> 109 us  [send(): return lax.ppermute(values, both_axes, pairs)]
  transfers between devices with their start and end apart: 78 -> 78, of which waited for: 28 -> 31; matrix products, arithmetic and copies ran while one was open for 1% -> 1% of each run, Pallas kernels for 36% -> 36%
where the time goes in v5:
time: 525 us; the launch traced here: 516 us
  Pallas kernels  221 us (42%)
  waiting for transfers between devices  169 us (32%)
  starting transfers between devices  109 us (21%)
  local copies, waits for them, and re-layouts  8.97 us (2%)
    pallas_call x68, Pallas kernels, run(): pl.pallas_call(body_of, out_shape=[jax.ShapeDtypeStruct(shape, dtype) for...  221 us
    ppermute x78, waiting for transfers between devices, send(): return lax.ppermute(values, both_axes, pairs)  169 us
    ppermute x78, starting transfers between devices, send(): return lax.ppermute(values, both_axes, pairs)  109 us
  transfers between devices with their start and end apart: 78, of which 31 were waited for; matrix products, arithmetic and copies ran while one was open for 1% of the time, Pallas kernels for 36%

profile of v5, /device:TPU:0, one launch (start us, length us, event | category | flops | bytes accessed | tf_op | source)
XLA Modules:
  0.0 515.7 jit_solution(3560561626151045423)
XLA Ops:
  4.6 3.1 collective-permute-start
  10.4 4.4 collective-permute-done.refs_1_
  14.8 8.5 %collective-permute-done.1.refs_2_ = bf16[1,112,768]{2,1,0:T(8,128)(2,1)S(1)} collective-permute-done((bf16[1,112,768]{2,1,0:T(8,128)(2,1)S(1)}, bf16[1,112,768]{2,1,0:T(8,128)(2,1)S(1)}, u32[]{:S(2)}, u32[]{:S(2)}) %collective-permute-start.1) | collective-permute-done | bytes 172064 | tf_op jit(solution)/shard_map/ppermute | solution.py:52
  32.2 6.1 %collective-permute-done.3.refs_2_ = bf16[3,1,96,768]{3,2,1,0:T(8,128)(2,1)S(1)} collective-permute-done((bf16[3,1,96,768]{3,2,1,0:T(8,128)(2,1)S(1)}, bf16[3,1,96,768]{3,2,1,0:T(8,128)(2,1)S(1)}, u32[]{:S(2)}, u32[]{:S(2)}) %collective-permute-start.3) | collective-permute-done | bytes 442400 | tf_op jit(solution)/shard_map/ppermute | solution.py:52
  41.1 9.9 %collective-permute-done.7.refs_2_ = bf16[2,96,768]{2,1,0:T(8,128)(2,1)S(1)} collective-permute-done((bf16[2,96,768]{2,1,0:T(8,128)(2,1)S(1)}, bf16[2,96,768]{2,1,0:T(8,128)(2,1)S(1)}, u32[]{:S(2)}, u32[]{:S(2)}) %collective-permute-start.7) | collective-permute-done | bytes 294944 | tf_op jit(solution)/shard_map/ppermute | solution.py:52
  56.0 6.2 %collective-permute-start.12 = (bf16[2,96,768]{2,1,0:T(8,128)(2,1)S(1)}, bf16[2,96,768]{2,1,0:T(8,128)(2,1)S(1)}, u32[]{:S(2)}, u32[]{:S(2)}) collective-permute-start(bf16[2,96,768]{2,1,0:T(8,128)(2,1)S(1)} %get-tuple-element.188.refs_4_), channel_id=1, source_target_pairs={{0,2},{1,3},{2,0},{3,1},{4,6},{5,7},{6,4},{7,5},{8,10},{9,11},{10,... | collective-permute-start | bytes 884744 | tf_op jit(solution)/shard_map/ppermute | solution.py:52
  70.0 7.8 %attend_forward.2 = (bf16[3,256,768]{2,1,0:T(8,128)(2,1)}, bf16[256,2304]{1,0:T(8,128)(2,1)S(1)}, f32[256,128]{1,0:T(8,128)S(1)}, f32[256,768]{1,0:T(8,128)S(1)}, f32[256,768]{1,0:T(8,128)S(1)}) custom-call(s32[4]{0:T(128)S(1)} %pad_add_fusion.refs_0_, f32[256,768]{1,0:T(8,128)S(1)} %convert_select_fusion.refs_1_, ...), custom_call_target="tpu_custom_call" | custom-call | flops 67499999232 | bytes 1000 | tf_op jit(solution)/shard_map/attend_forward/pallas_call | solution.py:104
  77.8 7.9 %collective-permute-done.13.refs_2_ = bf16[2,96,768]{2,1,0:T(8,128)(2,1)S(1)} collective-permute-done((bf16[2,96,768]{2,1,0:T(8,128)(2,1)S(1)}, bf16[2,96,768]{2,1,0:T(8,128)(2,1)S(1)}, u32[]{:S(2)}, u32[]{:S(2)}) %collective-permute-start.13) | collective-permute-done | bytes 294944 | tf_op jit(solution)/shard_map/ppermute | solution.py:52
  91.5 6.1 %collective-permute-start.18 = (bf16[2,96,768]{2,1,0:T(8,128)(2,1)S(1)}, bf16[2,96,768]{2,1,0:T(8,128)(2,1)S(1)}, u32[]{:S(2)}, u32[]{:S(2)}) collective-permute-start(bf16[2,96,768]{2,1,0:T(8,128)(2,1)S(1)} %get-tuple-element.200.refs_4_), channel_id=1, source_target_pairs={{0,2},{1,3},{2,0},{3,1},{4,6},{5,7},{6,4},{7,5},{8,10},{9,11},{10,... | collective-permute-start | bytes 884744 | tf_op jit(solution)/shard_map/ppermute | solution.py:52
  107.3 6.6 %gate_forward.2 = (bf16[256,3072]{1,0:T(8,128)(2,1)}, bf16[2,256,3072]{2,1,0:T(8,128)(2,1)S(1)}) custom-call(s32[4]{0:T(128)S(1)} %pad_add_fusion.refs_0_, bf16[3,256,768]{2,1,0:T(8,128)(2,1)} %get-tuple-element.195.refs_1_.refs_3_, bf16[768,6144]{1,0:T(8,128)(2,1)S(1)} %assemble_gate_up.2.refs_2_.refs_3_.refs_4_.refs_6_.refs_7_, ...), custom_call_target="tpu_custom_call" | custom-call | flops 62999998464 | bytes 1000 | tf_op jit(solution)/shard_map/gate_forward/pallas_call | solution.py:104
  114.0 7.1 %collective-permute-done.19.refs_2_ = bf16[2,96,768]{2,1,0:T(8,128)(2,1)S(1)} collective-permute-done((bf16[2,96,768]{2,1,0:T(8,128)(2,1)S(1)}, bf16[2,96,768]{2,1,0:T(8,128)(2,1)S(1)}, u32[]{:S(2)}, u32[]{:S(2)}) %collective-permute-start.19) | collective-permute-done | bytes 294944 | tf_op jit(solution)/shard_map/ppermute | solution.py:52
  129.6 6.1 %collective-permute-start.24 = (bf16[1,96,768]{2,1,0:T(8,128)(2,1)}, bf16[1,96,768]{2,1,0:T(8,128)(2,1)}, u32[]{:S(2)}, u32[]{:S(2)}) collective-permute-start(bf16[1,96,768]{2,1,0:T(8,128)(2,1)} %get-tuple-element.210.refs_5_), channel_id=1, source_target_pairs={{0,2},{1,3},{2,0},{3,1},{4,6},{5,7},{6,4},{7,5},{8,10},{9,11},{10,... | collective-permute-start | bytes 442376 | tf_op jit(solution)/shard_map/ppermute | solution.py:52
  144.9 6.7 %assemble_down.2.refs_5_.refs_2_ = bf16[3072,768]{1,0:T(8,128)(2,1)S(1)} custom-call(s32[4]{0:T(128)S(1)} %pad_add_fusion.refs_0_, bf16[4,1,96,768]{3,2,1,0:T(8,128)(2,1)S(1)} %get-tuple-element.206.refs_1_, bf16[2,3,2,96,768]{4,3,2,1,0:T(8,128)(2,1)S(1)} %get-tuple-element.207.refs_3_.refs_2_, ...), custom_call_target="tpu_custom_call" | custom-call | flops 44999999488 | bytes 1000 | tf_op jit(solution)/shard_map/assemble_down/pallas_call | solution.py:104
  154.5 4.7 down_forward.2
  159.3 7.8 %attend_forward.3 = (bf16[3,256,768]{2,1,0:T(8,128)(2,1)}, bf16[256,2304]{1,0:T(8,128)(2,1)S(1)}, f32[256,128]{1,0:T(8,128)S(1)}, f32[256,768]{1,0:T(8,128)S(1)}, f32[256,768]{1,0:T(8,128)S(1)}) custom-call(s32[4]{0:T(128)S(1)} %pad_add_fusion.refs_0_, f32[256,768]{1,0:T(8,128)S(1)} %get-tuple-element.217.refs_1_, ...), custom_call_target="tpu_custom_call" | custom-call | flops 67499999232 | bytes 1000 | tf_op jit(solution)/shard_map/attend_forward/pallas_call | solution.py:104
  173.3 6.8 %collective-permute-done.28.refs_2_ = bf16[3,1,96,768]{3,2,1,0:T(8,128)(2,1)S(1)} collective-permute-done((bf16[3,1,96,768]{3,2,1,0:T(8,128)(2,1)S(1)}, bf16[3,1,96,768]{3,2,1,0:T(8,128)(2,1)S(1)}, u32[]{:S(2)}, u32[]{:S(2)}) %collective-permute-start.28) | collective-permute-done | bytes 442400 | tf_op jit(solution)/shard_map/ppermute | solution.py:52
  184.8 6.3 %gate_forward.3 = (bf16[256,3072]{1,0:T(8,128)(2,1)}, bf16[2,256,3072]{2,1,0:T(8,128)(2,1)S(1)}) custom-call(s32[4]{0:T(128)S(1)} %pad_add_fusion.refs_0_, bf16[3,256,768]{2,1,0:T(8,128)(2,1)} %get-tuple-element.220.refs_1_.refs_3_, bf16[768,6144]{1,0:T(8,128)(2,1)S(1)} %assemble_gate_up.3.refs_2_.refs_3_.refs_4_.refs_6_.refs_7_, ...), custom_call_target="tpu_custom_call" | custom-call | flops 62999998464 | bytes 1000 | tf_op jit(solution)/shard_map/gate_forward/pallas_call | solution.py:104
  191.1 3.2 collective-permute-done.29.refs_3_
  197.4 4.1 collective-permute-done.30.refs_4_
  201.4 6.7 %assemble_down.3.refs_2_.refs_5_ = bf16[3072,768]{1,0:T(8,128)(2,1)S(1)} custom-call(s32[4]{0:T(128)S(1)} %pad_add_fusion.refs_0_, bf16[4,1,96,768]{3,2,1,0:T(8,128)(2,1)S(1)} %get-tuple-element.230.refs_1_, bf16[2,3,1,96,768]{4,3,2,1,0:T(8,128)(2,1)S(1)} %get-tuple-element.231.refs_2_, bf16[2,3,1,96,768]{4,3,2,1,0:T(8,128)(2,1)S(1)} %collective-permute-done.29.refs_3_, ...), custom_call_target="tpu_custom_call" | custom-call | flops 44999999488 | bytes 1000 | tf_op jit(solution)/shard_map/assemble_down/pallas_call | solution.py:104
  208.2 4.4 down_forward.3
  212.7 11.3 %feed_backward.2 = (bf16[2,256,3072]{2,1,0:T(8,128)(2,1)S(1)}, bf16[256,3840]{1,0:T(8,128)(2,1)S(1)}, bf16[256,768]{1,0:T(8,128)(2,1)S(1)}, f32[256,768]{1,0:T(8...) custom-call(s32[4]{0:T(128)S(1)} %pad_add_fusion.refs_0_, ...), custom_call_target="tpu_custom_call" | custom-call | flops 117000003584 | bytes 1000 | tf_op jit(solution)/shard_map/feed_backward/pallas_call | solution.py:104
  224.3 7.3 %attend_backward.2 = (bf16[256,2304]{1,0:T(8,128)(2,1)S(1)}, bf16[256,1152]{1,0:T(8,128)(2,1)S(1)}, f32[256,768]{1,0:T(8,128)S(1)}) custom-call(s32[4]{0:T(128)S(1)} %pad_add_fusion.refs_0_, bf16[256,768]{1,0:T(8,128)(2,1)S(1)} %get-tuple-element.239.refs_1_, bf16[256,2304]{1,0:T(8,128)(2,1)S(1)} %get-tuple-element.240.refs_2_, f32[256,128]{1,0:T(8,128)S(1)} %copy-done.38, ...), custom_call_target="tpu_custom_call" | custom-call | flops 71999995904 | bytes 1000 | tf_op jit(solution)/shard_map/attend_backward/pallas_call | solution.py:104
  232.0 9.3 %grad_gate_up.2 = (bf16[2,4,2,2,96,384]{5,4,3,2,1,0:T(8,128)(2,1)}, bf16[2,4,2,2,96,384]{5,4,3,2,1,0:T(8,128)(2,1)S(1)}) custom-call(s32[4]{0:T(128)S(1)} %pad_add_fusion.refs_0_, bf16[3,256,768]{2,1,0:T(8,128)(2,1)} %get-tuple-element.220.refs_1_.refs_3_, bf16[3,256,768]{2,1,0:T(8,128)(2,1)} %collective-permute-done.33.refs_9_.refs_2_.refs_4_, ...), custom_call_target="tpu_custom_call" | custom-call | flops 80999997440 | bytes 1000 | tf_op jit(solution)/shard_map/grad_gate_up/pallas_call | solution.py:104
  242.1 5.2 %grad_down.2 = (bf16[2,4,2,2,96,384]{5,4,3,2,1,0:T(8,128)(2,1)S(1)}, bf16[2,4,2,2,96,384]{5,4,3,2,1,0:T(8,128)(2,1)S(1)}) custom-call(s32[4]{0:T(128)S(1)} %pad_add_fusion.refs_0_, bf16[256,3072]{1,0:T(8,128)(2,1)} %get-tuple-element.229.refs_4_.refs_1_, bf16[256,3072]{1,0:T(8,128)(2,1)} %collective-permute-done.34.refs_10_.refs_2_, ...), custom_call_target="tpu_custom_call" | custom-call | flops 44999999488 | bytes 1000 | tf_op jit(solution)/shard_map/grad_down/pallas_call | solution.py:104
  248.9 7.1 %grad_attend.2 = (bf16[2,4,2,2,96,384]{5,4,3,2,1,0:T(8,128)(2,1)}, bf16[2,4,2,2,96,384]{5,4,3,2,1,0:T(8,128)(2,1)S(1)}) custom-call(s32[4]{0:T(128)S(1)} %pad_add_fusion.refs_0_, bf16[3,256,768]{2,1,0:T(8,128)(2,1)} %get-tuple-element.220.refs_1_.refs_3_, ...), custom_call_target="tpu_custom_call", output_to_operand_aliasing={{0}: (9, {}), {1}: (10, {})} | custom-call | flops 54000001024 | bytes 1000 | tf_op jit(solution)/shard_map/grad_attend/pallas_call | solution.py:104
  259.1 10.9 %feed_backward.3 = (bf16[2,256,3072]{2,1,0:T(8,128)(2,1)S(1)}, bf16[256,3840]{1,0:T(8,128)(2,1)S(1)}, bf16[256,768]{1,0:T(8,128)(2,1)S(1)}, f32[256,768]{1,0:T(8...) custom-call(s32[4]{0:T(128)S(1)} %pad_add_fusion.refs_0_, ...), custom_call_target="tpu_custom_call" | custom-call | flops 117000003584 | bytes 1000 | tf_op jit(solution)/shard_map/feed_backward/pallas_call | solution.py:104
  270.5 3.4 add_halves.4
  275.4 9.3 %grad_gate_up.3 = (bf16[2,4,2,2,96,384]{5,4,3,2,1,0:T(8,128)(2,1)}, bf16[2,4,2,2,96,384]{5,4,3,2,1,0:T(8,128)(2,1)S(1)}) custom-call(s32[4]{0:T(128)S(1)} %pad_add_fusion.refs_0_, bf16[3,256,768]{2,1,0:T(8,128)(2,1)} %get-tuple-element.195.refs_1_.refs_3_, bf16[3,256,768]{2,1,0:T(8,128)(2,1)} %collective-permute-done.31.refs_7_.refs_2_.refs_4_, ...), custom_call_target="tpu_custom_call" | custom-call | flops 80999997440 | bytes 1000 | tf_op jit(solution)/shard_map/grad_gate_up/pallas_call | solution.py:104
  285.3 17.6 %collective-permute-done.38.refs_2_ = bf16[4,2,2,96,384]{4,3,2,1,0:T(8,128)(2,1)S(1)} collective-permute-done((bf16[4,2,2,96,384]{4,3,2,1,0:T(8,128)(2,1)S(1)}, bf16[4,2,2,96,384]{4,3,2,1,0:T(8,128)(2,1)S(1)}, u32[]{:S(2)}, u32[]{:S(2)}) %collective-permute-start.38) | collective-permute-done | bytes 1179680 | tf_op jit(solution)/shard_map/ppermute | solution.py:52
  303.7 6.2 %collective-permute-start.40 = (bf16[2,2,96,384]{3,2,1,0:T(8,128)(2,1)S(1)}, bf16[2,2,96,384]{3,2,1,0:T(8,128)(2,1)S(1)}, u32[]{:S(2)}, u32[]{:S(2)}) collective-permute-start(bf16[2,2,96,384]{3,2,1,0:T(8,128)(2,1)S(1)} %get-tuple-element.267), channel_id=1, source_target_pairs={{0,2},{1,3},{2,0},{3,1},{4,6},{5,7},{6,4},{7,5},{8,10},{9,11},{10,... | collective-permute-start | bytes 884744 | tf_op jit(solution)/shard_map/ppermute | solution.py:52
  312.3 4.6 add_halves.5
  318.5 3.1 collective-permute-done.40.refs_2_
  321.7 11.7 %collective-permute-done.41.refs_3_ = bf16[2,2,96,384]{3,2,1,0:T(8,128)(2,1)S(1)} collective-permute-done((bf16[2,2,96,384]{3,2,1,0:T(8,128)(2,1)S(1)}, bf16[2,2,96,384]{3,2,1,0:T(8,128)(2,1)S(1)}, u32[]{:S(2)}, u32[]{:S(2)}) %collective-permute-start.41) | collective-permute-done | bytes 294944 | tf_op jit(solution)/shard_map/ppermute | solution.py:52
  334.1 7.3 %attend_backward.3 = (bf16[256,2304]{1,0:T(8,128)(2,1)S(1)}, bf16[256,1152]{1,0:T(8,128)(2,1)S(1)}, f32[256,768]{1,0:T(8,128)S(1)}) custom-call(s32[4]{0:T(128)S(1)} %pad_add_fusion.refs_0_, bf16[256,768]{1,0:T(8,128)(2,1)S(1)} %get-tuple-element.256.refs_1_, bf16[256,2304]{1,0:T(8,128)(2,1)S(1)} %get-tuple-element.257.refs_2_, f32[256,128]{1,0:T(8,128)S(1)} %copy-done.36, ...), custom_call_target="tpu_custom_call" | custom-call | flops 71999995904 | bytes 1000 | tf_op jit(solution)/shard_map/attend_backward/pallas_call | solution.py:104
  341.5 5.2 %grad_down.3 = (bf16[2,4,2,2,96,384]{5,4,3,2,1,0:T(8,128)(2,1)S(1)}, bf16[2,4,2,2,96,384]{5,4,3,2,1,0:T(8,128)(2,1)S(1)}) custom-call(s32[4]{0:T(128)S(1)} %pad_add_fusion.refs_0_, bf16[256,3072]{1,0:T(8,128)(2,1)} %get-tuple-element.205.refs_4_.refs_1_, bf16[256,3072]{1,0:T(8,128)(2,1)} %collective-permute-done.32.refs_8_.refs_2_, ...), custom_call_target="tpu_custom_call" | custom-call | flops 44999999488 | bytes 1000 | tf_op jit(solution)/shard_map/grad_down/pallas_call | solution.py:104
  347.1 5.7 %grad_attend.3 = (bf16[2,4,2,2,96,384]{5,4,3,2,1,0:T(8,128)(2,1)S(1)}, bf16[2,4,2,2,96,384]{5,4,3,2,1,0:T(8,128)(2,1)S(1)}) custom-call(s32[4]{0:T(128)S(1)} %pad_add_fusion.refs_0_, bf16[3,256,768]{2,1,0:T(8,128)(2,1)} %get-tuple-element.195.refs_1_.refs_3_, ...), custom_call_target="tpu_custom_call", output_to_operand_aliasing={{0}: (9, {}), {1}: (10, {})} | custom-call | flops 54000001024 | bytes 1000 | tf_op jit(solution)/shard_map/grad_attend/pallas_call | solution.py:104
  355.7 5.1 collective-permute-start.46
  363.2 3.4 add_halves.6
  368.0 6.5 %collective-permute-done.46.refs_2_ = bf16[2,2,96,384]{3,2,1,0:T(8,128)(2,1)S(1)} collective-permute-done((bf16[2,2,96,384]{3,2,1,0:T(8,128)(2,1)S(1)}, bf16[2,2,96,384]{3,2,1,0:T(8,128)(2,1)S(1)}, u32[]{:S(2)}, u32[]{:S(2)}) %collective-permute-start.46) | collective-permute-done | bytes 294944 | tf_op jit(solution)/shard_map/ppermute | solution.py:52
  374.5 9.7 %collective-permute-done.47.refs_3_ = bf16[2,2,96,384]{3,2,1,0:T(8,128)(2,1)S(1)} collective-permute-done((bf16[2,2,96,384]{3,2,1,0:T(8,128)(2,1)S(1)}, bf16[2,2,96,384]{3,2,1,0:T(8,128)(2,1)S(1)}, u32[]{:S(2)}, u32[]{:S(2)}) %collective-permute-start.47) | collective-permute-done | bytes 294944 | tf_op jit(solution)/shard_map/ppermute | solution.py:52
  385.0 8.9 %collective-permute-done.50.refs_2_ = bf16[4,2,2,96,384]{4,3,2,1,0:T(8,128)(2,1)S(1)} collective-permute-done((bf16[4,2,2,96,384]{4,3,2,1,0:T(8,128)(2,1)S(1)}, bf16[4,2,2,96,384]{4,3,2,1,0:T(8,128)(2,1)S(1)}, u32[]{:S(2)}, u32[]{:S(2)}) %collective-permute-start.50) | collective-permute-done | bytes 1179680 | tf_op jit(solution)/shard_map/ppermute | solution.py:52
  405.1 16.0 %collective-permute-done.55.refs_2_ = bf16[2,2,96,384]{3,2,1,0:T(8,128)(2,1)S(1)} collective-permute-done((bf16[2,2,96,384]{3,2,1,0:T(8,128)(2,1)S(1)}, bf16[2,2,96,384]{3,2,1,0:T(8,128)(2,1)S(1)}, u32[]{:S(2)}, u32[]{:S(2)}) %collective-permute-start.55) | collective-permute-done | bytes 294944 | tf_op jit(solution)/shard_map/ppermute | solution.py:52
  438.0 7.0 %collective-permute-done.62.refs_2_ = bf16[2,2,2,96,384]{4,3,2,1,0:T(8,128)(2,1)S(1)} collective-permute-done((bf16[2,2,2,96,384]{4,3,2,1,0:T(8,128)(2,1)S(1)}, bf16[2,2,2,96,384]{4,3,2,1,0:T(8,128)(2,1)S(1)}, u32[]{:S(2)}, u32[]{:S(2)}) %collective-permute-start.62) | collective-permute-done | bytes 589856 | tf_op jit(solution)/shard_map/ppermute | solution.py:52
  452.5 7.3 %collective-permute-done.72.refs_2_ = bf16[2,2,2,96,384]{4,3,2,1,0:T(8,128)(2,1)S(1)} collective-permute-done((bf16[2,2,2,96,384]{4,3,2,1,0:T(8,128)(2,1)S(1)}, bf16[2,2,2,96,384]{4,3,2,1,0:T(8,128)(2,1)S(1)}, u32[]{:S(2)}, u32[]{:S(2)}) %collective-permute-start.72) | collective-permute-done | bytes 589856 | tf_op jit(solution)/shard_map/ppermute | solution.py:52
  469.0 4.0 collective-permute-done.75.refs_2_
  480.9 3.8 collective-permute-done.70
  487.5 26.9 %adam_all.1 = (f32[2,96,2304]{2,1,0:T(8,128)}, f32[2,96,2304]{2,1,0:T(8,128)}, f32[2,96,2304]{2,1,0:T(8,128)}, f32[2,96,768]{2,1,0:T(8,128)}, f32[2,96,768]{2,1,...) custom-call(s32[4]{0:T(128)} %copy-done.11, ...), custom_call_target="tpu_custom_call" | custom-call | flops 269999996928 | bytes 1000 | tf_op jit(solution)/shard_map/adam_all/pallas_call | solution.py:104
  (327 shorter events, 156.3 us)
Async XLA Ops:
  7.7 15.6 %collective-permute-start.1 = (bf16[1,112,768]{2,1,0:T(8,128)(2,1)S(1)}, bf16[1,112,768]{2,1,0:T(8,128)(2,1)S(1)}, u32[]{:S(2)}, u32[]{:S(2)}) collective-permute-start(bf16[1,112,768]{2,1,0:T(8,128)(2,1)S(1)} %get-tuple-element.181.refs_4_), channel_id=1, source_target_pairs={{0,4},{1,5},{2,6},{3,7},{4,0},{5,1},{6,2},{7,3},{8,12},{9,13},{10,... | collective-permute-start | bytes 516104 | tf_op jit(solution)/shard_map/ppermute | solution.py:52
  24.7 16.4 %collective-permute-start.6 = (bf16[2,96,768]{2,1,0:T(8,128)(2,1)S(1)}, bf16[2,96,768]{2,1,0:T(8,128)(2,1)S(1)}, u32[]{:S(2)}, u32[]{:S(2)}) collective-permute-start(bf16[2,96,768]{2,1,0:T(8,128)(2,1)S(1)} %get-tuple-element.184.refs_4_), channel_id=1, source_target_pairs={{0,2},{1,3},{2,0},{3,1},{4,6},{5,7},{6,4},{7,5},{8,10},{9,11},{10,... | collective-permute-start | bytes 884744 | tf_op jit(solution)/shard_map/ppermute | solution.py:52
  27.6 23.4 %collective-permute-start.7 = (bf16[2,96,768]{2,1,0:T(8,128)(2,1)S(1)}, bf16[2,96,768]{2,1,0:T(8,128)(2,1)S(1)}, u32[]{:S(2)}, u32[]{:S(2)}) collective-permute-start(bf16[2,96,768]{2,1,0:T(8,128)(2,1)S(1)} %get-tuple-element.184.refs_4_), channel_id=1, source_target_pairs={{0,4},{1,5},{2,6},{3,7},{4,0},{5,1},{6,2},{7,3},{8,12},{9,13},{10,... | collective-permute-start | bytes 884744 | tf_op jit(solution)/shard_map/ppermute | solution.py:52
  28.7 22.4 %collective-permute-start.8 = (bf16[2,96,768]{2,1,0:T(8,128)(2,1)S(1)}, bf16[2,96,768]{2,1,0:T(8,128)(2,1)S(1)}, u32[]{:S(2)}, u32[]{:S(2)}) collective-permute-start(bf16[2,96,768]{2,1,0:T(8,128)(2,1)S(1)} %get-tuple-element.184.refs_4_), channel_id=1, source_target_pairs={{0,6},{1,7},{2,4},{3,5},{4,2},{5,3},{6,0},{7,1},{8,14},{9,15},{10,... | collective-permute-start | bytes 884744 | tf_op jit(solution)/shard_map/ppermute | solution.py:52
  39.4 14.6 %collective-permute-start.5 = (bf16[2,3,1,96,768]{4,3,2,1,0:T(8,128)(2,1)S(1)}, bf16[2,3,1,96,768]{4,3,2,1,0:T(8,128)(2,1)S(1)}, u32[]{:S(2)}, u32[]{:S(2)}) collective-permute-start(bf16[2,3,1,96,768]{4,3,2,1,0:T(8,128)(2,1)S(1)} %get-tuple-element.185.refs_2_), channel_id=1, source_target_pairs={{0,8},{1,17},{2,10},{3,19},{4,12},{5,21},{6,14},{7,23},{8,0},{9,25... | collective-permute-start | bytes 2654216 | tf_op jit(solution)/shard_map/ppermute | solution.py:52
  56.0 21.8 %collective-permute-start.12 = (bf16[2,96,768]{2,1,0:T(8,128)(2,1)S(1)}, bf16[2,96,768]{2,1,0:T(8,128)(2,1)S(1)}, u32[]{:S(2)}, u32[]{:S(2)}) collective-permute-start(bf16[2,96,768]{2,1,0:T(8,128)(2,1)S(1)} %get-tuple-element.188.refs_4_), channel_id=1, source_target_pairs={{0,2},{1,3},{2,0},{3,1},{4,6},{5,7},{6,4},{7,5},{8,10},{9,11},{10,... | collective-permute-start | bytes 884744 | tf_op jit(solution)/shard_map/ppermute | solution.py:52
  62.3 23.4 %collective-permute-start.13 = (bf16[2,96,768]{2,1,0:T(8,128)(2,1)S(1)}, bf16[2,96,768]{2,1,0:T(8,128)(2,1)S(1)}, u32[]{:S(2)}, u32[]{:S(2)}) collective-permute-start(bf16[2,96,768]{2,1,0:T(8,128)(2,1)S(1)} %get-tuple-element.188.refs_4_), channel_id=1, source_target_pairs={{0,4},{1,5},{2,6},{3,7},{4,0},{5,1},{6,2},{7,3},{8,12},{9,13},{10,... | collective-permute-start | bytes 884744 | tf_op jit(solution)/shard_map/ppermute | solution.py:52
  63.3 22.4 %collective-permute-start.14 = (bf16[2,96,768]{2,1,0:T(8,128)(2,1)S(1)}, bf16[2,96,768]{2,1,0:T(8,128)(2,1)S(1)}, u32[]{:S(2)}, u32[]{:S(2)}) collective-permute-start(bf16[2,96,768]{2,1,0:T(8,128)(2,1)S(1)} %get-tuple-element.188.refs_4_), channel_id=1, source_target_pairs={{0,6},{1,7},{2,4},{3,5},{4,2},{5,3},{6,0},{7,1},{8,14},{9,15},{10,... | collective-permute-start | bytes 884744 | tf_op jit(solution)/shard_map/ppermute | solution.py:52
  65.7 22.6 %collective-permute-start.11 = (bf16[2,3,2,96,768]{4,3,2,1,0:T(8,128)(2,1)S(1)}, bf16[2,3,2,96,768]{4,3,2,1,0:T(8,128)(2,1)S(1)}, u32[]{:S(2)}, u32[]{:S(2)}) collective-permute-start(bf16[2,3,2,96,768]{4,3,2,1,0:T(8,128)(2,1)S(1)} %get-tuple-element.197.refs_2_), channel_id=1, source_target_pairs={{0,8},{1,17},{2,10},{3,19},{4,12},{5,21},{6,14},{7,23},{8,0},{9,25... | collective-permute-start | bytes 5308424 | tf_op jit(solution)/shard_map/ppermute | solution.py:52
  89.8 15.7 %collective-permute-start.15 = (bf16[16,2,96,768]{3,2,1,0:T(8,128)(2,1)S(1)}, bf16[16,2,96,768]{3,2,1,0:T(8,128)(2,1)S(1)}, u32[]{:S(2)}, u32[]{:S(2)}) collective-permute-start(bf16[16,2,96,768]{3,2,1,0:T(8,128)(2,1)S(1)} %get-tuple-element.201), channel_id=1, source_target_pairs={{0,1},{1,0},{2,3},{3,2},{4,5},{5,4},{6,7},{7,6},{8,9},{9,8},{10,11... | collective-permute-start | bytes 14155784 | tf_op jit(solution)/shard_map/ppermute | solution.py:52
  91.5 22.5 %collective-permute-start.18 = (bf16[2,96,768]{2,1,0:T(8,128)(2,1)S(1)}, bf16[2,96,768]{2,1,0:T(8,128)(2,1)S(1)}, u32[]{:S(2)}, u32[]{:S(2)}) collective-permute-start(bf16[2,96,768]{2,1,0:T(8,128)(2,1)S(1)} %get-tuple-element.200.refs_4_), channel_id=1, source_target_pairs={{0,2},{1,3},{2,0},{3,1},{4,6},{5,7},{6,4},{7,5},{8,10},{9,11},{10,... | collective-permute-start | bytes 884744 | tf_op jit(solution)/shard_map/ppermute | solution.py:52
  97.6 23.4 %collective-permute-start.19 = (bf16[2,96,768]{2,1,0:T(8,128)(2,1)S(1)}, bf16[2,96,768]{2,1,0:T(8,128)(2,1)S(1)}, u32[]{:S(2)}, u32[]{:S(2)}) collective-permute-start(bf16[2,96,768]{2,1,0:T(8,128)(2,1)S(1)} %get-tuple-element.200.refs_4_), channel_id=1, source_target_pairs={{0,4},{1,5},{2,6},{3,7},{4,0},{5,1},{6,2},{7,3},{8,12},{9,13},{10,... | collective-permute-start | bytes 884744 | tf_op jit(solution)/shard_map/ppermute | solution.py:52
  98.6 22.4 %collective-permute-start.20 = (bf16[2,96,768]{2,1,0:T(8,128)(2,1)S(1)}, bf16[2,96,768]{2,1,0:T(8,128)(2,1)S(1)}, u32[]{:S(2)}, u32[]{:S(2)}) collective-permute-start(bf16[2,96,768]{2,1,0:T(8,128)(2,1)S(1)} %get-tuple-element.200.refs_4_), channel_id=1, source_target_pairs={{0,6},{1,7},{2,4},{3,5},{4,2},{5,3},{6,0},{7,1},{8,14},{9,15},{10,... | collective-permute-start | bytes 884744 | tf_op jit(solution)/shard_map/ppermute | solution.py:52
  103.9 22.6 %collective-permute-start.17 = (bf16[2,3,2,96,768]{4,3,2,1,0:T(8,128)(2,1)S(1)}, bf16[2,3,2,96,768]{4,3,2,1,0:T(8,128)(2,1)S(1)}, u32[]{:S(2)}, u32[]{:S(2)}) collective-permute-start(bf16[2,3,2,96,768]{4,3,2,1,0:T(8,128)(2,1)S(1)} %get-tuple-element.207.refs_3_.refs_2_), channel_id=1, source_target_pairs={{0,8},{1,17},{2,10},{3,19},{4,12},{5,21},{6,14},{7,23},{8,0},{9,25... | collective-permute-start | bytes 5308424 | tf_op jit(solution)/shard_map/ppermute | solution.py:52
  128.0 16.9 %collective-permute-start.21 = (bf16[16,2,96,768]{3,2,1,0:T(8,128)(2,1)S(1)}, bf16[16,2,96,768]{3,2,1,0:T(8,128)(2,1)S(1)}, u32[]{:S(2)}, u32[]{:S(2)}) collective-permute-start(bf16[16,2,96,768]{3,2,1,0:T(8,128)(2,1)S(1)} %get-tuple-element.211), channel_id=1, source_target_pairs={{0,1},{1,0},{2,3},{3,2},{4,5},{5,4},{6,7},{7,6},{8,9},{9,8},{10,11... | collective-permute-start | bytes 14155784 | tf_op jit(solution)/shard_map/ppermute | solution.py:52
  129.6 37.5 %collective-permute-start.24 = (bf16[1,96,768]{2,1,0:T(8,128)(2,1)}, bf16[1,96,768]{2,1,0:T(8,128)(2,1)}, u32[]{:S(2)}, u32[]{:S(2)}) collective-permute-start(bf16[1,96,768]{2,1,0:T(8,128)(2,1)} %get-tuple-element.210.refs_5_), channel_id=1, source_target_pairs={{0,2},{1,3},{2,0},{3,1},{4,6},{5,7},{6,4},{7,5},{8,10},{9,11},{10,... | collective-permute-start | bytes 442376 | tf_op jit(solution)/shard_map/ppermute | solution.py:52
  135.8 31.4 %collective-permute-start.25 = (bf16[1,96,768]{2,1,0:T(8,128)(2,1)}, bf16[1,96,768]{2,1,0:T(8,128)(2,1)}, u32[]{:S(2)}, u32[]{:S(2)}) collective-permute-start(bf16[1,96,768]{2,1,0:T(8,128)(2,1)} %get-tuple-element.210.refs_5_), channel_id=1, source_target_pairs={{0,4},{1,5},{2,6},{3,7},{4,0},{5,1},{6,2},{7,3},{8,12},{9,13},{10,... | collective-permute-start | bytes 442376 | tf_op jit(solution)/shard_map/ppermute | solution.py:52
  136.8 30.4 %collective-permute-start.26 = (bf16[1,96,768]{2,1,0:T(8,128)(2,1)}, bf16[1,96,768]{2,1,0:T(8,128)(2,1)}, u32[]{:S(2)}, u32[]{:S(2)}) collective-permute-start(bf16[1,96,768]{2,1,0:T(8,128)(2,1)} %get-tuple-element.210.refs_5_), channel_id=1, source_target_pairs={{0,6},{1,7},{2,4},{3,5},{4,2},{5,3},{6,0},{7,1},{8,14},{9,15},{10,... | collective-permute-start | bytes 442376 | tf_op jit(solution)/shard_map/ppermute | solution.py:52
  143.3 25.5 %collective-permute-start.23 = (bf16[2,3,2,96,768]{4,3,2,1,0:T(8,128)(2,1)}, bf16[2,3,2,96,768]{4,3,2,1,0:T(8,128)(2,1)}, u32[]{:S(2)}, u32[]{:S(2)}) collective-permute-start(bf16[2,3,2,96,768]{4,3,2,1,0:T(8,128)(2,1)} %get-tuple-element.222.refs_2_), channel_id=1, source_target_pairs={{0,8},{1,17},{2,10},{3,19},{4,12},{5,21},{6,14},{7,23},{8,0},{9,25... | collective-permute-start | bytes 5308424 | tf_op jit(solution)/shard_map/ppermute | solution.py:52
  196.2 28.0 %collective-permute-start.31 = (bf16[3,256,768]{2,1,0:T(8,128)(2,1)}, bf16[3,256,768]{2,1,0:T(8,128)(2,1)}, u32[]{:S(2)}, u32[]{:S(2)}) collective-permute-start(bf16[3,256,768]{2,1,0:T(8,128)(2,1)} %get-tuple-element.195.refs_1_.refs_3_), channel_id=1, source_target_pairs={{0,1},{1,0},{2,3},{3,2},{4,5},{5,4},{6,7},{7,6},{8,9},{9,8},{10,11... | collective-permute-start | bytes 3538952 | tf_op jit(solution)/shard_map/ppermute | solution.py:52
  196.8 27.5 %collective-permute-start.32 = (bf16[256,3072]{1,0:T(8,128)(2,1)}, bf16[256,3072]{1,0:T(8,128)(2,1)}, u32[]{:S(2)}, u32[]{:S(2)}) collective-permute-start(bf16[256,3072]{1,0:T(8,128)(2,1)} %get-tuple-element.205.refs_4_.refs_1_), channel_id=1, source_target_pairs={{0,1},{1,0},{2,3},{3,2},{4,5},{5,4},{6,7},{7,6},{8,9},{9,8},{10,11... | collective-permute-start | bytes 4718600 | tf_op jit(solution)/shard_map/ppermute | solution.py:52
  196.8 27.4 %collective-permute-start.33 = (bf16[3,256,768]{2,1,0:T(8,128)(2,1)}, bf16[3,256,768]{2,1,0:T(8,128)(2,1)}, u32[]{:S(2)}, u32[]{:S(2)}) collective-permute-start(bf16[3,256,768]{2,1,0:T(8,128)(2,1)} %get-tuple-element.220.refs_1_.refs_3_), channel_id=1, source_target_pairs={{0,1},{1,0},{2,3},{3,2},{4,5},{5,4},{6,7},{7,6},{8,9},{9,8},{10,11... | collective-permute-start | bytes 3538952 | tf_op jit(solution)/shard_map/ppermute | solution.py:52
  197.3 27.0 %collective-permute-start.34 = (bf16[256,3072]{1,0:T(8,128)(2,1)}, bf16[256,3072]{1,0:T(8,128)(2,1)}, u32[]{:S(2)}, u32[]{:S(2)}) collective-permute-start(bf16[256,3072]{1,0:T(8,128)(2,1)} %get-tuple-element.229.refs_4_.refs_1_), channel_id=1, source_target_pairs={{0,1},{1,0},{2,3},{3,2},{4,5},{5,4},{6,7},{7,6},{8,9},{9,8},{10,11... | collective-permute-start | bytes 4718600 | tf_op jit(solution)/shard_map/ppermute | solution.py:52
  231.6 17.3 %collective-permute-start.35 = (bf16[256,1152]{1,0:T(8,128)(2,1)S(1)}, bf16[256,1152]{1,0:T(8,128)(2,1)S(1)}, u32[]{:S(2)}, u32[]{:S(2)}) collective-permute-start(bf16[256,1152]{1,0:T(8,128)(2,1)S(1)} %get-tuple-element.247), channel_id=1, source_target_pairs={{0,1},{1,0},{2,3},{3,2},{4,5},{5,4},{6,7},{7,6},{8,9},{9,8},{10,11... | collective-permute-start | bytes 1769480 | tf_op jit(solution)/shard_map/ppermute | solution.py:52
  241.3 29.2 %collective-permute-start.37 = (bf16[2,4,2,2,96,384]{5,4,3,2,1,0:T(8,128)(2,1)}, bf16[2,4,2,2,96,384]{5,4,3,2,1,0:T(8,128)(2,1)}, u32[]{:S(2)}, u32[]{:S(2)}) collective-permute-start(bf16[2,4,2,2,96,384]{5,4,3,2,1,0:T(8,128)(2,1)} %get-tuple-element.252.refs_5_), channel_id=1, source_target_pairs={{0,8},{1,17},{2,10},{3,19},{4,12},{5,21},{6,14},{7,23},{8,0},{9,25... | collective-permute-start | bytes 7077896 | tf_op jit(solution)/shard_map/ppermute | solution.py:52
  256.0 56.4 %collective-permute-start.43 = (bf16[2,4,2,2,96,384]{5,4,3,2,1,0:T(8,128)(2,1)}, bf16[2,4,2,2,96,384]{5,4,3,2,1,0:T(8,128)(2,1)}, u32[]{:S(2)}, u32[]{:S(2)}) collective-permute-start(bf16[2,4,2,2,96,384]{5,4,3,2,1,0:T(8,128)(2,1)} %get-tuple-element.255.refs_10_), channel_id=1, source_target_pairs={{0,8},{1,17},{2,10},{3,19},{4,12},{5,21},{6,14},{7,23},{8,0},{9,25... | collective-permute-start | bytes 7077896 | tf_op jit(solution)/shard_map/ppermute | solution.py:52
  273.9 29.0 %collective-permute-start.38 = (bf16[4,2,2,96,384]{4,3,2,1,0:T(8,128)(2,1)S(1)}, bf16[4,2,2,96,384]{4,3,2,1,0:T(8,128)(2,1)S(1)}, u32[]{:S(2)}, u32[]{:S(2)}) collective-permute-start(bf16[4,2,2,96,384]{4,3,2,1,0:T(8,128)(2,1)S(1)} %get-tuple-element.262.refs_5_), channel_id=1, source_target_pairs={{0,16},{1,9},{2,18},{3,11},{4,20},{5,13},{6,22},{7,15},{8,24},{9,1... | collective-permute-start | bytes 3538952 | tf_op jit(solution)/shard_map/ppermute | solution.py:52
  284.7 78.5 %collective-permute-start.49 = (bf16[2,4,2,2,96,384]{5,4,3,2,1,0:T(8,128)(2,1)}, bf16[2,4,2,2,96,384]{5,4,3,2,1,0:T(8,128)(2,1)}, u32[]{:S(2)}, u32[]{:S(2)}) collective-permute-start(bf16[2,4,2,2,96,384]{5,4,3,2,1,0:T(8,128)(2,1)} %get-tuple-element.265.refs_3_), channel_id=1, source_target_pairs={{0,8},{1,17},{2,10},{3,19},{4,12},{5,21},{6,14},{7,23},{8,0},{9,25... | collective-permute-start | bytes 7077896 | tf_op jit(solution)/shard_map/ppermute | solution.py:52
  303.7 18.0 %collective-permute-start.40 = (bf16[2,2,96,384]{3,2,1,0:T(8,128)(2,1)S(1)}, bf16[2,2,96,384]{3,2,1,0:T(8,128)(2,1)S(1)}, u32[]{:S(2)}, u32[]{:S(2)}) collective-permute-start(bf16[2,2,96,384]{3,2,1,0:T(8,128)(2,1)S(1)} %get-tuple-element.267), channel_id=1, source_target_pairs={{0,2},{1,3},{2,0},{3,1},{4,6},{5,7},{6,4},{7,5},{8,10},{9,11},{10,... | collective-permute-start | bytes 884744 | tf_op jit(solution)/shard_map/ppermute | solution.py:52
  309.9 23.5 %collective-permute-start.41 = (bf16[2,2,96,384]{3,2,1,0:T(8,128)(2,1)S(1)}, bf16[2,2,96,384]{3,2,1,0:T(8,128)(2,1)S(1)}, u32[]{:S(2)}, u32[]{:S(2)}) collective-permute-start(bf16[2,2,96,384]{3,2,1,0:T(8,128)(2,1)S(1)} %get-tuple-element.268), channel_id=1, source_target_pairs={{0,4},{1,5},{2,6},{3,7},{4,0},{5,1},{6,2},{7,3},{8,12},{9,13},{10,... | collective-permute-start | bytes 884744 | tf_op jit(solution)/shard_map/ppermute | solution.py:52
  310.9 22.4 %collective-permute-start.42 = (bf16[2,2,96,384]{3,2,1,0:T(8,128)(2,1)S(1)}, bf16[2,2,96,384]{3,2,1,0:T(8,128)(2,1)S(1)}, u32[]{:S(2)}, u32[]{:S(2)}) collective-permute-start(bf16[2,2,96,384]{3,2,1,0:T(8,128)(2,1)S(1)} %get-tuple-element.269), channel_id=1, source_target_pairs={{0,6},{1,7},{2,4},{3,5},{4,2},{5,3},{6,0},{7,1},{8,14},{9,15},{10,... | collective-permute-start | bytes 884744 | tf_op jit(solution)/shard_map/ppermute | solution.py:52
  316.9 36.6 %collective-permute-start.44 = (bf16[4,2,2,96,384]{4,3,2,1,0:T(8,128)(2,1)}, bf16[4,2,2,96,384]{4,3,2,1,0:T(8,128)(2,1)}, u32[]{:S(2)}, u32[]{:S(2)}) collective-permute-start(bf16[4,2,2,96,384]{4,3,2,1,0:T(8,128)(2,1)} %get-tuple-element.271.refs_5_), channel_id=1, source_target_pairs={{0,16},{1,9},{2,18},{3,11},{4,20},{5,13},{6,22},{7,15},{8,24},{9,1... | collective-permute-start | bytes 3538952 | tf_op jit(solution)/shard_map/ppermute | solution.py:52
  352.8 47.2 %collective-permute-start.54 = (bf16[2,4,2,2,96,384]{5,4,3,2,1,0:T(8,128)(2,1)S(1)}, bf16[2,4,2,2,96,384]{5,4,3,2,1,0:T(8,128)(2,1)S(1)}, u32[]{:S(2)}, u32[]{:S(2)}) collective-permute-start(bf16[2,4,2,2,96,384]{5,4,3,2,1,0:T(8,128)(2,1)S(1)} %get-tuple-element.281.refs_3_), channel_id=1, source_target_pairs={{0,8},{1,17},{2,10},{3,19},{4,12},{5,21},{6,14},{7,23},{8,0},{9,25... | collective-permute-start | bytes 7077896 | tf_op jit(solution)/shard_map/ppermute | solution.py:52
  355.7 18.8 %collective-permute-start.46 = (bf16[2,2,96,384]{3,2,1,0:T(8,128)(2,1)S(1)}, bf16[2,2,96,384]{3,2,1,0:T(8,128)(2,1)S(1)}, u32[]{:S(2)}, u32[]{:S(2)}) collective-permute-start(bf16[2,2,96,384]{3,2,1,0:T(8,128)(2,1)S(1)} %get-tuple-element.283), channel_id=1, source_target_pairs={{0,2},{1,3},{2,0},{3,1},{4,6},{5,7},{6,4},{7,5},{8,10},{9,11},{10,... | collective-permute-start | bytes 884744 | tf_op jit(solution)/shard_map/ppermute | solution.py:52
  360.8 23.5 %collective-permute-start.47 = (bf16[2,2,96,384]{3,2,1,0:T(8,128)(2,1)S(1)}, bf16[2,2,96,384]{3,2,1,0:T(8,128)(2,1)S(1)}, u32[]{:S(2)}, u32[]{:S(2)}) collective-permute-start(bf16[2,2,96,384]{3,2,1,0:T(8,128)(2,1)S(1)} %get-tuple-element.284), channel_id=1, source_target_pairs={{0,4},{1,5},{2,6},{3,7},{4,0},{5,1},{6,2},{7,3},{8,12},{9,13},{10,... | collective-permute-start | bytes 884744 | tf_op jit(solution)/shard_map/ppermute | solution.py:52
  361.8 22.4 %collective-permute-start.48 = (bf16[2,2,96,384]{3,2,1,0:T(8,128)(2,1)S(1)}, bf16[2,2,96,384]{3,2,1,0:T(8,128)(2,1)S(1)}, u32[]{:S(2)}, u32[]{:S(2)}) collective-permute-start(bf16[2,2,96,384]{3,2,1,0:T(8,128)(2,1)S(1)} %get-tuple-element.285), channel_id=1, source_target_pairs={{0,6},{1,7},{2,4},{3,5},{4,2},{5,3},{6,0},{7,1},{8,14},{9,15},{10,... | collective-permute-start | bytes 884744 | tf_op jit(solution)/shard_map/ppermute | solution.py:52
  366.6 27.2 %collective-permute-start.50 = (bf16[4,2,2,96,384]{4,3,2,1,0:T(8,128)(2,1)S(1)}, bf16[4,2,2,96,384]{4,3,2,1,0:T(8,128)(2,1)S(1)}, u32[]{:S(2)}, u32[]{:S(2)}) collective-permute-start(bf16[4,2,2,96,384]{4,3,2,1,0:T(8,128)(2,1)S(1)} %get-tuple-element.287.refs_5_), channel_id=1, source_target_pairs={{0,16},{1,9},{2,18},{3,11},{4,20},{5,13},{6,22},{7,15},{8,24},{9,1... | collective-permute-start | bytes 3538952 | tf_op jit(solution)/shard_map/ppermute | solution.py:52
  394.7 28.4 %collective-permute-start.51 = (bf16[2,2,96,384]{3,2,1,0:T(8,128)(2,1)S(1)}, bf16[2,2,96,384]{3,2,1,0:T(8,128)(2,1)S(1)}, u32[]{:S(2)}, u32[]{:S(2)}) collective-permute-start(bf16[2,2,96,384]{3,2,1,0:T(8,128)(2,1)S(1)} %get-tuple-element.291), channel_id=1, source_target_pairs={{0,2},{1,3},{2,0},{3,1},{4,6},{5,7},{6,4},{7,5},{8,10},{9,11},{10,... | collective-permute-start | bytes 884744 | tf_op jit(solution)/shard_map/ppermute | solution.py:52
  397.5 27.2 %collective-permute-start.52 = (bf16[2,2,96,384]{3,2,1,0:T(8,128)(2,1)S(1)}, bf16[2,2,96,384]{3,2,1,0:T(8,128)(2,1)S(1)}, u32[]{:S(2)}, u32[]{:S(2)}) collective-permute-start(bf16[2,2,96,384]{3,2,1,0:T(8,128)(2,1)S(1)} %get-tuple-element.292), channel_id=1, source_target_pairs={{0,4},{1,5},{2,6},{3,7},{4,0},{5,1},{6,2},{7,3},{8,12},{9,13},{10,... | collective-permute-start | bytes 884744 | tf_op jit(solution)/shard_map/ppermute | solution.py:52
  398.6 26.1 %collective-permute-start.53 = (bf16[2,2,96,384]{3,2,1,0:T(8,128)(2,1)S(1)}, bf16[2,2,96,384]{3,2,1,0:T(8,128)(2,1)S(1)}, u32[]{:S(2)}, u32[]{:S(2)}) collective-permute-start(bf16[2,2,96,384]{3,2,1,0:T(8,128)(2,1)S(1)} %get-tuple-element.293), channel_id=1, source_target_pairs={{0,6},{1,7},{2,4},{3,5},{4,2},{5,3},{6,0},{7,1},{8,14},{9,15},{10,... | collective-permute-start | bytes 884744 | tf_op jit(solution)/shard_map/ppermute | solution.py:52
  401.7 23.8 %collective-permute-start.56 = (bf16[4,2,2,96,384]{4,3,2,1,0:T(8,128)(2,1)S(1)}, bf16[4,2,2,96,384]{4,3,2,1,0:T(8,128)(2,1)S(1)}, u32[]{:S(2)}, u32[]{:S(2)}) collective-permute-start(bf16[4,2,2,96,384]{4,3,2,1,0:T(8,128)(2,1)S(1)} %get-tuple-element.296.refs_2_), channel_id=1, source_target_pairs={{0,16},{1,9},{2,18},{3,11},{4,20},{5,13},{6,22},{7,15},{8,24},{9,1... | collective-permute-start | bytes 3538952 | tf_op jit(solution)/shard_map/ppermute | solution.py:52
  403.7 17.4 %collective-permute-start.55 = (bf16[2,2,96,384]{3,2,1,0:T(8,128)(2,1)S(1)}, bf16[2,2,96,384]{3,2,1,0:T(8,128)(2,1)S(1)}, u32[]{:S(2)}, u32[]{:S(2)}) collective-permute-start(bf16[2,2,96,384]{3,2,1,0:T(8,128)(2,1)S(1)} %get-tuple-element.297), channel_id=1, source_target_pairs={{0,16},{1,9},{2,18},{3,11},{4,20},{5,13},{6,22},{7,15},{8,24},{9,1... | collective-permute-start | bytes 884744 | tf_op jit(solution)/shard_map/ppermute | solution.py:52
  426.3 22.4 %collective-permute-start.57 = (bf16[2,2,96,384]{3,2,1,0:T(8,128)(2,1)S(1)}, bf16[2,2,96,384]{3,2,1,0:T(8,128)(2,1)S(1)}, u32[]{:S(2)}, u32[]{:S(2)}) collective-permute-start(bf16[2,2,96,384]{3,2,1,0:T(8,128)(2,1)S(1)} %get-tuple-element.305), channel_id=1, source_target_pairs={{0,2},{1,3},{2,0},{3,1},{4,6},{5,7},{6,4},{7,5},{8,10},{9,11},{10,... | collective-permute-start | bytes 884744 | tf_op jit(solution)/shard_map/ppermute | solution.py:52
  427.5 23.4 %collective-permute-start.58 = (bf16[2,2,96,384]{3,2,1,0:T(8,128)(2,1)S(1)}, bf16[2,2,96,384]{3,2,1,0:T(8,128)(2,1)S(1)}, u32[]{:S(2)}, u32[]{:S(2)}) collective-permute-start(bf16[2,2,96,384]{3,2,1,0:T(8,128)(2,1)S(1)} %get-tuple-element.306), channel_id=1, source_target_pairs={{0,4},{1,5},{2,6},{3,7},{4,0},{5,1},{6,2},{7,3},{8,12},{9,13},{10,... | collective-permute-start | bytes 884744 | tf_op jit(solution)/shard_map/ppermute | solution.py:52
  429.4 21.6 %collective-permute-start.59 = (bf16[2,2,96,384]{3,2,1,0:T(8,128)(2,1)S(1)}, bf16[2,2,96,384]{3,2,1,0:T(8,128)(2,1)S(1)}, u32[]{:S(2)}, u32[]{:S(2)}) collective-permute-start(bf16[2,2,96,384]{3,2,1,0:T(8,128)(2,1)S(1)} %get-tuple-element.307), channel_id=1, source_target_pairs={{0,6},{1,7},{2,4},{3,5},{4,2},{5,3},{6,0},{7,1},{8,14},{9,15},{10,... | collective-permute-start | bytes 884744 | tf_op jit(solution)/shard_map/ppermute | solution.py:52
  432.4 13.5 %collective-permute-start.61 = (bf16[2,2,96,384]{3,2,1,0:T(8,128)(2,1)S(1)}, bf16[2,2,96,384]{3,2,1,0:T(8,128)(2,1)S(1)}, u32[]{:S(2)}, u32[]{:S(2)}) collective-permute-start(bf16[2,2,96,384]{3,2,1,0:T(8,128)(2,1)S(1)} %get-tuple-element.311), channel_id=1, source_target_pairs={{0,16},{1,9},{2,18},{3,11},{4,20},{5,13},{6,22},{7,15},{8,24},{9,1... | collective-permute-start | bytes 884744 | tf_op jit(solution)/shard_map/ppermute | solution.py:52
  445.1 14.6 %collective-permute-start.73 = (bf16[4,2,2,96,384]{4,3,2,1,0:T(8,128)(2,1)S(1)}, bf16[4,2,2,96,384]{4,3,2,1,0:T(8,128)(2,1)S(1)}, u32[]{:S(2)}, u32[]{:S(2)}) collective-permute-start(bf16[4,2,2,96,384]{4,3,2,1,0:T(8,128)(2,1)S(1)} %get-tuple-element.323.refs_24_), channel_id=1, source_target_pairs={{0,1},{1,0},{2,3},{3,2},{4,5},{5,4},{6,7},{7,6},{8,9},{9,8},{10,11... | collective-permute-start | bytes 3538952 | tf_op jit(solution)/shard_map/ppermute | solution.py:52
  469.0 18.5 %collective-permute-start.77 = (bf16[4,2,2,96,384]{4,3,2,1,0:T(8,128)(2,1)S(1)}, bf16[4,2,2,96,384]{4,3,2,1,0:T(8,128)(2,1)}, u32[]{:S(2)}, u32[]{:S(2)}) collective-permute-start(bf16[4,2,2,96,384]{4,3,2,1,0:T(8,128)(2,1)S(1)} %get-tuple-element.329.refs_22_), channel_id=1, source_target_pairs={{0,1},{1,0},{2,3},{3,2},{4,5},{5,4},{6,7},{7,6},{8,9},{9,8},{10,11... | collective-permute-start | bytes 3538952 | tf_op jit(solution)/shard_map/ppermute | solution.py:52
  (93 other events, 1201.4 us)

commit v6 on v5

--- a/solution.py
+++ b/solution.py
@@ -483,8 +483,7 @@
         start = 0
         if more:
             quarters[:, rows:] = jnp.zeros((sum(counts), more, D), low_type)
-            count, width = norm_params.shape
-            quarters[0, rows : rows + count, :width] = refs[len(used)][...].astype(low_type)
+            quarters[0, rows:, :SEQ_LEN] = refs[len(used)][...].astype(low_type)
         for (kind, layer), own, count in zip(chunks, owns, counts):
             if kind == "attend":
                 for part in range(3):
@@ -689,20 +688,19 @@
     )
 
 
-def norm_columns(near, other, norm_params, where, after=()):
-    count, width = norm_params.shape
-
+def norm_columns(near, other, padded, width, where, after=()):
     def kernel(where, own_ref, near_ref, other_ref, out_ref):
         for shard in range(8):
             side = (shard % 2) ^ where[1]
             chip = (shard // 2) ^ where[0]
-            here = near_ref[jnp.maximum(chip, 1) - 1, :count, :width].astype(wide_type)
+            here = near_ref[jnp.maximum(chip, 1) - 1].astype(wide_type)
             here = jnp.where(chip == 0, own_ref[...].astype(low_type).astype(wide_type), here)
-            there = other_ref[chip, :count, :width].astype(wide_type)
-            out_ref[:, shard * width : (shard + 1) * width] = jnp.where(side == 0, here, there)
-
-    args = (norm_params, near, other)
-    outs = [((count, 8 * width), wide_type)]
+            there = other_ref[chip].astype(wide_type)
+            values = jnp.where(side == 0, here, there)
+            out_ref[:, shard * width : (shard + 1) * width] = values[:8, :width]
+
+    args = (padded, near, other)
+    outs = [((8, 8 * width), wide_type)]
     specs = [full(outs[0][0])]
     return run(kernel, "norm_columns", where, args, fulls(args), outs, specs, after=after)
 
@@ -1119,6 +1117,8 @@
 def forward_neighbours(hidden, states, norm_params, chain):
     layer_count = states[0].shape[0]
     norm_params = norm_params.reshape(8, -1)
+    width = norm_params.shape[1]
+    padded = jnp.pad(norm_params, ((0, NORM_ROWS - 8), (0, SEQ_LEN - width)))
     rows = states[0].shape[1]
     kept_list = [None] * layer_count
     weight_list = [()] * layer_count
@@ -1132,7 +1132,7 @@
     norms = []
 
     def start(at):
-        more = norm_params if at == 0 else None
+        more = padded if at == 0 else None
         *owns[at], quarters = chain(own_chunks, groups[at], states, more)
         started[at] = [send(quarters, move) for move in (Z_ONE, Z_TWO, Z_THREE)]
 
@@ -1140,11 +1140,8 @@
         near[at], rest = chain(stack_chips, started[at], rows)
         across[at] = send(near[at], FLIP_SECOND)
         if at == 0:
-            count, width = norm_params.shape
-            own = jnp.pad(
-                norm_params.astype(low_type), ((0, NORM_ROWS - count), (0, SEQ_LEN - width))
-            )
-            other_rest = send(jnp.concatenate([own[None], rest]), FLIP_CORE)
+            whole = jnp.concatenate([padded.astype(low_type)[None], rest])
+            other_rest = send(whole, FLIP_CORE)
             norms.extend((rest, other_rest))
 
     def spread_on(at):
@@ -1182,7 +1179,7 @@
     start(0)
     spread(0)
     start(1)
-    norms[:] = chain(norm_columns, *norms, norm_params)
+    norms[:] = chain(norm_columns, *norms, padded, width)
     spread_on(0)
     for at in range(len(groups)):
         if at < last:
@@ -1273,10 +1270,15 @@
         )
         sums[layer]["wide"] = (held, send(sent, FLIP_FIRST))
 
+    def product_down(layer, made):
+        kept = kept_list[layer]
+        left, left_other = kept["product"], kept["product_other"]
+        made["down"] = chain(grad_down, left, left_other, made["branch"], made["feed_other"])
+
     def product_rest(layer, made):
         kept = kept_list[layer]
         other = made["feed_other"]
-        filled = chain(grad_down, kept["product"], kept["product_other"], made["branch"], other)
+        filled = made["down"]
         qkv, qkv_other = made["qkv"], made["qkv_other"]
         trio, trio_other = kept["trio"], kept["trio_other"]
         sent, held = chain(
@@ -1326,15 +1328,18 @@
     layer = layer_count - 1
     grad = attention(layer, made)
     product_wide(layer, made)
+    product_down(layer, made)
     product_rest(layer, made)
     while layer > 0:
         made = feed(layer - 1, grad)
         halves(layer, "wide")
         product_wide(layer - 1, made)
+        grad = attention(layer - 1, made)
+        product_down(layer - 1, made)
+        chain.wait(made["qkv_other"])
         parts = chips(layer, "wide")
         halves(layer, "rest")
         wide = total(parts)
-        grad = attention(layer - 1, made)
         product_rest(layer - 1, made)
         parts = chips(layer, "rest")
         halves(layer - 1, "wide")

time: 525 us -> 520 us (level); the launches traced: 516 us -> 516 us
  Pallas kernels: 221 us -> 232 us
  starting transfers between devices: 109 us -> 101 us
    pallas_call x68, Pallas kernels: 221 us -> 232 us  [run(): pl.pallas_call(body_of, out_shape=[jax.ShapeDtypeStruct(shape, dtype) for...]
    ppermute x78, starting transfers between devices: 109 us -> 101 us  [send(): return lax.ppermute(values, both_axes, pairs)]
  transfers between devices with their start and end apart: 78 -> 78, of which waited for: 31 -> 32; matrix products, arithmetic and copies ran while one was open for 1% -> 1% of each run, Pallas kernels for 36% -> 38%
where the time goes in v6:
time: 520 us; the launch traced here: 516 us
  Pallas kernels  232 us (45%)
  waiting for transfers between devices  166 us (32%)
  starting transfers between devices  101 us (19%)
  local copies, waits for them, and re-layouts  8.54 us (2%)
    pallas_call x68, Pallas kernels, run(): pl.pallas_call(body_of, out_shape=[jax.ShapeDtypeStruct(shape, dtype) for...  232 us
    ppermute x78, waiting for transfers between devices, send(): return lax.ppermute(values, both_axes, pairs)  166 us
    ppermute x78, starting transfers between devices, send(): return lax.ppermute(values, both_axes, pairs)  101 us
  transfers between devices with their start and end apart: 78, of which 32 were waited for; matrix products, arithmetic and copies ran while one was open for 1% of the time, Pallas kernels for 38%

profile of v6, /device:TPU:0, one launch (start us, length us, event | category | flops | bytes accessed | tf_op | source)
XLA Modules:
  0.0 516.4 jit_solution(16600646523376278011)
XLA Ops:
  4.6 3.1 collective-permute-start
  10.3 4.5 collective-permute-done.refs_1_
  14.8 8.5 %collective-permute-done.1.refs_2_ = bf16[1,112,768]{2,1,0:T(8,128)(2,1)S(1)} collective-permute-done((bf16[1,112,768]{2,1,0:T(8,128)(2,1)S(1)}, bf16[1,112,768]{2,1,0:T(8,128)(2,1)S(1)}, u32[]{:S(2)}, u32[]{:S(2)}) %collective-permute-start.1) | collective-permute-done | bytes 172064 | tf_op jit(solution)/shard_map/ppermute | solution.py:52
  32.2 6.1 %collective-permute-done.3.refs_2_ = bf16[3,1,96,768]{3,2,1,0:T(8,128)(2,1)S(1)} collective-permute-done((bf16[3,1,96,768]{3,2,1,0:T(8,128)(2,1)S(1)}, bf16[3,1,96,768]{3,2,1,0:T(8,128)(2,1)S(1)}, u32[]{:S(2)}, u32[]{:S(2)}) %collective-permute-start.3) | collective-permute-done | bytes 442400 | tf_op jit(solution)/shard_map/ppermute | solution.py:52
  41.1 9.9 %collective-permute-done.7.refs_2_ = bf16[2,96,768]{2,1,0:T(8,128)(2,1)S(1)} collective-permute-done((bf16[2,96,768]{2,1,0:T(8,128)(2,1)S(1)}, bf16[2,96,768]{2,1,0:T(8,128)(2,1)S(1)}, u32[]{:S(2)}, u32[]{:S(2)}) %collective-permute-start.7) | collective-permute-done | bytes 294944 | tf_op jit(solution)/shard_map/ppermute | solution.py:52
  56.1 6.2 %collective-permute-start.12 = (bf16[2,96,768]{2,1,0:T(8,128)(2,1)S(1)}, bf16[2,96,768]{2,1,0:T(8,128)(2,1)S(1)}, u32[]{:S(2)}, u32[]{:S(2)}) collective-permute-start(bf16[2,96,768]{2,1,0:T(8,128)(2,1)S(1)} %get-tuple-element.188.refs_4_), channel_id=1, source_target_pairs={{0,2},{1,3},{2,0},{3,1},{4,6},{5,7},{6,4},{7,5},{8,10},{9,11},{10,... | collective-permute-start | bytes 884744 | tf_op jit(solution)/shard_map/ppermute | solution.py:52
  70.0 7.8 %attend_forward.2 = (bf16[3,256,768]{2,1,0:T(8,128)(2,1)}, bf16[256,2304]{1,0:T(8,128)(2,1)S(1)}, f32[256,128]{1,0:T(8,128)S(1)}, f32[256,768]{1,0:T(8,128)S(1)}, f32[256,768]{1,0:T(8,128)S(1)}) custom-call(s32[4]{0:T(128)S(1)} %pad_add_fusion.refs_0_, f32[256,768]{1,0:T(8,128)S(1)} %convert_select_fusion.refs_1_, ...), custom_call_target="tpu_custom_call" | custom-call | flops 67499999232 | bytes 1000 | tf_op jit(solution)/shard_map/attend_forward/pallas_call | solution.py:104
  77.8 7.9 %collective-permute-done.13.refs_2_ = bf16[2,96,768]{2,1,0:T(8,128)(2,1)S(1)} collective-permute-done((bf16[2,96,768]{2,1,0:T(8,128)(2,1)S(1)}, bf16[2,96,768]{2,1,0:T(8,128)(2,1)S(1)}, u32[]{:S(2)}, u32[]{:S(2)}) %collective-permute-start.13) | collective-permute-done | bytes 294944 | tf_op jit(solution)/shard_map/ppermute | solution.py:52
  91.5 6.1 %collective-permute-start.18 = (bf16[2,96,768]{2,1,0:T(8,128)(2,1)S(1)}, bf16[2,96,768]{2,1,0:T(8,128)(2,1)S(1)}, u32[]{:S(2)}, u32[]{:S(2)}) collective-permute-start(bf16[2,96,768]{2,1,0:T(8,128)(2,1)S(1)} %get-tuple-element.200.refs_4_), channel_id=1, source_target_pairs={{0,2},{1,3},{2,0},{3,1},{4,6},{5,7},{6,4},{7,5},{8,10},{9,11},{10,... | collective-permute-start | bytes 884744 | tf_op jit(solution)/shard_map/ppermute | solution.py:52
  107.4 6.6 %gate_forward.2 = (bf16[256,3072]{1,0:T(8,128)(2,1)}, bf16[2,256,3072]{2,1,0:T(8,128)(2,1)S(1)}) custom-call(s32[4]{0:T(128)S(1)} %pad_add_fusion.refs_0_, bf16[3,256,768]{2,1,0:T(8,128)(2,1)} %get-tuple-element.195.refs_1_.refs_3_, bf16[768,6144]{1,0:T(8,128)(2,1)S(1)} %assemble_gate_up.2.refs_2_.refs_3_.refs_4_.refs_6_.refs_7_, ...), custom_call_target="tpu_custom_call" | custom-call | flops 62999998464 | bytes 1000 | tf_op jit(solution)/shard_map/gate_forward/pallas_call | solution.py:104
  114.0 7.1 %collective-permute-done.19.refs_2_ = bf16[2,96,768]{2,1,0:T(8,128)(2,1)S(1)} collective-permute-done((bf16[2,96,768]{2,1,0:T(8,128)(2,1)S(1)}, bf16[2,96,768]{2,1,0:T(8,128)(2,1)S(1)}, u32[]{:S(2)}, u32[]{:S(2)}) %collective-permute-start.19) | collective-permute-done | bytes 294944 | tf_op jit(solution)/shard_map/ppermute | solution.py:52
  129.6 6.1 %collective-permute-start.24 = (bf16[1,96,768]{2,1,0:T(8,128)(2,1)}, bf16[1,96,768]{2,1,0:T(8,128)(2,1)}, u32[]{:S(2)}, u32[]{:S(2)}) collective-permute-start(bf16[1,96,768]{2,1,0:T(8,128)(2,1)} %get-tuple-element.210.refs_5_), channel_id=1, source_target_pairs={{0,2},{1,3},{2,0},{3,1},{4,6},{5,7},{6,4},{7,5},{8,10},{9,11},{10,... | collective-permute-start | bytes 442376 | tf_op jit(solution)/shard_map/ppermute | solution.py:52
  144.9 6.7 %assemble_down.2.refs_5_.refs_2_ = bf16[3072,768]{1,0:T(8,128)(2,1)S(1)} custom-call(s32[4]{0:T(128)S(1)} %pad_add_fusion.refs_0_, bf16[4,1,96,768]{3,2,1,0:T(8,128)(2,1)S(1)} %get-tuple-element.206.refs_1_, bf16[2,3,2,96,768]{4,3,2,1,0:T(8,128)(2,1)S(1)} %get-tuple-element.207.refs_3_.refs_2_, ...), custom_call_target="tpu_custom_call" | custom-call | flops 44999999488 | bytes 1000 | tf_op jit(solution)/shard_map/assemble_down/pallas_call | solution.py:104
  151.6 13.8 %assemble_attend.3 = (bf16[768,2304]{1,0:T(8,128)(2,1)S(1)}, bf16[768,768]{1,0:T(8,128)(2,1)S(1)}) custom-call(s32[4]{0:T(128)S(1)} %pad_add_fusion.refs_0_, bf16[4,1,96,768]{3,2,1,0:T(8,128)(2,1)S(1)} %get-tuple-element.208.refs_2_.refs_1_, bf16[2,3,2,96,768]{4,3,2,1,0:T(8,128)(2,1)S(1)} %get-tuple-element.207.refs_3_.refs_2_, ...), custom_call_target="tpu_custom_call" | custom-call | flops 27000000512 | bytes 1000 | tf_op jit(solution)/shard_map/assemble_attend/pallas_call | solution.py:104
  165.5 4.7 down_forward.2
  170.3 7.8 %attend_forward.3 = (bf16[3,256,768]{2,1,0:T(8,128)(2,1)}, bf16[256,2304]{1,0:T(8,128)(2,1)S(1)}, f32[256,128]{1,0:T(8,128)S(1)}, f32[256,768]{1,0:T(8,128)S(1)}, f32[256,768]{1,0:T(8,128)S(1)}) custom-call(s32[4]{0:T(128)S(1)} %pad_add_fusion.refs_0_, f32[256,768]{1,0:T(8,128)S(1)} %get-tuple-element.217.refs_1_, ...), custom_call_target="tpu_custom_call" | custom-call | flops 67499999232 | bytes 1000 | tf_op jit(solution)/shard_map/attend_forward/pallas_call | solution.py:104
  184.3 6.8 %collective-permute-done.28.refs_2_ = bf16[3,1,96,768]{3,2,1,0:T(8,128)(2,1)S(1)} collective-permute-done((bf16[3,1,96,768]{3,2,1,0:T(8,128)(2,1)S(1)}, bf16[3,1,96,768]{3,2,1,0:T(8,128)(2,1)S(1)}, u32[]{:S(2)}, u32[]{:S(2)}) %collective-permute-start.28) | collective-permute-done | bytes 442400 | tf_op jit(solution)/shard_map/ppermute | solution.py:52
  195.7 6.3 %gate_forward.3 = (bf16[256,3072]{1,0:T(8,128)(2,1)}, bf16[2,256,3072]{2,1,0:T(8,128)(2,1)S(1)}) custom-call(s32[4]{0:T(128)S(1)} %pad_add_fusion.refs_0_, bf16[3,256,768]{2,1,0:T(8,128)(2,1)} %get-tuple-element.220.refs_1_.refs_3_, bf16[768,6144]{1,0:T(8,128)(2,1)S(1)} %assemble_gate_up.3.refs_2_.refs_3_.refs_4_.refs_6_.refs_7_, ...), custom_call_target="tpu_custom_call" | custom-call | flops 62999998464 | bytes 1000 | tf_op jit(solution)/shard_map/gate_forward/pallas_call | solution.py:104
  202.0 3.2 collective-permute-done.29.refs_3_
  208.3 4.1 collective-permute-done.30.refs_4_
  212.4 6.7 %assemble_down.3.refs_2_.refs_5_ = bf16[3072,768]{1,0:T(8,128)(2,1)S(1)} custom-call(s32[4]{0:T(128)S(1)} %pad_add_fusion.refs_0_, bf16[4,1,96,768]{3,2,1,0:T(8,128)(2,1)S(1)} %get-tuple-element.230.refs_1_, bf16[2,3,1,96,768]{4,3,2,1,0:T(8,128)(2,1)S(1)} %get-tuple-element.231.refs_2_, bf16[2,3,1,96,768]{4,3,2,1,0:T(8,128)(2,1)S(1)} %collective-permute-done.29.refs_3_, ...), custom_call_target="tpu_custom_call" | custom-call | flops 44999999488 | bytes 1000 | tf_op jit(solution)/shard_map/assemble_down/pallas_call | solution.py:104
  219.2 4.4 down_forward.3
  223.6 10.9 %feed_backward.2 = (bf16[2,256,3072]{2,1,0:T(8,128)(2,1)S(1)}, bf16[256,3840]{1,0:T(8,128)(2,1)S(1)}, bf16[256,768]{1,0:T(8,128)(2,1)S(1)}, f32[256,768]{1,0:T(8...) custom-call(s32[4]{0:T(128)S(1)} %pad_add_fusion.refs_0_, ...), custom_call_target="tpu_custom_call" | custom-call | flops 117000003584 | bytes 1000 | tf_op jit(solution)/shard_map/feed_backward/pallas_call | solution.py:104
  234.8 7.3 %attend_backward.2 = (bf16[256,2304]{1,0:T(8,128)(2,1)S(1)}, bf16[256,1152]{1,0:T(8,128)(2,1)S(1)}, f32[256,768]{1,0:T(8,128)S(1)}) custom-call(s32[4]{0:T(128)S(1)} %pad_add_fusion.refs_0_, bf16[256,768]{1,0:T(8,128)(2,1)S(1)} %get-tuple-element.239.refs_1_, bf16[256,2304]{1,0:T(8,128)(2,1)S(1)} %get-tuple-element.240.refs_2_, f32[256,128]{1,0:T(8,128)S(1)} %copy-done.31, ...), custom_call_target="tpu_custom_call" | custom-call | flops 71999995904 | bytes 1000 | tf_op jit(solution)/shard_map/attend_backward/pallas_call | solution.py:104
  242.6 9.7 %grad_gate_up.2 = (bf16[2,4,2,2,96,384]{5,4,3,2,1,0:T(8,128)(2,1)}, bf16[2,4,2,2,96,384]{5,4,3,2,1,0:T(8,128)(2,1)S(1)}) custom-call(s32[4]{0:T(128)S(1)} %pad_add_fusion.refs_0_, bf16[3,256,768]{2,1,0:T(8,128)(2,1)} %get-tuple-element.220.refs_1_.refs_3_, bf16[3,256,768]{2,1,0:T(8,128)(2,1)} %collective-permute-done.33.refs_9_.refs_2_.refs_4_, ...), custom_call_target="tpu_custom_call" | custom-call | flops 80999997440 | bytes 1000 | tf_op jit(solution)/shard_map/grad_gate_up/pallas_call | solution.py:104
  253.1 5.2 %grad_down.2 = (bf16[2,4,2,2,96,384]{5,4,3,2,1,0:T(8,128)(2,1)S(1)}, bf16[2,4,2,2,96,384]{5,4,3,2,1,0:T(8,128)(2,1)S(1)}) custom-call(s32[4]{0:T(128)S(1)} %pad_add_fusion.refs_0_, bf16[256,3072]{1,0:T(8,128)(2,1)} %get-tuple-element.229.refs_4_.refs_1_, bf16[256,3072]{1,0:T(8,128)(2,1)} %collective-permute-done.34.refs_10_.refs_2_, ...), custom_call_target="tpu_custom_call" | custom-call | flops 44999999488 | bytes 1000 | tf_op jit(solution)/shard_map/grad_down/pallas_call | solution.py:104
  259.8 7.1 %grad_attend.2 = (bf16[2,4,2,2,96,384]{5,4,3,2,1,0:T(8,128)(2,1)}, bf16[2,4,2,2,96,384]{5,4,3,2,1,0:T(8,128)(2,1)S(1)}) custom-call(s32[4]{0:T(128)S(1)} %pad_add_fusion.refs_0_, bf16[3,256,768]{2,1,0:T(8,128)(2,1)} %get-tuple-element.220.refs_1_.refs_3_, ...), custom_call_target="tpu_custom_call", output_to_operand_aliasing={{0}: (9, {}), {1}: (10, {})} | custom-call | flops 54000001024 | bytes 1000 | tf_op jit(solution)/shard_map/grad_attend/pallas_call | solution.py:104
  270.1 10.9 %feed_backward.3 = (bf16[2,256,3072]{2,1,0:T(8,128)(2,1)S(1)}, bf16[256,3840]{1,0:T(8,128)(2,1)S(1)}, bf16[256,768]{1,0:T(8,128)(2,1)S(1)}, f32[256,768]{1,0:T(8...) custom-call(s32[4]{0:T(128)S(1)} %pad_add_fusion.refs_0_, ...), custom_call_target="tpu_custom_call" | custom-call | flops 117000003584 | bytes 1000 | tf_op jit(solution)/shard_map/feed_backward/pallas_call | solution.py:104
  281.4 4.4 add_halves.4
  287.4 9.6 %grad_gate_up.3 = (bf16[2,4,2,2,96,384]{5,4,3,2,1,0:T(8,128)(2,1)}, bf16[2,4,2,2,96,384]{5,4,3,2,1,0:T(8,128)(2,1)S(1)}) custom-call(s32[4]{0:T(128)S(1)} %pad_add_fusion.refs_0_, bf16[3,256,768]{2,1,0:T(8,128)(2,1)} %get-tuple-element.195.refs_1_.refs_3_, bf16[3,256,768]{2,1,0:T(8,128)(2,1)} %collective-permute-done.31.refs_7_.refs_2_.refs_4_, ...), custom_call_target="tpu_custom_call" | custom-call | flops 80999997440 | bytes 1000 | tf_op jit(solution)/shard_map/grad_gate_up/pallas_call | solution.py:104
  297.6 7.4 %attend_backward.3 = (bf16[256,2304]{1,0:T(8,128)(2,1)S(1)}, bf16[256,1152]{1,0:T(8,128)(2,1)S(1)}, f32[256,768]{1,0:T(8,128)S(1)}) custom-call(s32[4]{0:T(128)S(1)} %pad_add_fusion.refs_0_, bf16[256,768]{1,0:T(8,128)(2,1)S(1)} %get-tuple-element.256.refs_1_, bf16[256,2304]{1,0:T(8,128)(2,1)S(1)} %get-tuple-element.257.refs_2_, f32[256,128]{1,0:T(8,128)S(1)} %copy-done.29, ...), custom_call_target="tpu_custom_call" | custom-call | flops 71999995904 | bytes 1000 | tf_op jit(solution)/shard_map/attend_backward/pallas_call | solution.py:104
  305.1 5.2 %grad_down.3 = (bf16[2,4,2,2,96,384]{5,4,3,2,1,0:T(8,128)(2,1)S(1)}, bf16[2,4,2,2,96,384]{5,4,3,2,1,0:T(8,128)(2,1)S(1)}) custom-call(s32[4]{0:T(128)S(1)} %pad_add_fusion.refs_0_, bf16[256,3072]{1,0:T(8,128)(2,1)} %get-tuple-element.205.refs_4_.refs_1_, bf16[256,3072]{1,0:T(8,128)(2,1)} %collective-permute-done.32.refs_8_.refs_2_, ...), custom_call_target="tpu_custom_call" | custom-call | flops 44999999488 | bytes 1000 | tf_op jit(solution)/shard_map/grad_down/pallas_call | solution.py:104
  310.4 4.7 collective-permute-done.39.refs_2_
  317.2 6.2 %collective-permute-start.41 = (bf16[2,2,96,384]{3,2,1,0:T(8,128)(2,1)S(1)}, bf16[2,2,96,384]{3,2,1,0:T(8,128)(2,1)S(1)}, u32[]{:S(2)}, u32[]{:S(2)}) collective-permute-start(bf16[2,2,96,384]{3,2,1,0:T(8,128)(2,1)S(1)} %get-tuple-element.271), channel_id=1, source_target_pairs={{0,2},{1,3},{2,0},{3,1},{4,6},{5,7},{6,4},{7,5},{8,10},{9,11},{10,... | collective-permute-start | bytes 884744 | tf_op jit(solution)/shard_map/ppermute | solution.py:52
  325.9 3.4 add_halves.5
  330.9 4.2 collective-permute-done.41.refs_2_
  335.1 11.8 %collective-permute-done.42.refs_3_ = bf16[2,2,96,384]{3,2,1,0:T(8,128)(2,1)S(1)} collective-permute-done((bf16[2,2,96,384]{3,2,1,0:T(8,128)(2,1)S(1)}, bf16[2,2,96,384]{3,2,1,0:T(8,128)(2,1)S(1)}, u32[]{:S(2)}, u32[]{:S(2)}) %collective-permute-start.42) | collective-permute-done | bytes 294944 | tf_op jit(solution)/shard_map/ppermute | solution.py:52
  347.7 5.7 %grad_attend.3 = (bf16[2,4,2,2,96,384]{5,4,3,2,1,0:T(8,128)(2,1)S(1)}, bf16[2,4,2,2,96,384]{5,4,3,2,1,0:T(8,128)(2,1)S(1)}) custom-call(s32[4]{0:T(128)S(1)} %pad_add_fusion.refs_0_, bf16[3,256,768]{2,1,0:T(8,128)(2,1)} %get-tuple-element.195.refs_1_.refs_3_, ...), custom_call_target="tpu_custom_call", output_to_operand_aliasing={{0}: (9, {}), {1}: (10, {})} | custom-call | flops 54000001024 | bytes 1000 | tf_op jit(solution)/shard_map/grad_attend/pallas_call | solution.py:104
  354.1 4.1 collective-permute-done.45.refs_2_
  363.6 3.4 add_halves.6
  370.9 12.8 %collective-permute-done.47.refs_3_ = bf16[2,2,96,384]{3,2,1,0:T(8,128)(2,1)S(1)} collective-permute-done((bf16[2,2,96,384]{3,2,1,0:T(8,128)(2,1)S(1)}, bf16[2,2,96,384]{3,2,1,0:T(8,128)(2,1)S(1)}, u32[]{:S(2)}, u32[]{:S(2)}) %collective-permute-start.47) | collective-permute-done | bytes 294944 | tf_op jit(solution)/shard_map/ppermute | solution.py:52
  384.4 9.8 %collective-permute-done.50.refs_2_ = bf16[4,2,2,96,384]{4,3,2,1,0:T(8,128)(2,1)S(1)} collective-permute-done((bf16[4,2,2,96,384]{4,3,2,1,0:T(8,128)(2,1)S(1)}, bf16[4,2,2,96,384]{4,3,2,1,0:T(8,128)(2,1)S(1)}, u32[]{:S(2)}, u32[]{:S(2)}) %collective-permute-start.50) | collective-permute-done | bytes 1179680 | tf_op jit(solution)/shard_map/ppermute | solution.py:52
  404.7 16.0 %collective-permute-done.55.refs_2_ = bf16[2,2,96,384]{3,2,1,0:T(8,128)(2,1)S(1)} collective-permute-done((bf16[2,2,96,384]{3,2,1,0:T(8,128)(2,1)S(1)}, bf16[2,2,96,384]{3,2,1,0:T(8,128)(2,1)S(1)}, u32[]{:S(2)}, u32[]{:S(2)}) %collective-permute-start.55) | collective-permute-done | bytes 294944 | tf_op jit(solution)/shard_map/ppermute | solution.py:52
  436.2 8.7 %collective-permute-done.62.refs_2_ = bf16[2,2,2,96,384]{4,3,2,1,0:T(8,128)(2,1)S(1)} collective-permute-done((bf16[2,2,2,96,384]{4,3,2,1,0:T(8,128)(2,1)S(1)}, bf16[2,2,2,96,384]{4,3,2,1,0:T(8,128)(2,1)S(1)}, u32[]{:S(2)}, u32[]{:S(2)}) %collective-permute-start.62) | collective-permute-done | bytes 589856 | tf_op jit(solution)/shard_map/ppermute | solution.py:52
  452.3 7.3 %collective-permute-done.72.refs_2_ = bf16[2,2,2,96,384]{4,3,2,1,0:T(8,128)(2,1)S(1)} collective-permute-done((bf16[2,2,2,96,384]{4,3,2,1,0:T(8,128)(2,1)S(1)}, bf16[2,2,2,96,384]{4,3,2,1,0:T(8,128)(2,1)S(1)}, u32[]{:S(2)}, u32[]{:S(2)}) %collective-permute-start.72) | collective-permute-done | bytes 589856 | tf_op jit(solution)/shard_map/ppermute | solution.py:52
  467.0 5.7 %collective-permute-done.75.refs_2_ = bf16[2,2,2,96,384]{4,3,2,1,0:T(8,128)(2,1)S(1)} collective-permute-done((bf16[2,2,2,96,384]{4,3,2,1,0:T(8,128)(2,1)S(1)}, bf16[2,2,2,96,384]{4,3,2,1,0:T(8,128)(2,1)S(1)}, u32[]{:S(2)}, u32[]{:S(2)}) %collective-permute-start.75) | collective-permute-done | bytes 589856 | tf_op jit(solution)/shard_map/ppermute | solution.py:52
  475.5 3.7 collective-permute-start.69
  488.1 27.0 %adam_all.1 = (f32[2,96,2304]{2,1,0:T(8,128)}, f32[2,96,2304]{2,1,0:T(8,128)}, f32[2,96,2304]{2,1,0:T(8,128)}, f32[2,96,768]{2,1,0:T(8,128)}, f32[2,96,768]{2,1,...) custom-call(s32[4]{0:T(128)} %copy-done.4, ...), custom_call_target="tpu_custom_call" | custom-call | flops 269999996928 | bytes 1000 | tf_op jit(solution)/shard_map/adam_all/pallas_call | solution.py:104
  (316 shorter events, 154.7 us)
Async XLA Ops:
  7.7 15.6 %collective-permute-start.1 = (bf16[1,112,768]{2,1,0:T(8,128)(2,1)S(1)}, bf16[1,112,768]{2,1,0:T(8,128)(2,1)S(1)}, u32[]{:S(2)}, u32[]{:S(2)}) collective-permute-start(bf16[1,112,768]{2,1,0:T(8,128)(2,1)S(1)} %get-tuple-element.181.refs_4_), channel_id=1, source_target_pairs={{0,4},{1,5},{2,6},{3,7},{4,0},{5,1},{6,2},{7,3},{8,12},{9,13},{10,... | collective-permute-start | bytes 516104 | tf_op jit(solution)/shard_map/ppermute | solution.py:52
  24.7 16.4 %collective-permute-start.6 = (bf16[2,96,768]{2,1,0:T(8,128)(2,1)S(1)}, bf16[2,96,768]{2,1,0:T(8,128)(2,1)S(1)}, u32[]{:S(2)}, u32[]{:S(2)}) collective-permute-start(bf16[2,96,768]{2,1,0:T(8,128)(2,1)S(1)} %get-tuple-element.184.refs_4_), channel_id=1, source_target_pairs={{0,2},{1,3},{2,0},{3,1},{4,6},{5,7},{6,4},{7,5},{8,10},{9,11},{10,... | collective-permute-start | bytes 884744 | tf_op jit(solution)/shard_map/ppermute | solution.py:52
  27.6 23.4 %collective-permute-start.7 = (bf16[2,96,768]{2,1,0:T(8,128)(2,1)S(1)}, bf16[2,96,768]{2,1,0:T(8,128)(2,1)S(1)}, u32[]{:S(2)}, u32[]{:S(2)}) collective-permute-start(bf16[2,96,768]{2,1,0:T(8,128)(2,1)S(1)} %get-tuple-element.184.refs_4_), channel_id=1, source_target_pairs={{0,4},{1,5},{2,6},{3,7},{4,0},{5,1},{6,2},{7,3},{8,12},{9,13},{10,... | collective-permute-start | bytes 884744 | tf_op jit(solution)/shard_map/ppermute | solution.py:52
  28.7 22.4 %collective-permute-start.8 = (bf16[2,96,768]{2,1,0:T(8,128)(2,1)S(1)}, bf16[2,96,768]{2,1,0:T(8,128)(2,1)S(1)}, u32[]{:S(2)}, u32[]{:S(2)}) collective-permute-start(bf16[2,96,768]{2,1,0:T(8,128)(2,1)S(1)} %get-tuple-element.184.refs_4_), channel_id=1, source_target_pairs={{0,6},{1,7},{2,4},{3,5},{4,2},{5,3},{6,0},{7,1},{8,14},{9,15},{10,... | collective-permute-start | bytes 884744 | tf_op jit(solution)/shard_map/ppermute | solution.py:52
  39.4 14.6 %collective-permute-start.5 = (bf16[2,3,1,96,768]{4,3,2,1,0:T(8,128)(2,1)S(1)}, bf16[2,3,1,96,768]{4,3,2,1,0:T(8,128)(2,1)S(1)}, u32[]{:S(2)}, u32[]{:S(2)}) collective-permute-start(bf16[2,3,1,96,768]{4,3,2,1,0:T(8,128)(2,1)S(1)} %get-tuple-element.185.refs_2_), channel_id=1, source_target_pairs={{0,8},{1,17},{2,10},{3,19},{4,12},{5,21},{6,14},{7,23},{8,0},{9,25... | collective-permute-start | bytes 2654216 | tf_op jit(solution)/shard_map/ppermute | solution.py:52
  56.1 21.8 %collective-permute-start.12 = (bf16[2,96,768]{2,1,0:T(8,128)(2,1)S(1)}, bf16[2,96,768]{2,1,0:T(8,128)(2,1)S(1)}, u32[]{:S(2)}, u32[]{:S(2)}) collective-permute-start(bf16[2,96,768]{2,1,0:T(8,128)(2,1)S(1)} %get-tuple-element.188.refs_4_), channel_id=1, source_target_pairs={{0,2},{1,3},{2,0},{3,1},{4,6},{5,7},{6,4},{7,5},{8,10},{9,11},{10,... | collective-permute-start | bytes 884744 | tf_op jit(solution)/shard_map/ppermute | solution.py:52
  62.3 23.4 %collective-permute-start.13 = (bf16[2,96,768]{2,1,0:T(8,128)(2,1)S(1)}, bf16[2,96,768]{2,1,0:T(8,128)(2,1)S(1)}, u32[]{:S(2)}, u32[]{:S(2)}) collective-permute-start(bf16[2,96,768]{2,1,0:T(8,128)(2,1)S(1)} %get-tuple-element.188.refs_4_), channel_id=1, source_target_pairs={{0,4},{1,5},{2,6},{3,7},{4,0},{5,1},{6,2},{7,3},{8,12},{9,13},{10,... | collective-permute-start | bytes 884744 | tf_op jit(solution)/shard_map/ppermute | solution.py:52
  63.3 22.4 %collective-permute-start.14 = (bf16[2,96,768]{2,1,0:T(8,128)(2,1)S(1)}, bf16[2,96,768]{2,1,0:T(8,128)(2,1)S(1)}, u32[]{:S(2)}, u32[]{:S(2)}) collective-permute-start(bf16[2,96,768]{2,1,0:T(8,128)(2,1)S(1)} %get-tuple-element.188.refs_4_), channel_id=1, source_target_pairs={{0,6},{1,7},{2,4},{3,5},{4,2},{5,3},{6,0},{7,1},{8,14},{9,15},{10,... | collective-permute-start | bytes 884744 | tf_op jit(solution)/shard_map/ppermute | solution.py:52
  65.7 22.6 %collective-permute-start.11 = (bf16[2,3,2,96,768]{4,3,2,1,0:T(8,128)(2,1)S(1)}, bf16[2,3,2,96,768]{4,3,2,1,0:T(8,128)(2,1)S(1)}, u32[]{:S(2)}, u32[]{:S(2)}) collective-permute-start(bf16[2,3,2,96,768]{4,3,2,1,0:T(8,128)(2,1)S(1)} %get-tuple-element.197.refs_2_), channel_id=1, source_target_pairs={{0,8},{1,17},{2,10},{3,19},{4,12},{5,21},{6,14},{7,23},{8,0},{9,25... | collective-permute-start | bytes 5308424 | tf_op jit(solution)/shard_map/ppermute | solution.py:52
  89.8 15.7 %collective-permute-start.15 = (bf16[16,2,96,768]{3,2,1,0:T(8,128)(2,1)S(1)}, bf16[16,2,96,768]{3,2,1,0:T(8,128)(2,1)S(1)}, u32[]{:S(2)}, u32[]{:S(2)}) collective-permute-start(bf16[16,2,96,768]{3,2,1,0:T(8,128)(2,1)S(1)} %get-tuple-element.201), channel_id=1, source_target_pairs={{0,1},{1,0},{2,3},{3,2},{4,5},{5,4},{6,7},{7,6},{8,9},{9,8},{10,11... | collective-permute-start | bytes 14155784 | tf_op jit(solution)/shard_map/ppermute | solution.py:52
  91.5 22.5 %collective-permute-start.18 = (bf16[2,96,768]{2,1,0:T(8,128)(2,1)S(1)}, bf16[2,96,768]{2,1,0:T(8,128)(2,1)S(1)}, u32[]{:S(2)}, u32[]{:S(2)}) collective-permute-start(bf16[2,96,768]{2,1,0:T(8,128)(2,1)S(1)} %get-tuple-element.200.refs_4_), channel_id=1, source_target_pairs={{0,2},{1,3},{2,0},{3,1},{4,6},{5,7},{6,4},{7,5},{8,10},{9,11},{10,... | collective-permute-start | bytes 884744 | tf_op jit(solution)/shard_map/ppermute | solution.py:52
  97.6 23.4 %collective-permute-start.19 = (bf16[2,96,768]{2,1,0:T(8,128)(2,1)S(1)}, bf16[2,96,768]{2,1,0:T(8,128)(2,1)S(1)}, u32[]{:S(2)}, u32[]{:S(2)}) collective-permute-start(bf16[2,96,768]{2,1,0:T(8,128)(2,1)S(1)} %get-tuple-element.200.refs_4_), channel_id=1, source_target_pairs={{0,4},{1,5},{2,6},{3,7},{4,0},{5,1},{6,2},{7,3},{8,12},{9,13},{10,... | collective-permute-start | bytes 884744 | tf_op jit(solution)/shard_map/ppermute | solution.py:52
  98.6 22.4 %collective-permute-start.20 = (bf16[2,96,768]{2,1,0:T(8,128)(2,1)S(1)}, bf16[2,96,768]{2,1,0:T(8,128)(2,1)S(1)}, u32[]{:S(2)}, u32[]{:S(2)}) collective-permute-start(bf16[2,96,768]{2,1,0:T(8,128)(2,1)S(1)} %get-tuple-element.200.refs_4_), channel_id=1, source_target_pairs={{0,6},{1,7},{2,4},{3,5},{4,2},{5,3},{6,0},{7,1},{8,14},{9,15},{10,... | collective-permute-start | bytes 884744 | tf_op jit(solution)/shard_map/ppermute | solution.py:52
  103.9 22.6 %collective-permute-start.17 = (bf16[2,3,2,96,768]{4,3,2,1,0:T(8,128)(2,1)S(1)}, bf16[2,3,2,96,768]{4,3,2,1,0:T(8,128)(2,1)S(1)}, u32[]{:S(2)}, u32[]{:S(2)}) collective-permute-start(bf16[2,3,2,96,768]{4,3,2,1,0:T(8,128)(2,1)S(1)} %get-tuple-element.207.refs_3_.refs_2_), channel_id=1, source_target_pairs={{0,8},{1,17},{2,10},{3,19},{4,12},{5,21},{6,14},{7,23},{8,0},{9,25... | collective-permute-start | bytes 5308424 | tf_op jit(solution)/shard_map/ppermute | solution.py:52
  128.0 16.9 %collective-permute-start.21 = (bf16[16,2,96,768]{3,2,1,0:T(8,128)(2,1)S(1)}, bf16[16,2,96,768]{3,2,1,0:T(8,128)(2,1)S(1)}, u32[]{:S(2)}, u32[]{:S(2)}) collective-permute-start(bf16[16,2,96,768]{3,2,1,0:T(8,128)(2,1)S(1)} %get-tuple-element.211), channel_id=1, source_target_pairs={{0,1},{1,0},{2,3},{3,2},{4,5},{5,4},{6,7},{7,6},{8,9},{9,8},{10,11... | collective-permute-start | bytes 14155784 | tf_op jit(solution)/shard_map/ppermute | solution.py:52
  129.6 48.5 %collective-permute-start.24 = (bf16[1,96,768]{2,1,0:T(8,128)(2,1)}, bf16[1,96,768]{2,1,0:T(8,128)(2,1)}, u32[]{:S(2)}, u32[]{:S(2)}) collective-permute-start(bf16[1,96,768]{2,1,0:T(8,128)(2,1)} %get-tuple-element.210.refs_5_), channel_id=1, source_target_pairs={{0,2},{1,3},{2,0},{3,1},{4,6},{5,7},{6,4},{7,5},{8,10},{9,11},{10,... | collective-permute-start | bytes 442376 | tf_op jit(solution)/shard_map/ppermute | solution.py:52
  135.8 42.4 %collective-permute-start.25 = (bf16[1,96,768]{2,1,0:T(8,128)(2,1)}, bf16[1,96,768]{2,1,0:T(8,128)(2,1)}, u32[]{:S(2)}, u32[]{:S(2)}) collective-permute-start(bf16[1,96,768]{2,1,0:T(8,128)(2,1)} %get-tuple-element.210.refs_5_), channel_id=1, source_target_pairs={{0,4},{1,5},{2,6},{3,7},{4,0},{5,1},{6,2},{7,3},{8,12},{9,13},{10,... | collective-permute-start | bytes 442376 | tf_op jit(solution)/shard_map/ppermute | solution.py:52
  136.8 41.4 %collective-permute-start.26 = (bf16[1,96,768]{2,1,0:T(8,128)(2,1)}, bf16[1,96,768]{2,1,0:T(8,128)(2,1)}, u32[]{:S(2)}, u32[]{:S(2)}) collective-permute-start(bf16[1,96,768]{2,1,0:T(8,128)(2,1)} %get-tuple-element.210.refs_5_), channel_id=1, source_target_pairs={{0,6},{1,7},{2,4},{3,5},{4,2},{5,3},{6,0},{7,1},{8,14},{9,15},{10,... | collective-permute-start | bytes 442376 | tf_op jit(solution)/shard_map/ppermute | solution.py:52
  143.3 36.5 %collective-permute-start.23 = (bf16[2,3,2,96,768]{4,3,2,1,0:T(8,128)(2,1)}, bf16[2,3,2,96,768]{4,3,2,1,0:T(8,128)(2,1)}, u32[]{:S(2)}, u32[]{:S(2)}) collective-permute-start(bf16[2,3,2,96,768]{4,3,2,1,0:T(8,128)(2,1)} %get-tuple-element.222.refs_2_), channel_id=1, source_target_pairs={{0,8},{1,17},{2,10},{3,19},{4,12},{5,21},{6,14},{7,23},{8,0},{9,25... | collective-permute-start | bytes 5308424 | tf_op jit(solution)/shard_map/ppermute | solution.py:52
  207.2 27.6 %collective-permute-start.31 = (bf16[3,256,768]{2,1,0:T(8,128)(2,1)}, bf16[3,256,768]{2,1,0:T(8,128)(2,1)}, u32[]{:S(2)}, u32[]{:S(2)}) collective-permute-start(bf16[3,256,768]{2,1,0:T(8,128)(2,1)} %get-tuple-element.195.refs_1_.refs_3_), channel_id=1, source_target_pairs={{0,1},{1,0},{2,3},{3,2},{4,5},{5,4},{6,7},{7,6},{8,9},{9,8},{10,11... | collective-permute-start | bytes 3538952 | tf_op jit(solution)/shard_map/ppermute | solution.py:52
  207.7 27.1 %collective-permute-start.32 = (bf16[256,3072]{1,0:T(8,128)(2,1)}, bf16[256,3072]{1,0:T(8,128)(2,1)}, u32[]{:S(2)}, u32[]{:S(2)}) collective-permute-start(bf16[256,3072]{1,0:T(8,128)(2,1)} %get-tuple-element.205.refs_4_.refs_1_), channel_id=1, source_target_pairs={{0,1},{1,0},{2,3},{3,2},{4,5},{5,4},{6,7},{7,6},{8,9},{9,8},{10,11... | collective-permute-start | bytes 4718600 | tf_op jit(solution)/shard_map/ppermute | solution.py:52
  207.8 27.0 %collective-permute-start.33 = (bf16[3,256,768]{2,1,0:T(8,128)(2,1)}, bf16[3,256,768]{2,1,0:T(8,128)(2,1)}, u32[]{:S(2)}, u32[]{:S(2)}) collective-permute-start(bf16[3,256,768]{2,1,0:T(8,128)(2,1)} %get-tuple-element.220.refs_1_.refs_3_), channel_id=1, source_target_pairs={{0,1},{1,0},{2,3},{3,2},{4,5},{5,4},{6,7},{7,6},{8,9},{9,8},{10,11... | collective-permute-start | bytes 3538952 | tf_op jit(solution)/shard_map/ppermute | solution.py:52
  208.2 26.6 %collective-permute-start.34 = (bf16[256,3072]{1,0:T(8,128)(2,1)}, bf16[256,3072]{1,0:T(8,128)(2,1)}, u32[]{:S(2)}, u32[]{:S(2)}) collective-permute-start(bf16[256,3072]{1,0:T(8,128)(2,1)} %get-tuple-element.229.refs_4_.refs_1_), channel_id=1, source_target_pairs={{0,1},{1,0},{2,3},{3,2},{4,5},{5,4},{6,7},{7,6},{8,9},{9,8},{10,11... | collective-permute-start | bytes 4718600 | tf_op jit(solution)/shard_map/ppermute | solution.py:52
  242.1 17.7 %collective-permute-start.35 = (bf16[256,1152]{1,0:T(8,128)(2,1)S(1)}, bf16[256,1152]{1,0:T(8,128)(2,1)S(1)}, u32[]{:S(2)}, u32[]{:S(2)}) collective-permute-start(bf16[256,1152]{1,0:T(8,128)(2,1)S(1)} %get-tuple-element.247), channel_id=1, source_target_pairs={{0,1},{1,0},{2,3},{3,2},{4,5},{5,4},{6,7},{7,6},{8,9},{9,8},{10,11... | collective-permute-start | bytes 1769480 | tf_op jit(solution)/shard_map/ppermute | solution.py:52
  252.3 29.2 %collective-permute-start.38 = (bf16[2,4,2,2,96,384]{5,4,3,2,1,0:T(8,128)(2,1)}, bf16[2,4,2,2,96,384]{5,4,3,2,1,0:T(8,128)(2,1)}, u32[]{:S(2)}, u32[]{:S(2)}) collective-permute-start(bf16[2,4,2,2,96,384]{5,4,3,2,1,0:T(8,128)(2,1)} %get-tuple-element.252.refs_5_), channel_id=1, source_target_pairs={{0,8},{1,17},{2,10},{3,19},{4,12},{5,21},{6,14},{7,23},{8,0},{9,25... | collective-permute-start | bytes 7077896 | tf_op jit(solution)/shard_map/ppermute | solution.py:52
  267.0 58.9 %collective-permute-start.44 = (bf16[2,4,2,2,96,384]{5,4,3,2,1,0:T(8,128)(2,1)}, bf16[2,4,2,2,96,384]{5,4,3,2,1,0:T(8,128)(2,1)}, u32[]{:S(2)}, u32[]{:S(2)}) collective-permute-start(bf16[2,4,2,2,96,384]{5,4,3,2,1,0:T(8,128)(2,1)} %get-tuple-element.255.refs_10_), channel_id=1, source_target_pairs={{0,8},{1,17},{2,10},{3,19},{4,12},{5,21},{6,14},{7,23},{8,0},{9,25... | collective-permute-start | bytes 7077896 | tf_op jit(solution)/shard_map/ppermute | solution.py:52
  285.9 29.2 %collective-permute-start.39 = (bf16[4,2,2,96,384]{4,3,2,1,0:T(8,128)(2,1)}, bf16[4,2,2,96,384]{4,3,2,1,0:T(8,128)(2,1)}, u32[]{:S(2)}, u32[]{:S(2)}) collective-permute-start(bf16[4,2,2,96,384]{4,3,2,1,0:T(8,128)(2,1)} %get-tuple-element.263.refs_5_), channel_id=1, source_target_pairs={{0,16},{1,9},{2,18},{3,11},{4,20},{5,13},{6,22},{7,15},{8,24},{9,1... | collective-permute-start | bytes 3538952 | tf_op jit(solution)/shard_map/ppermute | solution.py:52
  297.0 66.5 %collective-permute-start.49 = (bf16[2,4,2,2,96,384]{5,4,3,2,1,0:T(8,128)(2,1)}, bf16[2,4,2,2,96,384]{5,4,3,2,1,0:T(8,128)(2,1)}, u32[]{:S(2)}, u32[]{:S(2)}) collective-permute-start(bf16[2,4,2,2,96,384]{5,4,3,2,1,0:T(8,128)(2,1)} %get-tuple-element.264.refs_6_), channel_id=1, source_target_pairs={{0,8},{1,17},{2,10},{3,19},{4,12},{5,21},{6,14},{7,23},{8,0},{9,25... | collective-permute-start | bytes 7077896 | tf_op jit(solution)/shard_map/ppermute | solution.py:52
  317.2 17.9 %collective-permute-start.41 = (bf16[2,2,96,384]{3,2,1,0:T(8,128)(2,1)S(1)}, bf16[2,2,96,384]{3,2,1,0:T(8,128)(2,1)S(1)}, u32[]{:S(2)}, u32[]{:S(2)}) collective-permute-start(bf16[2,2,96,384]{3,2,1,0:T(8,128)(2,1)S(1)} %get-tuple-element.271), channel_id=1, source_target_pairs={{0,2},{1,3},{2,0},{3,1},{4,6},{5,7},{6,4},{7,5},{8,10},{9,11},{10,... | collective-permute-start | bytes 884744 | tf_op jit(solution)/shard_map/ppermute | solution.py:52
  323.4 23.5 %collective-permute-start.42 = (bf16[2,2,96,384]{3,2,1,0:T(8,128)(2,1)S(1)}, bf16[2,2,96,384]{3,2,1,0:T(8,128)(2,1)S(1)}, u32[]{:S(2)}, u32[]{:S(2)}) collective-permute-start(bf16[2,2,96,384]{3,2,1,0:T(8,128)(2,1)S(1)} %get-tuple-element.272), channel_id=1, source_target_pairs={{0,4},{1,5},{2,6},{3,7},{4,0},{5,1},{6,2},{7,3},{8,12},{9,13},{10,... | collective-permute-start | bytes 884744 | tf_op jit(solution)/shard_map/ppermute | solution.py:52
  324.5 22.4 %collective-permute-start.43 = (bf16[2,2,96,384]{3,2,1,0:T(8,128)(2,1)S(1)}, bf16[2,2,96,384]{3,2,1,0:T(8,128)(2,1)S(1)}, u32[]{:S(2)}, u32[]{:S(2)}) collective-permute-start(bf16[2,2,96,384]{3,2,1,0:T(8,128)(2,1)S(1)} %get-tuple-element.273), channel_id=1, source_target_pairs={{0,6},{1,7},{2,4},{3,5},{4,2},{5,3},{6,0},{7,1},{8,14},{9,15},{10,... | collective-permute-start | bytes 884744 | tf_op jit(solution)/shard_map/ppermute | solution.py:52
  329.3 29.0 %collective-permute-start.45 = (bf16[4,2,2,96,384]{4,3,2,1,0:T(8,128)(2,1)S(1)}, bf16[4,2,2,96,384]{4,3,2,1,0:T(8,128)(2,1)S(1)}, u32[]{:S(2)}, u32[]{:S(2)}) collective-permute-start(bf16[4,2,2,96,384]{4,3,2,1,0:T(8,128)(2,1)S(1)} %get-tuple-element.275.refs_5_), channel_id=1, source_target_pairs={{0,16},{1,9},{2,18},{3,11},{4,20},{5,13},{6,22},{7,15},{8,24},{9,1... | collective-permute-start | bytes 3538952 | tf_op jit(solution)/shard_map/ppermute | solution.py:52
  353.4 46.2 %collective-permute-start.54 = (bf16[2,4,2,2,96,384]{5,4,3,2,1,0:T(8,128)(2,1)S(1)}, bf16[2,4,2,2,96,384]{5,4,3,2,1,0:T(8,128)(2,1)S(1)}, u32[]{:S(2)}, u32[]{:S(2)}) collective-permute-start(bf16[2,4,2,2,96,384]{5,4,3,2,1,0:T(8,128)(2,1)S(1)} %get-tuple-element.281.refs_3_), channel_id=1, source_target_pairs={{0,8},{1,17},{2,10},{3,19},{4,12},{5,21},{6,14},{7,23},{8,0},{9,25... | collective-permute-start | bytes 7077896 | tf_op jit(solution)/shard_map/ppermute | solution.py:52
  360.2 23.5 %collective-permute-start.47 = (bf16[2,2,96,384]{3,2,1,0:T(8,128)(2,1)S(1)}, bf16[2,2,96,384]{3,2,1,0:T(8,128)(2,1)S(1)}, u32[]{:S(2)}, u32[]{:S(2)}) collective-permute-start(bf16[2,2,96,384]{3,2,1,0:T(8,128)(2,1)S(1)} %get-tuple-element.284), channel_id=1, source_target_pairs={{0,4},{1,5},{2,6},{3,7},{4,0},{5,1},{6,2},{7,3},{8,12},{9,13},{10,... | collective-permute-start | bytes 884744 | tf_op jit(solution)/shard_map/ppermute | solution.py:52
  362.2 21.5 %collective-permute-start.48 = (bf16[2,2,96,384]{3,2,1,0:T(8,128)(2,1)S(1)}, bf16[2,2,96,384]{3,2,1,0:T(8,128)(2,1)S(1)}, u32[]{:S(2)}, u32[]{:S(2)}) collective-permute-start(bf16[2,2,96,384]{3,2,1,0:T(8,128)(2,1)S(1)} %get-tuple-element.285), channel_id=1, source_target_pairs={{0,6},{1,7},{2,4},{3,5},{4,2},{5,3},{6,0},{7,1},{8,14},{9,15},{10,... | collective-permute-start | bytes 884744 | tf_op jit(solution)/shard_map/ppermute | solution.py:52
  367.0 27.3 %collective-permute-start.50 = (bf16[4,2,2,96,384]{4,3,2,1,0:T(8,128)(2,1)S(1)}, bf16[4,2,2,96,384]{4,3,2,1,0:T(8,128)(2,1)S(1)}, u32[]{:S(2)}, u32[]{:S(2)}) collective-permute-start(bf16[4,2,2,96,384]{4,3,2,1,0:T(8,128)(2,1)S(1)} %get-tuple-element.287.refs_5_), channel_id=1, source_target_pairs={{0,16},{1,9},{2,18},{3,11},{4,20},{5,13},{6,22},{7,15},{8,24},{9,1... | collective-permute-start | bytes 3538952 | tf_op jit(solution)/shard_map/ppermute | solution.py:52
  395.1 27.8 %collective-permute-start.51 = (bf16[2,2,96,384]{3,2,1,0:T(8,128)(2,1)S(1)}, bf16[2,2,96,384]{3,2,1,0:T(8,128)(2,1)S(1)}, u32[]{:S(2)}, u32[]{:S(2)}) collective-permute-start(bf16[2,2,96,384]{3,2,1,0:T(8,128)(2,1)S(1)} %get-tuple-element.291), channel_id=1, source_target_pairs={{0,2},{1,3},{2,0},{3,1},{4,6},{5,7},{6,4},{7,5},{8,10},{9,11},{10,... | collective-permute-start | bytes 884744 | tf_op jit(solution)/shard_map/ppermute | solution.py:52
  397.0 27.0 %collective-permute-start.52 = (bf16[2,2,96,384]{3,2,1,0:T(8,128)(2,1)S(1)}, bf16[2,2,96,384]{3,2,1,0:T(8,128)(2,1)S(1)}, u32[]{:S(2)}, u32[]{:S(2)}) collective-permute-start(bf16[2,2,96,384]{3,2,1,0:T(8,128)(2,1)S(1)} %get-tuple-element.292), channel_id=1, source_target_pairs={{0,4},{1,5},{2,6},{3,7},{4,0},{5,1},{6,2},{7,3},{8,12},{9,13},{10,... | collective-permute-start | bytes 884744 | tf_op jit(solution)/shard_map/ppermute | solution.py:52
  398.2 25.7 %collective-permute-start.53 = (bf16[2,2,96,384]{3,2,1,0:T(8,128)(2,1)S(1)}, bf16[2,2,96,384]{3,2,1,0:T(8,128)(2,1)S(1)}, u32[]{:S(2)}, u32[]{:S(2)}) collective-permute-start(bf16[2,2,96,384]{3,2,1,0:T(8,128)(2,1)S(1)} %get-tuple-element.293), channel_id=1, source_target_pairs={{0,6},{1,7},{2,4},{3,5},{4,2},{5,3},{6,0},{7,1},{8,14},{9,15},{10,... | collective-permute-start | bytes 884744 | tf_op jit(solution)/shard_map/ppermute | solution.py:52
  401.3 23.4 %collective-permute-start.56 = (bf16[4,2,2,96,384]{4,3,2,1,0:T(8,128)(2,1)S(1)}, bf16[4,2,2,96,384]{4,3,2,1,0:T(8,128)(2,1)S(1)}, u32[]{:S(2)}, u32[]{:S(2)}) collective-permute-start(bf16[4,2,2,96,384]{4,3,2,1,0:T(8,128)(2,1)S(1)} %get-tuple-element.296.refs_2_), channel_id=1, source_target_pairs={{0,16},{1,9},{2,18},{3,11},{4,20},{5,13},{6,22},{7,15},{8,24},{9,1... | collective-permute-start | bytes 3538952 | tf_op jit(solution)/shard_map/ppermute | solution.py:52
  403.5 17.2 %collective-permute-start.55 = (bf16[2,2,96,384]{3,2,1,0:T(8,128)(2,1)S(1)}, bf16[2,2,96,384]{3,2,1,0:T(8,128)(2,1)S(1)}, u32[]{:S(2)}, u32[]{:S(2)}) collective-permute-start(bf16[2,2,96,384]{3,2,1,0:T(8,128)(2,1)S(1)} %get-tuple-element.297), channel_id=1, source_target_pairs={{0,16},{1,9},{2,18},{3,11},{4,20},{5,13},{6,22},{7,15},{8,24},{9,1... | collective-permute-start | bytes 884744 | tf_op jit(solution)/shard_map/ppermute | solution.py:52
  425.6 21.3 %collective-permute-start.57 = (bf16[2,2,96,384]{3,2,1,0:T(8,128)(2,1)S(1)}, bf16[2,2,96,384]{3,2,1,0:T(8,128)(2,1)S(1)}, u32[]{:S(2)}, u32[]{:S(2)}) collective-permute-start(bf16[2,2,96,384]{3,2,1,0:T(8,128)(2,1)S(1)} %get-tuple-element.305), channel_id=1, source_target_pairs={{0,2},{1,3},{2,0},{3,1},{4,6},{5,7},{6,4},{7,5},{8,10},{9,11},{10,... | collective-permute-start | bytes 884744 | tf_op jit(solution)/shard_map/ppermute | solution.py:52
  426.9 23.2 %collective-permute-start.58 = (bf16[2,2,96,384]{3,2,1,0:T(8,128)(2,1)S(1)}, bf16[2,2,96,384]{3,2,1,0:T(8,128)(2,1)S(1)}, u32[]{:S(2)}, u32[]{:S(2)}) collective-permute-start(bf16[2,2,96,384]{3,2,1,0:T(8,128)(2,1)S(1)} %get-tuple-element.306), channel_id=1, source_target_pairs={{0,4},{1,5},{2,6},{3,7},{4,0},{5,1},{6,2},{7,3},{8,12},{9,13},{10,... | collective-permute-start | bytes 884744 | tf_op jit(solution)/shard_map/ppermute | solution.py:52
  428.6 21.5 %collective-permute-start.59 = (bf16[2,2,96,384]{3,2,1,0:T(8,128)(2,1)S(1)}, bf16[2,2,96,384]{3,2,1,0:T(8,128)(2,1)S(1)}, u32[]{:S(2)}, u32[]{:S(2)}) collective-permute-start(bf16[2,2,96,384]{3,2,1,0:T(8,128)(2,1)S(1)} %get-tuple-element.307), channel_id=1, source_target_pairs={{0,6},{1,7},{2,4},{3,5},{4,2},{5,3},{6,0},{7,1},{8,14},{9,15},{10,... | collective-permute-start | bytes 884744 | tf_op jit(solution)/shard_map/ppermute | solution.py:52
  431.9 13.8 %collective-permute-start.61 = (bf16[2,2,96,384]{3,2,1,0:T(8,128)(2,1)S(1)}, bf16[2,2,96,384]{3,2,1,0:T(8,128)(2,1)S(1)}, u32[]{:S(2)}, u32[]{:S(2)}) collective-permute-start(bf16[2,2,96,384]{3,2,1,0:T(8,128)(2,1)S(1)} %get-tuple-element.311), channel_id=1, source_target_pairs={{0,16},{1,9},{2,18},{3,11},{4,20},{5,13},{6,22},{7,15},{8,24},{9,1... | collective-permute-start | bytes 884744 | tf_op jit(solution)/shard_map/ppermute | solution.py:52
  444.9 14.6 %collective-permute-start.73 = (bf16[4,2,2,96,384]{4,3,2,1,0:T(8,128)(2,1)S(1)}, bf16[4,2,2,96,384]{4,3,2,1,0:T(8,128)(2,1)S(1)}, u32[]{:S(2)}, u32[]{:S(2)}) collective-permute-start(bf16[4,2,2,96,384]{4,3,2,1,0:T(8,128)(2,1)S(1)} %get-tuple-element.323.refs_24_), channel_id=1, source_target_pairs={{0,1},{1,0},{2,3},{3,2},{4,5},{5,4},{6,7},{7,6},{8,9},{9,8},{10,11... | collective-permute-start | bytes 3538952 | tf_op jit(solution)/shard_map/ppermute | solution.py:52
  467.0 21.1 %collective-permute-start.77 = (bf16[4,2,2,96,384]{4,3,2,1,0:T(8,128)(2,1)S(1)}, bf16[4,2,2,96,384]{4,3,2,1,0:T(8,128)(2,1)}, u32[]{:S(2)}, u32[]{:S(2)}) collective-permute-start(bf16[4,2,2,96,384]{4,3,2,1,0:T(8,128)(2,1)S(1)} %get-tuple-element.329.refs_22_), channel_id=1, source_target_pairs={{0,1},{1,0},{2,3},{3,2},{4,5},{5,4},{6,7},{7,6},{8,9},{9,8},{10,11... | collective-permute-start | bytes 3538952 | tf_op jit(solution)/shard_map/ppermute | solution.py:52
  474.6 13.5 %collective-permute-start.76 = (bf16[4,2,2,96,384]{4,3,2,1,0:T(8,128)(2,1)}, bf16[4,2,2,96,384]{4,3,2,1,0:T(8,128)(2,1)}, u32[]{:S(2)}, u32[]{:S(2)}) collective-permute-start(bf16[4,2,2,96,384]{4,3,2,1,0:T(8,128)(2,1)} %get-tuple-element.328.refs_14_.refs_18_.refs_26_), channel_id=1, source_target_pairs={{0,1},{1,0},{2,3},{3,2},{4,5},{5,4},{6,7},{7,6},{8,9},{9,8},{10,11... | collective-permute-start | bytes 3538952 | tf_op jit(solution)/shard_map/ppermute | solution.py:52
  (88 other events, 1190.3 us)

commit v7 on v6

--- a/solution.py
+++ b/solution.py
@@ -90,7 +90,7 @@
     "adam_all": 30,
 }
 TIME_SCALE = 9.0
-VMEM_MIB = {"adam_all": 58, "gate_forward": 14, "feed_backward": 14, "assemble_gate_up": 14, "attend_forward": 14, "attend_backward": 14}
+VMEM_MIB = {"adam_all": 36, "gate_forward": 14, "feed_backward": 14, "assemble_gate_up": 14, "attend_forward": 14, "attend_backward": 14}
 
 
 def run(
@@ -717,8 +717,7 @@
 
 
 def chip_dot(left, right, right_other):
-    tokens = right.shape[0]
-    return dot(left[:, :tokens], right) + dot(left[:, tokens:], right_other)
+    return dot(left[...], jnp.concatenate([right, right_other], axis=0))
 
 
 def store_rows(out_ref, product, z, rows):

time: 520 us -> 528 us (1.015)
  local copies, waits for them, and re-layouts: 8.54 us -> 18.1 us
    unnamed x117 -> x131, local copies, waits for them, and re-layouts: 7.82 us -> 17.4 us
where the time goes in v7:
time: 528 us; the launch traced here: 524 us
  Pallas kernels  230 us (44%)
  waiting for transfers between devices  165 us (31%)
  starting transfers between devices  101 us (19%)
  local copies, waits for them, and re-layouts  18.1 us (3%)
    pallas_call x68, Pallas kernels, run(): pl.pallas_call(body_of, out_shape=[jax.ShapeDtypeStruct(shape, dtype) for...  230 us
    ppermute x78, waiting for transfers between devices, send(): return lax.ppermute(values, both_axes, pairs)  165 us
    ppermute x78, starting transfers between devices, send(): return lax.ppermute(values, both_axes, pairs)  101 us
    unnamed x131, local copies, waits for them, and re-layouts  17.4 us
  transfers between devices with their start and end apart: 78, of which 32 were waited for; matrix products, arithmetic and copies ran while one was open for 1% of the time, Pallas kernels for 38%

profile of v7, /device:TPU:0, one launch (start us, length us, event | category | flops | bytes accessed | tf_op | source)
XLA Modules:
  0.0 523.8 jit_solution(13045201276592575666)
XLA Ops:
  4.6 3.1 collective-permute-start
  10.3 4.5 collective-permute-done.refs_1_
  14.8 8.5 %collective-permute-done.1.refs_2_ = bf16[1,112,768]{2,1,0:T(8,128)(2,1)S(1)} collective-permute-done((bf16[1,112,768]{2,1,0:T(8,128)(2,1)S(1)}, bf16[1,112,768]{2,1,0:T(8,128)(2,1)S(1)}, u32[]{:S(2)}, u32[]{:S(2)}) %collective-permute-start.1) | collective-permute-done | bytes 172064 | tf_op jit(solution)/shard_map/ppermute | solution.py:52
  32.2 6.1 %collective-permute-done.3.refs_2_ = bf16[3,1,96,768]{3,2,1,0:T(8,128)(2,1)S(1)} collective-permute-done((bf16[3,1,96,768]{3,2,1,0:T(8,128)(2,1)S(1)}, bf16[3,1,96,768]{3,2,1,0:T(8,128)(2,1)S(1)}, u32[]{:S(2)}, u32[]{:S(2)}) %collective-permute-start.3) | collective-permute-done | bytes 442400 | tf_op jit(solution)/shard_map/ppermute | solution.py:52
  41.1 9.9 %collective-permute-done.7.refs_2_ = bf16[2,96,768]{2,1,0:T(8,128)(2,1)S(1)} collective-permute-done((bf16[2,96,768]{2,1,0:T(8,128)(2,1)S(1)}, bf16[2,96,768]{2,1,0:T(8,128)(2,1)S(1)}, u32[]{:S(2)}, u32[]{:S(2)}) %collective-permute-start.7) | collective-permute-done | bytes 294944 | tf_op jit(solution)/shard_map/ppermute | solution.py:52
  56.1 6.2 %collective-permute-start.12 = (bf16[2,96,768]{2,1,0:T(8,128)(2,1)S(1)}, bf16[2,96,768]{2,1,0:T(8,128)(2,1)S(1)}, u32[]{:S(2)}, u32[]{:S(2)}) collective-permute-start(bf16[2,96,768]{2,1,0:T(8,128)(2,1)S(1)} %get-tuple-element.188.refs_4_), channel_id=1, source_target_pairs={{0,2},{1,3},{2,0},{3,1},{4,6},{5,7},{6,4},{7,5},{8,10},{9,11},{10,... | collective-permute-start | bytes 884744 | tf_op jit(solution)/shard_map/ppermute | solution.py:52
  70.0 7.8 %attend_forward.2 = (bf16[3,256,768]{2,1,0:T(8,128)(2,1)}, bf16[256,2304]{1,0:T(8,128)(2,1)S(1)}, f32[256,128]{1,0:T(8,128)S(1)}, f32[256,768]{1,0:T(8,128)S(1)}, f32[256,768]{1,0:T(8,128)S(1)}) custom-call(s32[4]{0:T(128)S(1)} %pad_add_fusion.refs_0_, f32[256,768]{1,0:T(8,128)S(1)} %convert_select_fusion.refs_1_, ...), custom_call_target="tpu_custom_call" | custom-call | flops 67499999232 | bytes 1000 | tf_op jit(solution)/shard_map/attend_forward/pallas_call | solution.py:104
  77.8 7.9 %collective-permute-done.13.refs_2_ = bf16[2,96,768]{2,1,0:T(8,128)(2,1)S(1)} collective-permute-done((bf16[2,96,768]{2,1,0:T(8,128)(2,1)S(1)}, bf16[2,96,768]{2,1,0:T(8,128)(2,1)S(1)}, u32[]{:S(2)}, u32[]{:S(2)}) %collective-permute-start.13) | collective-permute-done | bytes 294944 | tf_op jit(solution)/shard_map/ppermute | solution.py:52
  91.5 6.1 %collective-permute-start.18 = (bf16[2,96,768]{2,1,0:T(8,128)(2,1)S(1)}, bf16[2,96,768]{2,1,0:T(8,128)(2,1)S(1)}, u32[]{:S(2)}, u32[]{:S(2)}) collective-permute-start(bf16[2,96,768]{2,1,0:T(8,128)(2,1)S(1)} %get-tuple-element.200.refs_4_), channel_id=1, source_target_pairs={{0,2},{1,3},{2,0},{3,1},{4,6},{5,7},{6,4},{7,5},{8,10},{9,11},{10,... | collective-permute-start | bytes 884744 | tf_op jit(solution)/shard_map/ppermute | solution.py:52
  107.4 6.6 %gate_forward.2 = (bf16[256,3072]{1,0:T(8,128)(2,1)}, bf16[2,256,3072]{2,1,0:T(8,128)(2,1)S(1)}) custom-call(s32[4]{0:T(128)S(1)} %pad_add_fusion.refs_0_, bf16[3,256,768]{2,1,0:T(8,128)(2,1)} %get-tuple-element.195.refs_1_.refs_3_, bf16[768,6144]{1,0:T(8,128)(2,1)S(1)} %assemble_gate_up.2.refs_2_.refs_3_.refs_4_.refs_6_.refs_7_, ...), custom_call_target="tpu_custom_call" | custom-call | flops 62999998464 | bytes 1000 | tf_op jit(solution)/shard_map/gate_forward/pallas_call | solution.py:104
  114.0 7.1 %collective-permute-done.19.refs_2_ = bf16[2,96,768]{2,1,0:T(8,128)(2,1)S(1)} collective-permute-done((bf16[2,96,768]{2,1,0:T(8,128)(2,1)S(1)}, bf16[2,96,768]{2,1,0:T(8,128)(2,1)S(1)}, u32[]{:S(2)}, u32[]{:S(2)}) %collective-permute-start.19) | collective-permute-done | bytes 294944 | tf_op jit(solution)/shard_map/ppermute | solution.py:52
  129.6 6.1 %collective-permute-start.24 = (bf16[1,96,768]{2,1,0:T(8,128)(2,1)}, bf16[1,96,768]{2,1,0:T(8,128)(2,1)}, u32[]{:S(2)}, u32[]{:S(2)}) collective-permute-start(bf16[1,96,768]{2,1,0:T(8,128)(2,1)} %get-tuple-element.210.refs_5_), channel_id=1, source_target_pairs={{0,2},{1,3},{2,0},{3,1},{4,6},{5,7},{6,4},{7,5},{8,10},{9,11},{10,... | collective-permute-start | bytes 442376 | tf_op jit(solution)/shard_map/ppermute | solution.py:52
  144.9 6.7 %assemble_down.2.refs_5_.refs_2_ = bf16[3072,768]{1,0:T(8,128)(2,1)S(1)} custom-call(s32[4]{0:T(128)S(1)} %pad_add_fusion.refs_0_, bf16[4,1,96,768]{3,2,1,0:T(8,128)(2,1)S(1)} %get-tuple-element.206.refs_1_, bf16[2,3,2,96,768]{4,3,2,1,0:T(8,128)(2,1)S(1)} %get-tuple-element.207.refs_3_.refs_2_, ...), custom_call_target="tpu_custom_call" | custom-call | flops 44999999488 | bytes 1000 | tf_op jit(solution)/shard_map/assemble_down/pallas_call | solution.py:104
  151.6 13.8 %assemble_attend.3 = (bf16[768,2304]{1,0:T(8,128)(2,1)S(1)}, bf16[768,768]{1,0:T(8,128)(2,1)S(1)}) custom-call(s32[4]{0:T(128)S(1)} %pad_add_fusion.refs_0_, bf16[4,1,96,768]{3,2,1,0:T(8,128)(2,1)S(1)} %get-tuple-element.208.refs_2_.refs_1_, bf16[2,3,2,96,768]{4,3,2,1,0:T(8,128)(2,1)S(1)} %get-tuple-element.207.refs_3_.refs_2_, ...), custom_call_target="tpu_custom_call" | custom-call | flops 27000000512 | bytes 1000 | tf_op jit(solution)/shard_map/assemble_attend/pallas_call | solution.py:104
  165.5 4.7 down_forward.2
  170.3 7.8 %attend_forward.3 = (bf16[3,256,768]{2,1,0:T(8,128)(2,1)}, bf16[256,2304]{1,0:T(8,128)(2,1)S(1)}, f32[256,128]{1,0:T(8,128)S(1)}, f32[256,768]{1,0:T(8,128)S(1)}, f32[256,768]{1,0:T(8,128)S(1)}) custom-call(s32[4]{0:T(128)S(1)} %pad_add_fusion.refs_0_, f32[256,768]{1,0:T(8,128)S(1)} %get-tuple-element.217.refs_1_, ...), custom_call_target="tpu_custom_call" | custom-call | flops 67499999232 | bytes 1000 | tf_op jit(solution)/shard_map/attend_forward/pallas_call | solution.py:104
  184.3 6.8 %collective-permute-done.28.refs_2_ = bf16[3,1,96,768]{3,2,1,0:T(8,128)(2,1)S(1)} collective-permute-done((bf16[3,1,96,768]{3,2,1,0:T(8,128)(2,1)S(1)}, bf16[3,1,96,768]{3,2,1,0:T(8,128)(2,1)S(1)}, u32[]{:S(2)}, u32[]{:S(2)}) %collective-permute-start.28) | collective-permute-done | bytes 442400 | tf_op jit(solution)/shard_map/ppermute | solution.py:52
  195.7 6.3 %gate_forward.3 = (bf16[256,3072]{1,0:T(8,128)(2,1)}, bf16[2,256,3072]{2,1,0:T(8,128)(2,1)S(1)}) custom-call(s32[4]{0:T(128)S(1)} %pad_add_fusion.refs_0_, bf16[3,256,768]{2,1,0:T(8,128)(2,1)} %get-tuple-element.220.refs_1_.refs_3_, bf16[768,6144]{1,0:T(8,128)(2,1)S(1)} %assemble_gate_up.3.refs_2_.refs_3_.refs_4_.refs_6_.refs_7_, ...), custom_call_target="tpu_custom_call" | custom-call | flops 62999998464 | bytes 1000 | tf_op jit(solution)/shard_map/gate_forward/pallas_call | solution.py:104
  202.0 3.2 collective-permute-done.29.refs_3_
  208.3 4.1 collective-permute-done.30.refs_4_
  212.4 6.7 %assemble_down.3.refs_2_.refs_5_ = bf16[3072,768]{1,0:T(8,128)(2,1)S(1)} custom-call(s32[4]{0:T(128)S(1)} %pad_add_fusion.refs_0_, bf16[4,1,96,768]{3,2,1,0:T(8,128)(2,1)S(1)} %get-tuple-element.230.refs_1_, bf16[2,3,1,96,768]{4,3,2,1,0:T(8,128)(2,1)S(1)} %get-tuple-element.231.refs_2_, bf16[2,3,1,96,768]{4,3,2,1,0:T(8,128)(2,1)S(1)} %collective-permute-done.29.refs_3_, ...), custom_call_target="tpu_custom_call" | custom-call | flops 44999999488 | bytes 1000 | tf_op jit(solution)/shard_map/assemble_down/pallas_call | solution.py:104
  219.1 4.4 down_forward.3
  223.6 10.9 %feed_backward.2 = (bf16[2,256,3072]{2,1,0:T(8,128)(2,1)S(1)}, bf16[256,3840]{1,0:T(8,128)(2,1)S(1)}, bf16[256,768]{1,0:T(8,128)(2,1)S(1)}, f32[256,768]{1,0:T(8...) custom-call(s32[4]{0:T(128)S(1)} %pad_add_fusion.refs_0_, ...), custom_call_target="tpu_custom_call" | custom-call | flops 117000003584 | bytes 1000 | tf_op jit(solution)/shard_map/feed_backward/pallas_call | solution.py:104
  234.8 7.3 %attend_backward.2 = (bf16[256,2304]{1,0:T(8,128)(2,1)S(1)}, bf16[256,1152]{1,0:T(8,128)(2,1)S(1)}, f32[256,768]{1,0:T(8,128)S(1)}) custom-call(s32[4]{0:T(128)S(1)} %pad_add_fusion.refs_0_, bf16[256,768]{1,0:T(8,128)(2,1)S(1)} %get-tuple-element.239.refs_1_, bf16[256,2304]{1,0:T(8,128)(2,1)S(1)} %get-tuple-element.240.refs_2_, f32[256,128]{1,0:T(8,128)S(1)} %copy-done.39, ...), custom_call_target="tpu_custom_call" | custom-call | flops 71999995904 | bytes 1000 | tf_op jit(solution)/shard_map/attend_backward/pallas_call | solution.py:104
  242.5 9.7 %grad_gate_up.2 = (bf16[2,4,2,2,96,384]{5,4,3,2,1,0:T(8,128)(2,1)}, bf16[2,4,2,2,96,384]{5,4,3,2,1,0:T(8,128)(2,1)S(1)}) custom-call(s32[4]{0:T(128)S(1)} %pad_add_fusion.refs_0_, bf16[3,256,768]{2,1,0:T(8,128)(2,1)} %get-tuple-element.220.refs_1_.refs_3_, bf16[3,256,768]{2,1,0:T(8,128)(2,1)} %collective-permute-done.33.refs_9_.refs_2_.refs_4_, ...), custom_call_target="tpu_custom_call" | custom-call | flops 80999997440 | bytes 1000 | tf_op jit(solution)/shard_map/grad_gate_up/pallas_call | solution.py:104
  253.1 5.2 %grad_down.2 = (bf16[2,4,2,2,96,384]{5,4,3,2,1,0:T(8,128)(2,1)S(1)}, bf16[2,4,2,2,96,384]{5,4,3,2,1,0:T(8,128)(2,1)S(1)}) custom-call(s32[4]{0:T(128)S(1)} %pad_add_fusion.refs_0_, bf16[256,3072]{1,0:T(8,128)(2,1)} %get-tuple-element.229.refs_4_.refs_1_, bf16[256,3072]{1,0:T(8,128)(2,1)} %collective-permute-done.34.refs_10_.refs_2_, ...), custom_call_target="tpu_custom_call" | custom-call | flops 44999999488 | bytes 1000 | tf_op jit(solution)/shard_map/grad_down/pallas_call | solution.py:104
  259.8 7.1 %grad_attend.2 = (bf16[2,4,2,2,96,384]{5,4,3,2,1,0:T(8,128)(2,1)}, bf16[2,4,2,2,96,384]{5,4,3,2,1,0:T(8,128)(2,1)S(1)}) custom-call(s32[4]{0:T(128)S(1)} %pad_add_fusion.refs_0_, bf16[3,256,768]{2,1,0:T(8,128)(2,1)} %get-tuple-element.220.refs_1_.refs_3_, ...), custom_call_target="tpu_custom_call", output_to_operand_aliasing={{0}: (9, {}), {1}: (10, {})} | custom-call | flops 54000001024 | bytes 1000 | tf_op jit(solution)/shard_map/grad_attend/pallas_call | solution.py:104
  270.0 10.9 %feed_backward.3 = (bf16[2,256,3072]{2,1,0:T(8,128)(2,1)S(1)}, bf16[256,3840]{1,0:T(8,128)(2,1)S(1)}, bf16[256,768]{1,0:T(8,128)(2,1)S(1)}, f32[256,768]{1,0:T(8...) custom-call(s32[4]{0:T(128)S(1)} %pad_add_fusion.refs_0_, ...), custom_call_target="tpu_custom_call" | custom-call | flops 117000003584 | bytes 1000 | tf_op jit(solution)/shard_map/feed_backward/pallas_call | solution.py:104
  281.4 4.4 add_halves.4
  287.4 9.6 %grad_gate_up.3 = (bf16[2,4,2,2,96,384]{5,4,3,2,1,0:T(8,128)(2,1)}, bf16[2,4,2,2,96,384]{5,4,3,2,1,0:T(8,128)(2,1)S(1)}) custom-call(s32[4]{0:T(128)S(1)} %pad_add_fusion.refs_0_, bf16[3,256,768]{2,1,0:T(8,128)(2,1)} %get-tuple-element.195.refs_1_.refs_3_, bf16[3,256,768]{2,1,0:T(8,128)(2,1)} %collective-permute-done.31.refs_7_.refs_2_.refs_4_, ...), custom_call_target="tpu_custom_call" | custom-call | flops 80999997440 | bytes 1000 | tf_op jit(solution)/shard_map/grad_gate_up/pallas_call | solution.py:104
  297.5 7.4 %attend_backward.3 = (bf16[256,2304]{1,0:T(8,128)(2,1)S(1)}, bf16[256,1152]{1,0:T(8,128)(2,1)S(1)}, f32[256,768]{1,0:T(8,128)S(1)}) custom-call(s32[4]{0:T(128)S(1)} %pad_add_fusion.refs_0_, bf16[256,768]{1,0:T(8,128)(2,1)S(1)} %get-tuple-element.256.refs_1_, bf16[256,2304]{1,0:T(8,128)(2,1)S(1)} %get-tuple-element.257.refs_2_, f32[256,128]{1,0:T(8,128)S(1)} %copy-done.37, ...), custom_call_target="tpu_custom_call" | custom-call | flops 71999995904 | bytes 1000 | tf_op jit(solution)/shard_map/attend_backward/pallas_call | solution.py:104
  305.1 5.3 %grad_down.3 = (bf16[2,4,2,2,96,384]{5,4,3,2,1,0:T(8,128)(2,1)S(1)}, bf16[2,4,2,2,96,384]{5,4,3,2,1,0:T(8,128)(2,1)S(1)}) custom-call(s32[4]{0:T(128)S(1)} %pad_add_fusion.refs_0_, bf16[256,3072]{1,0:T(8,128)(2,1)} %get-tuple-element.205.refs_4_.refs_1_, bf16[256,3072]{1,0:T(8,128)(2,1)} %collective-permute-done.32.refs_8_.refs_2_, ...), custom_call_target="tpu_custom_call" | custom-call | flops 44999999488 | bytes 1000 | tf_op jit(solution)/shard_map/grad_down/pallas_call | solution.py:104
  310.4 4.7 collective-permute-done.39.refs_2_
  317.1 6.2 %collective-permute-start.41 = (bf16[2,2,96,384]{3,2,1,0:T(8,128)(2,1)S(1)}, bf16[2,2,96,384]{3,2,1,0:T(8,128)(2,1)S(1)}, u32[]{:S(2)}, u32[]{:S(2)}) collective-permute-start(bf16[2,2,96,384]{3,2,1,0:T(8,128)(2,1)S(1)} %get-tuple-element.271), channel_id=1, source_target_pairs={{0,2},{1,3},{2,0},{3,1},{4,6},{5,7},{6,4},{7,5},{8,10},{9,11},{10,... | collective-permute-start | bytes 884744 | tf_op jit(solution)/shard_map/ppermute | solution.py:52
  325.8 3.4 add_halves.5
  330.8 4.2 collective-permute-done.41.refs_2_
  335.0 11.8 %collective-permute-done.42.refs_3_ = bf16[2,2,96,384]{3,2,1,0:T(8,128)(2,1)S(1)} collective-permute-done((bf16[2,2,96,384]{3,2,1,0:T(8,128)(2,1)S(1)}, bf16[2,2,96,384]{3,2,1,0:T(8,128)(2,1)S(1)}, u32[]{:S(2)}, u32[]{:S(2)}) %collective-permute-start.42) | collective-permute-done | bytes 294944 | tf_op jit(solution)/shard_map/ppermute | solution.py:52
  347.6 5.7 %grad_attend.3 = (bf16[2,4,2,2,96,384]{5,4,3,2,1,0:T(8,128)(2,1)S(1)}, bf16[2,4,2,2,96,384]{5,4,3,2,1,0:T(8,128)(2,1)S(1)}) custom-call(s32[4]{0:T(128)S(1)} %pad_add_fusion.refs_0_, bf16[3,256,768]{2,1,0:T(8,128)(2,1)} %get-tuple-element.195.refs_1_.refs_3_, ...), custom_call_target="tpu_custom_call", output_to_operand_aliasing={{0}: (9, {}), {1}: (10, {})} | custom-call | flops 54000001024 | bytes 1000 | tf_op jit(solution)/shard_map/grad_attend/pallas_call | solution.py:104
  354.1 4.1 collective-permute-done.45.refs_2_
  363.5 3.4 add_halves.6
  370.8 12.7 %collective-permute-done.47.refs_3_ = bf16[2,2,96,384]{3,2,1,0:T(8,128)(2,1)S(1)} collective-permute-done((bf16[2,2,96,384]{3,2,1,0:T(8,128)(2,1)S(1)}, bf16[2,2,96,384]{3,2,1,0:T(8,128)(2,1)S(1)}, u32[]{:S(2)}, u32[]{:S(2)}) %collective-permute-start.47) | collective-permute-done | bytes 294944 | tf_op jit(solution)/shard_map/ppermute | solution.py:52
  384.3 9.9 %collective-permute-done.50.refs_2_ = bf16[4,2,2,96,384]{4,3,2,1,0:T(8,128)(2,1)S(1)} collective-permute-done((bf16[4,2,2,96,384]{4,3,2,1,0:T(8,128)(2,1)S(1)}, bf16[4,2,2,96,384]{4,3,2,1,0:T(8,128)(2,1)S(1)}, u32[]{:S(2)}, u32[]{:S(2)}) %collective-permute-start.50) | collective-permute-done | bytes 1179680 | tf_op jit(solution)/shard_map/ppermute | solution.py:52
  404.6 16.0 %collective-permute-done.55.refs_2_ = bf16[2,2,96,384]{3,2,1,0:T(8,128)(2,1)S(1)} collective-permute-done((bf16[2,2,96,384]{3,2,1,0:T(8,128)(2,1)S(1)}, bf16[2,2,96,384]{3,2,1,0:T(8,128)(2,1)S(1)}, u32[]{:S(2)}, u32[]{:S(2)}) %collective-permute-start.55) | collective-permute-done | bytes 294944 | tf_op jit(solution)/shard_map/ppermute | solution.py:52
  436.1 8.7 %collective-permute-done.62.refs_2_ = bf16[2,2,2,96,384]{4,3,2,1,0:T(8,128)(2,1)S(1)} collective-permute-done((bf16[2,2,2,96,384]{4,3,2,1,0:T(8,128)(2,1)S(1)}, bf16[2,2,2,96,384]{4,3,2,1,0:T(8,128)(2,1)S(1)}, u32[]{:S(2)}, u32[]{:S(2)}) %collective-permute-start.62) | collective-permute-done | bytes 589856 | tf_op jit(solution)/shard_map/ppermute | solution.py:52
  452.2 7.2 %collective-permute-done.72.refs_2_ = bf16[2,2,2,96,384]{4,3,2,1,0:T(8,128)(2,1)S(1)} collective-permute-done((bf16[2,2,2,96,384]{4,3,2,1,0:T(8,128)(2,1)S(1)}, bf16[2,2,2,96,384]{4,3,2,1,0:T(8,128)(2,1)S(1)}, u32[]{:S(2)}, u32[]{:S(2)}) %collective-permute-start.72) | collective-permute-done | bytes 589856 | tf_op jit(solution)/shard_map/ppermute | solution.py:52
  467.4 5.7 %collective-permute-done.75.refs_2_ = bf16[2,2,2,96,384]{4,3,2,1,0:T(8,128)(2,1)S(1)} collective-permute-done((bf16[2,2,2,96,384]{4,3,2,1,0:T(8,128)(2,1)S(1)}, bf16[2,2,2,96,384]{4,3,2,1,0:T(8,128)(2,1)S(1)}, u32[]{:S(2)}, u32[]{:S(2)}) %collective-permute-start.75) | collective-permute-done | bytes 589856 | tf_op jit(solution)/shard_map/ppermute | solution.py:52
  475.9 3.7 collective-permute-start.69
  498.8 23.7 %adam_all.1 = (f32[2,96,2304]{2,1,0:T(8,128)}, f32[2,96,2304]{2,1,0:T(8,128)}, f32[2,96,2304]{2,1,0:T(8,128)}, f32[2,96,768]{2,1,0:T(8,128)}, f32[2,96,768]{2,1,...) custom-call(s32[4]{0:T(128)S(1)} %pad_add_fusion.refs_0_, ...), custom_call_target="tpu_custom_call" | custom-call | flops 269999996928 | bytes 1000 | tf_op jit(solution)/shard_map/adam_all/pallas_call | solution.py:104
  (330 shorter events, 165.3 us)
Async XLA Ops:
  7.7 15.6 %collective-permute-start.1 = (bf16[1,112,768]{2,1,0:T(8,128)(2,1)S(1)}, bf16[1,112,768]{2,1,0:T(8,128)(2,1)S(1)}, u32[]{:S(2)}, u32[]{:S(2)}) collective-permute-start(bf16[1,112,768]{2,1,0:T(8,128)(2,1)S(1)} %get-tuple-element.181.refs_4_), channel_id=1, source_target_pairs={{0,4},{1,5},{2,6},{3,7},{4,0},{5,1},{6,2},{7,3},{8,12},{9,13},{10,... | collective-permute-start | bytes 516104 | tf_op jit(solution)/shard_map/ppermute | solution.py:52
  24.7 16.4 %collective-permute-start.6 = (bf16[2,96,768]{2,1,0:T(8,128)(2,1)S(1)}, bf16[2,96,768]{2,1,0:T(8,128)(2,1)S(1)}, u32[]{:S(2)}, u32[]{:S(2)}) collective-permute-start(bf16[2,96,768]{2,1,0:T(8,128)(2,1)S(1)} %get-tuple-element.184.refs_4_), channel_id=1, source_target_pairs={{0,2},{1,3},{2,0},{3,1},{4,6},{5,7},{6,4},{7,5},{8,10},{9,11},{10,... | collective-permute-start | bytes 884744 | tf_op jit(solution)/shard_map/ppermute | solution.py:52
  27.6 23.4 %collective-permute-start.7 = (bf16[2,96,768]{2,1,0:T(8,128)(2,1)S(1)}, bf16[2,96,768]{2,1,0:T(8,128)(2,1)S(1)}, u32[]{:S(2)}, u32[]{:S(2)}) collective-permute-start(bf16[2,96,768]{2,1,0:T(8,128)(2,1)S(1)} %get-tuple-element.184.refs_4_), channel_id=1, source_target_pairs={{0,4},{1,5},{2,6},{3,7},{4,0},{5,1},{6,2},{7,3},{8,12},{9,13},{10,... | collective-permute-start | bytes 884744 | tf_op jit(solution)/shard_map/ppermute | solution.py:52
  28.7 22.4 %collective-permute-start.8 = (bf16[2,96,768]{2,1,0:T(8,128)(2,1)S(1)}, bf16[2,96,768]{2,1,0:T(8,128)(2,1)S(1)}, u32[]{:S(2)}, u32[]{:S(2)}) collective-permute-start(bf16[2,96,768]{2,1,0:T(8,128)(2,1)S(1)} %get-tuple-element.184.refs_4_), channel_id=1, source_target_pairs={{0,6},{1,7},{2,4},{3,5},{4,2},{5,3},{6,0},{7,1},{8,14},{9,15},{10,... | collective-permute-start | bytes 884744 | tf_op jit(solution)/shard_map/ppermute | solution.py:52
  39.4 14.6 %collective-permute-start.5 = (bf16[2,3,1,96,768]{4,3,2,1,0:T(8,128)(2,1)S(1)}, bf16[2,3,1,96,768]{4,3,2,1,0:T(8,128)(2,1)S(1)}, u32[]{:S(2)}, u32[]{:S(2)}) collective-permute-start(bf16[2,3,1,96,768]{4,3,2,1,0:T(8,128)(2,1)S(1)} %get-tuple-element.185.refs_2_), channel_id=1, source_target_pairs={{0,8},{1,17},{2,10},{3,19},{4,12},{5,21},{6,14},{7,23},{8,0},{9,25... | collective-permute-start | bytes 2654216 | tf_op jit(solution)/shard_map/ppermute | solution.py:52
  56.1 21.8 %collective-permute-start.12 = (bf16[2,96,768]{2,1,0:T(8,128)(2,1)S(1)}, bf16[2,96,768]{2,1,0:T(8,128)(2,1)S(1)}, u32[]{:S(2)}, u32[]{:S(2)}) collective-permute-start(bf16[2,96,768]{2,1,0:T(8,128)(2,1)S(1)} %get-tuple-element.188.refs_4_), channel_id=1, source_target_pairs={{0,2},{1,3},{2,0},{3,1},{4,6},{5,7},{6,4},{7,5},{8,10},{9,11},{10,... | collective-permute-start | bytes 884744 | tf_op jit(solution)/shard_map/ppermute | solution.py:52
  62.3 23.4 %collective-permute-start.13 = (bf16[2,96,768]{2,1,0:T(8,128)(2,1)S(1)}, bf16[2,96,768]{2,1,0:T(8,128)(2,1)S(1)}, u32[]{:S(2)}, u32[]{:S(2)}) collective-permute-start(bf16[2,96,768]{2,1,0:T(8,128)(2,1)S(1)} %get-tuple-element.188.refs_4_), channel_id=1, source_target_pairs={{0,4},{1,5},{2,6},{3,7},{4,0},{5,1},{6,2},{7,3},{8,12},{9,13},{10,... | collective-permute-start | bytes 884744 | tf_op jit(solution)/shard_map/ppermute | solution.py:52
  63.3 22.4 %collective-permute-start.14 = (bf16[2,96,768]{2,1,0:T(8,128)(2,1)S(1)}, bf16[2,96,768]{2,1,0:T(8,128)(2,1)S(1)}, u32[]{:S(2)}, u32[]{:S(2)}) collective-permute-start(bf16[2,96,768]{2,1,0:T(8,128)(2,1)S(1)} %get-tuple-element.188.refs_4_), channel_id=1, source_target_pairs={{0,6},{1,7},{2,4},{3,5},{4,2},{5,3},{6,0},{7,1},{8,14},{9,15},{10,... | collective-permute-start | bytes 884744 | tf_op jit(solution)/shard_map/ppermute | solution.py:52
  65.7 22.6 %collective-permute-start.11 = (bf16[2,3,2,96,768]{4,3,2,1,0:T(8,128)(2,1)S(1)}, bf16[2,3,2,96,768]{4,3,2,1,0:T(8,128)(2,1)S(1)}, u32[]{:S(2)}, u32[]{:S(2)}) collective-permute-start(bf16[2,3,2,96,768]{4,3,2,1,0:T(8,128)(2,1)S(1)} %get-tuple-element.197.refs_2_), channel_id=1, source_target_pairs={{0,8},{1,17},{2,10},{3,19},{4,12},{5,21},{6,14},{7,23},{8,0},{9,25... | collective-permute-start | bytes 5308424 | tf_op jit(solution)/shard_map/ppermute | solution.py:52
  89.8 15.7 %collective-permute-start.15 = (bf16[16,2,96,768]{3,2,1,0:T(8,128)(2,1)S(1)}, bf16[16,2,96,768]{3,2,1,0:T(8,128)(2,1)S(1)}, u32[]{:S(2)}, u32[]{:S(2)}) collective-permute-start(bf16[16,2,96,768]{3,2,1,0:T(8,128)(2,1)S(1)} %get-tuple-element.201), channel_id=1, source_target_pairs={{0,1},{1,0},{2,3},{3,2},{4,5},{5,4},{6,7},{7,6},{8,9},{9,8},{10,11... | collective-permute-start | bytes 14155784 | tf_op jit(solution)/shard_map/ppermute | solution.py:52
  91.5 22.5 %collective-permute-start.18 = (bf16[2,96,768]{2,1,0:T(8,128)(2,1)S(1)}, bf16[2,96,768]{2,1,0:T(8,128)(2,1)S(1)}, u32[]{:S(2)}, u32[]{:S(2)}) collective-permute-start(bf16[2,96,768]{2,1,0:T(8,128)(2,1)S(1)} %get-tuple-element.200.refs_4_), channel_id=1, source_target_pairs={{0,2},{1,3},{2,0},{3,1},{4,6},{5,7},{6,4},{7,5},{8,10},{9,11},{10,... | collective-permute-start | bytes 884744 | tf_op jit(solution)/shard_map/ppermute | solution.py:52
  97.6 23.4 %collective-permute-start.19 = (bf16[2,96,768]{2,1,0:T(8,128)(2,1)S(1)}, bf16[2,96,768]{2,1,0:T(8,128)(2,1)S(1)}, u32[]{:S(2)}, u32[]{:S(2)}) collective-permute-start(bf16[2,96,768]{2,1,0:T(8,128)(2,1)S(1)} %get-tuple-element.200.refs_4_), channel_id=1, source_target_pairs={{0,4},{1,5},{2,6},{3,7},{4,0},{5,1},{6,2},{7,3},{8,12},{9,13},{10,... | collective-permute-start | bytes 884744 | tf_op jit(solution)/shard_map/ppermute | solution.py:52
  98.6 22.4 %collective-permute-start.20 = (bf16[2,96,768]{2,1,0:T(8,128)(2,1)S(1)}, bf16[2,96,768]{2,1,0:T(8,128)(2,1)S(1)}, u32[]{:S(2)}, u32[]{:S(2)}) collective-permute-start(bf16[2,96,768]{2,1,0:T(8,128)(2,1)S(1)} %get-tuple-element.200.refs_4_), channel_id=1, source_target_pairs={{0,6},{1,7},{2,4},{3,5},{4,2},{5,3},{6,0},{7,1},{8,14},{9,15},{10,... | collective-permute-start | bytes 884744 | tf_op jit(solution)/shard_map/ppermute | solution.py:52
  103.9 22.6 %collective-permute-start.17 = (bf16[2,3,2,96,768]{4,3,2,1,0:T(8,128)(2,1)S(1)}, bf16[2,3,2,96,768]{4,3,2,1,0:T(8,128)(2,1)S(1)}, u32[]{:S(2)}, u32[]{:S(2)}) collective-permute-start(bf16[2,3,2,96,768]{4,3,2,1,0:T(8,128)(2,1)S(1)} %get-tuple-element.207.refs_3_.refs_2_), channel_id=1, source_target_pairs={{0,8},{1,17},{2,10},{3,19},{4,12},{5,21},{6,14},{7,23},{8,0},{9,25... | collective-permute-start | bytes 5308424 | tf_op jit(solution)/shard_map/ppermute | solution.py:52
  128.0 16.9 %collective-permute-start.21 = (bf16[16,2,96,768]{3,2,1,0:T(8,128)(2,1)S(1)}, bf16[16,2,96,768]{3,2,1,0:T(8,128)(2,1)S(1)}, u32[]{:S(2)}, u32[]{:S(2)}) collective-permute-start(bf16[16,2,96,768]{3,2,1,0:T(8,128)(2,1)S(1)} %get-tuple-element.211), channel_id=1, source_target_pairs={{0,1},{1,0},{2,3},{3,2},{4,5},{5,4},{6,7},{7,6},{8,9},{9,8},{10,11... | collective-permute-start | bytes 14155784 | tf_op jit(solution)/shard_map/ppermute | solution.py:52
  129.6 48.5 %collective-permute-start.24 = (bf16[1,96,768]{2,1,0:T(8,128)(2,1)}, bf16[1,96,768]{2,1,0:T(8,128)(2,1)}, u32[]{:S(2)}, u32[]{:S(2)}) collective-permute-start(bf16[1,96,768]{2,1,0:T(8,128)(2,1)} %get-tuple-element.210.refs_5_), channel_id=1, source_target_pairs={{0,2},{1,3},{2,0},{3,1},{4,6},{5,7},{6,4},{7,5},{8,10},{9,11},{10,... | collective-permute-start | bytes 442376 | tf_op jit(solution)/shard_map/ppermute | solution.py:52
  135.8 42.3 %collective-permute-start.25 = (bf16[1,96,768]{2,1,0:T(8,128)(2,1)}, bf16[1,96,768]{2,1,0:T(8,128)(2,1)}, u32[]{:S(2)}, u32[]{:S(2)}) collective-permute-start(bf16[1,96,768]{2,1,0:T(8,128)(2,1)} %get-tuple-element.210.refs_5_), channel_id=1, source_target_pairs={{0,4},{1,5},{2,6},{3,7},{4,0},{5,1},{6,2},{7,3},{8,12},{9,13},{10,... | collective-permute-start | bytes 442376 | tf_op jit(solution)/shard_map/ppermute | solution.py:52
  136.8 41.3 %collective-permute-start.26 = (bf16[1,96,768]{2,1,0:T(8,128)(2,1)}, bf16[1,96,768]{2,1,0:T(8,128)(2,1)}, u32[]{:S(2)}, u32[]{:S(2)}) collective-permute-start(bf16[1,96,768]{2,1,0:T(8,128)(2,1)} %get-tuple-element.210.refs_5_), channel_id=1, source_target_pairs={{0,6},{1,7},{2,4},{3,5},{4,2},{5,3},{6,0},{7,1},{8,14},{9,15},{10,... | collective-permute-start | bytes 442376 | tf_op jit(solution)/shard_map/ppermute | solution.py:52
  143.3 36.5 %collective-permute-start.23 = (bf16[2,3,2,96,768]{4,3,2,1,0:T(8,128)(2,1)}, bf16[2,3,2,96,768]{4,3,2,1,0:T(8,128)(2,1)}, u32[]{:S(2)}, u32[]{:S(2)}) collective-permute-start(bf16[2,3,2,96,768]{4,3,2,1,0:T(8,128)(2,1)} %get-tuple-element.222.refs_2_), channel_id=1, source_target_pairs={{0,8},{1,17},{2,10},{3,19},{4,12},{5,21},{6,14},{7,23},{8,0},{9,25... | collective-permute-start | bytes 5308424 | tf_op jit(solution)/shard_map/ppermute | solution.py:52
  207.2 27.6 %collective-permute-start.31 = (bf16[3,256,768]{2,1,0:T(8,128)(2,1)}, bf16[3,256,768]{2,1,0:T(8,128)(2,1)}, u32[]{:S(2)}, u32[]{:S(2)}) collective-permute-start(bf16[3,256,768]{2,1,0:T(8,128)(2,1)} %get-tuple-element.195.refs_1_.refs_3_), channel_id=1, source_target_pairs={{0,1},{1,0},{2,3},{3,2},{4,5},{5,4},{6,7},{7,6},{8,9},{9,8},{10,11... | collective-permute-start | bytes 3538952 | tf_op jit(solution)/shard_map/ppermute | solution.py:52
  207.7 27.0 %collective-permute-start.32 = (bf16[256,3072]{1,0:T(8,128)(2,1)}, bf16[256,3072]{1,0:T(8,128)(2,1)}, u32[]{:S(2)}, u32[]{:S(2)}) collective-permute-start(bf16[256,3072]{1,0:T(8,128)(2,1)} %get-tuple-element.205.refs_4_.refs_1_), channel_id=1, source_target_pairs={{0,1},{1,0},{2,3},{3,2},{4,5},{5,4},{6,7},{7,6},{8,9},{9,8},{10,11... | collective-permute-start | bytes 4718600 | tf_op jit(solution)/shard_map/ppermute | solution.py:52
  207.8 27.0 %collective-permute-start.33 = (bf16[3,256,768]{2,1,0:T(8,128)(2,1)}, bf16[3,256,768]{2,1,0:T(8,128)(2,1)}, u32[]{:S(2)}, u32[]{:S(2)}) collective-permute-start(bf16[3,256,768]{2,1,0:T(8,128)(2,1)} %get-tuple-element.220.refs_1_.refs_3_), channel_id=1, source_target_pairs={{0,1},{1,0},{2,3},{3,2},{4,5},{5,4},{6,7},{7,6},{8,9},{9,8},{10,11... | collective-permute-start | bytes 3538952 | tf_op jit(solution)/shard_map/ppermute | solution.py:52
  208.2 26.5 %collective-permute-start.34 = (bf16[256,3072]{1,0:T(8,128)(2,1)}, bf16[256,3072]{1,0:T(8,128)(2,1)}, u32[]{:S(2)}, u32[]{:S(2)}) collective-permute-start(bf16[256,3072]{1,0:T(8,128)(2,1)} %get-tuple-element.229.refs_4_.refs_1_), channel_id=1, source_target_pairs={{0,1},{1,0},{2,3},{3,2},{4,5},{5,4},{6,7},{7,6},{8,9},{9,8},{10,11... | collective-permute-start | bytes 4718600 | tf_op jit(solution)/shard_map/ppermute | solution.py:52
  242.1 17.7 %collective-permute-start.35 = (bf16[256,1152]{1,0:T(8,128)(2,1)S(1)}, bf16[256,1152]{1,0:T(8,128)(2,1)S(1)}, u32[]{:S(2)}, u32[]{:S(2)}) collective-permute-start(bf16[256,1152]{1,0:T(8,128)(2,1)S(1)} %get-tuple-element.247), channel_id=1, source_target_pairs={{0,1},{1,0},{2,3},{3,2},{4,5},{5,4},{6,7},{7,6},{8,9},{9,8},{10,11... | collective-permute-start | bytes 1769480 | tf_op jit(solution)/shard_map/ppermute | solution.py:52
  252.2 29.2 %collective-permute-start.38 = (bf16[2,4,2,2,96,384]{5,4,3,2,1,0:T(8,128)(2,1)}, bf16[2,4,2,2,96,384]{5,4,3,2,1,0:T(8,128)(2,1)}, u32[]{:S(2)}, u32[]{:S(2)}) collective-permute-start(bf16[2,4,2,2,96,384]{5,4,3,2,1,0:T(8,128)(2,1)} %get-tuple-element.252.refs_5_), channel_id=1, source_target_pairs={{0,8},{1,17},{2,10},{3,19},{4,12},{5,21},{6,14},{7,23},{8,0},{9,25... | collective-permute-start | bytes 7077896 | tf_op jit(solution)/shard_map/ppermute | solution.py:52
  266.9 58.9 %collective-permute-start.44 = (bf16[2,4,2,2,96,384]{5,4,3,2,1,0:T(8,128)(2,1)}, bf16[2,4,2,2,96,384]{5,4,3,2,1,0:T(8,128)(2,1)}, u32[]{:S(2)}, u32[]{:S(2)}) collective-permute-start(bf16[2,4,2,2,96,384]{5,4,3,2,1,0:T(8,128)(2,1)} %get-tuple-element.255.refs_10_), channel_id=1, source_target_pairs={{0,8},{1,17},{2,10},{3,19},{4,12},{5,21},{6,14},{7,23},{8,0},{9,25... | collective-permute-start | bytes 7077896 | tf_op jit(solution)/shard_map/ppermute | solution.py:52
  285.8 29.2 %collective-permute-start.39 = (bf16[4,2,2,96,384]{4,3,2,1,0:T(8,128)(2,1)}, bf16[4,2,2,96,384]{4,3,2,1,0:T(8,128)(2,1)}, u32[]{:S(2)}, u32[]{:S(2)}) collective-permute-start(bf16[4,2,2,96,384]{4,3,2,1,0:T(8,128)(2,1)} %get-tuple-element.263.refs_5_), channel_id=1, source_target_pairs={{0,16},{1,9},{2,18},{3,11},{4,20},{5,13},{6,22},{7,15},{8,24},{9,1... | collective-permute-start | bytes 3538952 | tf_op jit(solution)/shard_map/ppermute | solution.py:52
  297.0 66.5 %collective-permute-start.49 = (bf16[2,4,2,2,96,384]{5,4,3,2,1,0:T(8,128)(2,1)}, bf16[2,4,2,2,96,384]{5,4,3,2,1,0:T(8,128)(2,1)}, u32[]{:S(2)}, u32[]{:S(2)}) collective-permute-start(bf16[2,4,2,2,96,384]{5,4,3,2,1,0:T(8,128)(2,1)} %get-tuple-element.264.refs_6_), channel_id=1, source_target_pairs={{0,8},{1,17},{2,10},{3,19},{4,12},{5,21},{6,14},{7,23},{8,0},{9,25... | collective-permute-start | bytes 7077896 | tf_op jit(solution)/shard_map/ppermute | solution.py:52
  317.1 17.9 %collective-permute-start.41 = (bf16[2,2,96,384]{3,2,1,0:T(8,128)(2,1)S(1)}, bf16[2,2,96,384]{3,2,1,0:T(8,128)(2,1)S(1)}, u32[]{:S(2)}, u32[]{:S(2)}) collective-permute-start(bf16[2,2,96,384]{3,2,1,0:T(8,128)(2,1)S(1)} %get-tuple-element.271), channel_id=1, source_target_pairs={{0,2},{1,3},{2,0},{3,1},{4,6},{5,7},{6,4},{7,5},{8,10},{9,11},{10,... | collective-permute-start | bytes 884744 | tf_op jit(solution)/shard_map/ppermute | solution.py:52
  323.3 23.5 %collective-permute-start.42 = (bf16[2,2,96,384]{3,2,1,0:T(8,128)(2,1)S(1)}, bf16[2,2,96,384]{3,2,1,0:T(8,128)(2,1)S(1)}, u32[]{:S(2)}, u32[]{:S(2)}) collective-permute-start(bf16[2,2,96,384]{3,2,1,0:T(8,128)(2,1)S(1)} %get-tuple-element.272), channel_id=1, source_target_pairs={{0,4},{1,5},{2,6},{3,7},{4,0},{5,1},{6,2},{7,3},{8,12},{9,13},{10,... | collective-permute-start | bytes 884744 | tf_op jit(solution)/shard_map/ppermute | solution.py:52
  324.4 22.4 %collective-permute-start.43 = (bf16[2,2,96,384]{3,2,1,0:T(8,128)(2,1)S(1)}, bf16[2,2,96,384]{3,2,1,0:T(8,128)(2,1)S(1)}, u32[]{:S(2)}, u32[]{:S(2)}) collective-permute-start(bf16[2,2,96,384]{3,2,1,0:T(8,128)(2,1)S(1)} %get-tuple-element.273), channel_id=1, source_target_pairs={{0,6},{1,7},{2,4},{3,5},{4,2},{5,3},{6,0},{7,1},{8,14},{9,15},{10,... | collective-permute-start | bytes 884744 | tf_op jit(solution)/shard_map/ppermute | solution.py:52
  329.2 29.0 %collective-permute-start.45 = (bf16[4,2,2,96,384]{4,3,2,1,0:T(8,128)(2,1)S(1)}, bf16[4,2,2,96,384]{4,3,2,1,0:T(8,128)(2,1)S(1)}, u32[]{:S(2)}, u32[]{:S(2)}) collective-permute-start(bf16[4,2,2,96,384]{4,3,2,1,0:T(8,128)(2,1)S(1)} %get-tuple-element.275.refs_5_), channel_id=1, source_target_pairs={{0,16},{1,9},{2,18},{3,11},{4,20},{5,13},{6,22},{7,15},{8,24},{9,1... | collective-permute-start | bytes 3538952 | tf_op jit(solution)/shard_map/ppermute | solution.py:52
  353.3 46.2 %collective-permute-start.54 = (bf16[2,4,2,2,96,384]{5,4,3,2,1,0:T(8,128)(2,1)S(1)}, bf16[2,4,2,2,96,384]{5,4,3,2,1,0:T(8,128)(2,1)S(1)}, u32[]{:S(2)}, u32[]{:S(2)}) collective-permute-start(bf16[2,4,2,2,96,384]{5,4,3,2,1,0:T(8,128)(2,1)S(1)} %get-tuple-element.281.refs_3_), channel_id=1, source_target_pairs={{0,8},{1,17},{2,10},{3,19},{4,12},{5,21},{6,14},{7,23},{8,0},{9,25... | collective-permute-start | bytes 7077896 | tf_op jit(solution)/shard_map/ppermute | solution.py:52
  360.1 23.5 %collective-permute-start.47 = (bf16[2,2,96,384]{3,2,1,0:T(8,128)(2,1)S(1)}, bf16[2,2,96,384]{3,2,1,0:T(8,128)(2,1)S(1)}, u32[]{:S(2)}, u32[]{:S(2)}) collective-permute-start(bf16[2,2,96,384]{3,2,1,0:T(8,128)(2,1)S(1)} %get-tuple-element.284), channel_id=1, source_target_pairs={{0,4},{1,5},{2,6},{3,7},{4,0},{5,1},{6,2},{7,3},{8,12},{9,13},{10,... | collective-permute-start | bytes 884744 | tf_op jit(solution)/shard_map/ppermute | solution.py:52
  362.1 21.5 %collective-permute-start.48 = (bf16[2,2,96,384]{3,2,1,0:T(8,128)(2,1)S(1)}, bf16[2,2,96,384]{3,2,1,0:T(8,128)(2,1)S(1)}, u32[]{:S(2)}, u32[]{:S(2)}) collective-permute-start(bf16[2,2,96,384]{3,2,1,0:T(8,128)(2,1)S(1)} %get-tuple-element.285), channel_id=1, source_target_pairs={{0,6},{1,7},{2,4},{3,5},{4,2},{5,3},{6,0},{7,1},{8,14},{9,15},{10,... | collective-permute-start | bytes 884744 | tf_op jit(solution)/shard_map/ppermute | solution.py:52
  366.9 27.3 %collective-permute-start.50 = (bf16[4,2,2,96,384]{4,3,2,1,0:T(8,128)(2,1)S(1)}, bf16[4,2,2,96,384]{4,3,2,1,0:T(8,128)(2,1)S(1)}, u32[]{:S(2)}, u32[]{:S(2)}) collective-permute-start(bf16[4,2,2,96,384]{4,3,2,1,0:T(8,128)(2,1)S(1)} %get-tuple-element.287.refs_5_), channel_id=1, source_target_pairs={{0,16},{1,9},{2,18},{3,11},{4,20},{5,13},{6,22},{7,15},{8,24},{9,1... | collective-permute-start | bytes 3538952 | tf_op jit(solution)/shard_map/ppermute | solution.py:52
  395.0 27.8 %collective-permute-start.51 = (bf16[2,2,96,384]{3,2,1,0:T(8,128)(2,1)S(1)}, bf16[2,2,96,384]{3,2,1,0:T(8,128)(2,1)S(1)}, u32[]{:S(2)}, u32[]{:S(2)}) collective-permute-start(bf16[2,2,96,384]{3,2,1,0:T(8,128)(2,1)S(1)} %get-tuple-element.291), channel_id=1, source_target_pairs={{0,2},{1,3},{2,0},{3,1},{4,6},{5,7},{6,4},{7,5},{8,10},{9,11},{10,... | collective-permute-start | bytes 884744 | tf_op jit(solution)/shard_map/ppermute | solution.py:52
  396.8 27.0 %collective-permute-start.52 = (bf16[2,2,96,384]{3,2,1,0:T(8,128)(2,1)S(1)}, bf16[2,2,96,384]{3,2,1,0:T(8,128)(2,1)S(1)}, u32[]{:S(2)}, u32[]{:S(2)}) collective-permute-start(bf16[2,2,96,384]{3,2,1,0:T(8,128)(2,1)S(1)} %get-tuple-element.292), channel_id=1, source_target_pairs={{0,4},{1,5},{2,6},{3,7},{4,0},{5,1},{6,2},{7,3},{8,12},{9,13},{10,... | collective-permute-start | bytes 884744 | tf_op jit(solution)/shard_map/ppermute | solution.py:52
  398.1 25.7 %collective-permute-start.53 = (bf16[2,2,96,384]{3,2,1,0:T(8,128)(2,1)S(1)}, bf16[2,2,96,384]{3,2,1,0:T(8,128)(2,1)S(1)}, u32[]{:S(2)}, u32[]{:S(2)}) collective-permute-start(bf16[2,2,96,384]{3,2,1,0:T(8,128)(2,1)S(1)} %get-tuple-element.293), channel_id=1, source_target_pairs={{0,6},{1,7},{2,4},{3,5},{4,2},{5,3},{6,0},{7,1},{8,14},{9,15},{10,... | collective-permute-start | bytes 884744 | tf_op jit(solution)/shard_map/ppermute | solution.py:52
  401.2 23.4 %collective-permute-start.56 = (bf16[4,2,2,96,384]{4,3,2,1,0:T(8,128)(2,1)S(1)}, bf16[4,2,2,96,384]{4,3,2,1,0:T(8,128)(2,1)S(1)}, u32[]{:S(2)}, u32[]{:S(2)}) collective-permute-start(bf16[4,2,2,96,384]{4,3,2,1,0:T(8,128)(2,1)S(1)} %get-tuple-element.296.refs_2_), channel_id=1, source_target_pairs={{0,16},{1,9},{2,18},{3,11},{4,20},{5,13},{6,22},{7,15},{8,24},{9,1... | collective-permute-start | bytes 3538952 | tf_op jit(solution)/shard_map/ppermute | solution.py:52
  403.4 17.2 %collective-permute-start.55 = (bf16[2,2,96,384]{3,2,1,0:T(8,128)(2,1)S(1)}, bf16[2,2,96,384]{3,2,1,0:T(8,128)(2,1)S(1)}, u32[]{:S(2)}, u32[]{:S(2)}) collective-permute-start(bf16[2,2,96,384]{3,2,1,0:T(8,128)(2,1)S(1)} %get-tuple-element.297), channel_id=1, source_target_pairs={{0,16},{1,9},{2,18},{3,11},{4,20},{5,13},{6,22},{7,15},{8,24},{9,1... | collective-permute-start | bytes 884744 | tf_op jit(solution)/shard_map/ppermute | solution.py:52
  425.5 21.3 %collective-permute-start.57 = (bf16[2,2,96,384]{3,2,1,0:T(8,128)(2,1)S(1)}, bf16[2,2,96,384]{3,2,1,0:T(8,128)(2,1)S(1)}, u32[]{:S(2)}, u32[]{:S(2)}) collective-permute-start(bf16[2,2,96,384]{3,2,1,0:T(8,128)(2,1)S(1)} %get-tuple-element.305), channel_id=1, source_target_pairs={{0,2},{1,3},{2,0},{3,1},{4,6},{5,7},{6,4},{7,5},{8,10},{9,11},{10,... | collective-permute-start | bytes 884744 | tf_op jit(solution)/shard_map/ppermute | solution.py:52
  426.8 23.2 %collective-permute-start.58 = (bf16[2,2,96,384]{3,2,1,0:T(8,128)(2,1)S(1)}, bf16[2,2,96,384]{3,2,1,0:T(8,128)(2,1)S(1)}, u32[]{:S(2)}, u32[]{:S(2)}) collective-permute-start(bf16[2,2,96,384]{3,2,1,0:T(8,128)(2,1)S(1)} %get-tuple-element.306), channel_id=1, source_target_pairs={{0,4},{1,5},{2,6},{3,7},{4,0},{5,1},{6,2},{7,3},{8,12},{9,13},{10,... | collective-permute-start | bytes 884744 | tf_op jit(solution)/shard_map/ppermute | solution.py:52
  428.6 21.5 %collective-permute-start.59 = (bf16[2,2,96,384]{3,2,1,0:T(8,128)(2,1)S(1)}, bf16[2,2,96,384]{3,2,1,0:T(8,128)(2,1)S(1)}, u32[]{:S(2)}, u32[]{:S(2)}) collective-permute-start(bf16[2,2,96,384]{3,2,1,0:T(8,128)(2,1)S(1)} %get-tuple-element.307), channel_id=1, source_target_pairs={{0,6},{1,7},{2,4},{3,5},{4,2},{5,3},{6,0},{7,1},{8,14},{9,15},{10,... | collective-permute-start | bytes 884744 | tf_op jit(solution)/shard_map/ppermute | solution.py:52
  431.9 13.8 %collective-permute-start.61 = (bf16[2,2,96,384]{3,2,1,0:T(8,128)(2,1)S(1)}, bf16[2,2,96,384]{3,2,1,0:T(8,128)(2,1)S(1)}, u32[]{:S(2)}, u32[]{:S(2)}) collective-permute-start(bf16[2,2,96,384]{3,2,1,0:T(8,128)(2,1)S(1)} %get-tuple-element.311), channel_id=1, source_target_pairs={{0,16},{1,9},{2,18},{3,11},{4,20},{5,13},{6,22},{7,15},{8,24},{9,1... | collective-permute-start | bytes 884744 | tf_op jit(solution)/shard_map/ppermute | solution.py:52
  444.8 14.6 %collective-permute-start.73 = (bf16[4,2,2,96,384]{4,3,2,1,0:T(8,128)(2,1)S(1)}, bf16[4,2,2,96,384]{4,3,2,1,0:T(8,128)(2,1)S(1)}, u32[]{:S(2)}, u32[]{:S(2)}) collective-permute-start(bf16[4,2,2,96,384]{4,3,2,1,0:T(8,128)(2,1)S(1)} %get-tuple-element.323.refs_24_), channel_id=1, source_target_pairs={{0,1},{1,0},{2,3},{3,2},{4,5},{5,4},{6,7},{7,6},{8,9},{9,8},{10,11... | collective-permute-start | bytes 3538952 | tf_op jit(solution)/shard_map/ppermute | solution.py:52
  467.4 21.2 %collective-permute-start.77 = (bf16[4,2,2,96,384]{4,3,2,1,0:T(8,128)(2,1)}, bf16[4,2,2,96,384]{4,3,2,1,0:T(8,128)(2,1)}, u32[]{:S(2)}, u32[]{:S(2)}) collective-permute-start(bf16[4,2,2,96,384]{4,3,2,1,0:T(8,128)(2,1)} %get-tuple-element.329.refs_22_), channel_id=1, source_target_pairs={{0,1},{1,0},{2,3},{3,2},{4,5},{5,4},{6,7},{7,6},{8,9},{9,8},{10,11... | collective-permute-start | bytes 3538952 | tf_op jit(solution)/shard_map/ppermute | solution.py:52
  475.0 13.6 %collective-permute-start.76 = (bf16[4,2,2,96,384]{4,3,2,1,0:T(8,128)(2,1)}, bf16[4,2,2,96,384]{4,3,2,1,0:T(8,128)(2,1)}, u32[]{:S(2)}, u32[]{:S(2)}) collective-permute-start(bf16[4,2,2,96,384]{4,3,2,1,0:T(8,128)(2,1)} %get-tuple-element.328.refs_14_.refs_18_.refs_26_), channel_id=1, source_target_pairs={{0,1},{1,0},{2,3},{3,2},{4,5},{5,4},{6,7},{7,6},{8,9},{9,8},{10,11... | collective-permute-start | bytes 3538952 | tf_op jit(solution)/shard_map/ppermute | solution.py:52
  (95 other events, 746.4 us)
